TPU v7x, 32 devices: a whole 2x2x4 slice. The times are simulated.
32 devices in a mesh: dp: 8 (over y, x, core), fsdp: 4 (over z).
Axes of the slice: x: 2, y: 2, z: 4, core: 2. Of those that a mesh axis runs over, the one named last changes fastest.
Arguments:
- inputs: bfloat16 [32, 1024, 1024], P(('dp', 'fsdp')), may hold values from -6 to 6
- cotangent: bfloat16 [32, 1024, 1024], P(('dp', 'fsdp')), may hold values from -6 to 6
- frames: int32 [32], P(('dp', 'fsdp')), may hold values from 204 to 1024, as said below
- w_qkv: float32 [1024, 3072], P(('dp', 'fsdp')), may hold values from -0.1875 to 0.1875
- w_out: float32 [1024, 1024], P(('dp', 'fsdp')), may hold values from -1.5 to 1.5
- w_up: float32 [1024, 4096], P(('dp', 'fsdp')), may hold values from -0.1875 to 0.1875
- w_down: float32 [4096, 1024], P(('dp', 'fsdp')), may hold values from -0.09375 to 0.09375
- norm_gains: float32 [2, 1024], P(None, ('dp', 'fsdp')), may hold values from 0.8 to 6
- first_qkv: float32 [1024, 3072], P(('dp', 'fsdp')), may hold values from -6.1035156e-05 to 6.1035156e-05
- first_out: float32 [1024, 1024], P(('dp', 'fsdp')), may hold values from -6.1035156e-05 to 6.1035156e-05
- first_up: float32 [1024, 4096], P(('dp', 'fsdp')), may hold values from -1.9073486e-05 to 1.9073486e-05
- first_down: float32 [4096, 1024], P(('dp', 'fsdp')), may hold values from -3.0517578e-05 to 3.0517578e-05
- first_gains: float32 [2, 1024], P(None, ('dp', 'fsdp')), may hold values from -0.00024414062 to 0.00024414062
- second_qkv: float32 [1024, 3072], P(('dp', 'fsdp')), may hold values from 5.722046e-10 to 2.2649764e-09
- second_out: float32 [1024, 1024], P(('dp', 'fsdp')), may hold values from 5.722046e-10 to 2.2649764e-09
- second_up: float32 [1024, 4096], P(('dp', 'fsdp')), may hold values from 2.9802324e-11 to 1.192093e-10
- second_down: float32 [4096, 1024], P(('dp', 'fsdp')), may hold values from 5.960465e-11 to 2.384186e-10
- second_gains: float32 [2, 1024], P(None, ('dp', 'fsdp')), may hold values from 6.3180923e-09 to 2.503395e-08
- shadow_qkv: float32 [1024, 3072], P(('dp', 'fsdp')), may hold values from -0.1875 to 0.1875
- shadow_out: float32 [1024, 1024], P(('dp', 'fsdp')), may hold values from -1.5 to 1.5
- shadow_up: float32 [1024, 4096], P(('dp', 'fsdp')), may hold values from -0.1875 to 0.1875
- shadow_down: float32 [4096, 1024], P(('dp', 'fsdp')), may hold values from -0.09375 to 0.09375
- shadow_gains: float32 [2, 1024], P(None, ('dp', 'fsdp')), may hold values from 0.5 to 1.5
Outputs:
- out_layer: bfloat16 [32, 1024, 1024], P(('dp', 'fsdp'))
- grad_input: float32 [32, 1024, 1024], P(('dp', 'fsdp'))
- grad_norm: float32 [], replicated
- qkv_new: float32 [1024, 3072], P(('dp', 'fsdp'))
- out_new: float32 [1024, 1024], P(('dp', 'fsdp'))
- up_new: float32 [1024, 4096], P(('dp', 'fsdp'))
- down_new: float32 [4096, 1024], P(('dp', 'fsdp'))
- gains_new: float32 [2, 1024], P(None, ('dp', 'fsdp'))
- qkv_first: float32 [1024, 3072], P(('dp', 'fsdp'))
- out_first: float32 [1024, 1024], P(('dp', 'fsdp'))
- up_first: float32 [1024, 4096], P(('dp', 'fsdp'))
- down_first: float32 [4096, 1024], P(('dp', 'fsdp'))
- gains_first: float32 [2, 1024], P(None, ('dp', 'fsdp'))
- qkv_second: float32 [1024, 3072], P(('dp', 'fsdp'))
- out_second: float32 [1024, 1024], P(('dp', 'fsdp'))
- up_second: float32 [1024, 4096], P(('dp', 'fsdp'))
- down_second: float32 [4096, 1024], P(('dp', 'fsdp'))
- gains_second: float32 [2, 1024], P(None, ('dp', 'fsdp'))
- qkv_shadow: float32 [1024, 3072], P(('dp', 'fsdp'))
- out_shadow: float32 [1024, 1024], P(('dp', 'fsdp'))
- up_shadow: float32 [1024, 4096], P(('dp', 'fsdp'))
- down_shadow: float32 [4096, 1024], P(('dp', 'fsdp'))
- gains_shadow: float32 [2, 1024], P(None, ('dp', 'fsdp'))
Inputs may be any that keep to these rules, and one draw needn't show every extreme that they name: Each utterance's count of valid frames; some utterance has exactly 1024.
All inputs are finite; a program needn't handle non-finite values.
Results may differ from a plain program's by a relative error of at most 0.012.
The roundings to bfloat16 on the way count: a program that leaves them out, or rounds other values in their place, can miss the bound.
Values may be sent and summed in bfloat16 or wider, within the bound.
No kernel may reach another device: no remote copies, remote signals or barrier semaphores. Data moves between devices by JAX's collectives and lax.ppermute only.
A program may use at most 320 MiB of HBM per device.

v0:
```python
import jax
import jax.numpy as jnp
from jax import lax
from jax.sharding import PartitionSpec as P

D = 1024
HEAD_DIM = 64
FF = 4096
STEP = 7
FANO = 16


NORM_EPS = 1e-06
ADAM_EPS = 1e-08
BETA_ONE = 0.9
BETA_TWO = 0.95
SHADOW_KEEP = 0.8
CLIP_NORM = 1.0


def norm_apply(residual, gain_row):
    rms_inv = lax.rsqrt(jnp.mean(residual * residual, axis=-1, keepdims=True) + NORM_EPS)
    return residual * rms_inv * gain_row


def attend(queries, key_vecs, val_vecs, valid_count, block_rows):
    length, head_count, head_dim = queries.shape
    scaling = head_dim ** (-0.5)
    col_ids = jnp.arange(length)

    def one_block(offset):
        q_block = lax.dynamic_slice_in_dim(queries, offset, block_rows, 0)
        row_ids = offset + jnp.arange(block_rows)
        allowed = (col_ids[None, :] <= row_ids[:, None]) & (col_ids[None, :] < valid_count)
        scores = (
            jnp.einsum("qhd,khd->hqk", q_block, key_vecs, preferred_element_type=jnp.float32)
            * scaling
        )
        scores = jnp.where(allowed[None], scores, -1e30)
        peak_score = jnp.max(scores, axis=-1, keepdims=True)
        raised = jnp.exp(scores - peak_score)
        row_total = jnp.sum(raised, axis=-1, keepdims=True)
        attn_probs = (raised / row_total).astype(jnp.bfloat16)
        result = jnp.einsum(
            "hqk,khd->qhd", attn_probs, val_vecs, preferred_element_type=jnp.float32
        )
        return (result.astype(jnp.bfloat16), (peak_score + jnp.log(row_total))[..., 0])

    offsets = jnp.arange(length // block_rows) * block_rows
    results, log_total = lax.map(one_block, offsets)
    return (results.reshape(length, head_count * head_dim), log_total)


def attend_back(queries, key_vecs, val_vecs, head_grad, valid_count, log_total, block_rows):
    length, head_count, head_dim = queries.shape
    scaling = head_dim ** (-0.5)
    col_ids = jnp.arange(length)

    def one_block(running, packed):
        key_grad, val_grad = running
        offset, log_block = packed
        q_block = lax.dynamic_slice_in_dim(queries, offset, block_rows, 0)
        g_block = lax.dynamic_slice_in_dim(head_grad, offset, block_rows, 0)
        row_ids = offset + jnp.arange(block_rows)
        allowed = (col_ids[None, :] <= row_ids[:, None]) & (col_ids[None, :] < valid_count)
        scores = (
            jnp.einsum("qhd,khd->hqk", q_block, key_vecs, preferred_element_type=jnp.float32)
            * scaling
        )
        scores = jnp.where(allowed[None], scores, -1e30)
        attn_probs = jnp.exp(scores - log_block[..., None])
        probs_low = attn_probs.astype(jnp.bfloat16)
        val_grad = val_grad + jnp.einsum(
            "hqk,qhd->khd", probs_low, g_block, preferred_element_type=jnp.float32
        )
        prob_grad = jnp.einsum(
            "qhd,khd->hqk", g_block, val_vecs, preferred_element_type=jnp.float32
        )
        score_grad = attn_probs * (
            prob_grad - jnp.sum(attn_probs * prob_grad, axis=-1, keepdims=True)
        )
        score_low = score_grad.astype(jnp.bfloat16)
        query_grad = (
            jnp.einsum("hqk,khd->qhd", score_low, key_vecs, preferred_element_type=jnp.float32)
            * scaling
        )
        key_grad = (
            key_grad
            + jnp.einsum("hqk,qhd->khd", score_low, q_block, preferred_element_type=jnp.float32)
            * scaling
        )
        return ((key_grad, val_grad), query_grad)

    offsets = jnp.arange(length // block_rows) * block_rows
    zeros_kv = jnp.zeros((length, head_count, head_dim), jnp.float32)
    (key_grad, val_grad), query_grad = lax.scan(
        one_block, (zeros_kv, zeros_kv), (offsets, log_total)
    )
    model_width = head_count * head_dim
    return (
        query_grad.reshape(length, model_width),
        key_grad.reshape(length, model_width),
        val_grad.reshape(length, model_width),
    )


def adam_step(weight, first, second, gradient, clip_factor, step_rate, decay_rate, shadow):
    clipped = gradient * clip_factor
    first_new = BETA_ONE * first + (1.0 - BETA_ONE) * clipped
    second_new = BETA_TWO * second + (1.0 - BETA_TWO) * clipped * clipped
    first_hat = first_new / (1.0 - BETA_ONE**STEP)
    second_hat = second_new / (1.0 - BETA_TWO**STEP)
    weight_new = weight - step_rate * (
        first_hat / (jnp.sqrt(second_hat) + ADAM_EPS) + decay_rate * weight
    )
    shadow_new = SHADOW_KEEP * shadow + (1.0 - SHADOW_KEEP) * weight_new
    return (weight_new, first_new, second_new, shadow_new)


def body(
    inputs,
    cotangent,
    frames,
    w_qkv,
    w_out,
    w_up,
    w_down,
    norm_gains,
    first_qkv,
    first_out,
    first_up,
    first_down,
    first_gains,
    second_qkv,
    second_out,
    second_up,
    second_down,
    second_gains,
    shadow_qkv,
    shadow_out,
    shadow_up,
    shadow_down,
    shadow_gains,
):
    gathered = (
        lax.all_gather(w_qkv.astype(jnp.bfloat16), ("dp", "fsdp"), axis=0, tiled=True),
        lax.all_gather(w_out.astype(jnp.bfloat16), ("dp", "fsdp"), axis=0, tiled=True),
        lax.all_gather(w_up.astype(jnp.bfloat16), ("dp", "fsdp"), axis=0, tiled=True),
        lax.all_gather(w_down.astype(jnp.bfloat16), ("dp", "fsdp"), axis=0, tiled=True),
        lax.all_gather(norm_gains.astype(jnp.bfloat16), ("dp", "fsdp"), axis=1, tiled=True),
    )
    wq_full, wo_full, wu_full, wd_full, gain_full = gathered
    length = inputs.shape[1]
    model_width = inputs.shape[2]
    head_count = model_width // HEAD_DIM
    block_rows = min(512, length)
    residual = inputs[0].astype(jnp.float32)
    valid_count = frames[0]
    normed_one = norm_apply(residual, gain_full[0].astype(jnp.float32)).astype(jnp.bfloat16)
    qkv_vals = jnp.dot(normed_one, wq_full, preferred_element_type=jnp.float32).astype(jnp.bfloat16)
    queries = qkv_vals[:, :model_width].reshape(length, head_count, HEAD_DIM)
    key_vecs = qkv_vals[:, model_width : 2 * model_width].reshape(length, head_count, HEAD_DIM)
    val_vecs = qkv_vals[:, 2 * model_width :].reshape(length, head_count, HEAD_DIM)
    attn_out, log_total = attend(queries, key_vecs, val_vecs, valid_count, block_rows)
    middle = residual + jnp.dot(attn_out, wo_full, preferred_element_type=jnp.float32)
    normed_two = norm_apply(middle, gain_full[1].astype(jnp.float32)).astype(jnp.bfloat16)
    pre_act = jnp.dot(normed_two, wu_full, preferred_element_type=jnp.float32)
    activation = jax.nn.gelu(pre_act).astype(jnp.bfloat16)
    layer_out = middle + jnp.dot(activation, wd_full, preferred_element_type=jnp.float32)
    wq_back, wo_back, wu_back, wd_back, gain_back = (
        lax.all_gather(w_qkv.astype(jnp.bfloat16), ("dp", "fsdp"), axis=0, tiled=True),
        lax.all_gather(w_out.astype(jnp.bfloat16), ("dp", "fsdp"), axis=0, tiled=True),
        lax.all_gather(w_up.astype(jnp.bfloat16), ("dp", "fsdp"), axis=0, tiled=True),
        lax.all_gather(w_down.astype(jnp.bfloat16), ("dp", "fsdp"), axis=0, tiled=True),
        lax.all_gather(norm_gains.astype(jnp.bfloat16), ("dp", "fsdp"), axis=1, tiled=True),
    )
    positions = jnp.arange(length)
    valid_mask = (positions < valid_count).astype(jnp.float32)
    out_grad = cotangent[0].astype(jnp.float32) * valid_mask[:, None]
    branch_low = out_grad.astype(jnp.bfloat16)
    grad_down = jnp.einsum("tf,td->fd", activation, branch_low, preferred_element_type=jnp.float32)
    activ_grad = jnp.einsum("td,fd->tf", branch_low, wd_back, preferred_element_type=jnp.float32)
    _, gelu_pull = jax.vjp(jax.nn.gelu, pre_act)
    pre_grad = gelu_pull(activ_grad)[0].astype(jnp.bfloat16)
    grad_up = jnp.einsum("td,tf->df", normed_two, pre_grad, preferred_element_type=jnp.float32)
    normed_two_grad = jnp.einsum("tf,df->td", pre_grad, wu_back, preferred_element_type=jnp.float32)
    _, second_pull = jax.vjp(norm_apply, middle, gain_back[1].astype(jnp.float32))
    middle_part, gain_grad_two = second_pull(normed_two_grad)
    middle_grad = out_grad + middle_part
    attn_low = middle_grad.astype(jnp.bfloat16)
    grad_out = jnp.einsum("td,te->de", attn_out, attn_low, preferred_element_type=jnp.float32)
    head_grad = jnp.einsum("te,de->td", attn_low, wo_back, preferred_element_type=jnp.float32)
    head_grad = head_grad.astype(jnp.bfloat16).reshape(length, head_count, HEAD_DIM)
    query_grad, key_grad, val_grad = attend_back(
        queries, key_vecs, val_vecs, head_grad, valid_count, log_total, block_rows
    )
    qkv_grad = jnp.concatenate([query_grad, key_grad, val_grad], axis=1).astype(jnp.bfloat16)
    grad_qkv = jnp.einsum("td,te->de", normed_one, qkv_grad, preferred_element_type=jnp.float32)
    normed_one_grad = jnp.einsum("te,de->td", qkv_grad, wq_back, preferred_element_type=jnp.float32)
    _, first_pull = jax.vjp(norm_apply, residual, gain_back[0].astype(jnp.float32))
    residual_part, gain_grad_one = first_pull(normed_one_grad)
    input_grad = middle_grad + residual_part
    qkv_shard, out_shard, up_shard, down_shard, gain_shard = (
        lax.psum_scatter(grad_qkv, ("dp", "fsdp"), scatter_dimension=0, tiled=True),
        lax.psum_scatter(grad_out, ("dp", "fsdp"), scatter_dimension=0, tiled=True),
        lax.psum_scatter(grad_up, ("dp", "fsdp"), scatter_dimension=0, tiled=True),
        lax.psum_scatter(grad_down, ("dp", "fsdp"), scatter_dimension=0, tiled=True),
        lax.psum_scatter(
            jnp.stack([gain_grad_one, gain_grad_two]),
            ("dp", "fsdp"),
            scatter_dimension=1,
            tiled=True,
        ),
    )
    shards = (qkv_shard, out_shard, up_shard, down_shard, gain_shard)
    local_sq = sum((jnp.sum(grad_piece * grad_piece) for grad_piece in shards))
    total_sq = lax.psum(local_sq, ("dp", "fsdp"))
    grad_norm = jnp.sqrt(total_sq)
    clip_factor = jnp.minimum(1.0, CLIP_NORM / grad_norm)
    masters = (w_qkv, w_out, w_up, w_down, norm_gains)
    firsts = (first_qkv, first_out, first_up, first_down, first_gains)
    seconds = (second_qkv, second_out, second_up, second_down, second_gains)
    shadows = (shadow_qkv, shadow_out, shadow_up, shadow_down, shadow_gains)
    rates = (0.6 / D**0.5, 0.6 / FANO**0.5, 0.6 / D**0.5, 0.6 / FF**0.5, 1.0)
    decays = (0.1, 0.1, 0.1, 0.1, 0.0)
    updated = [
        adam_step(
            masters[index],
            firsts[index],
            seconds[index],
            shards[index],
            clip_factor,
            rates[index],
            decays[index],
            shadows[index],
        )
        for index in range(5)
    ]
    return (
        layer_out.astype(jnp.bfloat16)[None],
        input_grad[None],
        grad_norm,
        updated[0][0],
        updated[1][0],
        updated[2][0],
        updated[3][0],
        updated[4][0],
        updated[0][1],
        updated[1][1],
        updated[2][1],
        updated[3][1],
        updated[4][1],
        updated[0][2],
        updated[1][2],
        updated[2][2],
        updated[3][2],
        updated[4][2],
        updated[0][3],
        updated[1][3],
        updated[2][3],
        updated[3][3],
        updated[4][3],
    )


def solution(mesh):
    return jax.shard_map(
        body,
        mesh=mesh,
        in_specs=(
            P(("dp", "fsdp"), None, None),
            P(("dp", "fsdp"), None, None),
            P(("dp", "fsdp")),
            P(("dp", "fsdp"), None),
            P(("dp", "fsdp"), None),
            P(("dp", "fsdp"), None),
            P(("dp", "fsdp"), None),
            P(None, ("dp", "fsdp")),
            P(("dp", "fsdp"), None),
            P(("dp", "fsdp"), None),
            P(("dp", "fsdp"), None),
            P(("dp", "fsdp"), None),
            P(None, ("dp", "fsdp")),
            P(("dp", "fsdp"), None),
            P(("dp", "fsdp"), None),
            P(("dp", "fsdp"), None),
            P(("dp", "fsdp"), None),
            P(None, ("dp", "fsdp")),
            P(("dp", "fsdp"), None),
            P(("dp", "fsdp"), None),
            P(("dp", "fsdp"), None),
            P(("dp", "fsdp"), None),
            P(None, ("dp", "fsdp")),
        ),
        out_specs=(
            P(("dp", "fsdp"), None, None),
            P(("dp", "fsdp"), None, None),
            P(),
            P(("dp", "fsdp"), None),
            P(("dp", "fsdp"), None),
            P(("dp", "fsdp"), None),
            P(("dp", "fsdp"), None),
            P(None, ("dp", "fsdp")),
            P(("dp", "fsdp"), None),
            P(("dp", "fsdp"), None),
            P(("dp", "fsdp"), None),
            P(("dp", "fsdp"), None),
            P(None, ("dp", "fsdp")),
            P(("dp", "fsdp"), None),
            P(("dp", "fsdp"), None),
            P(("dp", "fsdp"), None),
            P(("dp", "fsdp"), None),
            P(None, ("dp", "fsdp")),
            P(("dp", "fsdp"), None),
            P(("dp", "fsdp"), None),
            P(("dp", "fsdp"), None),
            P(("dp", "fsdp"), None),
            P(None, ("dp", "fsdp")),
        ),
        check_vma=False,
    )
```

profile of v0, /device:TPU:0, one launch (start us, length us, event | category | flops | bytes accessed | tf_op | source)
XLA Modules:
  0.0 1830.0 jit_solution(17258193591502971408)
XLA Ops:
  16.3 69.6 %all-gather = bf16[32,32,2]{1,2,0:T(2,128)(2,1)S(1)} all-gather(bf16[1,32,2]{1,2,0:T(2,128)(2,1)S(1)} %convert_bitcast_fusion), channel_id=1, replica_groups=mesh['dp'=8,'fsdp'=4] {'dp','fsdp'}, dimensions={0}, use_global_device_ids=true | all-gather | bytes 4224 | tf_op jit(solution)/shard_map/all_gather | solution.py:150
  90.0 4.1 copy.83
  94.2 10.1 convolution_convert_fusion
  107.3 4.1 copy.80
  111.4 4.0 copy.79
  117.9 106.9 %while.30 = (s32[]{:T(128)}, bf16[2,512,16,64]{1,3,2,0:T(8,128)(2,1)}, f32[2,16,512]{2,1,0:T(8,128)S(1)}, s32[2]{0:T(128)S(1)}, s32[]{:T(128)}, /*index=5*/bf16[...) while((s32[]{:T(128)}, ...), condition=%wide.region_4.5_spmd.clone.clone, body=%wide.region_1.4_spmd.clone.clone.sunk | while | flops 2249713152 | bytes 126097648 | solution.py:50
  122.4 16.6 fusion.123
  139.0 15.2 fusion.124
  154.3 15.0 fusion.125
  174.9 16.5 fusion.123
  191.3 16.3 fusion.124
  207.6 15.5 fusion.125
  224.8 3.9 copy.81
  230.6 7.0 multiply_reduce_fusion.3
  237.7 16.3 fusion.77
  254.0 47.6 %all-gather.12.cloned.1.call-done = bf16[4096,1024]{1,0:T(8,128)(2,1)} async-done(((bf16[128,1024]{1,0:T(8,128)(2,1)}), bf16[4096,1024]{1,0:T(8,128)(2,1)}) %all-gather.12.cloned.1.call-update) | async-done | bytes 8388624 | tf_op jit(solution)/shard_map/all_gather | solution.py:149
  301.6 23.9 %fusion.41 = bf16[1024,4096]{1,0:T(8,128)(2,1)} fusion(f32[1024,4096]{1,0:T(8,128)} %fusion.77, bf16[4096,1024]{1,0:T(8,128)(2,1)} %all-gather.12.cloned.1.call-done, bf16[1,1024,1024]{1,2,0:T(8,128)(2,1)S(1)} %copy-done.6, f32[1024]{0:T(1024)S(1)} %copy-done.30), kind=kOutput, calls=%fused_computation.55 | convolution fusion | flops 8676966400 | bytes 35655680 | tf_op jit(solution)/shard_map/td,fd->tf/dot_general | solution.py:182
  325.5 15.6 multiply_reduce_fusion.1
  342.7 3.6 convolution_convert_fusion.1
  346.3 226.5 %while.31 = (s32[]{:T(128)}, f32[1024,16,64]{0,2,1:T(8,128)}, f32[1024,16,64]{0,2,1:T(8,128)}, bf16[2,512,16,64]{1,3,2,0:T(8,128)(2,1)}, s32[2]{0:T(128)S(1)}, /...) while((s32[]{:T(128)}, f32[1024,16,64]{0,2,1:T(8,128)}, ...), condition=%wide.region_9.10_spmd.clone.clone, body=%wide.region_7.9_spmd.clone.clone.sunk | while | flops 5501347328 | bytes 350460160 | solution.py:96
  351.0 17.7 fusion.135
  368.7 17.8 bitcast_add_fusion.5
  386.5 26.0 %multiply_reduce_fusion.10 = (f32[16,512]{1,0:T(8,128)S(1)}, f32[16,512,1024]{2,1,0:T(8,128)}) fusion(f32[16,512,1024]{2,1,0:T(8,128)} %fusion.135, f32[16,512]{1,0:T(8,128)S(1)} %dynamic-slice_bitcast_fusion.2, pred[512,1024]{1,0:T(8,128)(4,1)S(1)} %fusion.136, bf16[1024,16,64]{0,2,1:T(8,128)(2,1)} %get-tuple-element.610, ...), kind=kOutput, calls=%fused_computation.22.clone.1 | convolution fusion | flops 1115676672 | bytes 70844416 | tf_op jit(solution)/shard_map/while/body/eval_jaxpr/qhd,khd->hqk/dot_general | solution.py:76
  412.5 27.8 %multiply_convert_fusion.8 = bf16[16,512,1024]{2,1,0:T(8,128)(2,1)} fusion(f32[16,512,1024]{2,1,0:T(8,128)} %get-tuple-element.537, f32[16,512,1024]{2,1,0:T(8,128)} %fusion.135, f32[16,512]{1,0:T(8,128)S(1)} %get-tuple-element.538, f32[16,512]{1,0:T(8,128)S(1)} %dynamic-slice_bitcast_fusion.2, pred[512,1024]{1,0:T(8,128)(4,1)S(1)} %fusion.136), kind=kLoop, calls=%fused_computation.21.clone.1 | loop fusion | flops 50331648 | bytes 84475904 | tf_op jit(solution)/shard_map/while/body/eval_jaxpr/convert_element_type | solution.py:82
  440.3 10.3 bitcast_dynamic-update-slice_fusion.5
  451.8 6.7 bitcast_add_fusion.4
  462.8 17.6 fusion.135
  480.4 19.1 %bitcast_add_fusion.5 = f32[1024,16,64]{0,2,1:T(8,128)} fusion(f32[1024,16,64]{0,2,1:T(8,128)} %get-tuple-element.588, f32[16,512,1024]{2,1,0:T(8,128)} %fusion.135, f32[16,512]{1,0:T(8,128)S(1)} %dynamic-slice_bitcast_fusion.2, pred[512,1024]{1,0:T(8,128)(4,1)S(1)} %fusion.136, pred[]{:T(512)S(6)} %compare.3, ...), kind=kOutput, calls=%fused_computation.27.clone.1 | convolution fusion | flops 1109393408 | bytes 43548676 | tf_op jit(solution)/shard_map/while/body/eval_jaxpr/hqk,qhd->khd/dot_general | solution.py:73
  499.5 26.0 %multiply_reduce_fusion.10 = (f32[16,512]{1,0:T(8,128)S(1)}, f32[16,512,1024]{2,1,0:T(8,128)}) fusion(f32[16,512,1024]{2,1,0:T(8,128)} %fusion.135, f32[16,512]{1,0:T(8,128)S(1)} %dynamic-slice_bitcast_fusion.2, pred[512,1024]{1,0:T(8,128)(4,1)S(1)} %fusion.136, bf16[1024,16,64]{0,2,1:T(8,128)(2,1)} %get-tuple-element.610, ...), kind=kOutput, calls=%fused_computation.22.clone.1 | convolution fusion | flops 1115676672 | bytes 70844416 | tf_op jit(solution)/shard_map/while/body/eval_jaxpr/qhd,khd->hqk/dot_general | solution.py:76
  525.5 27.8 %multiply_convert_fusion.8 = bf16[16,512,1024]{2,1,0:T(8,128)(2,1)} fusion(f32[16,512,1024]{2,1,0:T(8,128)} %get-tuple-element.537, f32[16,512,1024]{2,1,0:T(8,128)} %fusion.135, f32[16,512]{1,0:T(8,128)S(1)} %get-tuple-element.538, f32[16,512]{1,0:T(8,128)S(1)} %dynamic-slice_bitcast_fusion.2, pred[512,1024]{1,0:T(8,128)(4,1)S(1)} %fusion.136), kind=kLoop, calls=%fused_computation.21.clone.1 | loop fusion | flops 50331648 | bytes 84475904 | tf_op jit(solution)/shard_map/while/body/eval_jaxpr/convert_element_type | solution.py:82
  553.3 10.3 bitcast_dynamic-update-slice_fusion.5
  564.8 7.9 bitcast_add_fusion.4
  572.9 3.9 copy.85
  584.3 8.8 fusion.45
  594.2 7.2 fusion.61
  601.5 14.0 fusion.52
  616.2 15.8 fusion.76
  632.6 19.8 %fusion.55 = f32[4096,1024]{1,0:T(8,128)} fusion(bf16[1,1024,1024]{1,2,0:T(8,128)(2,1)} %copy.83, f32[1024]{0:T(1024)S(1)} %copy-done.31, f32[1024,4096]{1,0:T(8,128)} %fusion.77), kind=kOutput, calls=%fused_computation.86 | convolution fusion | flops 8630829056 | bytes 35655680 | tf_op jit(solution)/shard_map/tf,td->fd/dot_general | solution.py:181
  652.5 16.7 fusion.54
  669.2 4.2 copy.89
  673.4 6.5 fusion.48
  679.9 47.5 %reduce-scatter.16.cloned.1.call-done = f32[32,2]{1,0:T(8,128)} async-done(((f32[1024,2]{1,0:T(8,128)}), f32[32,2]{1,0:T(8,128)}) %reduce-scatter.16.cloned.1.call-update) | async-done | bytes 272
  728.8 144.5 %reduce-scatter.10.cloned.1.call-done = f32[32,1024]{1,0:T(8,128)} async-done(((f32[1024,1024]{1,0:T(8,128)}), f32[32,1024]{1,0:T(8,128)}) %reduce-scatter.10.cloned.1.call-update) | async-done | bytes 131088 | tf_op jit(solution)/shard_map/reduce_scatter | solution.py:205
  874.8 160.1 %reduce-scatter.8.cloned.1.call-done = f32[32,3072]{1,0:T(8,128)} async-done(((f32[1024,3072]{1,0:T(8,128)}), f32[32,3072]{1,0:T(8,128)}) %reduce-scatter.8.cloned.1.call-update) | async-done | bytes 393232 | tf_op jit(solution)/shard_map/reduce_scatter | solution.py:204
  1037.9 362.6 %reduce-scatter.12.cloned.1.call-done = f32[32,4096]{1,0:T(8,128)} async-done(((f32[1024,4096]{1,0:T(8,128)}), f32[32,4096]{1,0:T(8,128)}) %reduce-scatter.12.cloned.1.call-update) | async-done | bytes 524304 | tf_op jit(solution)/shard_map/reduce_scatter | solution.py:206
  1402.9 362.0 %reduce-scatter.14.cloned.1.call-done = f32[128,1024]{1,0:T(8,128)} async-done(((f32[4096,1024]{1,0:T(8,128)}), f32[128,1024]{1,0:T(8,128)}) %reduce-scatter.14.cloned.1.call-update) | async-done | bytes 524304 | tf_op jit(solution)/shard_map/reduce_scatter | solution.py:207
  1768.1 5.4 copy.90
  1773.6 38.2 %psum.7 = f32[]{:T(128)} all-reduce(f32[]{:T(128)S(6)} %add.222), channel_id=1, replica_groups=mesh['dp'=8,'fsdp'=4] {'dp','fsdp'}, use_global_device_ids=true, to_apply=%region_23.24 | all-reduce | flops 1 | bytes 8 | tf_op jit(solution)/shard_map/psum | solution.py:217
  (180 shorter events, 63.1 us)
Async XLA Ops:
  7.2 87.0 %all-gather.6.cloned.1.call-start = ((), (), s32[]{:S(2)}) async-start(), calls=%async_computation.5 | async-start | bytes 6488064 | tf_op jit(solution)/shard_map/all_gather | solution.py:146
  9.0 221.7 %all-gather.8.cloned.1.call-start = ((), (), s32[]{:S(2)}) async-start(), calls=%async_computation.6 | async-start | bytes 2162688 | tf_op jit(solution)/shard_map/all_gather | solution.py:147
  10.6 227.0 %all-gather.10.cloned.1.call-start = ((), (), s32[]{:S(2)}) async-start(), calls=%async_computation.7 | async-start | bytes 8650752 | tf_op jit(solution)/shard_map/all_gather | solution.py:148
  12.4 289.1 %all-gather.12.cloned.1.call-start = ((), (), s32[]{:S(2)}) async-start(), calls=%async_computation.8 | async-start | bytes 8650752 | tf_op jit(solution)/shard_map/all_gather | solution.py:149
  14.3 713.1 %reduce-scatter.16.cloned.1.call-start = ((), (), s32[]{:S(2)}) async-start(), calls=%async_computation.13 | async-start | bytes 540672
  86.6 7.5 copy-start.38
  89.5 14.8 copy-start.2
  90.0 14.3 copy-start.28
  90.0 14.3 copy-start.36
  107.3 8.1 copy-start.7
  139.0 15.2 copy-start.16
  191.3 16.3 copy-start.16
  224.8 5.8 copy-start.3
  230.6 7.0 copy-start.34
  237.6 103.5 %copy-start.32 = (f32[1024]{0:T(1024)}, f32[1024]{0:T(1024)S(1)}, u32[]{:S(2)}) copy-start(f32[1024]{0:T(1024)S(1)} %fusion.72) | copy-start | bytes 12292
  237.6 63.9 %copy-start.6 = (bf16[1,1024,1024]{1,2,0:T(8,128)(2,1)S(1)}, bf16[1,1024,1024]{1,2,0:T(8,128)(2,1)}, u32[]{:S(2)}) copy-start(bf16[1,1024,1024]{1,2,0:T(8,128)(2,1)} %copy.83) | copy-start | bytes 6291460
  237.6 63.9 %copy-start.30 = (f32[1024]{0:T(1024)S(1)}, f32[1024]{0:T(1024)}, u32[]{:S(2)}) copy-start(f32[1024]{0:T(1024)} %fusion.70) | copy-start | bytes 12292
  325.5 15.6 copy-start.9
  440.3 11.5 copy-start
  553.3 11.5 copy-start
  572.8 4.5 copy-start.1
  577.4 6.3 copy-start.44
  577.7 15.4 copy-start.10
  577.7 6.5 copy-start.4
  577.7 6.5 copy-start.37
  577.7 6.5 copy-start.39
  581.4 11.7 copy-start.11
  584.3 8.8 copy-start.40
  594.2 279.1 %reduce-scatter.10.cloned.1.call-start = ((), (), s32[]{:S(2)}) async-start(), calls=%async_computation.10 | async-start | bytes 4325376 | tf_op jit(solution)/shard_map/reduce_scatter | solution.py:205
  601.4 433.5 %reduce-scatter.8.cloned.1.call-start = ((), (), s32[]{:S(2)}) async-start(), calls=%async_computation.9 | async-start | bytes 12976128 | tf_op jit(solution)/shard_map/reduce_scatter | solution.py:204
  615.5 785.0 %reduce-scatter.12.cloned.1.call-start = ((), (), s32[]{:S(2)}) async-start(), calls=%async_computation.11 | async-start | bytes 17301504 | tf_op jit(solution)/shard_map/reduce_scatter | solution.py:206
  632.0 1133.0 %reduce-scatter.14.cloned.1.call-start = ((), (), s32[]{:S(2)}) async-start(), calls=%async_computation.12 | async-start | bytes 17301504 | tf_op jit(solution)/shard_map/reduce_scatter | solution.py:207
  1768.1 44.5 %copy-start.41 = (f32[2,32]{1,0:T(2,128)S(1)}, f32[2,32]{1,0:T(2,128)}, u32[]{:S(2)}) copy-start(f32[2,32]{1,0:T(2,128)} %param.34) | copy-start | bytes 772
  1768.1 44.5 %copy-start.42 = (f32[2,32]{1,0:T(2,128)S(1)}, f32[2,32]{1,0:T(2,128)}, u32[]{:S(2)}) copy-start(f32[2,32]{1,0:T(2,128)} %param.49) | copy-start | bytes 772
  1768.1 44.5 %copy-start.43 = (f32[2,32]{1,0:T(2,128)S(1)}, f32[2,32]{1,0:T(2,128)}, u32[]{:S(2)}) copy-start(f32[2,32]{1,0:T(2,128)} %param.39) | copy-start | bytes 772
  1768.1 45.7 %copy-start.27 = (f32[32,1024]{1,0:T(8,128)S(1)}, f32[32,1024]{1,0:T(8,128)}, u32[]{:S(2)}) copy-start(f32[32,1024]{1,0:T(8,128)} %param.31) | copy-start | bytes 393220
  1768.1 47.7 %copy-start.19 = (f32[32,3072]{1,0:T(8,128)S(1)}, f32[32,3072]{1,0:T(8,128)}, u32[]{:S(2)}) copy-start(f32[32,3072]{1,0:T(8,128)} %param.30) | copy-start | bytes 1179652
  1768.1 47.7 %copy-start.20 = (f32[32,3072]{1,0:T(8,128)S(1)}, f32[32,3072]{1,0:T(8,128)}, u32[]{:S(2)}) copy-start(f32[32,3072]{1,0:T(8,128)} %reduce-scatter.8.cloned.1.call-done) | copy-start | bytes 1179652
  1773.6 45.0 %copy-start.12 = (f32[128,1024]{1,0:T(8,128)S(1)}, f32[128,1024]{1,0:T(8,128)}, u32[]{:S(2)}) copy-start(f32[128,1024]{1,0:T(8,128)} %param.33) | copy-start | bytes 1572868
  1773.6 45.0 %copy-start.15 = (f32[128,1024]{1,0:T(8,128)S(1)}, f32[128,1024]{1,0:T(8,128)}, u32[]{:S(2)}) copy-start(f32[128,1024]{1,0:T(8,128)} %reduce-scatter.14.cloned.1.call-done) | copy-start | bytes 1572868
  1773.6 45.0 %copy-start.21 = (f32[128,1024]{1,0:T(8,128)S(1)}, f32[128,1024]{1,0:T(8,128)}, u32[]{:S(2)}) copy-start(f32[128,1024]{1,0:T(8,128)} %param.48) | copy-start | bytes 1572868
  1773.6 45.0 %copy-start.22 = (f32[128,1024]{1,0:T(8,128)S(1)}, f32[128,1024]{1,0:T(8,128)}, u32[]{:S(2)}) copy-start(f32[128,1024]{1,0:T(8,128)} %param.38) | copy-start | bytes 1572868
  1773.6 45.0 %copy-start.23 = (f32[128,1024]{1,0:T(8,128)S(1)}, f32[128,1024]{1,0:T(8,128)}, u32[]{:S(2)}) copy-start(f32[128,1024]{1,0:T(8,128)} %param.43) | copy-start | bytes 1572868
  1815.8 4.5 copy-start.13
  1815.8 4.5 copy-start.14
  1815.8 4.5 copy-start.24
  1815.8 4.5 copy-start.25
  1815.8 4.5 copy-start.26
  (10 other events, 21.9 us)
Sparse Core Ops, SparseCore 0:
  11.5 72.2 all-gather.5
  87.3 54.9 all-gather.7
  145.9 76.2 all-gather.9
  225.5 75.9 all-gather.11
  594.3 133.0 reduce-scatter.15
  729.6 143.6 reduce-scatter.9
  880.3 154.5 reduce-scatter.7
  1037.2 363.2 reduce-scatter.11
  1402.8 362.1 reduce-scatter.13
where the time goes:
time: 1840 us; the launch traced here: 1830 us
  waiting for transfers between devices  1120 us (61%)
  matrix products  382 us (21%)
  other arithmetic  128 us (7%)
  blocking collectives  108 us (6%)
  local copies, waits for them, and re-layouts  57.5 us (3%)
  between operations  20.6 us (1%)
    reduce_scatter x1, waiting for transfers between devices, body(): lax.psum_scatter(grad_up, ('dp', 'fsdp'), scatter_dimension=0, tiled=True)  363 us
    reduce_scatter x1, waiting for transfers between devices, body(): lax.psum_scatter(grad_down, ('dp', 'fsdp'), scatter_dimension=0, tiled=True)  362 us
    reduce_scatter x1, waiting for transfers between devices, body(): lax.psum_scatter(grad_qkv, ('dp', 'fsdp'), scatter_dimension=0, tiled=True)  160 us
    reduce_scatter x1, waiting for transfers between devices, body(): lax.psum_scatter(grad_out, ('dp', 'fsdp'), scatter_dimension=0, tiled=True)  144 us
    all_gather x1, blocking collectives, body(): lax.all_gather(norm_gains.astype(jnp.bfloat16), ('dp', 'fsdp'), axis=1, t...  69.6 us
    dot_general x4, matrix products, one_block(): jnp.einsum('qhd,khd->hqk', q_block, key_vecs, preferred_element_type=jnp....  68.4 us
    convert_element_type x2, other arithmetic, one_block(): score_low = score_grad.astype(jnp.bfloat16)  55.5 us
    dot_general x2, matrix products, one_block(): jnp.einsum('qhd,khd->hqk', g_block, val_vecs, preferred_element_type=jnp....  52 us
  transfers between devices with their start and end apart: 9, of which 6 were waited for; matrix products, arithmetic and copies ran while one was open for 14% of the time, Pallas kernels for 0%

commit v1 on v0

v1 whole, which is shorter than its diff:
```python
import functools

import jax
import jax.numpy as jnp
import numpy as np
from jax import lax
from jax.experimental import pallas as pl
from jax.experimental.pallas import tpu as pltpu
from jax.sharding import PartitionSpec as P

D = 1024
HEAD_DIM = 64
FF = 4096
STEP = 7
FANO = 16

NORM_EPS = 1e-06
ADAM_EPS = 1e-08
BETA_ONE = 0.9
BETA_TWO = 0.95
SHADOW_KEEP = 0.8
CLIP_NORM = 1.0

AXES = ("dp", "fsdp")
CHUNKS = 4
GROUPS = 2
LANES = 128
VMEM = 62 << 20
f32 = jnp.float32
bf16 = jnp.bfloat16
NT = (((1,), (1,)), ((), ()))
TN = (((0,), (0,)), ((), ()))
GELU_A = 0.7978845608028654
GELU_B = 0.044715


def full(shape, single=False):
    rank = len(shape)
    mode = dict(pipeline_mode=pl.Buffered(1)) if single else {}
    return pl.BlockSpec(shape, lambda *_: (0,) * rank, **mode)


def params():
    return pltpu.CompilerParams(vmem_limit_bytes=VMEM)


def cost(flops, nbytes, trans=0):
    return pl.CostEstimate(flops=flops, bytes_accessed=nbytes, transcendentals=trans)


class Plan:
    def __init__(self, mesh):
        self.ndp, self.nfs = mesh.shape["dp"], mesh.shape["fsdp"]
        self.ndev = self.ndp * self.nfs
        self.bits = self.ndp.bit_length() - 1
        others = list(range(1, self.bits))
        half = len(others) // 2
        self.order = (others, others[half:] + others[:half])
        self.block = D // self.ndp
        tab = np.zeros((self.ndp, self.ndp), np.int32)
        for me in range(self.ndp):
            for rel in range(self.ndp):
                core = (me & 1) ^ (rel >> (self.bits - 1))
                nat = core
                for s, bit in enumerate(self.order[core]):
                    r = (rel >> (self.bits - 2 - s)) & 1
                    nat |= (((me >> bit) & 1) ^ r) << bit
                tab[me, rel] = nat
        self.tab = tab

    def pairs(self, flip):
        out = []
        for d in range(self.ndp):
            for f in range(self.nfs):
                out.append((d * self.nfs + f, flip(d) * self.nfs + f))
        return out

    def core_pairs(self):
        return self.pairs(lambda d: d ^ 1)

    def mix_pairs(self, s):
        return self.pairs(lambda d: d ^ (1 << self.order[d & 1][s]))

    def gather(self, held):
        pieces = [held]
        for s in reversed(range(self.bits - 1)):
            pieces = pieces + (yield pieces, self.mix_pairs(s))
        return pieces + (yield pieces, self.core_pairs())

    def scatter(self, sent, kept):
        (got,) = yield [sent], self.core_pairs()
        for s in range(self.bits - 1):
            rows = kept.shape[0] // 2
            total = lambda lo: (
                kept[lo : lo + rows].astype(f32) + got[lo : lo + rows].astype(f32)
            ).astype(bf16)
            sent, kept = total(rows), total(0)
            (got,) = yield [sent], self.mix_pairs(s)
        return kept.astype(f32) + got.astype(f32)


def tie(tree):
    leaves, form = jax.tree.flatten(tree)
    place = pl.BlockSpec(memory_space=pl.ANY)
    count = len(leaves)
    tied = pl.pallas_call(
        lambda *refs: None,
        in_specs=[place] * count,
        out_specs=[place] * count,
        out_shape=[jax.ShapeDtypeStruct(v.shape, v.dtype) for v in leaves],
        input_output_aliases={i: i for i in range(count)},
        name="tie",
    )(*leaves)
    return jax.tree.unflatten(form, tied)


class Flow:
    def __init__(self):
        self.live, self.flying, self.done = {}, {}, {}

    def add(self, name, transfer):
        self.live[name] = transfer

    def step(self, x, names):
        names = [n for n in names if n not in self.done]
        came = {n: self.flying.pop(n) for n in names if n in self.flying}
        x, came = tie((x, came))
        for n in names:
            try:
                if n in came:
                    arrays, pairs = self.live[n].send(came[n])
                else:
                    arrays, pairs = next(self.live[n])
                    x, arrays = tie((x, arrays))
                self.flying[n] = [lax.ppermute(v, AXES, pairs) for v in arrays]
            except StopIteration as stop:
                self.done[n] = stop.value
        return x

    def until(self, x, names):
        while any(n not in self.done for n in names):
            x = self.step(x, names)
        return x


def natural(dst, cols, pieces, src_cols, tab, block):
    j = 0
    for piece in pieces:
        for i in range(piece.shape[0] // block):
            row = pl.multiple_of(tab[j] * block, block)
            dst[pl.ds(row, block), cols] = piece[i * block : (i + 1) * block, src_cols]
            j += 1


def relative(sent, kept, cols, src, src_cols, tab, block):
    half = src.shape[0] // block // 2
    for j in range(2 * half):
        row = pl.multiple_of(tab[j] * block, block)
        out = kept if j < half else sent
        i = j % half
        out[i * block : (i + 1) * block, cols] = src[pl.ds(row, block), src_cols]


def qkv_kernel(count, block, tab, x_ref, *refs):
    gains, weights = refs[:count], refs[count : 2 * count]
    qkv_ref, u_ref, gain_ref, u_t_ref, w_nat, g_nat = refs[2 * count :]

    @pl.when(pl.program_id(0) == 0)
    def _():
        natural(g_nat, slice(None), gains, slice(None), tab, block)
        rows = g_nat[...].astype(f32).T
        gain_ref[...] = rows[:8]
        x = x_ref[...].astype(f32)
        r = lax.rsqrt(jnp.mean(x * x, axis=1, keepdims=True) + NORM_EPS)
        u = (x * r * rows[0:1]).astype(bf16)
        u_ref[...] = u
        u_t_ref[...] = u.T

    natural(w_nat, slice(None), weights, slice(None), tab, block)
    qkv_ref[...] = jnp.dot(u_ref[...], w_nat[...], preferred_element_type=f32).astype(bf16)


def project_qkv(tab, x, pieces, block):
    length, width = x.shape
    wide = 512
    count = len(pieces)
    columns = pieces[0].shape[1] - LANES
    last = columns // LANES
    return pl.pallas_call(
        functools.partial(qkv_kernel, count, block),
        grid_spec=pltpu.PrefetchScalarGridSpec(
            num_scalar_prefetch=1,
            grid=(columns // wide,),
            in_specs=[full((length, width), True)]
            + [pl.BlockSpec((p.shape[0], LANES), lambda j, t: (0, last)) for p in pieces]
            + [pl.BlockSpec((p.shape[0], wide), lambda j, t: (0, j)) for p in pieces],
            out_specs=[
                pl.BlockSpec((length, wide), lambda j, t: (0, j)),
                full((length, width)),
                full((8, width)),
                full((width, length)),
            ],
            scratch_shapes=[pltpu.VMEM((width, wide), bf16), pltpu.VMEM((width, LANES), bf16)],
        ),
        out_shape=[
            jax.ShapeDtypeStruct((length, columns), bf16),
            jax.ShapeDtypeStruct((length, width), bf16),
            jax.ShapeDtypeStruct((8, width), f32),
            jax.ShapeDtypeStruct((width, length), bf16),
        ],
        compiler_params=params(),
        cost_estimate=cost(2 * length * width * columns, 20 << 20),
        name="qkv",
    )(tab, x, *pieces, *pieces)


def attend_kernel(rows_of, n_ref, q_ref, k_ref, v_ref, o_ref, lse_ref):
    n = n_ref[0]
    length = q_ref.shape[0]
    lane = lax.broadcasted_iota(jnp.int32, (1, LANES), 1)
    masks = [(lane < HEAD_DIM).astype(bf16), (lane >= HEAD_DIM).astype(bf16)]
    v_t = v_ref[...].T
    for i in range(length // rows_of):
        rows = pl.ds(i * rows_of, rows_of)
        keys = (i + 1) * rows_of

        def run(limited):
            q = q_ref[rows, :] * bf16(HEAD_DIM**-0.5)
            k = k_ref[0:keys, :]
            parts = []
            for h in range(2):
                s = lax.dot_general(k, q * masks[h], NT, preferred_element_type=f32)
                if limited:
                    key = lax.broadcasted_iota(jnp.int32, (keys, rows_of), 0)
                    query = lax.broadcasted_iota(jnp.int32, (keys, rows_of), 1) + i * rows_of
                    s = jnp.where((key <= query) & (key < n), s, -1e30)
                else:
                    key = lax.broadcasted_iota(jnp.int32, (rows_of, rows_of), 0)
                    query = lax.broadcasted_iota(jnp.int32, (rows_of, rows_of), 1)
                    tail = jnp.where(key <= query, s[keys - rows_of :], -1e30)
                    s = tail if i == 0 else jnp.concatenate([s[: keys - rows_of], tail], axis=0)
                peak = jnp.max(s, axis=0, keepdims=True)
                e = jnp.exp(s - peak)
                total = jnp.sum(e, axis=0, keepdims=True)
                p = (e * (1.0 / total)).astype(bf16)
                v_h = v_t[h * HEAD_DIM : (h + 1) * HEAD_DIM, 0:keys]
                parts.append(jnp.dot(v_h, p, preferred_element_type=f32))
                query = lax.broadcasted_iota(jnp.int32, (1, rows_of), 1) + i * rows_of
                lse_ref[0, h : h + 1, rows] = jnp.where(query < n, peak + jnp.log(total), 1e30)
            o_ref[rows, :] = jnp.concatenate(parts, axis=0).astype(bf16).T

        @pl.when(n >= keys)
        def _():
            run(False)

        @pl.when(n < keys)
        def _():
            run(True)


def attend(frames, qkv, at, pairs):
    length, width = qkv.shape[0], pairs * LANES
    every = qkv.shape[1] // 3 // LANES
    part = lambda c: pl.BlockSpec((length, LANES), lambda j, n: (0, j + at + c * every))
    return pl.pallas_call(
        functools.partial(attend_kernel, 512),
        grid_spec=pltpu.PrefetchScalarGridSpec(
            num_scalar_prefetch=1,
            grid=(pairs,),
            in_specs=[part(0), part(1), part(2)],
            out_specs=[
                pl.BlockSpec((length, LANES), lambda j, n: (0, j)),
                pl.BlockSpec((1, 2, length), lambda j, n: (j, 0, 0)),
            ],
        ),
        out_shape=[
            jax.ShapeDtypeStruct((length, width), bf16),
            jax.ShapeDtypeStruct((pairs, 2, length), f32),
        ],
        compiler_params=params(),
        cost_estimate=cost(16 * length * length * width, 8 << 20, length * length * 16),
        name="attend",
    )(frames, qkv, qkv, qkv)


def mid_kernel(count, groups, block, tab, x_ref, gain_ref, *refs):
    o_refs, refs = refs[:groups], refs[groups:]
    weights = refs[:count]
    mid_ref, u_ref, u_t_ref, w_nat = refs[count:]

    @pl.when(pl.program_id(0) == 0)
    def _():
        natural(w_nat, slice(None), weights, slice(None), tab, block)

    o = jnp.concatenate([ref[...] for ref in o_refs], axis=1)
    mid = x_ref[...].astype(f32) + jnp.dot(o, w_nat[...], preferred_element_type=f32)
    r = lax.rsqrt(jnp.mean(mid * mid, axis=1, keepdims=True) + NORM_EPS)
    u = (mid * r * gain_ref[1:2, :]).astype(bf16)
    mid_ref[...] = mid
    u_ref[...] = u
    u_t_ref[...] = u.T


def middle(tab, o, x, gains, pieces, block):
    length, width = x.shape
    rows = 256
    row = pl.BlockSpec((rows, width), lambda i, t: (i, 0))
    return pl.pallas_call(
        functools.partial(mid_kernel, len(pieces), len(o), block),
        grid_spec=pltpu.PrefetchScalarGridSpec(
            num_scalar_prefetch=1,
            grid=(length // rows,),
            in_specs=[row, full((8, width))]
            + [pl.BlockSpec((rows, v.shape[1]), lambda i, t: (i, 0)) for v in o]
            + [full(p.shape) for p in pieces],
            out_specs=[row, row, pl.BlockSpec((width, rows), lambda i, t: (0, i))],
            scratch_shapes=[pltpu.VMEM((width, width), bf16)],
        ),
        out_shape=[
            jax.ShapeDtypeStruct((length, width), f32),
            jax.ShapeDtypeStruct((length, width), bf16),
            jax.ShapeDtypeStruct((width, length), bf16),
        ],
        compiler_params=params(),
        cost_estimate=cost(2 * length * width * width, 16 << 20),
        name="middle",
    )(tab, x, gains, *o, *pieces)


def gelu_both(z):
    sq = z * z
    t = jnp.tanh(z * (GELU_A + (GELU_A * GELU_B) * sq))
    half = 0.5 + 0.5 * t
    slope = half + (0.5 * z) * (1.0 - t * t) * (GELU_A + (3 * GELU_A * GELU_B) * sq)
    return z * half, slope


def mlp_kernel(count, block, first, last, steps, tab, u_ref, u_t_ref, g_ref, *refs):
    ups, downs = refs[:count], refs[count : 2 * count]
    refs = refs[2 * count :]
    held_out = refs[0]
    held_du = None if first else refs[1]
    out_ref, du_ref, sent, kept, up_nat, down_nat, out_acc, du_acc, a_s, dz_s, grad, sems = refs[
        (1 if first else 2) :
    ]
    width = u_ref.shape[1]
    wide = 512
    everything = slice(None)
    step = pl.program_id(0)
    load_out = pltpu.make_async_copy(held_out, out_acc, sems.at[0])
    load_du = None if first else pltpu.make_async_copy(held_du, du_acc, sems.at[1])

    @pl.when(step == 0)
    def _():
        load_out.start()
        if first:
            du_acc[...] = jnp.zeros_like(du_acc)
        else:
            load_du.start()

    natural(up_nat, everything, ups, everything, tab, block)
    natural(down_nat, everything, downs, everything, tab, block)
    for f in range(width // wide):
        cols = slice(f * wide, (f + 1) * wide)
        z = jnp.dot(u_ref[...], up_nat[:, cols], preferred_element_type=f32)
        a, slope = gelu_both(z)
        da = lax.dot_general(g_ref[...], down_nat[cols, :], NT, preferred_element_type=f32)
        a_s[...] = a.astype(bf16)
        dz_s[...] = (da * slope).astype(bf16)
        if f == 0:

            @pl.when(step == 0)
            def _():
                load_out.wait()
                if not first:
                    load_du.wait()

        out_acc[...] += jnp.dot(a_s[...], down_nat[cols, :], preferred_element_type=f32)
        du_acc[...] += lax.dot_general(dz_s[...], up_nat[:, cols], NT, preferred_element_type=f32)
        grad[:, cols] = jnp.dot(u_t_ref[...], dz_s[...], preferred_element_type=f32).astype(bf16)
        down = lax.dot_general(a_s[...], g_ref[...], TN, preferred_element_type=f32)
        grad[cols, width:] = down.astype(bf16)
    relative(sent, kept, everything, grad, everything, tab, block)

    @pl.when(step == steps - 1)
    def _():
        if last:
            out_ref[...] = out_acc[...].astype(bf16)
            save_out = None
        else:
            save_out = pltpu.make_async_copy(out_acc, out_ref, sems.at[0])
            save_out.start()
        save_du = pltpu.make_async_copy(du_acc, du_ref, sems.at[1])
        save_du.start()
        if save_out is not None:
            save_out.wait()
        save_du.wait()


def feed_forward(tab, u, u_t, g, pieces, held, block, first, last):
    length, width = u.shape
    steps = pieces[0].shape[1] // (2 * width)
    half = width // 2
    anywhere = pl.BlockSpec(memory_space=pl.ANY)
    count = len(pieces)
    held_inputs = held[:1] if first else held
    alias = {}
    base = 1 + 3 + 2 * count
    if not first:
        alias = {base + 1: 1}
        if not last:
            alias[base] = 0
    acc = jax.ShapeDtypeStruct((length, width), f32)
    return pl.pallas_call(
        functools.partial(mlp_kernel, count, block, first, last, steps),
        grid_spec=pltpu.PrefetchScalarGridSpec(
            num_scalar_prefetch=1,
            grid=(steps,),
            in_specs=[
                full((length, width), True),
                full((width, length), True),
                full((length, width), True),
            ]
            + [pl.BlockSpec((p.shape[0], width), lambda j, t: (0, 2 * j)) for p in pieces]
            + [pl.BlockSpec((p.shape[0], width), lambda j, t: (0, 2 * j + 1)) for p in pieces]
            + [anywhere] * len(held_inputs),
            out_specs=[
                full((length, width)) if last else anywhere,
                anywhere,
                pl.BlockSpec((half, 2 * width), lambda j, t: (0, j)),
                pl.BlockSpec((half, 2 * width), lambda j, t: (0, j)),
            ],
            scratch_shapes=[
                pltpu.VMEM((width, width), bf16),
                pltpu.VMEM((width, width), bf16),
                pltpu.VMEM((length, width), f32),
                pltpu.VMEM((length, width), f32),
                pltpu.VMEM((length, 512), bf16),
                pltpu.VMEM((length, 512), bf16),
                pltpu.VMEM((width, 2 * width), bf16),
                pltpu.SemaphoreType.DMA((2,)),
            ],
        ),
        out_shape=[
            jax.ShapeDtypeStruct((length, width), bf16) if last else acc,
            acc,
            jax.ShapeDtypeStruct((half, 2 * width * steps), bf16),
            jax.ShapeDtypeStruct((half, 2 * width * steps), bf16),
        ],
        input_output_aliases=alias,
        compiler_params=params(),
        cost_estimate=cost(12 * length * width * width * steps, 24 << 20),
        name="feed_forward",
    )(tab, u, u_t, g, *pieces, *pieces, *held_inputs)


def norm_back(v, gain, du):
    r = lax.rsqrt(jnp.mean(v * v, axis=1, keepdims=True) + NORM_EPS)
    up = du * gain
    return r * up - v * (r * r * r * jnp.mean(up * v, axis=1, keepdims=True))


def dmid_kernel(count, groups, block, steps, tab, n_ref, du_ref, mid_ref, cot_ref, gain_ref, *refs):
    o_refs, refs = refs[:groups], refs[groups:]
    weights = refs[:count]
    dmid_ref, do_ref, sent, kept, w_nat, total, grad = refs[count:]
    i = pl.program_id(0)
    rows = du_ref.shape[0]

    @pl.when(i == 0)
    def _():
        natural(w_nat, slice(None), weights, slice(None), tab, block)

    frame = lax.broadcasted_iota(jnp.int32, (rows, 1), 0) + i * rows
    g = jnp.where(frame < n_ref[0], cot_ref[...].astype(f32), 0.0)
    dmid = g + norm_back(mid_ref[...], gain_ref[1:2, :], du_ref[...])
    dmid_ref[...] = dmid
    low = dmid.astype(bf16)
    do_ref[...] = lax.dot_general(low, w_nat[...], NT, preferred_element_type=f32).astype(bf16)
    o = jnp.concatenate([ref[...] for ref in o_refs], axis=1)
    part = lax.dot_general(o, low, TN, preferred_element_type=f32)

    @pl.when(i == 0)
    def _():
        total[...] = part

    @pl.when(i > 0)
    def _():
        total[...] += part

    @pl.when(i == steps - 1)
    def _():
        grad[...] = total[...].astype(bf16)
        relative(sent, kept, slice(None), grad, slice(None), tab, block)


def middle_back(tab, frames, du, mid, cot, gains, o, pieces, block):
    length, width = mid.shape
    rows = 256
    steps = length // rows
    row = pl.BlockSpec((rows, width), lambda i, t, n: (i, 0))
    half = width // 2
    return pl.pallas_call(
        functools.partial(dmid_kernel, len(pieces), len(o), block, steps),
        grid_spec=pltpu.PrefetchScalarGridSpec(
            num_scalar_prefetch=2,
            grid=(steps,),
            in_specs=[row, row, row, full((8, width))]
            + [pl.BlockSpec((rows, v.shape[1]), lambda i, t, n: (i, 0)) for v in o]
            + [full(p.shape) for p in pieces],
            out_specs=[row, row, full((half, width)), full((half, width))],
            scratch_shapes=[
                pltpu.VMEM((width, width), bf16),
                pltpu.VMEM((width, width), f32),
                pltpu.VMEM((width, width), bf16),
            ],
        ),
        out_shape=[
            jax.ShapeDtypeStruct((length, width), f32),
            jax.ShapeDtypeStruct((length, width), bf16),
            jax.ShapeDtypeStruct((half, width), bf16),
            jax.ShapeDtypeStruct((half, width), bf16),
        ],
        compiler_params=params(),
        cost_estimate=cost(4 * length * width * width, 24 << 20),
        name="middle_back",
    )(tab, frames, du, mid, cot, gains, *o, *pieces)


def attend_back_kernel(rows_of, n_ref, q_ref, k_ref, v_ref, g_ref, lse_ref, d_ref, dk, dv):
    n = n_ref[0]
    length = q_ref.shape[0]
    scale = HEAD_DIM**-0.5
    lane = lax.broadcasted_iota(jnp.int32, (1, LANES), 1)
    masks = [(lane < HEAD_DIM).astype(bf16), (lane >= HEAD_DIM).astype(bf16)]
    dk[...] = jnp.zeros_like(dk)
    dv[...] = jnp.zeros_like(dv)
    for i in range(length // rows_of):
        rows = pl.ds(i * rows_of, rows_of)
        keys = (i + 1) * rows_of

        @pl.when(n > i * rows_of)
        def _():
            q = q_ref[rows, :] * bf16(scale)
            g = g_ref[rows, :]
            k, v = k_ref[0:keys, :], v_ref[0:keys, :]
            dq = None
            for h in range(2):
                q_h, g_h, k_h = q * masks[h], g * masks[h], k * masks[h]
                s = lax.dot_general(k, q_h, NT, preferred_element_type=f32)
                key = lax.broadcasted_iota(jnp.int32, (rows_of, rows_of), 0)
                query = lax.broadcasted_iota(jnp.int32, (rows_of, rows_of), 1)
                tail = jnp.where(key <= query, s[keys - rows_of :], -1e30)
                s = tail if i == 0 else jnp.concatenate([s[: keys - rows_of], tail], axis=0)
                p = jnp.exp(s - lse_ref[0, h : h + 1, rows])
                dp = lax.dot_general(v, g_h, NT, preferred_element_type=f32)
                delta = jnp.sum(p * dp, axis=0, keepdims=True)
                ds = (p * (dp - delta)).astype(bf16)
                dv[0:keys, :] += jnp.dot(p.astype(bf16), g_h, preferred_element_type=f32)
                dk[0:keys, :] += jnp.dot(ds, q_h, preferred_element_type=f32)
                part = lax.dot_general(ds, k_h, TN, preferred_element_type=f32)
                dq = part if dq is None else dq + part
            d_ref[0, rows, :] = (dq * scale).astype(bf16)

        @pl.when(n <= i * rows_of)
        def _():
            d_ref[0, rows, :] = jnp.zeros((rows_of, LANES), bf16)

    d_ref[1] = dk[...].astype(bf16)
    d_ref[2] = dv[...].astype(bf16)


def attend_back(frames, qkv, g, lse, at):
    length, pairs = qkv.shape[0], lse.shape[0]
    width = pairs * LANES
    every = qkv.shape[1] // 3 // LANES
    part = lambda c: pl.BlockSpec((length, LANES), lambda j, n: (0, j + at + c * every))
    return pl.pallas_call(
        functools.partial(attend_back_kernel, 256),
        grid_spec=pltpu.PrefetchScalarGridSpec(
            num_scalar_prefetch=1,
            grid=(pairs,),
            in_specs=[
                part(0),
                part(1),
                part(2),
                part(0),
                pl.BlockSpec((1, 2, length), lambda j, n: (j, 0, 0)),
            ],
            out_specs=pl.BlockSpec((3, length, LANES), lambda j, n: (0, 0, j)),
            scratch_shapes=[pltpu.VMEM((length, LANES), f32), pltpu.VMEM((length, LANES), f32)],
        ),
        out_shape=jax.ShapeDtypeStruct((3, length, width), bf16),
        compiler_params=params(),
        cost_estimate=cost(24 * length * length * width, 16 << 20, length * length * 16),
        name="attend_back",
    )(frames, qkv, qkv, qkv, g, lse)


def qkv_grad_kernel(block, tab, u_t_ref, d_ref, sent, kept, grad):
    total = jnp.dot(u_t_ref[...], d_ref[0], preferred_element_type=f32)
    grad[...] = total.astype(bf16)
    relative(sent, kept, slice(None), grad, slice(None), tab, block)


def qkv_grad(tab, u_t, d, block):
    width, length = u_t.shape
    wide = 512
    half = width // 2
    columns = d.shape[2]
    per = columns // wide
    out = pl.BlockSpec((half, wide), lambda j, t: (0, j))
    shape = jax.ShapeDtypeStruct((half, 3 * columns), bf16)
    return pl.pallas_call(
        functools.partial(qkv_grad_kernel, block),
        grid_spec=pltpu.PrefetchScalarGridSpec(
            num_scalar_prefetch=1,
            grid=(3 * per,),
            in_specs=[
                full((width, length), True),
                pl.BlockSpec((1, length, wide), lambda j, t: (j // per, 0, j % per)),
            ],
            out_specs=[out, out],
            scratch_shapes=[pltpu.VMEM((width, wide), bf16)],
        ),
        out_shape=[shape, shape],
        compiler_params=params(),
        cost_estimate=cost(6 * length * width * columns, 14 << 20),
        name="qkv_grad",
    )(tab, u_t, d)


def input_grad_kernel(count, groups, block, tab, dmid_ref, x_ref, gain_ref, *refs):
    d_refs, refs = refs[:groups], refs[groups:]
    weights = refs[:count]
    out_ref, w_nat = refs[count:]
    width = x_ref.shape[1]

    @pl.when(pl.program_id(0) == 0)
    def _():
        natural(w_nat, slice(None), weights, slice(None), tab, block)

    du = None
    for c in range(3):
        w = w_nat[:, c * width : (c + 1) * width]
        d = jnp.concatenate([ref[c] for ref in d_refs], axis=1)
        part = lax.dot_general(d, w, NT, preferred_element_type=f32)
        du = part if du is None else du + part
    out_ref[...] = dmid_ref[...] + norm_back(x_ref[...].astype(f32), gain_ref[0:1, :], du)


def input_grad(tab, d, dmid, x, gains, pieces, block):
    length, width = x.shape
    rows = 256
    row = pl.BlockSpec((rows, width), lambda i, t: (i, 0))
    return pl.pallas_call(
        functools.partial(input_grad_kernel, len(pieces), len(d), block),
        grid_spec=pltpu.PrefetchScalarGridSpec(
            num_scalar_prefetch=1,
            grid=(length // rows,),
            in_specs=[row, row, full((8, width))]
            + [pl.BlockSpec((3, rows, v.shape[2]), lambda i, t: (0, i, 0)) for v in d]
            + [pl.BlockSpec((p.shape[0], 3 * width), lambda i, t: (0, 0), pipeline_mode=pl.Buffered(1)) for p in pieces],
            out_specs=row,
            scratch_shapes=[pltpu.VMEM((width, 3 * width), bf16)],
        ),
        out_shape=jax.ShapeDtypeStruct((length, width), f32),
        compiler_params=params(),
        cost_estimate=cost(6 * length * width * width, 22 << 20),
        name="input_grad",
    )(tab, dmid, x, gains, *d, *pieces)


def adam_step(weight, first, second, gradient, clip_factor, step_rate, decay_rate, shadow):
    clipped = gradient * clip_factor
    first_new = BETA_ONE * first + (1.0 - BETA_ONE) * clipped
    second_new = BETA_TWO * second + (1.0 - BETA_TWO) * clipped * clipped
    first_hat = first_new / (1.0 - BETA_ONE**STEP)
    second_hat = second_new / (1.0 - BETA_TWO**STEP)
    weight_new = weight - step_rate * (
        first_hat / (jnp.sqrt(second_hat) + ADAM_EPS) + decay_rate * weight
    )
    shadow_new = SHADOW_KEEP * shadow + (1.0 - SHADOW_KEEP) * weight_new
    return (weight_new, first_new, second_new, shadow_new)


def body(plan, *args):
    inputs, cotangent, frames = args[:3]
    masters, firsts, seconds, shadows = args[3:8], args[8:13], args[13:18], args[18:23]
    w_qkv, w_out, w_up, w_down, norm_gains = masters
    block, ndev = plan.block, plan.ndev
    x = inputs[0]
    length = x.shape[0]
    own = D // ndev
    subs = FF // D
    per = subs // CHUNKS
    tab = lax.dynamic_index_in_dim(jnp.asarray(plan.tab), lax.axis_index("dp"), 0, keepdims=False)

    gain_cols = jnp.pad(norm_gains.astype(bf16).T, ((0, 0), (0, LANES - 2)))
    local_qkv = jnp.concatenate([w_qkv.astype(bf16), gain_cols], axis=1)
    up_low = w_up.astype(bf16).reshape(own, ndev, subs, own).transpose(2, 0, 1, 3).reshape(subs, own, D)
    down_low = w_down.astype(bf16).reshape(subs, own, D)
    local_mlp = [
        jnp.concatenate(
            [half for q in range(k * per, (k + 1) * per) for half in (up_low[q], down_low[q])], axis=1
        )
        for k in range(CHUNKS)
    ]
    flow = Flow()
    step = flow.step
    reach = lambda v: lax.all_gather(v, "fsdp", axis=0, tiled=True)
    flow.add("q", plan.gather(reach(local_qkv)))
    rest = reach(jnp.concatenate([w_out.astype(bf16)] + local_mlp, axis=1))
    flow.add("o", plan.gather(rest[:, :D]))
    size = 2 * per * D
    for k in range(CHUNKS):
        flow.add(f"m{k}", plan.gather(rest[:, D + k * size : D + (k + 1) * size]))

    x = step(x, ["q"])
    for _ in range(plan.bits - 1):
        x = step(x, ["q"])
    x = step(x, ["q", "o", "m0", "m1"])
    x = flow.until(x, ["q"])
    full_qkv = flow.done["q"]
    qkv, u_one, gains, u_one_t = project_qkv(tab, x, full_qkv, block)
    pairs = D // LANES // GROUPS
    qkv = step(qkv, ["o", "m0"])
    o0, lse0 = attend(frames, qkv, 0, pairs)
    o0, qkv = step((o0, qkv), ["o", "m0", "m1"])
    o1, lse1 = attend(frames, qkv, pairs, pairs)
    o, lse = [o0, o1], [lse0, lse1]
    o = step(o, ["o", "m0", "m1", "m2", "m3"])
    o = flow.until(o, ["o"])
    full_out = flow.done["o"]
    mid, u_two, u_two_t = middle(tab, o, x, gains, full_out, block)
    keep = (jnp.arange(length) < frames[0])[:, None]
    g_low = jnp.where(keep, cotangent[0], jnp.zeros((), bf16))
    held = [mid, None]
    plans = [["m1", "m2"], ["m1", "m2", "m3"], ["m2", "m3", "g0"], ["m3", "g0", "g1"]]
    u_two = step(u_two, ["m0", "m1", "m2"])
    for k in range(CHUNKS):
        u_two = flow.until(u_two, [f"m{k}"])
        out, du, sent, kept = feed_forward(
            tab, u_two, u_two_t, g_low, flow.done[f"m{k}"], held, block, k == 0, k == CHUNKS - 1
        )
        held = [out, du]
        flow.add(f"g{k}", plan.scatter(sent, kept))
        if k == 0:
            held = step(held, ["m1", "m2", "m3", "g0"])
        elif k == 1:
            held = step(held, ["m2", "m3", "g0", "g1"])
        elif k == 2:
            held = step(held, ["m3", "g0", "g1", "g2"])
        elif k == 3:
            held = step(held, ["g0", "g1", "g2", "g3"])
    out, du = held
    dmid, d_o, sent, kept = middle_back(
        tab, frames, du, mid, cotangent[0], gains, o, full_out, block
    )
    flow.add("go", plan.scatter(sent, kept))
    d_o = step(d_o, ["g1", "g2", "g3", "go"])
    d0 = attend_back(frames, qkv, d_o, lse[0], 0)
    d0 = step(d0, ["g2", "g3", "go"])
    sent, kept = qkv_grad(tab, u_one_t, d0, block)
    flow.add("gq0", plan.scatter(sent, kept))
    kept, qkv = step((kept, qkv), ["gq0", "g3", "go"])
    d1 = attend_back(frames, qkv, d_o, lse[1], pairs)
    d1 = step(d1, ["gq0", "go"])
    sent, kept = qkv_grad(tab, u_one_t, d1, block)
    flow.add("gq1", plan.scatter(sent, kept))
    kept, d = step((kept, [d0, d1]), ["gq0", "gq1"])
    grad_in = input_grad(tab, d, dmid, x, gains, full_qkv, block)
    grad_in = step(grad_in, ["gq0", "gq1"])
    grad_in = flow.until(grad_in, list(flow.live))
    own_rows = lambda n: lax.psum_scatter(flow.done[n], "fsdp", scatter_dimension=0, tiled=True)
    mlp_shards = [own_rows(f"g{k}") for k in range(CHUNKS)]
    out_shard = own_rows("go")
    parts = [own_rows("gq0"), own_rows("gq1")]
    wide = pairs * LANES
    qkv_shard = jnp.concatenate(
        [v[:, c * wide : (c + 1) * wide] for c in range(3) for v in parts], axis=1
    )

    ups, downs = [], []
    for k in range(CHUNKS):
        for i in range(per):
            at = 2 * i * D
            ups.append(mlp_shards[k][:, at : at + D])
            downs.append(mlp_shards[k][:, at + D : at + 2 * D])
    up_shard = (
        jnp.stack(ups).reshape(subs, own, ndev, own).transpose(1, 2, 0, 3).reshape(own, FF)
    )
    down_shard = jnp.concatenate(downs, axis=0)
    gain_low = norm_gains.astype(bf16).astype(f32)
    one = jnp.sum(w_qkv.astype(bf16).astype(f32) * qkv_shard, axis=1)
    two = jnp.sum(w_up.astype(bf16).astype(f32) * up_shard, axis=1)
    gain_shard = jnp.stack([one, two]) / gain_low
    shards = (qkv_shard, out_shard, up_shard, down_shard, gain_shard)
    local_sq = sum(jnp.sum(piece * piece) for piece in shards)
    everyone = lax.all_to_all(jnp.broadcast_to(local_sq, (ndev, 1, LANES)), AXES, 0, 0)
    grad_norm = jnp.sqrt(jnp.sum(everyone[:, 0, 0]))
    clip_factor = jnp.minimum(1.0, CLIP_NORM / grad_norm)
    rates = (0.6 / D**0.5, 0.6 / FANO**0.5, 0.6 / D**0.5, 0.6 / FF**0.5, 1.0)
    decays = (0.1, 0.1, 0.1, 0.1, 0.0)
    updated = [
        adam_step(
            masters[i], firsts[i], seconds[i], shards[i], clip_factor, rates[i], decays[i], shadows[i]
        )
        for i in range(5)
    ]
    return (
        out[None],
        grad_in[None],
        grad_norm,
        *(updated[i][part] for part in range(4) for i in range(5)),
    )


def solution(mesh):
    plan = Plan(mesh)
    split = P(AXES, None)
    lanes = P(None, AXES)
    weights = (split, split, split, split, lanes)
    return jax.shard_map(
        functools.partial(body, plan),
        mesh=mesh,
        in_specs=(P(AXES, None, None), P(AXES, None, None), P(AXES)) + weights * 4,
        out_specs=(P(AXES, None, None), P(AXES, None, None), P()) + weights * 4,
        check_vma=False,
    )
```

time: 1840 us -> 551 us (0.30)
  waiting for transfers between devices: 1120 us -> 82.5 us
  matrix products: 382 us -> 0 us
  Pallas kernels: 0 us -> 213 us
  blocking collectives: 108 us -> 28.1 us
  starting transfers between devices: 0.59 us -> 72.1 us
  other arithmetic: 128 us -> 63.6 us
    reduce_scatter x4 -> x7, waiting for transfers between devices: 1030 us -> 7.38 us  [body(): lax.psum_scatter(flow.done[n], 'fsdp', scatter_dimension=0, tiled=True)]
    dot_general x26 -> x0, matrix products: 382 us -> none  [the longest x4 68.4 us: one_block(): jnp.einsum('qhd,khd->hqk', q_block, key_vecs, preferred_element_type=jnp....]
    pallas_call x0 -> x47, Pallas kernels: none -> 213 us  [the longest x4 90.7 us: feed_forward(): pl.pallas_call(functools.partial(mlp_kernel, count, block, first, last, s...]
    ppermute x0 -> x63, waiting for transfers between devices: none -> 68.3 us  [step(): self.flying[n] = [lax.ppermute(v, AXES, pairs) for v in arrays]]
    ppermute x0 -> x63, starting transfers between devices: none -> 67.6 us  [step(): self.flying[n] = [lax.ppermute(v, AXES, pairs) for v in arrays]]
    all_gather x4 -> x1, waiting for transfers between devices: 47.6 us -> 0.01 us  [body(): reach = lambda v: lax.all_gather(v, 'fsdp', axis=0, tiled=True)]
    unnamed x10 -> x8, waiting for transfers between devices: 47.6 us -> 0.13 us
    all_gather x1, blocking collectives: 69.6 us -> 28.1 us  [body(): reach = lambda v: lax.all_gather(v, 'fsdp', axis=0, tiled=True)]
  transfers between devices with their start and end apart: 9 -> 72, of which waited for: 6 -> 16; matrix products, arithmetic and copies ran while one was open for 14% -> 14% of each run, Pallas kernels for 0% -> 39%
where the time goes in v1:
time: 551 us; the launch traced here: 546 us
  Pallas kernels  213 us (39%)
  waiting for transfers between devices  82.5 us (15%)
  starting transfers between devices  72.1 us (13%)
  local copies, waits for them, and re-layouts  65.3 us (12%)
  other arithmetic  63.6 us (12%)
  blocking collectives  28.1 us (5%)
  between operations  21.4 us (4%)
    pallas_call x4, Pallas kernels, feed_forward(): pl.pallas_call(functools.partial(mlp_kernel, count, block, first, last, s...  90.7 us
    ppermute x63, waiting for transfers between devices, step(): self.flying[n] = [lax.ppermute(v, AXES, pairs) for v in arrays]  68.3 us
    ppermute x63, starting transfers between devices, step(): self.flying[n] = [lax.ppermute(v, AXES, pairs) for v in arrays]  67.6 us
    unnamed x224, local copies, waits for them, and re-layouts  46.6 us
    convert_element_type x14, other arithmetic, scatter(): total = lambda lo: (kept[lo:lo + rows].astype(f32) + got[lo:lo + rows].as...  32.7 us
    pallas_call x2, Pallas kernels, attend(): pl.pallas_call(functools.partial(attend_kernel, 512), grid_spec=pltpu.Pre...  31.8 us
    all_gather x1, blocking collectives, body(): reach = lambda v: lax.all_gather(v, 'fsdp', axis=0, tiled=True)  28.1 us
    pallas_call x2, Pallas kernels, attend_back(): pl.pallas_call(functools.partial(attend_back_kernel, 256), grid_spec=pltp...  22.1 us
  transfers between devices with their start and end apart: 72, of which 16 were waited for; matrix products, arithmetic and copies ran while one was open for 14% of the time, Pallas kernels for 39%

profile of v1, /device:TPU:0, one launch (start us, length us, event | category | flops | bytes accessed | tf_op | source)
XLA Modules:
  0.0 545.6 jit_solution(3503949764561696785)
XLA Ops:
  7.2 3.2 copy.428
  14.4 28.1 %all_gather.6.refs_0_.refs_8_.refs_2_ = bf16[128,3200]{1,0:T(8,128)(2,1)S(1)} all-gather(bf16[32,3200]{1,0:T(8,128)(2,1)S(1)} %fusion.4), channel_id=1, replica_groups=mesh['dp'=8,'fsdp'=4] {'fsdp'}, dimensions={0}, use_global_device_ids=true | all-gather | bytes 1024000 | tf_op jit(solution)/shard_map/all_gather | solution.py:711
  46.4 16.9 %collective-permute-done.refs_1_ = bf16[128,3200]{1,0:T(8,128)(2,1)S(1)} collective-permute-done((bf16[128,3200]{1,0:T(8,128)(2,1)}, bf16[128,3200]{1,0:T(8,128)(2,1)S(1)}, u32[]{:S(2)}, u32[]{:S(2)}) %collective-permute-start) | collective-permute-done | bytes 819232 | tf_op jit(solution)/shard_map/ppermute | solution.py:135
  64.8 12.0 %collective-permute-done.2.refs_2_ = bf16[128,3200]{1,0:T(8,128)(2,1)S(1)} collective-permute-done((bf16[128,3200]{1,0:T(8,128)(2,1)}, bf16[128,3200]{1,0:T(8,128)(2,1)S(1)}, u32[]{:S(2)}, u32[]{:S(2)}) %collective-permute-start.2) | collective-permute-done | bytes 819232 | tf_op jit(solution)/shard_map/ppermute | solution.py:135
  82.3 2.6 fusion.12
  93.4 14.5 %qkv.1 = (bf16[1024,3072]{1,0:T(8,128)(2,1)}, bf16[1024,1024]{1,0:T(8,128)(2,1)}, f32[8,1024]{1,0:T(8,128)}, bf16[1024,1024]{1,0:T(8,128)(2,1)}) custom-call(s32[8]{0:T(128)} %dynamic-slice_bitcast_fusion.tab, bf16[1024,1024]{1,0:T(8,128)(2,1)} %get-tuple-element.191.x_ref, bf16[128,3200]{1,0:T(8,128)(2,1)} %copy-done.26, ...), custom_call_target="tpu_custom_call" | custom-call | flops 6442450944 | bytes 20971520 | tf_op jit(solution)/shard_map/qkv/pallas_call | solution.py:189
  108.0 2.1 collective-permute-start.10
  113.5 6.7 %collective-permute-done.12.refs_5_ = bf16[128,1024]{1,0:T(8,128)(2,1)S(1)} collective-permute-done((bf16[128,1024]{1,0:T(8,128)(2,1)S(1)}, bf16[128,1024]{1,0:T(8,128)(2,1)S(1)}, u32[]{:S(2)}, u32[]{:S(2)}) %collective-permute-start.12) | collective-permute-done | bytes 262176 | tf_op jit(solution)/shard_map/ppermute | solution.py:135
  120.3 2.1 collective-permute-start.18
  124.3 15.8 %attend.2 = (bf16[1024,512]{1,0:T(8,128)(2,1)}, f32[4,2,1024]{2,1,0:T(2,128)}) custom-call(s32[1]{0:T(128)} %copy.427.n_ref, bf16[1024,3072]{1,0:T(8,128)(2,1)} %get-tuple-element.200.q_ref.k_ref.v_ref.refs_1_, bf16[1024,3072]{1,0:T(8,128)(2,1)} %get-tuple-element.200.q_ref.k_ref.v_ref.refs_1_, bf16[1024,3072]{1,0:T(8,128)(2,1)} %get-tuple-element.200.q_ref.k_ref.v_ref.refs_1_), custom_call_target="tpu_custom_call" | custom-call | flops 8589934592 | bytes 8388608 | tf_op jit(solution)/shard_map/attend/pallas_call | solution.py:265
  140.7 2.0 collective-permute-start.19
  143.2 16.0 %attend.3 = (bf16[1024,512]{1,0:T(8,128)(2,1)}, f32[4,2,1024]{2,1,0:T(2,128)}) custom-call(s32[1]{0:T(128)} %copy.427.n_ref, bf16[1024,3072]{1,0:T(8,128)(2,1)} %get-tuple-element.206.q_ref.k_ref.v_ref.refs_1_, bf16[1024,3072]{1,0:T(8,128)(2,1)} %get-tuple-element.206.q_ref.k_ref.v_ref.refs_1_, bf16[1024,3072]{1,0:T(8,128)(2,1)} %get-tuple-element.206.q_ref.k_ref.v_ref.refs_1_), custom_call_target="tpu_custom_call" | custom-call | flops 8589934592 | bytes 8388608 | tf_op jit(solution)/shard_map/attend/pallas_call | solution.py:265
  164.5 9.4 %middle.1 = (f32[1024,1024]{1,0:T(8,128)}, bf16[1024,1024]{1,0:T(8,128)(2,1)}, bf16[1024,1024]{1,0:T(8,128)(2,1)}) custom-call(s32[8]{0:T(128)} %dynamic-slice_bitcast_fusion.tab, bf16[1024,1024]{1,0:T(8,128)(2,1)} %get-tuple-element.191.x_ref, f32[8,1024]{1,0:T(8,128)} %get-tuple-element.196.gain_ref, bf16[1024,512]{1,0:T(8,128)(2,1)} %get-tuple-element.217.refs_0_, ...), custom_call_target="tpu_custom_call" | custom-call | flops 2147483648 | bytes 16777216 | tf_op jit(solution)/shard_map/middle/pallas_call | solution.py:308
  177.1 21.7 %feed_forward.4 = (f32[1024,1024]{1,0:T(8,128)}, f32[1024,1024]{1,0:T(8,128)}, bf16[512,2048]{1,0:T(8,128)(2,1)}, bf16[512,2048]{1,0:T(8,128)(2,1)}) custom-call(s32[8]{0:T(128)} %dynamic-slice_bitcast_fusion.tab, bf16[1024,1024]{1,0:T(8,128)(2,1)} %get-tuple-element.227.u_ref, bf16[1024,1024]{1,0:T(8,128)(2,1)} %get-tuple-element.228.u_t_ref, ...), custom_call_target="tpu_custom_call" | custom-call | flops 12884901888 | bytes 25165824 | tf_op jit(solution)/shard_map/feed_forward/pallas_call | solution.py:414
  200.6 3.9 collective-permute-done.33.refs_3_
  204.9 4.1 collective-permute-done.37.refs_7_
  209.3 22.8 %feed_forward.5 = (f32[1024,1024]{1,0:T(8,128)}, f32[1024,1024]{1,0:T(8,128)}, bf16[512,2048]{1,0:T(8,128)(2,1)}, bf16[512,2048]{1,0:T(8,128)(2,1)}) custom-call(s32[8]{0:T(128)} %dynamic-slice_bitcast_fusion.tab, bf16[1024,1024]{1,0:T(8,128)(2,1)} %get-tuple-element.227.u_ref, ...), custom_call_target="tpu_custom_call", output_to_operand_aliasing={{1}: (21, {}), {0}: (20, {})} | custom-call | flops 12884901888 | bytes 25165824 | tf_op jit(solution)/shard_map/feed_forward/pallas_call | solution.py:414
  234.5 3.6 add_convert_fusion.6
  241.1 23.1 %feed_forward.6 = (f32[1024,1024]{1,0:T(8,128)}, f32[1024,1024]{1,0:T(8,128)}, bf16[512,2048]{1,0:T(8,128)(2,1)}, bf16[512,2048]{1,0:T(8,128)(2,1)}) custom-call(s32[8]{0:T(128)} %dynamic-slice_bitcast_fusion.tab, bf16[1024,1024]{1,0:T(8,128)(2,1)} %get-tuple-element.227.u_ref, ...), custom_call_target="tpu_custom_call", output_to_operand_aliasing={{1}: (21, {}), {0}: (20, {})} | custom-call | flops 12884901888 | bytes 25165824 | tf_op jit(solution)/shard_map/feed_forward/pallas_call | solution.py:414
  267.1 3.8 add_convert_fusion.4
  273.1 23.1 %feed_forward.7 = (bf16[1024,1024]{1,0:T(8,128)(2,1)}, f32[1024,1024]{1,0:T(8,128)}, bf16[512,2048]{1,0:T(8,128)(2,1)}, bf16[512,2048]{1,0:T(8,128)(2,1)}) custom-call(s32[8]{0:T(128)} %dynamic-slice_bitcast_fusion.tab, bf16[1024,1024]{1,0:T(8,128)(2,1)} %get-tuple-element.227.u_ref, ...), custom_call_target="tpu_custom_call", output_to_operand_aliasing={{1}: (21, {})} | custom-call | flops 12884901888 | bytes 25165824 | tf_op jit(solution)/shard_map/feed_forward/pallas_call | solution.py:414
  299.0 3.8 add_convert_fusion.2
  307.7 14.1 %middle_back.1 = (f32[1024,1024]{1,0:T(8,128)}, bf16[1024,1024]{1,0:T(8,128)(2,1)}, bf16[512,1024]{1,0:T(8,128)(2,1)}, bf16[512,1024]{1,0:T(8,128)(2,1)}) custom-call(s32[8]{0:T(128)} %dynamic-slice_bitcast_fusion.tab, s32[1]{0:T(128)} %copy.427.n_ref, f32[1024,1024]{1,0:T(8,128)} %get-tuple-element.288.du_ref, ...), custom_call_target="tpu_custom_call" | custom-call | flops 4294967296 | bytes 25165824 | tf_op jit(solution)/shard_map/middle_back/pallas_call | solution.py:503
  323.5 4.5 add_convert_fusion
  331.1 2.0 add_convert_fusion.19
  334.0 11.0 %attend_back.2.refs_0_ = bf16[3,1024,512]{2,1,0:T(8,128)(2,1)} custom-call(s32[1]{0:T(128)} %copy.427.n_ref, bf16[1024,3072]{1,0:T(8,128)(2,1)} %get-tuple-element.206.q_ref.k_ref.v_ref.refs_1_, bf16[1024,3072]{1,0:T(8,128)(2,1)} %get-tuple-element.206.q_ref.k_ref.v_ref.refs_1_, bf16[1024,3072]{1,0:T(8,128)(2,1)} %get-tuple-element.206.q_ref.k_ref.v_ref.refs_1_, ...), custom_call_target="tpu_custom_call" | custom-call | flops 12884901888 | bytes 16777216 | tf_op jit(solution)/shard_map/attend_back/pallas_call | solution.py:578
  346.3 2.4 collective-permute-done.52.refs_2_
  349.8 2.5 convert_add_fusion.1
  352.3 2.5 add_convert_fusion.16
  358.5 10.7 %collective-permute-start.54 = (bf16[128,2048]{1,0:T(8,128)(2,1)}, bf16[128,2048]{1,0:T(8,128)(2,1)S(1)}, u32[]{:S(2)}, u32[]{:S(2)}) collective-permute-start(bf16[128,2048]{1,0:T(8,128)(2,1)} %add_convert_fusion.18), channel_id=1, source_target_pairs={{0,16},{1,17},{2,18},{3,19},{4,12},{5,13},{6,14},{7,15},{8,24},{9,... | collective-permute-start | bytes 1572872 | tf_op jit(solution)/shard_map/ppermute | solution.py:135
  369.2 7.8 %qkv_grad.2 = (bf16[512,1536]{1,0:T(8,128)(2,1)}, bf16[512,1536]{1,0:T(8,128)(2,1)}) custom-call(s32[8]{0:T(128)} %dynamic-slice_bitcast_fusion.tab, bf16[1024,1024]{1,0:T(8,128)(2,1)} %get-tuple-element.290.u_t_ref, bf16[3,1024,512]{2,1,0:T(8,128)(2,1)} %get-tuple-element.304.d_ref.refs_1_), custom_call_target="tpu_custom_call" | custom-call | flops 3221225472 | bytes 14680064 | tf_op jit(solution)/shard_map/qkv_grad/pallas_call | solution.py:614
  377.1 2.7 copy.396.refs_0_
  384.4 2.4 convert_add_fusion
  386.9 11.0 %attend_back.3.refs_0_ = bf16[3,1024,512]{2,1,0:T(8,128)(2,1)} custom-call(s32[1]{0:T(128)} %copy.427.n_ref, bf16[1024,3072]{1,0:T(8,128)(2,1)} %get-tuple-element.312.q_ref.k_ref.v_ref, bf16[1024,3072]{1,0:T(8,128)(2,1)} %get-tuple-element.312.q_ref.k_ref.v_ref, bf16[1024,3072]{1,0:T(8,128)(2,1)} %get-tuple-element.312.q_ref.k_ref.v_ref, ...), custom_call_target="tpu_custom_call" | custom-call | flops 12884901888 | bytes 16777216 | tf_op jit(solution)/shard_map/attend_back/pallas_call | solution.py:578
  399.8 3.2 add_convert_fusion.10
  404.6 7.9 %qkv_grad.3 = (bf16[512,1536]{1,0:T(8,128)(2,1)}, bf16[512,1536]{1,0:T(8,128)(2,1)}) custom-call(s32[8]{0:T(128)} %dynamic-slice_bitcast_fusion.tab, bf16[1024,1024]{1,0:T(8,128)(2,1)} %get-tuple-element.290.u_t_ref, bf16[3,1024,512]{2,1,0:T(8,128)(2,1)} %get-tuple-element.316.d_ref.refs_2_), custom_call_target="tpu_custom_call" | custom-call | flops 3221225472 | bytes 14680064 | tf_op jit(solution)/shard_map/qkv_grad/pallas_call | solution.py:614
  412.5 2.7 copy.406.refs_0_
  416.0 13.6 %collective-permute-start.60 = (bf16[512,1536]{1,0:T(8,128)(2,1)}, bf16[512,1536]{1,0:T(8,128)(2,1)S(1)}, u32[]{:S(2)}, u32[]{:S(2)}) collective-permute-start(bf16[512,1536]{1,0:T(8,128)(2,1)} %get-tuple-element.326), channel_id=1, source_target_pairs={{0,4},{1,5},{2,6},{3,7},{4,0},{5,1},{6,2},{7,3},{8,12},{9,13},{10,... | collective-permute-start | bytes 4718600 | tf_op jit(solution)/shard_map/ppermute | solution.py:135
  432.5 3.4 collective-permute-start.59
  435.9 14.2 %input_grad.1.refs_0_ = f32[1024,1024]{1,0:T(8,128)} custom-call(s32[8]{0:T(128)} %dynamic-slice_bitcast_fusion.tab, f32[1024,1024]{1,0:T(8,128)} %get-tuple-element.289.dmid_ref, bf16[1024,1024]{1,0:T(8,128)(2,1)} %get-tuple-element.191.x_ref, f32[8,1024]{1,0:T(8,128)} %get-tuple-element.196.gain_ref, bf16[3,1024,512]{2,1,0:T(8,128)(2,1)} %get-tuple-element.323.refs_0_, ...), custom_call_target="tpu_custom_call" | custom-call | flops 6442450944 | bytes 23068672 | tf_op jit(solution)/shard_map/input_grad/pallas_call | solution.py:656
  457.0 9.1 %collective-permute-done.61.refs_1_ = bf16[256,1536]{1,0:T(8,128)(2,1)S(1)} collective-permute-done((bf16[256,1536]{1,0:T(8,128)(2,1)S(1)}, bf16[256,1536]{1,0:T(8,128)(2,1)S(1)}, u32[]{:S(2)}, u32[]{:S(2)}) %collective-permute-start.61) | collective-permute-done | bytes 786464 | tf_op jit(solution)/shard_map/ppermute | solution.py:135
  469.3 6.6 %collective-permute-done.62.refs_1_ = bf16[128,1536]{1,0:T(8,128)(2,1)S(1)} collective-permute-done((bf16[128,1536]{1,0:T(8,128)(2,1)S(1)}, bf16[128,1536]{1,0:T(8,128)(2,1)S(1)}, u32[]{:S(2)}, u32[]{:S(2)}) %collective-permute-start.62) | collective-permute-done | bytes 393248 | tf_op jit(solution)/shard_map/ppermute | solution.py:135
  477.8 2.0 convert_add_fusion.4
  492.3 2.7 multiply_reduce_fusion
  497.7 7.3 %reduce-scatter.10.cloned.1.call-done = f32[32,1536]{1,0:T(8,128)} async-done(((f32[128,1536]{1,0:T(8,128)}), f32[32,1536]{1,0:T(8,128)}) %reduce-scatter.10.cloned.1.call-update) | async-done | bytes 196624 | tf_op jit(solution)/shard_map/reduce_scatter | solution.py:775
  514.5 3.9 all-to-all-start
  518.8 6.7 %all-to-all-done = f32[32,1,128]{2,1,0:T(1,128)S(1)} async-done(((f32[32,1,128]{2,1,0:T(1,128)}), f32[32,1,128]{2,1,0:T(1,128)S(1)}, u32[]{:S(2)}, u32[]{:S(2)}) %all-to-all-start) | async-done | bytes 16416 | tf_op jit(solution)/shard_map/all_to_all | solution.py:800
  530.4 3.0 multiply_add_fusion
  (456 shorter events, 123.0 us)
Async XLA Ops:
  7.2 75.1 %all-gather.2.cloned.1.call-start = ((), (), s32[]{:S(2)}) async-start(), calls=%async_computation.8 | async-start | bytes 2949120 | tf_op jit(solution)/shard_map/all_gather | solution.py:711
  14.2 465.7 %reduce-scatter.14.cloned.1.call-start = ((), (), s32[]{:S(2)}) async-start(), calls=%async_computation.12 | async-start | bytes 1310720 | tf_op jit(solution)/shard_map/reduce_scatter | solution.py:775
  43.4 19.9 %collective-permute-start = (bf16[128,3200]{1,0:T(8,128)(2,1)}, bf16[128,3200]{1,0:T(8,128)(2,1)S(1)}, u32[]{:S(2)}, u32[]{:S(2)}) collective-permute-start(bf16[128,3200]{1,0:T(8,128)(2,1)} %get-tuple-element.182), channel_id=1, source_target_pairs={{0,16},{1,17},{2,18},{3,19},{4,12},{5,13},{6,14},{7,15},{8,24},{9,... | collective-permute-start | bytes 2457608 | tf_op jit(solution)/shard_map/ppermute | solution.py:135
  44.9 19.9 %collective-permute-start.1 = (bf16[128,3200]{1,0:T(8,128)(2,1)S(1)}, bf16[128,3200]{1,0:T(8,128)(2,1)S(1)}, u32[]{:S(2)}, u32[]{:S(2)}) collective-permute-start(bf16[128,3200]{1,0:T(8,128)(2,1)S(1)} %all_gather.6.refs_0_.refs_8_.refs_2_), channel_id=1, source_target_pairs={{0,8},{1,9},{2,10},{3,11},{4,20},{5,21},{6,22},{7,23},{8,0},{9,1},... | collective-permute-start | bytes 2457608 | tf_op jit(solution)/shard_map/ppermute | solution.py:135
  85.7 36.6 %collective-permute-start.9 = (bf16[128,2048]{1,0:T(8,128)(2,1)S(1)}, bf16[128,2048]{1,0:T(8,128)(2,1)}, u32[]{:S(2)}, u32[]{:S(2)}) collective-permute-start(bf16[128,2048]{1,0:T(8,128)(2,1)S(1)} %get-tuple-element.495.refs_0_.refs_8_), channel_id=1, source_target_pairs={{0,8},{1,9},{2,10},{3,11},{4,20},{5,21},{6,22},{7,23},{8,0},{9,1},... | collective-permute-start | bytes 1572872 | tf_op jit(solution)/shard_map/ppermute | solution.py:135
  90.0 17.9 %collective-permute-start.7 = (bf16[128,2048]{1,0:T(8,128)(2,1)}, bf16[128,2048]{1,0:T(8,128)(2,1)}, u32[]{:S(2)}, u32[]{:S(2)}) collective-permute-start(bf16[128,2048]{1,0:T(8,128)(2,1)} %get-tuple-element.198), channel_id=1, source_target_pairs={{0,16},{1,17},{2,18},{3,19},{4,12},{5,13},{6,14},{7,15},{8,24},{9,... | collective-permute-start | bytes 1572872 | tf_op jit(solution)/shard_map/ppermute | solution.py:135
  91.4 16.5 %collective-permute-start.8 = (bf16[128,1024]{1,0:T(8,128)(2,1)S(1)}, bf16[128,1024]{1,0:T(8,128)(2,1)}, u32[]{:S(2)}, u32[]{:S(2)}) collective-permute-start(bf16[128,1024]{1,0:T(8,128)(2,1)S(1)} %copy-done.59), channel_id=1, source_target_pairs={{0,16},{1,17},{2,18},{3,19},{4,12},{5,13},{6,14},{7,15},{8,24},{9,... | collective-permute-start | bytes 786440 | tf_op jit(solution)/shard_map/ppermute | solution.py:135
  92.3 27.9 %collective-permute-start.11 = (bf16[128,2048]{1,0:T(8,128)(2,1)}, bf16[128,2048]{1,0:T(8,128)(2,1)}, u32[]{:S(2)}, u32[]{:S(2)}) collective-permute-start(bf16[128,2048]{1,0:T(8,128)(2,1)} %get-tuple-element.203), channel_id=1, source_target_pairs={{0,16},{1,17},{2,18},{3,19},{4,12},{5,13},{6,14},{7,15},{8,24},{9,... | collective-permute-start | bytes 1572872 | tf_op jit(solution)/shard_map/ppermute | solution.py:135
  108.0 15.8 %collective-permute-start.10 = (bf16[128,2048]{1,0:T(8,128)(2,1)}, bf16[128,2048]{1,0:T(8,128)(2,1)}, u32[]{:S(2)}, u32[]{:S(2)}) collective-permute-start(bf16[128,2048]{1,0:T(8,128)(2,1)} %get-tuple-element.202.refs_1_.refs_9_), channel_id=1, source_target_pairs={{0,8},{1,9},{2,10},{3,11},{4,20},{5,21},{6,22},{7,23},{8,0},{9,1},... | collective-permute-start | bytes 1572872 | tf_op jit(solution)/shard_map/ppermute | solution.py:135
  120.2 19.9 %collective-permute-start.14 = (bf16[128,2048]{1,0:T(8,128)(2,1)S(1)}, bf16[128,2048]{1,0:T(8,128)(2,1)S(1)}, u32[]{:S(2)}, u32[]{:S(2)}) collective-permute-start(bf16[128,2048]{1,0:T(8,128)(2,1)S(1)} %get-tuple-element.495.refs_0_.refs_8_), channel_id=1, source_target_pairs={{0,4},{1,5},{2,6},{3,7},{4,0},{5,1},{6,2},{7,3},{8,12},{9,13},{10,... | collective-permute-start | bytes 1572872 | tf_op jit(solution)/shard_map/ppermute | solution.py:135
  120.3 20.4 %collective-permute-start.18 = (bf16[128,2048]{1,0:T(8,128)(2,1)}, bf16[128,2048]{1,0:T(8,128)(2,1)}, u32[]{:S(2)}, u32[]{:S(2)}) collective-permute-start(bf16[128,2048]{1,0:T(8,128)(2,1)} %get-tuple-element.494.refs_0_.refs_8_), channel_id=1, source_target_pairs={{0,8},{1,9},{2,10},{3,11},{4,20},{5,21},{6,22},{7,23},{8,0},{9,1},... | collective-permute-start | bytes 1572872 | tf_op jit(solution)/shard_map/ppermute | solution.py:135
  122.3 17.7 %collective-permute-start.20 = (bf16[128,1024]{1,0:T(8,128)(2,1)S(1)}, bf16[128,1024]{1,0:T(8,128)(2,1)}, u32[]{:S(2)}, u32[]{:S(2)}) collective-permute-start(bf16[128,1024]{1,0:T(8,128)(2,1)S(1)} %copy-done.61), channel_id=1, source_target_pairs={{0,4},{1,5},{2,6},{3,7},{4,0},{5,1},{6,2},{7,3},{8,12},{9,13},{10,... | collective-permute-start | bytes 786440 | tf_op jit(solution)/shard_map/ppermute | solution.py:135
  123.7 18.9 %collective-permute-start.15 = (bf16[128,2048]{1,0:T(8,128)(2,1)}, bf16[128,2048]{1,0:T(8,128)(2,1)}, u32[]{:S(2)}, u32[]{:S(2)}) collective-permute-start(bf16[128,2048]{1,0:T(8,128)(2,1)} %get-tuple-element.202.refs_1_.refs_9_), channel_id=1, source_target_pairs={{0,4},{1,5},{2,6},{3,7},{4,0},{5,1},{6,2},{7,3},{8,12},{9,13},{10,... | collective-permute-start | bytes 1572872 | tf_op jit(solution)/shard_map/ppermute | solution.py:135
  123.7 18.9 %collective-permute-start.21 = (bf16[128,1024]{1,0:T(8,128)(2,1)}, bf16[128,1024]{1,0:T(8,128)(2,1)}, u32[]{:S(2)}, u32[]{:S(2)}) collective-permute-start(bf16[128,1024]{1,0:T(8,128)(2,1)} %get-tuple-element.204.refs_3_), channel_id=1, source_target_pairs={{0,4},{1,5},{2,6},{3,7},{4,0},{5,1},{6,2},{7,3},{8,12},{9,13},{10,... | collective-permute-start | bytes 786440 | tf_op jit(solution)/shard_map/ppermute | solution.py:135
  140.1 19.7 %collective-permute-start.16 = (bf16[128,2048]{1,0:T(8,128)(2,1)}, bf16[128,2048]{1,0:T(8,128)(2,1)}, u32[]{:S(2)}, u32[]{:S(2)}) collective-permute-start(bf16[128,2048]{1,0:T(8,128)(2,1)} %get-tuple-element.208.refs_2_.refs_10_), channel_id=1, source_target_pairs={{0,4},{1,5},{2,6},{3,7},{4,0},{5,1},{6,2},{7,3},{8,12},{9,13},{10,... | collective-permute-start | bytes 1572872 | tf_op jit(solution)/shard_map/ppermute | solution.py:135
  140.2 19.6 %collective-permute-start.17 = (bf16[128,2048]{1,0:T(8,128)(2,1)}, bf16[128,2048]{1,0:T(8,128)(2,1)S(1)}, u32[]{:S(2)}, u32[]{:S(2)}) collective-permute-start(bf16[128,2048]{1,0:T(8,128)(2,1)} %get-tuple-element.209.refs_3_.refs_11_), channel_id=1, source_target_pairs={{0,4},{1,5},{2,6},{3,7},{4,0},{5,1},{6,2},{7,3},{8,12},{9,13},{10,... | collective-permute-start | bytes 1572872 | tf_op jit(solution)/shard_map/ppermute | solution.py:135
  140.7 19.2 %collective-permute-start.19 = (bf16[128,2048]{1,0:T(8,128)(2,1)}, bf16[128,2048]{1,0:T(8,128)(2,1)}, u32[]{:S(2)}, u32[]{:S(2)}) collective-permute-start(bf16[128,2048]{1,0:T(8,128)(2,1)} %get-tuple-element.210.refs_1_.refs_9_), channel_id=1, source_target_pairs={{0,8},{1,9},{2,10},{3,11},{4,20},{5,21},{6,22},{7,23},{8,0},{9,1},... | collective-permute-start | bytes 1572872 | tf_op jit(solution)/shard_map/ppermute | solution.py:135
  142.7 16.5 %collective-permute-start.22 = (bf16[128,1024]{1,0:T(8,128)(2,1)}, bf16[128,1024]{1,0:T(8,128)(2,1)S(1)}, u32[]{:S(2)}, u32[]{:S(2)}) collective-permute-start(bf16[128,1024]{1,0:T(8,128)(2,1)} %get-tuple-element.211.refs_4_), channel_id=1, source_target_pairs={{0,4},{1,5},{2,6},{3,7},{4,0},{5,1},{6,2},{7,3},{8,12},{9,13},{10,... | collective-permute-start | bytes 786440 | tf_op jit(solution)/shard_map/ppermute | solution.py:135
  142.7 16.6 %collective-permute-start.23 = (bf16[128,1024]{1,0:T(8,128)(2,1)}, bf16[128,1024]{1,0:T(8,128)(2,1)}, u32[]{:S(2)}, u32[]{:S(2)}) collective-permute-start(bf16[128,1024]{1,0:T(8,128)(2,1)} %get-tuple-element.212.refs_5_), channel_id=1, source_target_pairs={{0,4},{1,5},{2,6},{3,7},{4,0},{5,1},{6,2},{7,3},{8,12},{9,13},{10,... | collective-permute-start | bytes 786440 | tf_op jit(solution)/shard_map/ppermute | solution.py:135
  174.0 24.9 %collective-permute-start.29 = (bf16[128,2048]{1,0:T(8,128)(2,1)S(1)}, bf16[128,2048]{1,0:T(8,128)(2,1)}, u32[]{:S(2)}, u32[]{:S(2)}) collective-permute-start(bf16[128,2048]{1,0:T(8,128)(2,1)S(1)} %copy-done.51), channel_id=1, source_target_pairs={{0,8},{1,9},{2,10},{3,11},{4,20},{5,21},{6,22},{7,23},{8,0},{9,1},... | collective-permute-start | bytes 1572872 | tf_op jit(solution)/shard_map/ppermute | solution.py:135
  174.3 24.6 %collective-permute-start.31 = (bf16[128,2048]{1,0:T(8,128)(2,1)S(1)}, bf16[128,2048]{1,0:T(8,128)(2,1)}, u32[]{:S(2)}, u32[]{:S(2)}) collective-permute-start(bf16[128,2048]{1,0:T(8,128)(2,1)S(1)} %copy-done.44), channel_id=1, source_target_pairs={{0,16},{1,17},{2,18},{3,19},{4,12},{5,13},{6,14},{7,15},{8,24},{9,... | collective-permute-start | bytes 1572872 | tf_op jit(solution)/shard_map/ppermute | solution.py:135
  175.4 23.5 %collective-permute-start.30 = (bf16[128,2048]{1,0:T(8,128)(2,1)}, bf16[128,2048]{1,0:T(8,128)(2,1)}, u32[]{:S(2)}, u32[]{:S(2)}) collective-permute-start(bf16[128,2048]{1,0:T(8,128)(2,1)} %get-tuple-element.236.refs_1_.refs_9_), channel_id=1, source_target_pairs={{0,8},{1,9},{2,10},{3,11},{4,20},{5,21},{6,22},{7,23},{8,0},{9,1},... | collective-permute-start | bytes 1572872 | tf_op jit(solution)/shard_map/ppermute | solution.py:135
  198.9 33.2 %collective-permute-start.32 = (bf16[512,2048]{1,0:T(8,128)(2,1)}, bf16[512,2048]{1,0:T(8,128)(2,1)}, u32[]{:S(2)}, u32[]{:S(2)}) collective-permute-start(bf16[512,2048]{1,0:T(8,128)(2,1)} %get-tuple-element.250), channel_id=1, source_target_pairs={{0,4},{1,5},{2,6},{3,7},{4,0},{5,1},{6,2},{7,3},{8,12},{9,13},{10,... | collective-permute-start | bytes 6291464 | tf_op jit(solution)/shard_map/ppermute | solution.py:135
  200.0 32.1 %collective-permute-start.34 = (bf16[128,2048]{1,0:T(8,128)(2,1)}, bf16[128,2048]{1,0:T(8,128)(2,1)}, u32[]{:S(2)}, u32[]{:S(2)}) collective-permute-start(bf16[128,2048]{1,0:T(8,128)(2,1)} %get-tuple-element.236.refs_1_.refs_9_), channel_id=1, source_target_pairs={{0,4},{1,5},{2,6},{3,7},{4,0},{5,1},{6,2},{7,3},{8,12},{9,13},{10,... | collective-permute-start | bytes 1572872 | tf_op jit(solution)/shard_map/ppermute | solution.py:135
  200.6 31.6 %collective-permute-start.35 = (bf16[128,2048]{1,0:T(8,128)(2,1)}, bf16[128,2048]{1,0:T(8,128)(2,1)}, u32[]{:S(2)}, u32[]{:S(2)}) collective-permute-start(bf16[128,2048]{1,0:T(8,128)(2,1)} %get-tuple-element.251.refs_2_.refs_10_), channel_id=1, source_target_pairs={{0,4},{1,5},{2,6},{3,7},{4,0},{5,1},{6,2},{7,3},{8,12},{9,13},{10,... | collective-permute-start | bytes 1572872 | tf_op jit(solution)/shard_map/ppermute | solution.py:135
  204.5 27.7 %collective-permute-start.36 = (bf16[128,2048]{1,0:T(8,128)(2,1)}, bf16[128,2048]{1,0:T(8,128)(2,1)S(1)}, u32[]{:S(2)}, u32[]{:S(2)}) collective-permute-start(bf16[128,2048]{1,0:T(8,128)(2,1)} %get-tuple-element.252.refs_3_.refs_11_), channel_id=1, source_target_pairs={{0,4},{1,5},{2,6},{3,7},{4,0},{5,1},{6,2},{7,3},{8,12},{9,13},{10,... | collective-permute-start | bytes 1572872 | tf_op jit(solution)/shard_map/ppermute | solution.py:135
  209.0 23.2 %collective-permute-start.38 = (bf16[128,2048]{1,0:T(8,128)(2,1)}, bf16[128,2048]{1,0:T(8,128)(2,1)}, u32[]{:S(2)}, u32[]{:S(2)}) collective-permute-start(bf16[128,2048]{1,0:T(8,128)(2,1)} %get-tuple-element.238.refs_1_.refs_9_), channel_id=1, source_target_pairs={{0,8},{1,9},{2,10},{3,11},{4,20},{5,21},{6,22},{7,23},{8,0},{9,1},... | collective-permute-start | bytes 1572872 | tf_op jit(solution)/shard_map/ppermute | solution.py:135
  232.9 31.4 %collective-permute-start.40 = (bf16[512,2048]{1,0:T(8,128)(2,1)}, bf16[512,2048]{1,0:T(8,128)(2,1)}, u32[]{:S(2)}, u32[]{:S(2)}) collective-permute-start(bf16[512,2048]{1,0:T(8,128)(2,1)} %get-tuple-element.268), channel_id=1, source_target_pairs={{0,4},{1,5},{2,6},{3,7},{4,0},{5,1},{6,2},{7,3},{8,12},{9,13},{10,... | collective-permute-start | bytes 6291464 | tf_op jit(solution)/shard_map/ppermute | solution.py:135
  233.7 30.6 %collective-permute-start.42 = (bf16[128,2048]{1,0:T(8,128)(2,1)}, bf16[128,2048]{1,0:T(8,128)(2,1)}, u32[]{:S(2)}, u32[]{:S(2)}) collective-permute-start(bf16[128,2048]{1,0:T(8,128)(2,1)} %get-tuple-element.238.refs_1_.refs_9_), channel_id=1, source_target_pairs={{0,4},{1,5},{2,6},{3,7},{4,0},{5,1},{6,2},{7,3},{8,12},{9,13},{10,... | collective-permute-start | bytes 1572872 | tf_op jit(solution)/shard_map/ppermute | solution.py:135
  238.2 26.1 %collective-permute-start.39 = (bf16[256,2048]{1,0:T(8,128)(2,1)}, bf16[256,2048]{1,0:T(8,128)(2,1)S(1)}, u32[]{:S(2)}, u32[]{:S(2)}) collective-permute-start(bf16[256,2048]{1,0:T(8,128)(2,1)} %get-tuple-element.487), channel_id=1, source_target_pairs={{0,8},{1,9},{2,10},{3,11},{4,20},{5,21},{6,22},{7,23},{8,0},{9,1},... | collective-permute-start | bytes 3145736 | tf_op jit(solution)/shard_map/ppermute | solution.py:135
  239.8 24.4 %collective-permute-start.43 = (bf16[128,2048]{1,0:T(8,128)(2,1)}, bf16[128,2048]{1,0:T(8,128)(2,1)}, u32[]{:S(2)}, u32[]{:S(2)}) collective-permute-start(bf16[128,2048]{1,0:T(8,128)(2,1)} %get-tuple-element.253.refs_2_.refs_10_), channel_id=1, source_target_pairs={{0,4},{1,5},{2,6},{3,7},{4,0},{5,1},{6,2},{7,3},{8,12},{9,13},{10,... | collective-permute-start | bytes 1572872 | tf_op jit(solution)/shard_map/ppermute | solution.py:135
  240.6 23.6 %collective-permute-start.44 = (bf16[128,2048]{1,0:T(8,128)(2,1)}, bf16[128,2048]{1,0:T(8,128)(2,1)S(1)}, u32[]{:S(2)}, u32[]{:S(2)}) collective-permute-start(bf16[128,2048]{1,0:T(8,128)(2,1)} %get-tuple-element.254.refs_3_.refs_11_), channel_id=1, source_target_pairs={{0,4},{1,5},{2,6},{3,7},{4,0},{5,1},{6,2},{7,3},{8,12},{9,13},{10,... | collective-permute-start | bytes 1572872 | tf_op jit(solution)/shard_map/ppermute | solution.py:135
  265.5 30.8 %collective-permute-start.47 = (bf16[512,2048]{1,0:T(8,128)(2,1)}, bf16[512,2048]{1,0:T(8,128)(2,1)}, u32[]{:S(2)}, u32[]{:S(2)}) collective-permute-start(bf16[512,2048]{1,0:T(8,128)(2,1)} %get-tuple-element.283), channel_id=1, source_target_pairs={{0,4},{1,5},{2,6},{3,7},{4,0},{5,1},{6,2},{7,3},{8,12},{9,13},{10,... | collective-permute-start | bytes 6291464 | tf_op jit(solution)/shard_map/ppermute | solution.py:135
  270.9 25.4 %collective-permute-start.46 = (bf16[256,2048]{1,0:T(8,128)(2,1)}, bf16[256,2048]{1,0:T(8,128)(2,1)S(1)}, u32[]{:S(2)}, u32[]{:S(2)}) collective-permute-start(bf16[256,2048]{1,0:T(8,128)(2,1)} %get-tuple-element.485), channel_id=1, source_target_pairs={{0,8},{1,9},{2,10},{3,11},{4,20},{5,21},{6,22},{7,23},{8,0},{9,1},... | collective-permute-start | bytes 3145736 | tf_op jit(solution)/shard_map/ppermute | solution.py:135
  272.1 24.1 %collective-permute-start.45 = (bf16[128,2048]{1,0:T(8,128)(2,1)}, bf16[128,2048]{1,0:T(8,128)(2,1)S(1)}, u32[]{:S(2)}, u32[]{:S(2)}) collective-permute-start(bf16[128,2048]{1,0:T(8,128)(2,1)} %add_convert_fusion.21), channel_id=1, source_target_pairs={{0,16},{1,17},{2,18},{3,19},{4,12},{5,13},{6,14},{7,15},{8,24},{9,... | collective-permute-start | bytes 1572872 | tf_op jit(solution)/shard_map/ppermute | solution.py:135
  297.4 26.1 %collective-permute-start.50 = (bf16[512,2048]{1,0:T(8,128)(2,1)}, bf16[512,2048]{1,0:T(8,128)(2,1)}, u32[]{:S(2)}, u32[]{:S(2)}) collective-permute-start(bf16[512,2048]{1,0:T(8,128)(2,1)} %get-tuple-element.295), channel_id=1, source_target_pairs={{0,4},{1,5},{2,6},{3,7},{4,0},{5,1},{6,2},{7,3},{8,12},{9,13},{10,... | collective-permute-start | bytes 6291464 | tf_op jit(solution)/shard_map/ppermute | solution.py:135
  302.8 20.7 %collective-permute-start.49 = (bf16[256,2048]{1,0:T(8,128)(2,1)}, bf16[256,2048]{1,0:T(8,128)(2,1)}, u32[]{:S(2)}, u32[]{:S(2)}) collective-permute-start(bf16[256,2048]{1,0:T(8,128)(2,1)} %get-tuple-element.483), channel_id=1, source_target_pairs={{0,8},{1,9},{2,10},{3,11},{4,20},{5,21},{6,22},{7,23},{8,0},{9,1},... | collective-permute-start | bytes 3145736 | tf_op jit(solution)/shard_map/ppermute | solution.py:135
  305.7 175.3 %reduce-scatter.16.cloned.1.call-start = ((), (), s32[]{:S(2)}) async-start(), calls=%async_computation.13 | async-start | bytes 1310720 | tf_op jit(solution)/shard_map/reduce_scatter | solution.py:775
  328.0 20.7 %collective-permute-start.52 = (bf16[256,2048]{1,0:T(8,128)(2,1)}, bf16[256,2048]{1,0:T(8,128)(2,1)}, u32[]{:S(2)}, u32[]{:S(2)}) collective-permute-start(bf16[256,2048]{1,0:T(8,128)(2,1)} %get-tuple-element.481), channel_id=1, source_target_pairs={{0,8},{1,9},{2,10},{3,11},{4,20},{5,21},{6,22},{7,23},{8,0},{9,1},... | collective-permute-start | bytes 3145736 | tf_op jit(solution)/shard_map/ppermute | solution.py:135
  331.0 151.4 %reduce-scatter.18.cloned.1.call-start = ((), (), s32[]{:S(2)}) async-start(), calls=%async_computation.14 | async-start | bytes 1310720 | tf_op jit(solution)/shard_map/reduce_scatter | solution.py:775
  352.3 131.6 %reduce-scatter.20.cloned.1.call-start = ((), (), s32[]{:S(2)}) async-start(), calls=%async_computation.15 | async-start | bytes 1310720 | tf_op jit(solution)/shard_map/reduce_scatter | solution.py:775
  354.8 25.0 %collective-permute-start.55 = (bf16[256,1024]{1,0:T(8,128)(2,1)}, bf16[256,1024]{1,0:T(8,128)(2,1)S(1)}, u32[]{:S(2)}, u32[]{:S(2)}) collective-permute-start(bf16[256,1024]{1,0:T(8,128)(2,1)} %get-tuple-element.497), channel_id=1, source_target_pairs={{0,8},{1,9},{2,10},{3,11},{4,20},{5,21},{6,22},{7,23},{8,0},{9,1},... | collective-permute-start | bytes 1572872 | tf_op jit(solution)/shard_map/ppermute | solution.py:135
  358.5 21.9 %collective-permute-start.54 = (bf16[128,2048]{1,0:T(8,128)(2,1)}, bf16[128,2048]{1,0:T(8,128)(2,1)S(1)}, u32[]{:S(2)}, u32[]{:S(2)}) collective-permute-start(bf16[128,2048]{1,0:T(8,128)(2,1)} %add_convert_fusion.18), channel_id=1, source_target_pairs={{0,16},{1,17},{2,18},{3,19},{4,12},{5,13},{6,14},{7,15},{8,24},{9,... | collective-permute-start | bytes 1572872 | tf_op jit(solution)/shard_map/ppermute | solution.py:135
  386.8 108.4 %reduce-scatter.12.cloned.1.call-start = ((), (), s32[]{:S(2)}) async-start(), calls=%async_computation.11 | async-start | bytes 655360 | tf_op jit(solution)/shard_map/reduce_scatter | solution.py:775
  416.0 34.1 %collective-permute-start.60 = (bf16[512,1536]{1,0:T(8,128)(2,1)}, bf16[512,1536]{1,0:T(8,128)(2,1)S(1)}, u32[]{:S(2)}, u32[]{:S(2)}) collective-permute-start(bf16[512,1536]{1,0:T(8,128)(2,1)} %get-tuple-element.326), channel_id=1, source_target_pairs={{0,4},{1,5},{2,6},{3,7},{4,0},{5,1},{6,2},{7,3},{8,12},{9,13},{10,... | collective-permute-start | bytes 4718600 | tf_op jit(solution)/shard_map/ppermute | solution.py:135
  431.6 65.3 %reduce-scatter.8.cloned.1.call-start = ((), (), s32[]{:S(2)}) async-start(), calls=%async_computation.9 | async-start | bytes 983040 | tf_op jit(solution)/shard_map/reduce_scatter | solution.py:775
  432.5 17.6 %collective-permute-start.59 = (bf16[128,1536]{1,0:T(8,128)(2,1)}, bf16[128,1536]{1,0:T(8,128)(2,1)S(1)}, u32[]{:S(2)}, u32[]{:S(2)}) collective-permute-start(bf16[128,1536]{1,0:T(8,128)(2,1)} %add_convert_fusion.25), channel_id=1, source_target_pairs={{0,16},{1,17},{2,18},{3,19},{4,12},{5,13},{6,14},{7,15},{8,24},{9,... | collective-permute-start | bytes 1179656 | tf_op jit(solution)/shard_map/ppermute | solution.py:135
  456.5 48.5 %reduce-scatter.10.cloned.1.call-start = ((), (), s32[]{:S(2)}) async-start(), calls=%async_computation.10 | async-start | bytes 983040 | tf_op jit(solution)/shard_map/reduce_scatter | solution.py:775
  (123 other events, 1086.6 us)
Sparse Core Ops, SparseCore 0:
  14.3 58.6 all-gather.1
  305.9 27.5 reduce-scatter.13
  335.8 25.8 reduce-scatter.15
  363.8 27.3 reduce-scatter.17
  393.5 25.7 reduce-scatter.19
  431.7 24.1 reduce-scatter.11
  458.2 21.8 reduce-scatter.7
  482.4 22.5 reduce-scatter.9

commit v2 on v1

v2 whole, which is shorter than its diff:
```python
import functools

import jax
import jax.numpy as jnp
import numpy as np
from jax import lax
from jax.experimental import pallas as pl
from jax.experimental.pallas import tpu as pltpu
from jax.sharding import PartitionSpec as P

D = 1024
HEAD_DIM = 64
FF = 4096
STEP = 7
FANO = 16

NORM_EPS = 1e-06
ADAM_EPS = 1e-08
BETA_ONE = 0.9
BETA_TWO = 0.95
SHADOW_KEEP = 0.8
CLIP_NORM = 1.0

AXES = ("dp", "fsdp")
GROUPS = 2
LANES = 128
VMEM = 62 << 20
f32 = jnp.float32
bf16 = jnp.bfloat16
NT = (((1,), (1,)), ((), ()))
TN = (((0,), (0,)), ((), ()))
GELU_A = 0.7978845608028654
GELU_B = 0.044715


def full(shape, single=False):
    rank = len(shape)
    mode = dict(pipeline_mode=pl.Buffered(1)) if single else {}
    return pl.BlockSpec(shape, lambda *_: (0,) * rank, **mode)


def params():
    return pltpu.CompilerParams(vmem_limit_bytes=VMEM)


def cost(flops, nbytes, trans=0):
    return pl.CostEstimate(flops=flops, bytes_accessed=nbytes, transcendentals=trans)


class Plan:
    def __init__(self, mesh):
        self.ndp, self.nfs = mesh.shape["dp"], mesh.shape["fsdp"]
        self.ndev = self.ndp * self.nfs
        self.bits = self.ndp.bit_length() - 1
        others = list(range(1, self.bits))
        half = len(others) // 2
        self.order = (others, others[half:] + others[:half])
        self.block = D // self.ndp
        tab = np.zeros((self.ndp, self.ndp), np.int32)
        for me in range(self.ndp):
            for rel in range(self.ndp):
                core = (me & 1) ^ (rel >> (self.bits - 1))
                nat = core
                for s, bit in enumerate(self.order[core]):
                    r = (rel >> (self.bits - 2 - s)) & 1
                    nat |= (((me >> bit) & 1) ^ r) << bit
                tab[me, rel] = nat
        self.tab = tab

    def pairs(self, flip):
        out = []
        for d in range(self.ndp):
            for f in range(self.nfs):
                out.append((d * self.nfs + f, flip(d) * self.nfs + f))
        return out

    def core_pairs(self):
        return self.pairs(lambda d: d ^ 1)

    def mix_pairs(self, s):
        return self.pairs(lambda d: d ^ (1 << self.order[d & 1][s]))

    def gather(self, mine):
        for s in reversed(range(self.bits - 1)):
            wide = s == 0
            (got,) = yield [mine], self.mix_pairs(s), None if wide else ("join", mine)
            mine = mine if wide else got
        held = [mine, got]
        return held + (yield held, self.core_pairs(), None)

    def scatter(self, sent, kept):
        pairs = self.core_pairs()
        for s in range(self.bits - 1):
            kept, sent = yield [sent], pairs, ("sum", [kept], [bf16, bf16])
            pairs = self.mix_pairs(s)
        (total,) = yield [sent], pairs, ("sum", [kept], [bf16])
        return total

    def scatter_direct(self, sent, kept):
        count = self.ndp // 2
        kept, *sent = yield [sent], self.core_pairs(), ("sum", [kept], [f32] + [bf16] * (count - 1))
        pairs = [None] + [
            self.pairs(lambda d: d ^ self.mask(d & 1, rel)) for rel in range(1, count)
        ]
        (total,) = yield sent, pairs[1:], ("sum", [kept], [f32])
        return total

    def mask(self, core, rel):
        bits = enumerate(self.order[core])
        return sum(((rel >> (self.bits - 2 - s)) & 1) << bit for s, bit in bits)

    def own_rows(self, total, direct=False):
        if not direct or self.nfs > 4:
            return lax.psum_scatter(total, "fsdp", scatter_dimension=0, tiled=True).astype(f32)
        me, rows = lax.axis_index("fsdp"), total.shape[0] // self.nfs
        block = lambda f: lax.dynamic_slice_in_dim(total, f * rows, rows, 0)
        sum_ = block(me)
        for flip in range(1, self.nfs):
            pairs = [(i, i // self.nfs * self.nfs + (i % self.nfs ^ flip)) for i in range(self.ndev)]
            sum_ = sum_ + lax.ppermute(block(me ^ flip), AXES, pairs)
        return sum_


def tie_kernel(count, jobs, *refs):
    sems = refs[-1]
    free = iter(range(sems.shape[0]))
    copy = lambda x, y: pltpu.make_async_copy(x, y, sems.at[next(free)])
    total = count + sum(job["inputs"] for job in jobs)
    made = sum(len(job["outputs"]) for job in jobs)
    inputs, outputs = list(refs[count:total]), list(refs[total + count : total + count + made])
    scratch = list(refs[total + count + made : -1])
    steps = []
    for job in jobs:
        ins = [inputs.pop(0) for _ in range(job["inputs"])]
        outs = [outputs.pop(0) for _ in job["outputs"]]
        if job["kind"] == "cut":
            at, wide = job["cut"]
            held = scratch.pop(0)
            steps.append(([copy(ins[0].at[:, pl.ds(at, wide)], held)], None, copy(held, outs[0])))
        elif job["kind"] == "join":
            held = scratch.pop(0)
            rows = ins[0].shape[0]
            loads = [copy(v, held.at[pl.ds(i * rows, rows)]) for i, v in enumerate(ins)]
            steps.append((loads, None, copy(held, outs[0])))
        else:
            rows = outs[0].shape[0]
            for i, out in reversed(list(enumerate(outs))):
                held = [scratch.pop(0) for _ in range(len(ins) + 1)]
                loads = [copy(v.at[pl.ds(i * rows, rows)], h) for v, h in zip(ins, held)]
                steps.append((loads, held, copy(held[-1], out)))
    for loads, _, _ in steps:
        for c in loads:
            c.start()
    for loads, held, save in steps:
        for c in loads:
            c.wait()
        if held:
            total = held[0][...].astype(f32)
            for h in held[1:-1]:
                total = total + h[...].astype(f32)
            held[-1][...] = total.astype(held[-1].dtype)
        save.start()
    for _, _, save in steps:
        save.wait()


def tie(same, work=()):
    leaves, form = jax.tree.flatten(same)
    place = pl.BlockSpec(memory_space=pl.ANY)
    count = len(leaves)
    jobs, inputs, made, scratch, copies = [], list(leaves), [], [], 1
    shape = lambda dims, kind: jax.ShapeDtypeStruct(dims, kind)
    for kind, *rest in work:
        if kind == "cut":
            v, at, wide = rest
            arrays, outs = [v], [shape((v.shape[0], wide), v.dtype)]
            scratch.append(outs[0])
            copies += 2
        elif kind == "join":
            arrays = rest
            outs = [shape((2 * rest[0].shape[0], rest[0].shape[1]), rest[0].dtype)]
            scratch.append(outs[0])
            copies += 3
        else:
            arrays, kinds = rest
            rows = arrays[0].shape[0] // len(kinds)
            outs = [shape((rows, arrays[0].shape[1]), k) for k in kinds]
            for out in reversed(outs):
                scratch += [shape(out.shape, v.dtype) for v in arrays] + [out]
            copies += (len(arrays) + 1) * len(outs)
        inputs += arrays
        made.append(outs)
        jobs.append(dict(kind=kind, inputs=len(arrays), outputs=outs, cut=tuple(rest[1:3]) if kind == "cut" else None))
    if not inputs:
        return same, []
    outputs = [shape(v.shape, v.dtype) for v in leaves] + [v for outs in made for v in outs]
    out = list(
        pl.pallas_call(
            functools.partial(tie_kernel, count, jobs),
            in_specs=[place] * len(inputs),
            out_specs=[place] * len(outputs),
            out_shape=outputs,
            scratch_shapes=[pltpu.VMEM(v.shape, v.dtype) for v in scratch]
            + [pltpu.SemaphoreType.DMA((copies,))],
            input_output_aliases={i: i for i in range(count)},
            compiler_params=params(),
            name="tie",
        )(*inputs)
    )
    same, out = jax.tree.unflatten(form, out[:count]), out[count:]
    return same, [[out.pop(0) for _ in outs] for outs in made]


class Flow:
    def __init__(self, plan):
        self.plan = plan
        self.live, self.flying, self.done, self.waiting = {}, {}, {}, {}

    def gather(self, name, array, at=None, wide=None):
        self.waiting[name] = (array, at, wide)

    def scatter(self, name, sent, kept, direct=False):
        way = self.plan.scatter_direct if direct else self.plan.scatter
        self.live[name] = way(sent, kept)

    def step(self, x, names):
        names = [n for n in names if n not in self.done]
        came = {n: self.flying.pop(n) for n in names if n in self.flying}
        start = {n: self.waiting.pop(n) for n in names if n in self.waiting}
        plain = {n: got for n, (got, merge) in came.items() if merge is None}
        whole = {n: v for n, (v, at, _) in start.items() if at is None}
        work = {}
        for n, (got, merge) in came.items():
            if merge and merge[0] == "join":
                work[n] = ("join", merge[1], *got)
            elif merge:
                work[n] = ("sum", merge[1] + got, merge[2])
        work |= {n: ("cut", *v) for n, v in start.items() if v[1] is not None}
        (x, plain, whole), made = tie((x, plain, whole), list(work.values()))
        made = dict(zip(work, made))
        for n in start:
            self.live[n] = self.plan.gather(whole[n] if n in whole else made[n][0])
        for n in names:
            value = None if n in start else plain.get(n, made.get(n))
            try:
                sent, pairs, merge = self.live[n].send(value)
                each = pairs if isinstance(pairs[0], list) else [pairs] * len(sent)
                self.flying[n] = ([lax.ppermute(v, AXES, p) for v, p in zip(sent, each)], merge)
            except StopIteration as stop:
                self.done[n] = stop.value
        return x

    def until(self, x, names):
        while any(n not in self.done for n in names):
            x = self.step(x, names)
        return x


def natural(dst, cols, pieces, src_cols, tab, block):
    j = 0
    for piece in pieces:
        for i in range(piece.shape[0] // block):
            row = pl.multiple_of(tab[j] * block, block)
            dst[pl.ds(row, block), cols] = piece[i * block : (i + 1) * block, src_cols]
            j += 1


def relative(sent, kept, cols, src, src_cols, tab, block):
    half = src.shape[0] // block // 2
    for j in range(2 * half):
        row = pl.multiple_of(tab[j] * block, block)
        out = kept if j < half else sent
        i = j % half
        out[i * block : (i + 1) * block, cols] = src[pl.ds(row, block), src_cols]


def qkv_kernel(count, block, first, tab, *refs):
    if first:
        x_ref, refs = refs[0], refs[1:]
        gains, weights = refs[:count], refs[count : 2 * count]
        qkv_ref, u_ref, gain_ref, u_t_ref, w_nat, g_nat = refs[2 * count :]

        @pl.when(pl.program_id(0) == 0)
        def _():
            natural(g_nat, slice(None), gains, slice(None), tab, block)
            rows = g_nat[...].astype(f32).T
            gain_ref[...] = rows[:8]
            x = x_ref[...].astype(f32)
            r = lax.rsqrt(jnp.mean(x * x, axis=1, keepdims=True) + NORM_EPS)
            u = (x * r * rows[0:1]).astype(bf16)
            u_ref[...] = u
            u_t_ref[...] = u.T

    else:
        u_ref, weights, (qkv_ref, w_nat) = refs[0], refs[1 : 1 + count], refs[1 + count :]
    natural(w_nat, slice(None), weights, slice(None), tab, block)
    qkv_ref[...] = jnp.dot(u_ref[...], w_nat[...], preferred_element_type=f32).astype(bf16)


def project_qkv(tab, x, pieces, block, columns, first):
    length, width = x.shape
    wide = 512
    last = columns // LANES
    col = pl.BlockSpec((length, wide), lambda j, t: (0, j))
    extra = first * [full((length, width)), full((8, width)), full((width, length))]
    shapes = first * [
        jax.ShapeDtypeStruct((length, width), bf16),
        jax.ShapeDtypeStruct((8, width), f32),
        jax.ShapeDtypeStruct((width, length), bf16),
    ]
    gains = first * [pl.BlockSpec((p.shape[0], LANES), lambda j, t: (0, last)) for p in pieces]
    return pl.pallas_call(
        functools.partial(qkv_kernel, len(pieces), block, first),
        grid_spec=pltpu.PrefetchScalarGridSpec(
            num_scalar_prefetch=1,
            grid=(columns // wide,),
            in_specs=[full((length, width), True)]
            + gains
            + [pl.BlockSpec((p.shape[0], wide), lambda j, t: (0, j)) for p in pieces],
            out_specs=[col] + extra,
            scratch_shapes=[pltpu.VMEM((width, wide), bf16)]
            + first * [pltpu.VMEM((width, LANES), bf16)],
        ),
        out_shape=[jax.ShapeDtypeStruct((length, columns), bf16)] + shapes,
        compiler_params=params(),
        cost_estimate=cost(2 * length * width * columns, 20 << 20),
        name="qkv",
    )(tab, x, *(first * pieces), *pieces)


def fold(v, op):
    v = v.reshape(v.shape[0] // 64, 64, v.shape[1])
    return op(op(v, axis=0), axis=0, keepdims=True)


def attend_kernel(rows_of, n_ref, q_ref, k_ref, v_ref, o_ref, lse_ref):
    n = n_ref[0]
    length = q_ref.shape[0]
    lane = lax.broadcasted_iota(jnp.int32, (1, LANES), 1)
    masks = [(lane < HEAD_DIM).astype(bf16), (lane >= HEAD_DIM).astype(bf16)]
    v_t = v_ref[...].T
    for i in range(length // rows_of):
        rows = pl.ds(i * rows_of, rows_of)
        keys = (i + 1) * rows_of

        def run(limited):
            q = q_ref[rows, :] * bf16(HEAD_DIM**-0.5)
            k = k_ref[0:keys, :]
            parts = []
            for h in range(2):
                s = lax.dot_general(k, q * masks[h], NT, preferred_element_type=f32)
                if limited:
                    key = lax.broadcasted_iota(jnp.int32, (keys, rows_of), 0)
                    query = lax.broadcasted_iota(jnp.int32, (keys, rows_of), 1) + i * rows_of
                    s = jnp.where((key <= query) & (key < n), s, -1e30)
                else:
                    key = lax.broadcasted_iota(jnp.int32, (rows_of, rows_of), 0)
                    query = lax.broadcasted_iota(jnp.int32, (rows_of, rows_of), 1)
                    tail = jnp.where(key <= query, s[keys - rows_of :], -1e30)
                    s = tail if i == 0 else jnp.concatenate([s[: keys - rows_of], tail], axis=0)
                peak = fold(s, jnp.max)
                e = jnp.exp(s - peak)
                total = fold(e, jnp.sum)
                p = (e * (1.0 / total)).astype(bf16)
                v_h = v_t[h * HEAD_DIM : (h + 1) * HEAD_DIM, 0:keys]
                parts.append(jnp.dot(v_h, p, preferred_element_type=f32))
                query = lax.broadcasted_iota(jnp.int32, (1, rows_of), 1) + i * rows_of
                lse_ref[0, h : h + 1, rows] = jnp.where(query < n, peak + jnp.log(total), 1e30)
            o_ref[rows, :] = jnp.concatenate(parts, axis=0).astype(bf16).T

        @pl.when(n >= keys)
        def _():
            run(False)

        @pl.when(n < keys)
        def _():
            run(True)


def attend(frames, qkv):
    length, width = qkv.shape[0], qkv.shape[1] // 3
    pairs = width // LANES
    part = lambda c: pl.BlockSpec((length, LANES), lambda j, n: (0, 3 * j + c))
    return pl.pallas_call(
        functools.partial(attend_kernel, 512),
        grid_spec=pltpu.PrefetchScalarGridSpec(
            num_scalar_prefetch=1,
            grid=(pairs,),
            in_specs=[part(0), part(1), part(2)],
            out_specs=[
                pl.BlockSpec((length, LANES), lambda j, n: (0, j)),
                pl.BlockSpec((1, 2, length), lambda j, n: (j, 0, 0)),
            ],
        ),
        out_shape=[
            jax.ShapeDtypeStruct((length, width), bf16),
            jax.ShapeDtypeStruct((pairs, 2, length), f32),
        ],
        compiler_params=params(),
        cost_estimate=cost(16 * length * length * width, 8 << 20, length * length * 16),
        name="attend",
    )(frames, qkv, qkv, qkv)


def mid_kernel(count, groups, block, tab, x_ref, gain_ref, *refs):
    o_refs, refs = refs[:groups], refs[groups:]
    weights = refs[:count]
    mid_ref, u_ref, u_t_ref, w_nat = refs[count:]

    @pl.when(pl.program_id(0) == 0)
    def _():
        natural(w_nat, slice(None), weights, slice(None), tab, block)

    o = jnp.concatenate([ref[...] for ref in o_refs], axis=1)
    mid = x_ref[...].astype(f32) + jnp.dot(o, w_nat[...], preferred_element_type=f32)
    r = lax.rsqrt(jnp.mean(mid * mid, axis=1, keepdims=True) + NORM_EPS)
    u = (mid * r * gain_ref[1:2, :]).astype(bf16)
    mid_ref[...] = mid
    u_ref[...] = u
    u_t_ref[...] = u.T


def middle(tab, o, x, gains, pieces, block):
    length, width = x.shape
    rows = 256
    row = pl.BlockSpec((rows, width), lambda i, t: (i, 0))
    return pl.pallas_call(
        functools.partial(mid_kernel, len(pieces), len(o), block),
        grid_spec=pltpu.PrefetchScalarGridSpec(
            num_scalar_prefetch=1,
            grid=(length // rows,),
            in_specs=[row, full((8, width))]
            + [pl.BlockSpec((rows, v.shape[1]), lambda i, t: (i, 0)) for v in o]
            + [full(p.shape) for p in pieces],
            out_specs=[row, row, pl.BlockSpec((width, rows), lambda i, t: (0, i))],
            scratch_shapes=[pltpu.VMEM((width, width), bf16)],
        ),
        out_shape=[
            jax.ShapeDtypeStruct((length, width), f32),
            jax.ShapeDtypeStruct((length, width), bf16),
            jax.ShapeDtypeStruct((width, length), bf16),
        ],
        compiler_params=params(),
        cost_estimate=cost(2 * length * width * width, 16 << 20),
        name="middle",
    )(tab, x, gains, *o, *pieces)


def gelu_both(z):
    sq = z * z
    t = jnp.tanh(z * (GELU_A + (GELU_A * GELU_B) * sq))
    half = 0.5 + 0.5 * t
    slope = half + (0.5 * z) * (1.0 - t * t) * (GELU_A + (3 * GELU_A * GELU_B) * sq)
    return z * half, slope


def mlp_kernel(count, block, sub, first, last, tab, *refs):
    u_hbm, u_t_hbm, g_hbm = refs[:3]
    pieces, refs = refs[3 : 3 + count], refs[3 + count :]
    held_out, refs = refs[0], refs[1:]
    if not first:
        held_du, refs = refs[0], refs[1:]
    out_hbm, du_hbm, sent, kept = refs[:4]
    u, u_t, g, up, down, out_acc, du_acc, a_s, dz_s, grad, low, sems = refs[4:]
    width = u.shape[1]
    wide = 512
    halves = width // wide
    blocks = width // block
    base = 2 * sub * width
    free = iter(range(sems.shape[0]))

    def copy(src, dst):
        return pltpu.make_async_copy(src, dst, sems.at[next(free)])

    def rows(at, columns, dst, dst_columns):
        out, j = [], 0
        for piece in pieces:
            for i in range(piece.shape[0] // block):
                row = pl.multiple_of(tab[j] * block, block)
                src = piece.at[pl.ds(i * block, block), pl.ds(at, columns)]
                out.append(copy(src, dst.at[pl.ds(row, block), dst_columns]))
                j += 1
        return out

    get_u = [copy(u_hbm, u)]
    get_up = [rows(base + f * wide, wide, up, pl.ds(f * wide, wide)) for f in range(halves)]
    get_g = [copy(g_hbm, g)]
    get_down = rows(base + width, width, down, pl.ds(0, width))
    get_acc = [copy(held_out, out_acc)] + ([] if first else [copy(held_du, du_acc)])
    get_t = [copy(u_t_hbm, u_t)]

    def start(copies):
        for c in copies:
            c.start()

    def wait(copies):
        for c in copies:
            c.wait()

    start(get_u + get_up[0] + get_g + get_down + get_t)
    for f in range(1, halves):
        start(get_up[f])
    start(get_acc)
    for f in range(halves):
        cols = slice(f * wide, (f + 1) * wide)
        wait((get_u if f == 0 else []) + get_up[f])
        z = jnp.dot(u[...], up[:, cols], preferred_element_type=f32)
        a, slope = gelu_both(z)
        if f == 0:
            wait(get_g + get_down)
        da = lax.dot_general(g[...], down[cols, :], NT, preferred_element_type=f32)
        a_s[:, cols] = a.astype(bf16)
        dz_s[:, cols] = (da * slope).astype(bf16)
        if f == 0:
            wait(get_t)
        grad[:, cols] = jnp.dot(u_t[...], dz_s[:, cols], preferred_element_type=f32).astype(bf16)
        turned = lax.dot_general(a_s[:, cols], g[...], TN, preferred_element_type=f32)
        grad[cols, width:] = turned.astype(bf16)
    saved = []
    for j in range(blocks):
        row = pl.multiple_of(tab[j] * block, block)
        out = kept if j < blocks // 2 else sent
        at = j % (blocks // 2) * block
        saved.append(copy(grad.at[pl.ds(row, block)], out.at[pl.ds(at, block)]))
    start(saved)
    wait(get_acc)
    half = u.shape[0] // 2
    for i in range(2):
        part = pl.ds(i * half, half)
        out = out_acc[part, :] + jnp.dot(a_s[part, :], down[...], preferred_element_type=f32)
        if last:
            low[part, :] = out.astype(bf16)
            saved.append(copy(low.at[part], out_hbm.at[part]))
        else:
            out_acc[part, :] = out
            saved.append(copy(out_acc.at[part], out_hbm.at[part]))
        saved[-1].start()
    for i in range(2):
        part = pl.ds(i * half, half)
        du = lax.dot_general(dz_s[part, :], up[...], NT, preferred_element_type=f32)
        du_acc[part, :] = du if first else du_acc[part, :] + du
        saved.append(copy(du_acc.at[part], du_hbm.at[part]))
        saved[-1].start()
    wait(saved)


def feed_forward(tab, u, u_t, g, pieces, sub, held, block, first, last):
    length, width = u.shape
    half = width // 2
    anywhere = pl.BlockSpec(memory_space=pl.ANY)
    held = held[:1] if first else held
    inputs = [u, u_t, g, *pieces, *held]
    alias = {}
    if not first:
        alias[len(inputs)] = 1
        if not last:
            alias[len(inputs) - 1] = 0
    acc = jax.ShapeDtypeStruct((length, width), f32)
    part = jax.ShapeDtypeStruct((half, 2 * width), bf16)
    blocks = width // block
    return pl.pallas_call(
        functools.partial(mlp_kernel, len(pieces), block, sub, first, last),
        grid_spec=pltpu.PrefetchScalarGridSpec(
            num_scalar_prefetch=1,
            grid=(1,),
            in_specs=[anywhere] * len(inputs),
            out_specs=[anywhere] * 4,
            scratch_shapes=[
                pltpu.VMEM((length, width), bf16),
                pltpu.VMEM((width, length), bf16),
                pltpu.VMEM((length, width), bf16),
                pltpu.VMEM((width, width), bf16),
                pltpu.VMEM((width, width), bf16),
                pltpu.VMEM((length, width), f32),
                pltpu.VMEM((length, width), f32),
                pltpu.VMEM((length, width), bf16),
                pltpu.VMEM((length, width), bf16),
                pltpu.VMEM((width, 2 * width), bf16),
                pltpu.VMEM((length, width) if last else (16, LANES), bf16),
                pltpu.SemaphoreType.DMA((4 * blocks + 12,)),
            ],
        ),
        out_shape=[jax.ShapeDtypeStruct((length, width), bf16) if last else acc, acc, part, part],
        input_output_aliases=alias,
        compiler_params=params(),
        cost_estimate=cost(12 * length * width * width, 24 << 20),
        name="feed_forward",
    )(tab, *inputs)


def norm_back(v, gain, du):
    r = lax.rsqrt(jnp.mean(v * v, axis=1, keepdims=True) + NORM_EPS)
    up = du * gain
    return r * up - v * (r * r * r * jnp.mean(up * v, axis=1, keepdims=True))


def dmid_kernel(count, groups, block, steps, tab, n_ref, du_ref, mid_ref, cot_ref, gain_ref, *refs):
    o_refs, refs = refs[:groups], refs[groups:]
    weights = refs[:count]
    dmid_ref, do_ref, sent, kept, w_nat, total, grad = refs[count:]
    i = pl.program_id(0)
    rows = du_ref.shape[0]

    @pl.when(i == 0)
    def _():
        natural(w_nat, slice(None), weights, slice(None), tab, block)

    frame = lax.broadcasted_iota(jnp.int32, (rows, 1), 0) + i * rows
    g = jnp.where(frame < n_ref[0], cot_ref[...].astype(f32), 0.0)
    dmid = g + norm_back(mid_ref[...], gain_ref[1:2, :], du_ref[...])
    dmid_ref[...] = dmid
    low = dmid.astype(bf16)
    do_ref[...] = lax.dot_general(low, w_nat[...], NT, preferred_element_type=f32).astype(bf16)
    o = jnp.concatenate([ref[...] for ref in o_refs], axis=1)
    part = lax.dot_general(o, low, TN, preferred_element_type=f32)

    @pl.when(i == 0)
    def _():
        total[...] = part

    @pl.when(i > 0)
    def _():
        total[...] += part

    @pl.when(i == steps - 1)
    def _():
        grad[...] = total[...].astype(bf16)
        relative(sent, kept, slice(None), grad, slice(None), tab, block)


def middle_back(tab, frames, du, mid, cot, gains, o, pieces, block):
    length, width = mid.shape
    rows = 256
    steps = length // rows
    row = pl.BlockSpec((rows, width), lambda i, t, n: (i, 0))
    half = width // 2
    return pl.pallas_call(
        functools.partial(dmid_kernel, len(pieces), len(o), block, steps),
        grid_spec=pltpu.PrefetchScalarGridSpec(
            num_scalar_prefetch=2,
            grid=(steps,),
            in_specs=[row, row, row, full((8, width))]
            + [pl.BlockSpec((rows, v.shape[1]), lambda i, t, n: (i, 0)) for v in o]
            + [full(p.shape) for p in pieces],
            out_specs=[row, row, full((half, width)), full((half, width))],
            scratch_shapes=[
                pltpu.VMEM((width, width), bf16),
                pltpu.VMEM((width, width), f32),
                pltpu.VMEM((width, width), bf16),
            ],
        ),
        out_shape=[
            jax.ShapeDtypeStruct((length, width), f32),
            jax.ShapeDtypeStruct((length, width), bf16),
            jax.ShapeDtypeStruct((half, width), bf16),
            jax.ShapeDtypeStruct((half, width), bf16),
        ],
        compiler_params=params(),
        cost_estimate=cost(4 * length * width * width, 24 << 20),
        name="middle_back",
    )(tab, frames, du, mid, cot, gains, *o, *pieces)


def attend_back_kernel(
    rows_of, block, n_ref, tab, q_ref, k_ref, v_ref, g_ref, lse_ref, u_t_ref, d_ref, sent, kept, dk, dv, d_s, grad
):
    n = n_ref[0]
    length = q_ref.shape[0]
    scale = HEAD_DIM**-0.5
    lane = lax.broadcasted_iota(jnp.int32, (1, LANES), 1)
    masks = [(lane < HEAD_DIM).astype(bf16), (lane >= HEAD_DIM).astype(bf16)]
    dk[...] = jnp.zeros_like(dk)
    dv[...] = jnp.zeros_like(dv)
    for i in range(length // rows_of):
        rows = pl.ds(i * rows_of, rows_of)
        keys = (i + 1) * rows_of

        @pl.when(n > i * rows_of)
        def _():
            q = q_ref[rows, :] * bf16(scale)
            g = g_ref[rows, :]
            k, v = k_ref[0:keys, :], v_ref[0:keys, :]
            dq = None
            for h in range(2):
                q_h, g_h, k_h = q * masks[h], g * masks[h], k * masks[h]
                s = lax.dot_general(k, q_h, NT, preferred_element_type=f32)
                key = lax.broadcasted_iota(jnp.int32, (rows_of, rows_of), 0)
                query = lax.broadcasted_iota(jnp.int32, (rows_of, rows_of), 1)
                tail = jnp.where(key <= query, s[keys - rows_of :], -1e30)
                s = tail if i == 0 else jnp.concatenate([s[: keys - rows_of], tail], axis=0)
                p = jnp.exp(s - lse_ref[0, h : h + 1, rows])
                dp = lax.dot_general(v, g_h, NT, preferred_element_type=f32)
                delta = fold(p * dp, jnp.sum)
                ds = (p * (dp - delta)).astype(bf16)
                dv[0:keys, :] += jnp.dot(p.astype(bf16), g_h, preferred_element_type=f32)
                dk[0:keys, :] += jnp.dot(ds, q_h, preferred_element_type=f32)
                part = lax.dot_general(ds, k_h, TN, preferred_element_type=f32)
                dq = part if dq is None else dq + part
            d_s[rows, 0:LANES] = (dq * scale).astype(bf16)

        @pl.when(n <= i * rows_of)
        def _():
            d_s[rows, 0:LANES] = jnp.zeros((rows_of, LANES), bf16)

    d_s[:, LANES : 2 * LANES] = dk[...].astype(bf16)
    d_s[:, 2 * LANES :] = dv[...].astype(bf16)
    d_ref[...] = d_s[...]
    grad[...] = jnp.dot(u_t_ref[...], d_s[...], preferred_element_type=f32)
    relative(sent, kept, slice(None), grad, slice(None), tab, block)


def attend_back(frames, tab, qkv, g, lse, u_t, first, at, pairs, block):
    length, width = qkv.shape[0], u_t.shape[0]
    wide = 3 * LANES
    part = lambda c: pl.BlockSpec((length, LANES), lambda j, n, t: (0, 3 * (j + at) + c))
    half = width // 2
    out = pl.BlockSpec((half, wide), lambda j, n, t: (0, j))
    shape = jax.ShapeDtypeStruct((half, pairs * wide), f32)
    return pl.pallas_call(
        functools.partial(attend_back_kernel, 256, block),
        grid_spec=pltpu.PrefetchScalarGridSpec(
            num_scalar_prefetch=2,
            grid=(pairs,),
            in_specs=[
                part(0),
                part(1),
                part(2),
                pl.BlockSpec((length, LANES), lambda j, n, t: (0, j + first)),
                pl.BlockSpec((1, 2, length), lambda j, n, t: (j + at, 0, 0)),
                full((width, length), True),
            ],
            out_specs=[pl.BlockSpec((length, wide), lambda j, n, t: (0, j)), out, out],
            scratch_shapes=[
                pltpu.VMEM((length, LANES), f32),
                pltpu.VMEM((length, LANES), f32),
                pltpu.VMEM((length, wide), bf16),
                pltpu.VMEM((width, wide), f32),
            ],
        ),
        out_shape=[jax.ShapeDtypeStruct((length, pairs * wide), bf16), shape, shape],
        compiler_params=params(),
        cost_estimate=cost(40 * length * length * pairs * LANES, 16 << 20, length * length * 2 * pairs),
        name="attend_back",
    )(frames, tab, qkv, qkv, qkv, g, lse, u_t)


def input_grad_kernel(groups, parts, block, tab, dmid_ref, x_ref, gain_ref, *refs):
    d_refs, refs = refs[:parts], refs[parts:]
    weights, out_ref, nats = refs[: -1 - groups], refs[-1 - groups], refs[-groups:]
    count = len(weights) // groups

    @pl.when(pl.program_id(0) == 0)
    def _():
        for i, nat in enumerate(nats):
            natural(nat, slice(None), weights[i * count : (i + 1) * count], slice(None), tab, block)

    du = None
    for i, nat in enumerate(nats):
        mine = d_refs[i * parts // groups : (i + 1) * parts // groups]
        d = jnp.concatenate([ref[...] for ref in mine], axis=1)
        part = lax.dot_general(d, nat[...], NT, preferred_element_type=f32)
        du = part if du is None else du + part
    out_ref[...] = dmid_ref[...] + norm_back(x_ref[...].astype(f32), gain_ref[0:1, :], du)


def input_grad(tab, d, dmid, x, gains, pieces, block, lo, hi):
    length, width = x.shape
    rows = 256
    groups = len(pieces)
    columns = 3 * width // groups
    row = lambda w: pl.BlockSpec((rows, w), lambda i, t: (i + lo, 0))
    weights = [
        pl.BlockSpec((p.shape[0], columns), lambda i, t: (0, 0), pipeline_mode=pl.Buffered(1))
        for group in pieces
        for p in group
    ]
    return pl.pallas_call(
        functools.partial(input_grad_kernel, groups, len(d), block),
        grid_spec=pltpu.PrefetchScalarGridSpec(
            num_scalar_prefetch=1,
            grid=(hi - lo,),
            in_specs=[row(width), row(width), full((8, width))] + [row(v.shape[1]) for v in d] + weights,
            out_specs=pl.BlockSpec((rows, width), lambda i, t: (i, 0)),
            scratch_shapes=[pltpu.VMEM((width, columns), bf16)] * groups,
        ),
        out_shape=jax.ShapeDtypeStruct(((hi - lo) * rows, width), f32),
        compiler_params=params(),
        cost_estimate=cost(6 * length * width * width * (hi - lo) // 4, 22 << 20),
        name="input_grad",
    )(tab, dmid, x, gains, *d, *[p for group in pieces for p in group])


def adam_step(weight, first, second, gradient, clip_factor, step_rate, decay_rate, shadow):
    clipped = gradient * clip_factor
    first_new = BETA_ONE * first + (1.0 - BETA_ONE) * clipped
    second_new = BETA_TWO * second + (1.0 - BETA_TWO) * clipped * clipped
    first_hat = first_new / (1.0 - BETA_ONE**STEP)
    second_hat = second_new / (1.0 - BETA_TWO**STEP)
    weight_new = weight - step_rate * (
        first_hat / (jnp.sqrt(second_hat) + ADAM_EPS) + decay_rate * weight
    )
    shadow_new = SHADOW_KEEP * shadow + (1.0 - SHADOW_KEEP) * weight_new
    return (weight_new, first_new, second_new, shadow_new)


def square(v):
    return jnp.sum(v * v)


def norm_kernel(parts, subs, *refs):
    grads, rest = refs[: parts + 1 + subs], refs[parts + 1 + subs :]
    weights, (gains, everyone, gain_grad) = rest[: parts + subs], rest[parts + subs :]
    rows, width = grads[parts].shape
    one = two = jnp.zeros((rows, 1), f32)
    total = square(grads[parts][...])
    for i in range(parts):
        grad = grads[i][...]
        total = total + square(grad)
        one = one + jnp.sum(weights[i][...].astype(f32) * grad, axis=1, keepdims=True)
    for i in range(subs):
        grad = grads[parts + 1 + i][...]
        total = total + square(grad)
        up = weights[parts + i][...].astype(f32) * grad[:, :width]
        two = two + jnp.sum(up, axis=1, keepdims=True)
    lane = lax.broadcasted_iota(jnp.int32, (rows, LANES), 1)
    both = jnp.where(lane == 0, one, two)
    both = both.T[0:2, :] / gains[...].astype(bf16).astype(f32)
    gain_grad[...] = both
    everyone[...] = jnp.broadcast_to(total + square(both), everyone.shape)


def square_sums(parts, out, mlp, weights, gains, ndev):
    place = pl.BlockSpec(memory_space=pltpu.VMEM)
    inputs = [*parts, out, *mlp, *weights, gains]
    return pl.pallas_call(
        functools.partial(norm_kernel, len(parts), len(mlp)),
        in_specs=[place] * len(inputs),
        out_specs=[place] * 2,
        out_shape=[
            jax.ShapeDtypeStruct((ndev, 1, LANES), f32),
            jax.ShapeDtypeStruct(gains.shape, f32),
        ],
        compiler_params=params(),
        name="square_sums",
    )(*inputs)


def adam_kernel(parts, subs, rates, decays, sums_ref, *refs):
    count = parts + 2 + subs
    grads, states, outs = refs[:count], refs[count : count + 20], refs[count + 20 :]
    norm = jnp.sqrt(jnp.sum(sums_ref[...], axis=0))
    outs[20][...] = norm
    clip = jnp.minimum(1.0, CLIP_NORM / norm[:, 0:1])

    def update(i, rows, cols, grad):
        w, m, v, s = [states[4 * i + k][rows, cols] for k in range(4)]
        new = adam_step(w, m, v, grad, clip, rates[i], decays[i], s)
        for k in range(4):
            outs[4 * i + k][rows, cols] = new[k]

    wide = D // LANES // parts
    every = slice(None)
    for c in range(3):
        for p in range(parts):
            for j in range(wide):
                at = c * D + (p * wide + j) * LANES
                src = (3 * j + c) * LANES
                update(0, every, slice(at, at + LANES), grads[p][:, src : src + LANES])
    update(1, every, every, grads[parts][...])
    mlp = grads[parts + 1 : parts + 1 + subs]
    own = mlp[0].shape[0]
    size = subs * own
    for at in range(0, FF, LANES):
        grad = jnp.concatenate(
            [
                mlp[q][:, dev * own : (dev + 1) * own]
                for dev in range(at // size, (at + LANES) // size)
                for q in range(subs)
            ],
            axis=1,
        )
        update(2, every, slice(at, at + LANES), grad)
    for q in range(subs):
        update(3, slice(q * own, (q + 1) * own), every, mlp[q][:, D:])
    update(4, every, every, grads[-1][...])


def adam(sums, parts, out, mlp, gain, states, rates, decays):
    place = pl.BlockSpec(memory_space=pltpu.VMEM)
    inputs = [sums, *parts, out, *mlp, gain, *[v for group in states for v in group]]
    outputs = [jax.ShapeDtypeStruct(v.shape, f32) for group in states for v in group]
    outputs.append(jax.ShapeDtypeStruct((1, LANES), f32))
    done = pl.pallas_call(
        functools.partial(adam_kernel, len(parts), len(mlp), rates, decays),
        in_specs=[place] * len(inputs),
        out_specs=[place] * len(outputs),
        out_shape=outputs,
        compiler_params=params(),
        name="adam",
    )(*inputs)
    return [done[4 * i : 4 * i + 4] for i in range(5)], done[-1][0, 0]


def body(plan, *args):
    inputs, cotangent, frames = args[:3]
    masters, firsts, seconds, shadows = args[3:8], args[8:13], args[13:18], args[18:23]
    w_qkv, w_out, w_up, w_down, norm_gains = masters
    block, ndev = plan.block, plan.ndev
    x = inputs[0]
    length = x.shape[0]
    own = D // ndev
    subs = FF // D
    tab = lax.dynamic_index_in_dim(jnp.asarray(plan.tab), lax.axis_index("dp"), 0, keepdims=False)

    wide = D // GROUPS
    pairs = wide // LANES
    columns = 3 * wide
    every = D // LANES
    qkv_low = w_qkv.astype(bf16).reshape(own, 3, every, LANES).transpose(0, 2, 1, 3).reshape(own, 3 * D)
    gain_cols = jnp.pad(norm_gains.astype(bf16).T, ((0, 0), (0, LANES - 2)))
    local_q0 = jnp.concatenate([qkv_low[:, :columns], gain_cols], axis=1)
    up_low = w_up.astype(bf16).reshape(own, ndev, subs, own).transpose(2, 0, 1, 3).reshape(subs, own, D)
    down_low = w_down.astype(bf16).reshape(subs, own, D)
    local_mlp = [v for q in range(subs) for v in (up_low[q], down_low[q])]
    early = jnp.concatenate([qkv_low[:, columns:], w_out.astype(bf16)] + local_mlp[:2], axis=1)
    late = jnp.concatenate(local_mlp[2:], axis=1)

    flow = Flow(plan)
    step = flow.step
    reach = lambda v: lax.all_gather(v, "fsdp", axis=0, tiled=True)
    early = reach(early)
    held_q0 = reach(local_q0)
    flow.gather("q0", held_q0)
    step(None, ["q0"])
    late = reach(late)
    flow.gather("q1", early, 0, columns)
    flow.gather("o", early, columns, D)
    flow.gather("m0", early, columns + D, 2 * D)
    for k in range(1, subs):
        flow.gather(f"m{k}", late, 2 * (k - 1) * D, 2 * D)
    step(None, ["q0"])
    step(None, ["q0"])
    flow.until(None, ["q0"])
    step(None, ["q1", "o", "m0"])
    qkv0, u_one, gains, u_one_t = project_qkv(tab, x, flow.done["q0"], block, columns, True)
    qkv0, u_one = step((qkv0, u_one), ["q1", "o"])
    o0, lse0 = attend(frames, qkv0)
    o0, u_one = step((o0, u_one), ["q1", "o", "m0", "m1"])
    u_one = flow.until(u_one, ["q1"])
    (qkv1,) = project_qkv(tab, u_one, flow.done["q1"], block, columns, False)
    qkv1 = step(qkv1, ["o", "m1", "m2"])
    o1, lse1 = attend(frames, qkv1)
    qkv, o, lse = [qkv0, qkv1], [o0, o1], [lse0, lse1]
    o = step(o, ["o", "m0", "m2"])
    o = flow.until(o, ["o"])
    full_out = flow.done["o"]
    mid, u_two, u_two_t = middle(tab, o, x, gains, full_out, block)
    keep = (jnp.arange(length) < frames[0])[:, None]
    g_low = jnp.where(keep, cotangent[0], jnp.zeros((), bf16))
    u_two = step(u_two, ["m0", "m1", "m3"])
    held = [mid, None]
    plans = [
        ["m1", "m2", "m3", "g0"],
        ["m2", "m3", "g0", "g1"],
        ["m3", "g0", "g1", "g2"],
        ["g0", "g1", "g2", "g3"],
    ]
    for k in range(subs):
        u_two = flow.until(u_two, [f"m{k}"])
        out, du, sent, kept = feed_forward(
            tab, u_two, u_two_t, g_low, flow.done[f"m{k}"], 0, held, block, k == 0, k == subs - 1
        )
        held = [out, du]
        flow.scatter(f"g{k}", sent, kept)
        held[1] = step(held[1], plans[k])
    out, du = held
    dmid, d_o, sent, kept = middle_back(
        tab, frames, du, mid, cotangent[0], gains, o, full_out, block
    )
    flow.scatter("go", sent, kept)
    d_o = step(d_o, ["g1", "g2", "g3", "go"])
    calls = 4
    per = every // calls
    d_qkv = []
    plans = [["g2", "g3", "go", "gq0"], ["g3", "go", "gq0", "gq1"], ["go", "gq0", "gq1", "gq2"]]
    for i in range(calls):
        group, at = divmod(i * per, pairs)
        d, sent, kept = attend_back(
            frames, tab, qkv[group], d_o, lse[group], u_one_t, i * per, at, per, block
        )
        d_qkv.append(d)
        flow.scatter(f"gq{i}", sent, kept, True)
        if i < calls - 1:
            d_o = step(d_o, plans[i])
    dmid = step(dmid, ["gq1", "gq2", "gq3"])
    blocks = length // 256
    held_q = [flow.done["q0"], flow.done["q1"]]
    top = input_grad(tab, d_qkv, dmid, x, gains, held_q, block, 0, blocks // 2)
    top, dmid = step((top, dmid), ["gq2", "gq3"])
    low = input_grad(tab, d_qkv, dmid, x, gains, held_q, block, blocks // 2, blocks)
    low = step(low, ["gq3"])
    flow.until(None, list(flow.live))
    grad_in = jnp.concatenate([top, low], axis=0)
    own_rows = lambda n, direct=False: plan.own_rows(flow.done[n], direct)
    mlp_shards = [own_rows(f"g{k}") for k in range(subs)]
    out_shard = own_rows("go")
    parts = [own_rows(f"gq{i}", i == calls - 1) for i in range(calls)]

    size = per * 3 * LANES
    weights = [qkv_low[:, i * size : (i + 1) * size] for i in range(calls)] + list(up_low)
    sums, gain_shard = square_sums(parts, out_shard, mlp_shards, weights, norm_gains, ndev)
    everyone = lax.all_to_all(sums, AXES, 0, 0)
    rates = (0.6 / D**0.5, 0.6 / FANO**0.5, 0.6 / D**0.5, 0.6 / FF**0.5, 1.0)
    decays = (0.1, 0.1, 0.1, 0.1, 0.0)
    states = [(masters[i], firsts[i], seconds[i], shadows[i]) for i in range(5)]
    updated, grad_norm = adam(
        everyone, parts, out_shard, mlp_shards, gain_shard, states, rates, decays
    )
    return (
        out[None],
        grad_in[None],
        grad_norm,
        *(updated[i][part] for part in range(4) for i in range(5)),
    )


def solution(mesh):
    plan = Plan(mesh)
    split = P(AXES, None)
    lanes = P(None, AXES)
    weights = (split, split, split, split, lanes)
    return jax.shard_map(
        functools.partial(body, plan),
        mesh=mesh,
        in_specs=(P(AXES, None, None), P(AXES, None, None), P(AXES)) + weights * 4,
        out_specs=(P(AXES, None, None), P(AXES, None, None), P()) + weights * 4,
        check_vma=False,
    )
```

time: 551 us -> 503 us (0.913)
  Pallas kernels: 213 us -> 309 us
  other arithmetic: 63.6 us -> 19.4 us
  local copies, waits for them, and re-layouts: 65.3 us -> 25.1 us
  waiting for transfers between devices: 82.5 us -> 56 us
  starting transfers between devices: 72.1 us -> 53.2 us
  blocking collectives: 28.1 us -> 19.2 us
    pallas_call x43 -> x36, Pallas kernels: 157 us -> 256 us  [the longest x4 79.3 us: feed_forward(): pl.pallas_call(functools.partial(mlp_kernel, len(pieces), block, sub, fir...]
    unnamed x224 -> x92, local copies, waits for them, and re-layouts: 46.6 us -> 19.6 us
    convert_element_type x15 -> x6, other arithmetic: 32.7 us -> 8.03 us  [the longest x5 8.02 us: own_rows(): lax.psum_scatter(total, 'fsdp', scatter_dimension=0, tiled=True).astype(f32)]
    ppermute x63 -> x62, starting transfers between devices: 67.6 us -> 47.8 us  [the longest x59 43.3 us: step(): lax.ppermute(v, AXES, p)]
    add x14 -> x1, other arithmetic: 19.7 us -> 1.54 us  [own_rows(): sum_ = sum_ + lax.ppermute(block(me ^ flip), AXES, pairs)]
    ppermute x63 -> x62, waiting for transfers between devices: 68.3 us -> 53.5 us  [the longest x59 51.8 us: step(): lax.ppermute(v, AXES, p)]
    all_gather x1, blocking collectives: 28.1 us -> 19.2 us  [body(): reach = lambda v: lax.all_gather(v, 'fsdp', axis=0, tiled=True)]
    reduce_sum x7 -> x0, other arithmetic: 8.15 us -> none  [the longest x4 6.65 us: body(): local_sq = sum((jnp.sum(piece * piece) for piece in shards))]
  transfers between devices with their start and end apart: 72 -> 73, of which waited for: 16 -> 11; matrix products, arithmetic and copies ran while one was open for 14% -> 4% of each run, Pallas kernels for 39% -> 60%
where the time goes in v2:
time: 503 us; the launch traced here: 498 us
  Pallas kernels  309 us (61%)
  waiting for transfers between devices  56 us (11%)
  starting transfers between devices  53.2 us (11%)
  local copies, waits for them, and re-layouts  25.1 us (5%)
  other arithmetic  19.4 us (4%)
  blocking collectives  19.2 us (4%)
  between operations  16.2 us (3%)
    pallas_call x4, Pallas kernels, feed_forward(): pl.pallas_call(functools.partial(mlp_kernel, len(pieces), block, sub, fir...  79.3 us
    pallas_call x4, Pallas kernels, attend_back(): pl.pallas_call(functools.partial(attend_back_kernel, 256, block), grid_sp...  73 us
    pallas_call x22, Pallas kernels, tie(): pl.pallas_call(functools.partial(tie_kernel, count, jobs), in_specs=[plac...  55.6 us
    ppermute x59, waiting for transfers between devices, step(): lax.ppermute(v, AXES, p)  51.8 us
    ppermute x59, starting transfers between devices, step(): lax.ppermute(v, AXES, p)  43.3 us
    pallas_call x2, Pallas kernels, attend(): pl.pallas_call(functools.partial(attend_kernel, 512), grid_spec=pltpu.Pre...  30.4 us
    pallas_call x2, Pallas kernels, input_grad(): pl.pallas_call(functools.partial(input_grad_kernel, groups, len(d), block...  20.9 us
    unnamed x92, local copies, waits for them, and re-layouts  19.6 us
  transfers between devices with their start and end apart: 73, of which 11 were waited for; matrix products, arithmetic and copies ran while one was open for 4% of the time, Pallas kernels for 60%

profile of v2, /device:TPU:0, one launch (start us, length us, event | category | flops | bytes accessed | tf_op | source)
XLA Modules:
  0.0 498.3 jit_solution(2591602108073782163)
XLA Ops:
  13.8 19.2 %all_gather.9.refs_0_ = bf16[128,1664]{1,0:T(8,128)(2,1)} all-gather(bf16[32,1664]{1,0:T(8,128)(2,1)S(1)} %fusion.1), channel_id=1, replica_groups=mesh['dp'=8,'fsdp'=4] {'fsdp'}, dimensions={0}, use_global_device_ids=true | all-gather | bytes 532480 | tf_op jit(solution)/shard_map/all_gather | solution.py:930
  34.6 6.8 %collective-permute-done.refs_1_ = bf16[128,1664]{1,0:T(8,128)(2,1)S(1)} collective-permute-done((bf16[128,1664]{1,0:T(8,128)(2,1)}, bf16[128,1664]{1,0:T(8,128)(2,1)S(1)}, u32[]{:S(2)}, u32[]{:S(2)}) %collective-permute-start) | collective-permute-done | bytes 426016 | tf_op jit(solution)/shard_map/ppermute | solution.py:248
  46.6 10.6 %collective-permute-done.1.refs_0_ = bf16[256,1664]{1,0:T(8,128)(2,1)S(1)} collective-permute-done((bf16[256,1664]{1,0:T(8,128)(2,1)}, bf16[256,1664]{1,0:T(8,128)(2,1)S(1)}, u32[]{:S(2)}, u32[]{:S(2)}) %collective-permute-start.1) | collective-permute-done | bytes 852000 | tf_op jit(solution)/shard_map/ppermute | solution.py:248
  67.7 9.7 %qkv.2 = (bf16[1024,1536]{1,0:T(8,128)(2,1)}, bf16[1024,1024]{1,0:T(8,128)(2,1)}, f32[8,1024]{1,0:T(8,128)}, bf16[1024,1024]{1,0:T(8,128)(2,1)}) custom-call(s32[8]{0:T(128)} %fusion.2.tab, bf16[1024,1024]{1,0:T(8,128)(2,1)} %bitcast.31, bf16[256,1664]{1,0:T(8,128)(2,1)} %tie.23.refs_1_.refs_5_.refs_4_, bf16[256,1664]{1,0:T(8,128)(2,1)} %tie.24.refs_2_.refs_6_.refs_5_, ...), custom_call_target="tpu_custom_call" | custom-call | flops 3221225472 | bytes 20971520 | tf_op jit(solution)/shard_map/qkv/pallas_call | solution.py:312
  78.2 2.2 tie.27
  82.5 15.1 %attend.2 = (bf16[1024,512]{1,0:T(8,128)(2,1)}, f32[4,2,1024]{2,1,0:T(2,128)}) custom-call(s32[1]{0:T(128)} %copy.159.n_ref, bf16[1024,1536]{1,0:T(8,128)(2,1)} %get-tuple-element.194.q_ref.k_ref.v_ref, bf16[1024,1536]{1,0:T(8,128)(2,1)} %get-tuple-element.194.q_ref.k_ref.v_ref, bf16[1024,1536]{1,0:T(8,128)(2,1)} %get-tuple-element.194.q_ref.k_ref.v_ref), custom_call_target="tpu_custom_call" | custom-call | flops 8589934592 | bytes 8388608 | tf_op jit(solution)/shard_map/attend/pallas_call | solution.py:384
  99.3 2.4 tie.28
  105.5 8.0 %qkv.3.refs_0_ = bf16[1024,1536]{1,0:T(8,128)(2,1)} custom-call(s32[8]{0:T(128)} %fusion.2.tab, bf16[1024,1024]{1,0:T(8,128)(2,1)} %get-tuple-element.203.refs_0_, bf16[256,1536]{1,0:T(8,128)(2,1)} %get-tuple-element.198.refs_1_.refs_8_, bf16[256,1536]{1,0:T(8,128)(2,1)} %get-tuple-element.202.refs_2_.refs_9_, ...), custom_call_target="tpu_custom_call" | custom-call | flops 3221225472 | bytes 20971520 | tf_op jit(solution)/shard_map/qkv/pallas_call | solution.py:312
  113.5 3.3 collective-permute-done.13.refs_4_
  116.8 2.4 tie.30
  121.8 15.3 %attend.3 = (bf16[1024,512]{1,0:T(8,128)(2,1)}, f32[4,2,1024]{2,1,0:T(2,128)}) custom-call(s32[1]{0:T(128)} %copy.159.n_ref, bf16[1024,1536]{1,0:T(8,128)(2,1)} %get-tuple-element.208.q_ref.k_ref.v_ref, bf16[1024,1536]{1,0:T(8,128)(2,1)} %get-tuple-element.208.q_ref.k_ref.v_ref, bf16[1024,1536]{1,0:T(8,128)(2,1)} %get-tuple-element.208.q_ref.k_ref.v_ref), custom_call_target="tpu_custom_call" | custom-call | flops 8589934592 | bytes 8388608 | tf_op jit(solution)/shard_map/attend/pallas_call | solution.py:384
  138.0 2.2 tie.31
  140.3 3.1 broadcast_select_fusion.refs_2_
  144.9 9.1 %middle.1 = (f32[1024,1024]{1,0:T(8,128)}, bf16[1024,1024]{1,0:T(8,128)(2,1)}, bf16[1024,1024]{1,0:T(8,128)(2,1)}) custom-call(s32[8]{0:T(128)} %fusion.2.tab, bf16[1024,1024]{1,0:T(8,128)(2,1)} %bitcast.32, f32[8,1024]{1,0:T(8,128)} %get-tuple-element.189.gain_ref, bf16[1024,512]{1,0:T(8,128)(2,1)} %get-tuple-element.212.refs_0_, ...), custom_call_target="tpu_custom_call" | custom-call | flops 2147483648 | bytes 16777216 | tf_op jit(solution)/shard_map/middle/pallas_call | solution.py:427
  157.8 19.6 %feed_forward.4 = (f32[1024,1024]{1,0:T(8,128)}, f32[1024,1024]{1,0:T(8,128)}, bf16[512,2048]{1,0:T(8,128)(2,1)}, bf16[512,2048]{1,0:T(8,128)(2,1)}) custom-call(s32[8]{0:T(128)} %fusion.2.tab, bf16[1024,1024]{1,0:T(8,128)(2,1)} %get-tuple-element.219.refs_0_, bf16[1024,1024]{1,0:T(8,128)(2,1)} %get-tuple-element.220.refs_1_, ...), custom_call_target="tpu_custom_call" | custom-call | flops 12884901888 | bytes 25165824 | tf_op jit(solution)/shard_map/feed_forward/pallas_call | solution.py:561
  179.2 2.2 tie.33
  183.6 20.0 %feed_forward.5 = (f32[1024,1024]{1,0:T(8,128)}, f32[1024,1024]{1,0:T(8,128)}, bf16[512,2048]{1,0:T(8,128)(2,1)}, bf16[512,2048]{1,0:T(8,128)(2,1)}) custom-call(s32[8]{0:T(128)} %fusion.2.tab, bf16[1024,1024]{1,0:T(8,128)(2,1)} %get-tuple-element.219.refs_0_, ...), custom_call_target="tpu_custom_call", output_to_operand_aliasing={{1}: (9, {}), {0}: (8, {})} | custom-call | flops 12884901888 | bytes 25165824 | tf_op jit(solution)/shard_map/feed_forward/pallas_call | solution.py:561
  204.2 3.4 tie.34
  208.2 19.8 %feed_forward.6 = (f32[1024,1024]{1,0:T(8,128)}, f32[1024,1024]{1,0:T(8,128)}, bf16[512,2048]{1,0:T(8,128)(2,1)}, bf16[512,2048]{1,0:T(8,128)(2,1)}) custom-call(s32[8]{0:T(128)} %fusion.2.tab, bf16[1024,1024]{1,0:T(8,128)(2,1)} %get-tuple-element.219.refs_0_, ...), custom_call_target="tpu_custom_call", output_to_operand_aliasing={{1}: (9, {}), {0}: (8, {})} | custom-call | flops 12884901888 | bytes 25165824 | tf_op jit(solution)/shard_map/feed_forward/pallas_call | solution.py:561
  229.2 4.5 tie.35
  235.5 19.8 %feed_forward.7 = (bf16[1024,1024]{1,0:T(8,128)(2,1)}, f32[1024,1024]{1,0:T(8,128)}, bf16[512,2048]{1,0:T(8,128)(2,1)}, bf16[512,2048]{1,0:T(8,128)(2,1)}) custom-call(s32[8]{0:T(128)} %fusion.2.tab, bf16[1024,1024]{1,0:T(8,128)(2,1)} %get-tuple-element.219.refs_0_, bf16[1024,1024]{1,0:T(8,128)(2,1)} %get-tuple-element.220.refs_1_, ...), custom_call_target="tpu_custom_call", output_to_operand_aliasing={{1}: (9, {})} | custom-call | flops 12884901888 | bytes 25165824 | tf_op jit(solution)/shard_map/feed_forward/pallas_call | solution.py:561
  255.8 9.1 %collective-permute-done.31.refs_2_ = bf16[128,2048]{1,0:T(8,128)(2,1)S(1)} collective-permute-done((bf16[128,2048]{1,0:T(8,128)(2,1)}, bf16[128,2048]{1,0:T(8,128)(2,1)S(1)}, u32[]{:S(2)}, u32[]{:S(2)}) %collective-permute-start.31) | collective-permute-done | bytes 524320 | tf_op jit(solution)/shard_map/ppermute | solution.py:248
  266.1 5.4 %tie.36 = (f32[1024,1024]{1,0:T(8,128)}, bf16[128,2048]{1,0:T(8,128)(2,1)}, bf16[128,2048]{1,0:T(8,128)(2,1)}, bf16[128,2048]{1,0:T(8,128)(2,1)}, bf16[256,2048]{1,0:T(8,128)(2,1)}, /*index=5*/bf16[256,2048]{1,0:T(8,128)(2,1)}) custom-call(f32[1024,1024]{1,0:T(8,128)} %get-tuple-element.252.refs_0_, ...), custom_call_target="tpu_custom_call", output_to_operand_aliasing={{0}: (0, {})} | custom-call | tf_op jit(solution)/shard_map/tie/pallas_call | solution.py:198
  273.7 13.9 %middle_back.1 = (f32[1024,1024]{1,0:T(8,128)}, bf16[1024,1024]{1,0:T(8,128)(2,1)}, bf16[512,1024]{1,0:T(8,128)(2,1)}, bf16[512,1024]{1,0:T(8,128)(2,1)}) custom-call(s32[8]{0:T(128)} %fusion.2.tab, s32[1]{0:T(128)} %copy.159.n_ref, f32[1024,1024]{1,0:T(8,128)} %get-tuple-element.259.du_ref, f32[1024,1024]{1,0:T(8,128)} %get-tuple-element.223.refs_7_.mid_ref, ...), custom_call_target="tpu_custom_call" | custom-call | flops 4294967296 | bytes 25165824 | tf_op jit(solution)/shard_map/middle_back/pallas_call | solution.py:637
  287.7 3.2 collective-permute-done.35.refs_4_
  291.9 5.1 %tie.37 = (bf16[1024,1024]{1,0:T(8,128)(2,1)}, bf16[128,2048]{1,0:T(8,128)(2,1)}, bf16[128,2048]{1,0:T(8,128)(2,1)}, bf16[128,2048]{1,0:T(8,128)(2,1)}, bf16[256...) custom-call(bf16[1024,1024]{1,0:T(8,128)(2,1)} %get-tuple-element.261.refs_0_, ...), custom_call_target="tpu_custom_call", output_to_operand_aliasing={{0}: (0, {})} | custom-call | tf_op jit(solution)/shard_map/tie/pallas_call | solution.py:198
  299.3 18.1 %attend_back.4 = (bf16[1024,768]{1,0:T(8,128)(2,1)}, f32[512,768]{1,0:T(8,128)}, f32[512,768]{1,0:T(8,128)}) custom-call(s32[1]{0:T(128)} %copy.159.n_ref, s32[8]{0:T(128)} %fusion.2.tab, bf16[1024,1536]{1,0:T(8,128)(2,1)} %get-tuple-element.194.q_ref.k_ref.v_ref, bf16[1024,1536]{1,0:T(8,128)(2,1)} %get-tuple-element.194.q_ref.k_ref.v_ref, ...), custom_call_target="tpu_custom_call" | custom-call | flops 10737418240 | bytes 16777216 | tf_op jit(solution)/shard_map/attend_back/pallas_call | solution.py:719
  317.4 3.9 tie.38
  322.7 18.3 %attend_back.5 = (bf16[1024,768]{1,0:T(8,128)(2,1)}, f32[512,768]{1,0:T(8,128)}, f32[512,768]{1,0:T(8,128)}) custom-call(s32[1]{0:T(128)} %copy.159.n_ref, s32[8]{0:T(128)} %fusion.2.tab, bf16[1024,1536]{1,0:T(8,128)(2,1)} %get-tuple-element.194.q_ref.k_ref.v_ref, bf16[1024,1536]{1,0:T(8,128)(2,1)} %get-tuple-element.194.q_ref.k_ref.v_ref, ...), custom_call_target="tpu_custom_call" | custom-call | flops 10737418240 | bytes 16777216 | tf_op jit(solution)/shard_map/attend_back/pallas_call | solution.py:719
  341.1 9.3 %collective-permute-done.41.refs_4_ = bf16[256,1024]{1,0:T(8,128)(2,1)S(1)} collective-permute-done((bf16[256,1024]{1,0:T(8,128)(2,1)}, bf16[256,1024]{1,0:T(8,128)(2,1)S(1)}, u32[]{:S(2)}, u32[]{:S(2)}) %collective-permute-start.41) | collective-permute-done | bytes 524320 | tf_op jit(solution)/shard_map/ppermute | solution.py:248
  352.3 3.9 tie.39
  359.9 18.3 %attend_back.6 = (bf16[1024,768]{1,0:T(8,128)(2,1)}, f32[512,768]{1,0:T(8,128)}, f32[512,768]{1,0:T(8,128)}) custom-call(s32[1]{0:T(128)} %copy.159.n_ref, s32[8]{0:T(128)} %fusion.2.tab, bf16[1024,1536]{1,0:T(8,128)(2,1)} %get-tuple-element.208.q_ref.k_ref.v_ref, bf16[1024,1536]{1,0:T(8,128)(2,1)} %get-tuple-element.208.q_ref.k_ref.v_ref, ...), custom_call_target="tpu_custom_call" | custom-call | flops 10737418240 | bytes 16777216 | tf_op jit(solution)/shard_map/attend_back/pallas_call | solution.py:719
  379.2 3.5 tie.40
  382.8 18.4 %attend_back.7 = (bf16[1024,768]{1,0:T(8,128)(2,1)}, f32[512,768]{1,0:T(8,128)}, f32[512,768]{1,0:T(8,128)}) custom-call(s32[1]{0:T(128)} %copy.159.n_ref, s32[8]{0:T(128)} %fusion.2.tab, bf16[1024,1536]{1,0:T(8,128)(2,1)} %get-tuple-element.208.q_ref.k_ref.v_ref, bf16[1024,1536]{1,0:T(8,128)(2,1)} %get-tuple-element.208.q_ref.k_ref.v_ref, ...), custom_call_target="tpu_custom_call" | custom-call | flops 10737418240 | bytes 16777216 | tf_op jit(solution)/shard_map/attend_back/pallas_call | solution.py:719
  401.4 3.4 collective-permute-start.50
  404.8 8.3 %collective-permute-done.48.refs_2_ = bf16[128,768]{1,0:T(8,128)(2,1)S(1)} collective-permute-done((bf16[128,768]{1,0:T(8,128)(2,1)}, bf16[128,768]{1,0:T(8,128)(2,1)S(1)}, u32[]{:S(2)}, u32[]{:S(2)}) %collective-permute-start.48) | collective-permute-done | bytes 196640 | tf_op jit(solution)/shard_map/ppermute | solution.py:248
  413.8 3.1 tie.41
  418.1 2.5 collective-permute-start.54
  420.6 10.5 %input_grad.2.refs_0_ = f32[512,1024]{1,0:T(8,128)} custom-call(s32[8]{0:T(128)} %fusion.2.tab, f32[1024,1024]{1,0:T(8,128)} %get-tuple-element.300.dmid_ref.refs_1_, bf16[1024,1024]{1,0:T(8,128)(2,1)} %bitcast.33, f32[8,1024]{1,0:T(8,128)} %get-tuple-element.189.gain_ref, bf16[1024,768]{1,0:T(8,128)(2,1)} %get-tuple-element.301.refs_0_, ...), custom_call_target="tpu_custom_call" | custom-call | flops 3221225472 | bytes 23068672 | tf_op jit(solution)/shard_map/input_grad/pallas_call | solution.py:777
  432.4 3.1 tie.42
  436.6 2.4 collective-permute-start.58
  439.0 10.5 %input_grad.3.refs_0_ = f32[512,1024]{1,0:T(8,128)} custom-call(s32[8]{0:T(128)} %fusion.2.tab, f32[1024,1024]{1,0:T(8,128)} %get-tuple-element.313.dmid_ref, bf16[1024,1024]{1,0:T(8,128)(2,1)} %bitcast.34, f32[8,1024]{1,0:T(8,128)} %get-tuple-element.189.gain_ref, bf16[1024,768]{1,0:T(8,128)(2,1)} %get-tuple-element.301.refs_0_, ...), custom_call_target="tpu_custom_call" | custom-call | flops 3221225472 | bytes 23068672 | tf_op jit(solution)/shard_map/input_grad/pallas_call | solution.py:777
  453.6 3.0 collective-permute-start.60
  469.8 2.5 square_sums.1
  472.3 4.4 all-to-all-start
  476.8 4.8 maximum_bitcast_fusion
  481.6 2.3 all-to-all-done.sums_ref
  484.5 6.6 %adam.1 = (f32[32,3072]{1,0:T(8,128)}, f32[32,3072]{1,0:T(8,128)}, f32[32,3072]{1,0:T(8,128)}, f32[32,3072]{1,0:T(8,128)}, f32[32,1024]{1,0:T(8,128)}, /*index=5...) custom-call(f32[32,1,128]{2,1,0:T(1,128)} %copy-done.41, ...), custom_call_target="tpu_custom_call" | custom-call | tf_op jit(solution)/shard_map/adam/pallas_call | solution.py:893
  (272 shorter events, 85.2 us)
Async XLA Ops:
  7.2 51.7 %all-gather.3.cloned.1.call-start = ((), (), s32[]{:S(2)}) async-start(), calls=%async_computation.9 | async-start | bytes 1474560 | tf_op jit(solution)/shard_map/all_gather | solution.py:930
  13.6 84.0 %all-gather.5.cloned.1.call-start = ((), (), s32[]{:S(2)}) async-start(), calls=%async_computation.10 | async-start | bytes 1966080 | tf_op jit(solution)/shard_map/all_gather | solution.py:930
  45.9 412.7 %reduce-scatter.17.cloned.1.call-start = ((), (), s32[]{:S(2)}) async-start(), calls=%async_computation.15 | async-start | bytes 655360 | tf_op jit(solution)/shard_map/reduce_scatter | solution.py:114
  46.5 19.4 %collective-permute-start.2 = (bf16[256,1664]{1,0:T(8,128)(2,1)}, bf16[256,1664]{1,0:T(8,128)(2,1)S(1)}, u32[]{:S(2)}, u32[]{:S(2)}) collective-permute-start(bf16[256,1664]{1,0:T(8,128)(2,1)} %tie.23.refs_1_.refs_5_.refs_4_), channel_id=1, source_target_pairs={{0,4},{1,5},{2,6},{3,7},{4,0},{5,1},{6,2},{7,3},{8,12},{9,13},{10,... | collective-permute-start | bytes 2555912 | tf_op jit(solution)/shard_map/ppermute | solution.py:248
  61.0 16.5 %collective-permute-start.4 = (bf16[128,1536]{1,0:T(8,128)(2,1)}, bf16[128,1536]{1,0:T(8,128)(2,1)}, u32[]{:S(2)}, u32[]{:S(2)}) collective-permute-start(bf16[128,1536]{1,0:T(8,128)(2,1)} %get-tuple-element.192.refs_2_), channel_id=1, source_target_pairs={{0,16},{1,17},{2,18},{3,19},{4,12},{5,13},{6,14},{7,15},{8,24},{9,... | collective-permute-start | bytes 1179656 | tf_op jit(solution)/shard_map/ppermute | solution.py:248
  64.3 33.3 %collective-permute-start.8 = (bf16[128,2048]{1,0:T(8,128)(2,1)}, bf16[128,2048]{1,0:T(8,128)(2,1)}, u32[]{:S(2)}, u32[]{:S(2)}) collective-permute-start(bf16[128,2048]{1,0:T(8,128)(2,1)} %get-tuple-element.199.refs_4_), channel_id=1, source_target_pairs={{0,16},{1,17},{2,18},{3,19},{4,12},{5,13},{6,14},{7,15},{8,24},{9,... | collective-permute-start | bytes 1572872 | tf_op jit(solution)/shard_map/ppermute | solution.py:248
  80.4 18.0 %collective-permute-start.7 = (bf16[256,1536]{1,0:T(8,128)(2,1)}, bf16[256,1536]{1,0:T(8,128)(2,1)S(1)}, u32[]{:S(2)}, u32[]{:S(2)}) collective-permute-start(bf16[256,1536]{1,0:T(8,128)(2,1)} %get-tuple-element.198.refs_1_.refs_8_), channel_id=1, source_target_pairs={{0,8},{1,9},{2,10},{3,11},{4,20},{5,21},{6,22},{7,23},{8,0},{9,1},... | collective-permute-start | bytes 2359304 | tf_op jit(solution)/shard_map/ppermute | solution.py:248
  82.0 21.3 %collective-permute-start.9 = (bf16[256,1536]{1,0:T(8,128)(2,1)}, bf16[256,1536]{1,0:T(8,128)(2,1)S(1)}, u32[]{:S(2)}, u32[]{:S(2)}) collective-permute-start(bf16[256,1536]{1,0:T(8,128)(2,1)} %get-tuple-element.198.refs_1_.refs_8_), channel_id=1, source_target_pairs={{0,4},{1,5},{2,6},{3,7},{4,0},{5,1},{6,2},{7,3},{8,12},{9,13},{10,... | collective-permute-start | bytes 2359304 | tf_op jit(solution)/shard_map/ppermute | solution.py:248
  82.0 16.4 %collective-permute-start.6 = (bf16[256,1024]{1,0:T(8,128)(2,1)}, bf16[256,1024]{1,0:T(8,128)(2,1)}, u32[]{:S(2)}, u32[]{:S(2)}) collective-permute-start(bf16[256,1024]{1,0:T(8,128)(2,1)} %get-tuple-element.197.refs_2_), channel_id=1, source_target_pairs={{0,8},{1,9},{2,10},{3,11},{4,20},{5,21},{6,22},{7,23},{8,0},{9,1},... | collective-permute-start | bytes 1572872 | tf_op jit(solution)/shard_map/ppermute | solution.py:248
  103.3 33.9 %collective-permute-start.14 = (bf16[256,2048]{1,0:T(8,128)(2,1)}, bf16[256,2048]{1,0:T(8,128)(2,1)}, u32[]{:S(2)}, u32[]{:S(2)}) collective-permute-start(bf16[256,2048]{1,0:T(8,128)(2,1)} %get-tuple-element.210.refs_3_), channel_id=1, source_target_pairs={{0,8},{1,9},{2,10},{3,11},{4,20},{5,21},{6,22},{7,23},{8,0},{9,1},... | collective-permute-start | bytes 3145736 | tf_op jit(solution)/shard_map/ppermute | solution.py:248
  104.6 49.4 %collective-permute-start.16 = (bf16[256,2048]{1,0:T(8,128)(2,1)}, bf16[256,2048]{1,0:T(8,128)(2,1)}, u32[]{:S(2)}, u32[]{:S(2)}) collective-permute-start(bf16[256,2048]{1,0:T(8,128)(2,1)} %get-tuple-element.210.refs_3_), channel_id=1, source_target_pairs={{0,4},{1,5},{2,6},{3,7},{4,0},{5,1},{6,2},{7,3},{8,12},{9,13},{10,... | collective-permute-start | bytes 3145736 | tf_op jit(solution)/shard_map/ppermute | solution.py:248
  119.2 18.0 %collective-permute-start.15 = (bf16[128,2048]{1,0:T(8,128)(2,1)}, bf16[128,2048]{1,0:T(8,128)(2,1)S(1)}, u32[]{:S(2)}, u32[]{:S(2)}) collective-permute-start(bf16[128,2048]{1,0:T(8,128)(2,1)} %get-tuple-element.211.refs_3_), channel_id=1, source_target_pairs={{0,16},{1,17},{2,18},{3,19},{4,12},{5,13},{6,14},{7,15},{8,24},{9,... | collective-permute-start | bytes 1572872 | tf_op jit(solution)/shard_map/ppermute | solution.py:248
  120.6 33.4 %collective-permute-start.18 = (bf16[256,2048]{1,0:T(8,128)(2,1)}, bf16[256,2048]{1,0:T(8,128)(2,1)S(1)}, u32[]{:S(2)}, u32[]{:S(2)}) collective-permute-start(bf16[256,2048]{1,0:T(8,128)(2,1)} %get-tuple-element.218.refs_3_), channel_id=1, source_target_pairs={{0,8},{1,9},{2,10},{3,11},{4,20},{5,21},{6,22},{7,23},{8,0},{9,1},... | collective-permute-start | bytes 3145736 | tf_op jit(solution)/shard_map/ppermute | solution.py:248
  143.4 34.5 %collective-permute-start.19 = (bf16[256,2048]{1,0:T(8,128)(2,1)}, bf16[256,2048]{1,0:T(8,128)(2,1)}, u32[]{:S(2)}, u32[]{:S(2)}) collective-permute-start(bf16[256,2048]{1,0:T(8,128)(2,1)} %get-tuple-element.218.refs_3_), channel_id=1, source_target_pairs={{0,4},{1,5},{2,6},{3,7},{4,0},{5,1},{6,2},{7,3},{8,12},{9,13},{10,... | collective-permute-start | bytes 3145736 | tf_op jit(solution)/shard_map/ppermute | solution.py:248
  143.9 34.1 %collective-permute-start.21 = (bf16[256,2048]{1,0:T(8,128)(2,1)}, bf16[256,2048]{1,0:T(8,128)(2,1)}, u32[]{:S(2)}, u32[]{:S(2)}) collective-permute-start(bf16[256,2048]{1,0:T(8,128)(2,1)} %get-tuple-element.226.refs_3_), channel_id=1, source_target_pairs={{0,8},{1,9},{2,10},{3,11},{4,20},{5,21},{6,22},{7,23},{8,0},{9,1},... | collective-permute-start | bytes 3145736 | tf_op jit(solution)/shard_map/ppermute | solution.py:248
  156.9 21.2 %collective-permute-start.20 = (bf16[256,2048]{1,0:T(8,128)(2,1)}, bf16[256,2048]{1,0:T(8,128)(2,1)S(1)}, u32[]{:S(2)}, u32[]{:S(2)}) collective-permute-start(bf16[256,2048]{1,0:T(8,128)(2,1)} %get-tuple-element.225.refs_4_), channel_id=1, source_target_pairs={{0,4},{1,5},{2,6},{3,7},{4,0},{5,1},{6,2},{7,3},{8,12},{9,13},{10,... | collective-permute-start | bytes 3145736 | tf_op jit(solution)/shard_map/ppermute | solution.py:248
  157.4 20.6 %collective-permute-start.22 = (bf16[128,2048]{1,0:T(8,128)(2,1)}, bf16[128,2048]{1,0:T(8,128)(2,1)S(1)}, u32[]{:S(2)}, u32[]{:S(2)}) collective-permute-start(bf16[128,2048]{1,0:T(8,128)(2,1)} %get-tuple-element.227.refs_4_), channel_id=1, source_target_pairs={{0,16},{1,17},{2,18},{3,19},{4,12},{5,13},{6,14},{7,15},{8,24},{9,... | collective-permute-start | bytes 1572872 | tf_op jit(solution)/shard_map/ppermute | solution.py:248
  177.4 26.8 %collective-permute-start.26 = (bf16[512,2048]{1,0:T(8,128)(2,1)}, bf16[512,2048]{1,0:T(8,128)(2,1)}, u32[]{:S(2)}, u32[]{:S(2)}) collective-permute-start(bf16[512,2048]{1,0:T(8,128)(2,1)} %get-tuple-element.236), channel_id=1, source_target_pairs={{0,4},{1,5},{2,6},{3,7},{4,0},{5,1},{6,2},{7,3},{8,12},{9,13},{10,... | collective-permute-start | bytes 6291464 | tf_op jit(solution)/shard_map/ppermute | solution.py:248
  177.9 25.8 %collective-permute-start.23 = (bf16[256,2048]{1,0:T(8,128)(2,1)}, bf16[256,2048]{1,0:T(8,128)(2,1)}, u32[]{:S(2)}, u32[]{:S(2)}) collective-permute-start(bf16[256,2048]{1,0:T(8,128)(2,1)} %get-tuple-element.226.refs_3_), channel_id=1, source_target_pairs={{0,4},{1,5},{2,6},{3,7},{4,0},{5,1},{6,2},{7,3},{8,12},{9,13},{10,... | collective-permute-start | bytes 3145736 | tf_op jit(solution)/shard_map/ppermute | solution.py:248
  181.4 22.8 %collective-permute-start.24 = (bf16[256,2048]{1,0:T(8,128)(2,1)}, bf16[256,2048]{1,0:T(8,128)(2,1)}, u32[]{:S(2)}, u32[]{:S(2)}) collective-permute-start(bf16[256,2048]{1,0:T(8,128)(2,1)} %get-tuple-element.234.refs_4_), channel_id=1, source_target_pairs={{0,4},{1,5},{2,6},{3,7},{4,0},{5,1},{6,2},{7,3},{8,12},{9,13},{10,... | collective-permute-start | bytes 3145736 | tf_op jit(solution)/shard_map/ppermute | solution.py:248
  181.9 22.3 %collective-permute-start.25 = (bf16[256,2048]{1,0:T(8,128)(2,1)}, bf16[256,2048]{1,0:T(8,128)(2,1)}, u32[]{:S(2)}, u32[]{:S(2)}) collective-permute-start(bf16[256,2048]{1,0:T(8,128)(2,1)} %get-tuple-element.228.refs_3_), channel_id=1, source_target_pairs={{0,8},{1,9},{2,10},{3,11},{4,20},{5,21},{6,22},{7,23},{8,0},{9,1},... | collective-permute-start | bytes 3145736 | tf_op jit(solution)/shard_map/ppermute | solution.py:248
  203.7 24.6 %collective-permute-start.30 = (bf16[512,2048]{1,0:T(8,128)(2,1)}, bf16[512,2048]{1,0:T(8,128)(2,1)}, u32[]{:S(2)}, u32[]{:S(2)}) collective-permute-start(bf16[512,2048]{1,0:T(8,128)(2,1)} %get-tuple-element.246), channel_id=1, source_target_pairs={{0,4},{1,5},{2,6},{3,7},{4,0},{5,1},{6,2},{7,3},{8,12},{9,13},{10,... | collective-permute-start | bytes 6291464 | tf_op jit(solution)/shard_map/ppermute | solution.py:248
  203.7 24.5 %collective-permute-start.27 = (bf16[256,2048]{1,0:T(8,128)(2,1)}, bf16[256,2048]{1,0:T(8,128)(2,1)S(1)}, u32[]{:S(2)}, u32[]{:S(2)}) collective-permute-start(bf16[256,2048]{1,0:T(8,128)(2,1)} %get-tuple-element.228.refs_3_), channel_id=1, source_target_pairs={{0,4},{1,5},{2,6},{3,7},{4,0},{5,1},{6,2},{7,3},{8,12},{9,13},{10,... | collective-permute-start | bytes 3145736 | tf_op jit(solution)/shard_map/ppermute | solution.py:248
  207.7 20.5 %collective-permute-start.28 = (bf16[256,2048]{1,0:T(8,128)(2,1)}, bf16[256,2048]{1,0:T(8,128)(2,1)}, u32[]{:S(2)}, u32[]{:S(2)}) collective-permute-start(bf16[256,2048]{1,0:T(8,128)(2,1)} %get-tuple-element.237.refs_4_), channel_id=1, source_target_pairs={{0,4},{1,5},{2,6},{3,7},{4,0},{5,1},{6,2},{7,3},{8,12},{9,13},{10,... | collective-permute-start | bytes 3145736 | tf_op jit(solution)/shard_map/ppermute | solution.py:248
  207.8 20.4 %collective-permute-start.29 = (bf16[256,2048]{1,0:T(8,128)(2,1)}, bf16[256,2048]{1,0:T(8,128)(2,1)}, u32[]{:S(2)}, u32[]{:S(2)}) collective-permute-start(bf16[256,2048]{1,0:T(8,128)(2,1)} %get-tuple-element.244), channel_id=1, source_target_pairs={{0,8},{1,9},{2,10},{3,11},{4,20},{5,21},{6,22},{7,23},{8,0},{9,1},... | collective-permute-start | bytes 3145736 | tf_op jit(solution)/shard_map/ppermute | solution.py:248
  228.0 36.9 %collective-permute-start.33 = (bf16[512,2048]{1,0:T(8,128)(2,1)}, bf16[512,2048]{1,0:T(8,128)(2,1)}, u32[]{:S(2)}, u32[]{:S(2)}) collective-permute-start(bf16[512,2048]{1,0:T(8,128)(2,1)} %get-tuple-element.258), channel_id=1, source_target_pairs={{0,4},{1,5},{2,6},{3,7},{4,0},{5,1},{6,2},{7,3},{8,12},{9,13},{10,... | collective-permute-start | bytes 6291464 | tf_op jit(solution)/shard_map/ppermute | solution.py:248
  233.7 31.2 %collective-permute-start.32 = (bf16[256,2048]{1,0:T(8,128)(2,1)}, bf16[256,2048]{1,0:T(8,128)(2,1)S(1)}, u32[]{:S(2)}, u32[]{:S(2)}) collective-permute-start(bf16[256,2048]{1,0:T(8,128)(2,1)} %get-tuple-element.256), channel_id=1, source_target_pairs={{0,8},{1,9},{2,10},{3,11},{4,20},{5,21},{6,22},{7,23},{8,0},{9,1},... | collective-permute-start | bytes 3145736 | tf_op jit(solution)/shard_map/ppermute | solution.py:248
  255.3 35.6 %collective-permute-start.36 = (bf16[512,2048]{1,0:T(8,128)(2,1)}, bf16[512,2048]{1,0:T(8,128)(2,1)}, u32[]{:S(2)}, u32[]{:S(2)}) collective-permute-start(bf16[512,2048]{1,0:T(8,128)(2,1)} %get-tuple-element.267), channel_id=1, source_target_pairs={{0,4},{1,5},{2,6},{3,7},{4,0},{5,1},{6,2},{7,3},{8,12},{9,13},{10,... | collective-permute-start | bytes 6291464 | tf_op jit(solution)/shard_map/ppermute | solution.py:248
  271.5 19.5 %collective-permute-start.35 = (bf16[256,2048]{1,0:T(8,128)(2,1)}, bf16[256,2048]{1,0:T(8,128)(2,1)S(1)}, u32[]{:S(2)}, u32[]{:S(2)}) collective-permute-start(bf16[256,2048]{1,0:T(8,128)(2,1)} %get-tuple-element.265), channel_id=1, source_target_pairs={{0,8},{1,9},{2,10},{3,11},{4,20},{5,21},{6,22},{7,23},{8,0},{9,1},... | collective-permute-start | bytes 3145736 | tf_op jit(solution)/shard_map/ppermute | solution.py:248
  271.9 188.3 %reduce-scatter.19.cloned.1.call-start = ((), (), s32[]{:S(2)}) async-start(), calls=%async_computation.16 | async-start | bytes 655360 | tf_op jit(solution)/shard_map/reduce_scatter | solution.py:114
  287.6 29.7 %collective-permute-start.39 = (bf16[512,1024]{1,0:T(8,128)(2,1)}, bf16[512,1024]{1,0:T(8,128)(2,1)}, u32[]{:S(2)}, u32[]{:S(2)}) collective-permute-start(bf16[512,1024]{1,0:T(8,128)(2,1)} %get-tuple-element.274), channel_id=1, source_target_pairs={{0,4},{1,5},{2,6},{3,7},{4,0},{5,1},{6,2},{7,3},{8,12},{9,13},{10,... | collective-permute-start | bytes 3145736 | tf_op jit(solution)/shard_map/ppermute | solution.py:248
  297.1 20.3 %collective-permute-start.38 = (bf16[256,2048]{1,0:T(8,128)(2,1)}, bf16[256,2048]{1,0:T(8,128)(2,1)}, u32[]{:S(2)}, u32[]{:S(2)}) collective-permute-start(bf16[256,2048]{1,0:T(8,128)(2,1)} %get-tuple-element.272), channel_id=1, source_target_pairs={{0,8},{1,9},{2,10},{3,11},{4,20},{5,21},{6,22},{7,23},{8,0},{9,1},... | collective-permute-start | bytes 3145736 | tf_op jit(solution)/shard_map/ppermute | solution.py:248
  298.7 18.7 %collective-permute-start.37 = (bf16[128,2048]{1,0:T(8,128)(2,1)}, bf16[128,2048]{1,0:T(8,128)(2,1)}, u32[]{:S(2)}, u32[]{:S(2)}) collective-permute-start(bf16[128,2048]{1,0:T(8,128)(2,1)} %get-tuple-element.270), channel_id=1, source_target_pairs={{0,16},{1,17},{2,18},{3,19},{4,12},{5,13},{6,14},{7,15},{8,24},{9,... | collective-permute-start | bytes 1572872 | tf_op jit(solution)/shard_map/ppermute | solution.py:248
  299.2 162.6 %reduce-scatter.21.cloned.1.call-start = ((), (), s32[]{:S(2)}) async-start(), calls=%async_computation.17 | async-start | bytes 655360 | tf_op jit(solution)/shard_map/reduce_scatter | solution.py:114
  317.3 33.1 %collective-permute-start.42 = (f32[512,768]{1,0:T(8,128)}, f32[512,768]{1,0:T(8,128)S(1)}, u32[]{:S(2)}, u32[]{:S(2)}) collective-permute-start(f32[512,768]{1,0:T(8,128)} %get-tuple-element.283), channel_id=1, source_target_pairs={{0,4},{1,5},{2,6},{3,7},{4,0},{5,1},{6,2},{7,3},{8,12},{9,13},{10,... | collective-permute-start | bytes 4718600 | tf_op jit(solution)/shard_map/ppermute | solution.py:248
  321.3 19.8 %collective-permute-start.40 = (bf16[128,2048]{1,0:T(8,128)(2,1)}, bf16[128,2048]{1,0:T(8,128)(2,1)}, u32[]{:S(2)}, u32[]{:S(2)}) collective-permute-start(bf16[128,2048]{1,0:T(8,128)(2,1)} %get-tuple-element.277), channel_id=1, source_target_pairs={{0,16},{1,17},{2,18},{3,19},{4,12},{5,13},{6,14},{7,15},{8,24},{9,... | collective-permute-start | bytes 1572872 | tf_op jit(solution)/shard_map/ppermute | solution.py:248
  322.7 140.8 %reduce-scatter.23.cloned.1.call-start = ((), (), s32[]{:S(2)}) async-start(), calls=%async_computation.18 | async-start | bytes 655360 | tf_op jit(solution)/shard_map/reduce_scatter | solution.py:114
  341.0 37.4 %collective-permute-start.47 = (f32[512,768]{1,0:T(8,128)}, f32[512,768]{1,0:T(8,128)}, u32[]{:S(2)}, u32[]{:S(2)}) collective-permute-start(f32[512,768]{1,0:T(8,128)} %get-tuple-element.292), channel_id=1, source_target_pairs={{0,4},{1,5},{2,6},{3,7},{4,0},{5,1},{6,2},{7,3},{8,12},{9,13},{10,... | collective-permute-start | bytes 4718600 | tf_op jit(solution)/shard_map/ppermute | solution.py:248
  356.2 108.9 %reduce-scatter.15.cloned.1.call-start = ((), (), s32[]{:S(2)}) async-start(), calls=%async_computation.14 | async-start | bytes 327680 | tf_op jit(solution)/shard_map/reduce_scatter | solution.py:114
  356.3 22.1 %collective-permute-start.43 = (bf16[128,1024]{1,0:T(8,128)(2,1)}, bf16[128,1024]{1,0:T(8,128)(2,1)S(1)}, u32[]{:S(2)}, u32[]{:S(2)}) collective-permute-start(bf16[128,1024]{1,0:T(8,128)(2,1)} %get-tuple-element.286), channel_id=1, source_target_pairs={{0,16},{1,17},{2,18},{3,19},{4,12},{5,13},{6,14},{7,15},{8,24},{9,... | collective-permute-start | bytes 786440 | tf_op jit(solution)/shard_map/ppermute | solution.py:248
  356.3 21.9 %collective-permute-start.44 = (bf16[128,768]{1,0:T(8,128)(2,1)}, bf16[128,768]{1,0:T(8,128)(2,1)S(1)}, u32[]{:S(2)}, u32[]{:S(2)}) collective-permute-start(bf16[128,768]{1,0:T(8,128)(2,1)} %get-tuple-element.288), channel_id=1, source_target_pairs={{0,16},{1,17},{2,18},{3,19},{4,12},{5,13},{6,14},{7,15},{8,24},{9,... | collective-permute-start | bytes 589832 | tf_op jit(solution)/shard_map/ppermute | solution.py:248
  358.4 20.0 %collective-permute-start.45 = (bf16[128,768]{1,0:T(8,128)(2,1)}, bf16[128,768]{1,0:T(8,128)(2,1)S(1)}, u32[]{:S(2)}, u32[]{:S(2)}) collective-permute-start(bf16[128,768]{1,0:T(8,128)(2,1)} %get-tuple-element.289), channel_id=1, source_target_pairs={{0,8},{1,9},{2,10},{3,11},{4,20},{5,21},{6,22},{7,23},{8,0},{9,1},... | collective-permute-start | bytes 589832 | tf_op jit(solution)/shard_map/ppermute | solution.py:248
  358.4 20.0 %collective-permute-start.46 = (bf16[128,768]{1,0:T(8,128)(2,1)}, bf16[128,768]{1,0:T(8,128)(2,1)S(1)}, u32[]{:S(2)}, u32[]{:S(2)}) collective-permute-start(bf16[128,768]{1,0:T(8,128)(2,1)} %get-tuple-element.290), channel_id=1, source_target_pairs={{0,24},{1,25},{2,26},{3,27},{4,28},{5,29},{6,30},{7,31},{8,16},{9,... | collective-permute-start | bytes 589832 | tf_op jit(solution)/shard_map/ppermute | solution.py:248
  378.2 34.9 %collective-permute-start.51 = (f32[512,768]{1,0:T(8,128)}, f32[512,768]{1,0:T(8,128)}, u32[]{:S(2)}, u32[]{:S(2)}) collective-permute-start(f32[512,768]{1,0:T(8,128)} %get-tuple-element.299), channel_id=1, source_target_pairs={{0,4},{1,5},{2,6},{3,7},{4,0},{5,1},{6,2},{7,3},{8,12},{9,13},{10,... | collective-permute-start | bytes 4718600 | tf_op jit(solution)/shard_map/ppermute | solution.py:248
  382.7 87.1 %reduce-scatter.9.cloned.1.call-start = ((), (), s32[]{:S(2)}) async-start(), calls=%async_computation.11 | async-start | bytes 491520 | tf_op jit(solution)/shard_map/reduce_scatter | solution.py:114
  401.1 30.0 %collective-permute-start.55 = (f32[512,768]{1,0:T(8,128)}, f32[512,768]{1,0:T(8,128)S(1)}, u32[]{:S(2)}, u32[]{:S(2)}) collective-permute-start(f32[512,768]{1,0:T(8,128)} %get-tuple-element.311), channel_id=1, source_target_pairs={{0,4},{1,5},{2,6},{3,7},{4,0},{5,1},{6,2},{7,3},{8,12},{9,13},{10,... | collective-permute-start | bytes 4718600 | tf_op jit(solution)/shard_map/ppermute | solution.py:248
  401.2 68.7 %reduce-scatter.11.cloned.1.call-start = ((), (), s32[]{:S(2)}) async-start(), calls=%async_computation.12 | async-start | bytes 491520 | tf_op jit(solution)/shard_map/reduce_scatter | solution.py:114
  417.0 52.8 %reduce-scatter.13.cloned.1.call-start = ((), (), s32[]{:S(2)}) async-start(), calls=%async_computation.13 | async-start | bytes 491520 | tf_op jit(solution)/shard_map/reduce_scatter | solution.py:114
  (68 other events, 404.5 us)
Sparse Core Ops, SparseCore 0:
  13.7 35.2 all-gather.2
  51.2 35.9 all-gather.4
  272.0 21.8 reduce-scatter.16
  299.3 21.6 reduce-scatter.18
  323.7 20.7 reduce-scatter.20
  356.3 20.6 reduce-scatter.22
  382.8 18.7 reduce-scatter.14
  404.6 18.8 reduce-scatter.8
  426.4 18.8 reduce-scatter.10
  448.1 20.6 reduce-scatter.12

commit v3 on v2

--- a/solution.py
+++ b/solution.py
@@ -93,7 +93,7 @@
         for s in range(self.bits - 1):
             kept, sent = yield [sent], pairs, ("sum", [kept], [bf16, bf16])
             pairs = self.mix_pairs(s)
-        (total,) = yield [sent], pairs, ("sum", [kept], [bf16])
+        (total,) = yield [sent], pairs, ("sum", [kept], [f32])
         return total
 
     def scatter_direct(self, sent, kept):
@@ -111,7 +111,7 @@
 
     def own_rows(self, total, direct=False):
         if not direct or self.nfs > 4:
-            return lax.psum_scatter(total, "fsdp", scatter_dimension=0, tiled=True).astype(f32)
+            return lax.psum_scatter(total, "fsdp", scatter_dimension=0, tiled=True)
         me, rows = lax.axis_index("fsdp"), total.shape[0] // self.nfs
         block = lambda f: lax.dynamic_slice_in_dim(total, f * rows, rows, 0)
         sum_ = block(me)
@@ -214,7 +214,7 @@
 class Flow:
     def __init__(self, plan):
         self.plan = plan
-        self.live, self.flying, self.done, self.waiting = {}, {}, {}, {}
+        self.live, self.flying, self.done, self.waiting, self.shards = {}, {}, {}, {}, {}
 
     def gather(self, name, array, at=None, wide=None):
         self.waiting[name] = (array, at, wide)
@@ -223,7 +223,10 @@
         way = self.plan.scatter_direct if direct else self.plan.scatter
         self.live[name] = way(sent, kept)
 
-    def step(self, x, names):
+    def own_rows(self, name, total=None):
+        self.shards[name] = self.plan.own_rows(self.done[name] if total is None else total)
+
+    def step(self, x, names, pinned=()):
         names = [n for n in names if n not in self.done]
         came = {n: self.flying.pop(n) for n in names if n in self.flying}
         start = {n: self.waiting.pop(n) for n in names if n in self.waiting}
@@ -236,7 +239,9 @@
             elif merge:
                 work[n] = ("sum", merge[1] + got, merge[2])
         work |= {n: ("cut", *v) for n, v in start.items() if v[1] is not None}
-        (x, plain, whole), made = tie((x, plain, whole), list(work.values()))
+        held = {n: self.shards[n] for n in pinned}
+        (x, plain, whole, held), made = tie((x, plain, whole, held), list(work.values()))
+        self.shards |= held
         made = dict(zip(work, made))
         for n in start:
             self.live[n] = self.plan.gather(whole[n] if n in whole else made[n][0])
@@ -454,27 +459,42 @@
     return z * half, slope
 
 
-def mlp_kernel(count, block, sub, first, last, tab, *refs):
-    u_hbm, u_t_hbm, g_hbm = refs[:3]
-    pieces, refs = refs[3 : 3 + count], refs[3 + count :]
-    held_out, refs = refs[0], refs[1:]
-    if not first:
-        held_du, refs = refs[0], refs[1:]
-    out_hbm, du_hbm, sent, kept = refs[:4]
-    u, u_t, g, up, down, out_acc, du_acc, a_s, dz_s, grad, low, sems = refs[4:]
-    width = u.shape[1]
+def norm_back(v, gain, du):
+    r = lax.rsqrt(jnp.mean(v * v, axis=1, keepdims=True) + NORM_EPS)
+    up = du * gain
+    return r * up - v * (r * r * r * jnp.mean(up * v, axis=1, keepdims=True))
+
+
+def mlp_kernel(counts, block, first, last, outs, tab, *refs):
+    refs = list(refs)
+    take = lambda n: [refs.pop(0) for _ in range(n)]
+    u_hbm, u_t_hbm, g_hbm = take(3)
+    pieces = [take(count) for count in counts]
+    (held_out,) = take(1)
+    held_du = None if first else take(1)[0]
+    if last:
+        mid_hbm, gain_hbm = take(2)
+        o_hbm, w_hbm = take(outs[0]), take(outs[1])
+    (out_hbm,) = take(1)
+    if last:
+        dmid_hbm, do_hbm, out_sent, out_kept = take(4)
+    else:
+        (du_hbm,) = take(1)
+    sent, kept = take(2)
+    u, u_t, g, up_s, down_s, out_acc, du_acc, a_s, dz_s, grad, low, gain, sems = refs
+    length, width = u.shape
     wide = 512
     halves = width // wide
     blocks = width // block
-    base = 2 * sub * width
+    subs = len(counts)
     free = iter(range(sems.shape[0]))
 
     def copy(src, dst):
         return pltpu.make_async_copy(src, dst, sems.at[next(free)])
 
-    def rows(at, columns, dst, dst_columns):
+    def rows(held, at, columns, dst, dst_columns):
         out, j = [], 0
-        for piece in pieces:
+        for piece in held:
             for i in range(piece.shape[0] // block):
                 row = pl.multiple_of(tab[j] * block, block)
                 src = piece.at[pl.ds(i * block, block), pl.ds(at, columns)]
@@ -482,12 +502,14 @@
                 j += 1
         return out
 
-    get_u = [copy(u_hbm, u)]
-    get_up = [rows(base + f * wide, wide, up, pl.ds(f * wide, wide)) for f in range(halves)]
-    get_g = [copy(g_hbm, g)]
-    get_down = rows(base + width, width, down, pl.ds(0, width))
-    get_acc = [copy(held_out, out_acc)] + ([] if first else [copy(held_du, du_acc)])
-    get_t = [copy(u_t_hbm, u_t)]
+    def back(columns, sent_to, kept_to, at):
+        out = []
+        for j in range(blocks):
+            row = pl.multiple_of(tab[j] * block, block)
+            to = kept_to if j < blocks // 2 else sent_to
+            dst = to.at[pl.ds(j % (blocks // 2) * block, block), pl.ds(at, columns)]
+            out.append(copy(grad.at[pl.ds(row, block), pl.ds(0, columns)], dst))
+        return out
 
     def start(copies):
         for c in copies:
@@ -497,168 +519,143 @@
         for c in copies:
             c.wait()
 
-    start(get_u + get_up[0] + get_g + get_down + get_t)
+    get_u, get_g, get_t = [copy(u_hbm, u)], [copy(g_hbm, g)], [copy(u_t_hbm, u_t)]
+    get_up = [
+        [rows(pieces[i], f * wide, wide, up_s.at[i], pl.ds(f * wide, wide)) for f in range(halves)]
+        for i in range(subs)
+    ]
+    get_down = [rows(pieces[i], width, width, down_s.at[i], pl.ds(0, width)) for i in range(subs)]
+    get_acc = [copy(held_out, out_acc)] + ([] if first else [copy(held_du, du_acc)])
+    start(get_u + get_up[0][0] + get_g + get_down[0] + get_t)
     for f in range(1, halves):
-        start(get_up[f])
+        start(get_up[0][f])
     start(get_acc)
-    for f in range(halves):
-        cols = slice(f * wide, (f + 1) * wide)
-        wait((get_u if f == 0 else []) + get_up[f])
-        z = jnp.dot(u[...], up[:, cols], preferred_element_type=f32)
-        a, slope = gelu_both(z)
-        if f == 0:
-            wait(get_g + get_down)
-        da = lax.dot_general(g[...], down[cols, :], NT, preferred_element_type=f32)
-        a_s[:, cols] = a.astype(bf16)
-        dz_s[:, cols] = (da * slope).astype(bf16)
-        if f == 0:
-            wait(get_t)
-        grad[:, cols] = jnp.dot(u_t[...], dz_s[:, cols], preferred_element_type=f32).astype(bf16)
-        turned = lax.dot_general(a_s[:, cols], g[...], TN, preferred_element_type=f32)
-        grad[cols, width:] = turned.astype(bf16)
-    saved = []
-    for j in range(blocks):
-        row = pl.multiple_of(tab[j] * block, block)
-        out = kept if j < blocks // 2 else sent
-        at = j % (blocks // 2) * block
-        saved.append(copy(grad.at[pl.ds(row, block)], out.at[pl.ds(at, block)]))
-    start(saved)
-    wait(get_acc)
-    half = u.shape[0] // 2
-    for i in range(2):
-        part = pl.ds(i * half, half)
-        out = out_acc[part, :] + jnp.dot(a_s[part, :], down[...], preferred_element_type=f32)
-        if last:
-            low[part, :] = out.astype(bf16)
-            saved.append(copy(low.at[part], out_hbm.at[part]))
-        else:
-            out_acc[part, :] = out
-            saved.append(copy(out_acc.at[part], out_hbm.at[part]))
-        saved[-1].start()
-    for i in range(2):
-        part = pl.ds(i * half, half)
-        du = lax.dot_general(dz_s[part, :], up[...], NT, preferred_element_type=f32)
-        du_acc[part, :] = du if first else du_acc[part, :] + du
-        saved.append(copy(du_acc.at[part], du_hbm.at[part]))
-        saved[-1].start()
-    wait(saved)
-
-
-def feed_forward(tab, u, u_t, g, pieces, sub, held, block, first, last):
+    for i in range(1, subs):
+        start(sum(get_up[i], []) + get_down[i])
+    waiting, saved = [], []
+    half = length // 2
+    for i in range(subs):
+        up, down = up_s.at[i], down_s.at[i]
+        final = i == subs - 1
+        for f in range(halves):
+            cols = slice(f * wide, (f + 1) * wide)
+            wait((get_u if i + f == 0 else []) + get_up[i][f])
+            z = jnp.dot(u[...], up[:, cols], preferred_element_type=f32)
+            a, slope = gelu_both(z)
+            if f == 0:
+                wait((get_g if i == 0 else []) + get_down[i])
+            da = lax.dot_general(g[...], down[cols, :], NT, preferred_element_type=f32)
+            a_s[:, cols] = a.astype(bf16)
+            dz_s[:, cols] = (da * slope).astype(bf16)
+            if f == 0:
+                wait((get_t if i == 0 else []) + waiting)
+            part = jnp.dot(u_t[...], dz_s[:, cols], preferred_element_type=f32)
+            grad[:, cols] = part.astype(bf16)
+            turned = lax.dot_general(a_s[:, cols], g[...], TN, preferred_element_type=f32)
+            grad[cols, width:] = turned.astype(bf16)
+        waiting = back(2 * width, sent, kept, 2 * i * width)
+        start(waiting)
+        if i == 0:
+            wait(get_acc)
+        for r in range(2):
+            part = pl.ds(r * half, half)
+            out = out_acc[part, :] + jnp.dot(a_s[part, :], down[...], preferred_element_type=f32)
+            if last and final:
+                low[part, :] = out.astype(bf16)
+                saved.append(copy(low.at[part], out_hbm.at[part]))
+                saved[-1].start()
+            else:
+                out_acc[part, :] = out
+                if final:
+                    saved.append(copy(out_acc.at[part], out_hbm.at[part]))
+                    saved[-1].start()
+        if last and final:
+            get_w = rows(w_hbm, 0, width, down, pl.ds(0, width)) + [copy(gain_hbm, gain)]
+            start(get_w)
+            get_mid = [copy(mid_hbm, out_acc)]
+            at = 0
+            for o in o_hbm:
+                get_mid.append(copy(o, a_s.at[:, pl.ds(at, o.shape[1])]))
+                at += o.shape[1]
+            start(get_mid)
+        for r in range(2):
+            part = pl.ds(r * half, half)
+            du = lax.dot_general(dz_s[part, :], up[...], NT, preferred_element_type=f32)
+            du_acc[part, :] = du if first and i == 0 else du_acc[part, :] + du
+            if final and not last:
+                saved.append(copy(du_acc.at[part], du_hbm.at[part]))
+                saved[-1].start()
+    if last:
+        wait(get_w + get_mid)
+        size = 256
+        for r in range(length // size):
+            part = pl.ds(r * size, size)
+            dmid = g[part, :].astype(f32) + norm_back(out_acc[part, :], gain[1:2, :], du_acc[part, :])
+            du_acc[part, :] = dmid
+            u[part, :] = dmid.astype(bf16)
+            saved.append(copy(du_acc.at[part], dmid_hbm.at[part]))
+            saved[-1].start()
+            do = lax.dot_general(u[part, :], down_s[subs - 1], NT, preferred_element_type=f32)
+            dz_s[part, :] = do.astype(bf16)
+            saved.append(copy(dz_s.at[part], do_hbm.at[part]))
+            saved[-1].start()
+        wait(waiting)
+        turned = lax.dot_general(a_s[...], u[...], TN, preferred_element_type=f32)
+        grad[:, 0:width] = turned.astype(bf16)
+        waiting = back(width, out_sent, out_kept, 0)
+        start(waiting)
+    wait(waiting + saved)
+
+
+def feed_forward(tab, u, u_t, g, pieces, held, block, first, last=None):
     length, width = u.shape
     half = width // 2
     anywhere = pl.BlockSpec(memory_space=pl.ANY)
     held = held[:1] if first else held
-    inputs = [u, u_t, g, *pieces, *held]
-    alias = {}
-    if not first:
-        alias[len(inputs)] = 1
-        if not last:
-            alias[len(inputs) - 1] = 0
+    inputs = [u, u_t, g, *[p for group in pieces for p in group], *held]
     acc = jax.ShapeDtypeStruct((length, width), f32)
-    part = jax.ShapeDtypeStruct((half, 2 * width), bf16)
+    low = jax.ShapeDtypeStruct((length, width), bf16)
+    shard = lambda w: jax.ShapeDtypeStruct((half, w), bf16)
+    alias, outs = {}, (0, 0)
+    if last:
+        mid, gains, o, w_out = last
+        inputs += [mid, gains, *o, *w_out]
+        outputs = [low, acc, low, shard(width), shard(width)]
+        outs = (len(o), len(w_out))
+    else:
+        outputs = [acc, acc]
+    outputs += [shard(2 * width * len(pieces))] * 2
     blocks = width // block
+    subs = len(pieces)
     return pl.pallas_call(
-        functools.partial(mlp_kernel, len(pieces), block, sub, first, last),
+        functools.partial(mlp_kernel, [len(p) for p in pieces], block, first, last is not None, outs),
         grid_spec=pltpu.PrefetchScalarGridSpec(
             num_scalar_prefetch=1,
             grid=(1,),
             in_specs=[anywhere] * len(inputs),
-            out_specs=[anywhere] * 4,
+            out_specs=[anywhere] * len(outputs),
             scratch_shapes=[
                 pltpu.VMEM((length, width), bf16),
                 pltpu.VMEM((width, length), bf16),
                 pltpu.VMEM((length, width), bf16),
-                pltpu.VMEM((width, width), bf16),
-                pltpu.VMEM((width, width), bf16),
+                pltpu.VMEM((subs, width, width), bf16),
+                pltpu.VMEM((subs, width, width), bf16),
                 pltpu.VMEM((length, width), f32),
                 pltpu.VMEM((length, width), f32),
                 pltpu.VMEM((length, width), bf16),
                 pltpu.VMEM((length, width), bf16),
                 pltpu.VMEM((width, 2 * width), bf16),
                 pltpu.VMEM((length, width) if last else (16, LANES), bf16),
-                pltpu.SemaphoreType.DMA((4 * blocks + 12,)),
+                pltpu.VMEM((8, width), f32),
+                pltpu.SemaphoreType.DMA(((4 * subs + 2) * blocks + 32,)),
             ],
         ),
-        out_shape=[jax.ShapeDtypeStruct((length, width), bf16) if last else acc, acc, part, part],
+        out_shape=outputs,
         input_output_aliases=alias,
         compiler_params=params(),
-        cost_estimate=cost(12 * length * width * width, 24 << 20),
+        cost_estimate=cost((12 * subs + 4 * outs[0]) * length * width * width, 48 << 20),
         name="feed_forward",
     )(tab, *inputs)
-
-
-def norm_back(v, gain, du):
-    r = lax.rsqrt(jnp.mean(v * v, axis=1, keepdims=True) + NORM_EPS)
-    up = du * gain
-    return r * up - v * (r * r * r * jnp.mean(up * v, axis=1, keepdims=True))
-
-
-def dmid_kernel(count, groups, block, steps, tab, n_ref, du_ref, mid_ref, cot_ref, gain_ref, *refs):
-    o_refs, refs = refs[:groups], refs[groups:]
-    weights = refs[:count]
-    dmid_ref, do_ref, sent, kept, w_nat, total, grad = refs[count:]
-    i = pl.program_id(0)
-    rows = du_ref.shape[0]
-
-    @pl.when(i == 0)
-    def _():
-        natural(w_nat, slice(None), weights, slice(None), tab, block)
-
-    frame = lax.broadcasted_iota(jnp.int32, (rows, 1), 0) + i * rows
-    g = jnp.where(frame < n_ref[0], cot_ref[...].astype(f32), 0.0)
-    dmid = g + norm_back(mid_ref[...], gain_ref[1:2, :], du_ref[...])
-    dmid_ref[...] = dmid
-    low = dmid.astype(bf16)
-    do_ref[...] = lax.dot_general(low, w_nat[...], NT, preferred_element_type=f32).astype(bf16)
-    o = jnp.concatenate([ref[...] for ref in o_refs], axis=1)
-    part = lax.dot_general(o, low, TN, preferred_element_type=f32)
-
-    @pl.when(i == 0)
-    def _():
-        total[...] = part
-
-    @pl.when(i > 0)
-    def _():
-        total[...] += part
-
-    @pl.when(i == steps - 1)
-    def _():
-        grad[...] = total[...].astype(bf16)
-        relative(sent, kept, slice(None), grad, slice(None), tab, block)
-
-
-def middle_back(tab, frames, du, mid, cot, gains, o, pieces, block):
-    length, width = mid.shape
-    rows = 256
-    steps = length // rows
-    row = pl.BlockSpec((rows, width), lambda i, t, n: (i, 0))
-    half = width // 2
-    return pl.pallas_call(
-        functools.partial(dmid_kernel, len(pieces), len(o), block, steps),
-        grid_spec=pltpu.PrefetchScalarGridSpec(
-            num_scalar_prefetch=2,
-            grid=(steps,),
-            in_specs=[row, row, row, full((8, width))]
-            + [pl.BlockSpec((rows, v.shape[1]), lambda i, t, n: (i, 0)) for v in o]
-            + [full(p.shape) for p in pieces],
-            out_specs=[row, row, full((half, width)), full((half, width))],
-            scratch_shapes=[
-                pltpu.VMEM((width, width), bf16),
-                pltpu.VMEM((width, width), f32),
-                pltpu.VMEM((width, width), bf16),
-            ],
-        ),
-        out_shape=[
-            jax.ShapeDtypeStruct((length, width), f32),
-            jax.ShapeDtypeStruct((length, width), bf16),
-            jax.ShapeDtypeStruct((half, width), bf16),
-            jax.ShapeDtypeStruct((half, width), bf16),
-        ],
-        compiler_params=params(),
-        cost_estimate=cost(4 * length * width * width, 24 << 20),
-        name="middle_back",
-    )(tab, frames, du, mid, cot, gains, *o, *pieces)
 
 
 def attend_back_kernel(
@@ -744,7 +741,8 @@
     )(frames, tab, qkv, qkv, qkv, g, lse, u_t)
 
 
-def input_grad_kernel(groups, parts, block, tab, dmid_ref, x_ref, gain_ref, *refs):
+def input_grad_kernel(groups, parts, more, block, tab, dmid_ref, x_ref, gain_ref, *refs):
+    refs = refs[more:]
     d_refs, refs = refs[:parts], refs[parts:]
     weights, out_ref, nats = refs[: -1 - groups], refs[-1 - groups], refs[-groups:]
     count = len(weights) // groups
@@ -763,7 +761,7 @@
     out_ref[...] = dmid_ref[...] + norm_back(x_ref[...].astype(f32), gain_ref[0:1, :], du)
 
 
-def input_grad(tab, d, dmid, x, gains, pieces, block, lo, hi):
+def input_grad(tab, d, dmid, x, gains, pieces, block, lo, hi, done=()):
     length, width = x.shape
     rows = 256
     groups = len(pieces)
@@ -775,19 +773,23 @@
         for p in group
     ]
     return pl.pallas_call(
-        functools.partial(input_grad_kernel, groups, len(d), block),
+        functools.partial(input_grad_kernel, groups, len(d), len(done), block),
         grid_spec=pltpu.PrefetchScalarGridSpec(
             num_scalar_prefetch=1,
             grid=(hi - lo,),
-            in_specs=[row(width), row(width), full((8, width))] + [row(v.shape[1]) for v in d] + weights,
-            out_specs=pl.BlockSpec((rows, width), lambda i, t: (i, 0)),
+            in_specs=[row(width), row(width), full((8, width))]
+            + [pl.BlockSpec(memory_space=pl.ANY)] * len(done)
+            + [row(v.shape[1]) for v in d]
+            + weights,
+            out_specs=row(width),
             scratch_shapes=[pltpu.VMEM((width, columns), bf16)] * groups,
         ),
-        out_shape=jax.ShapeDtypeStruct(((hi - lo) * rows, width), f32),
+        out_shape=jax.ShapeDtypeStruct((length, width), f32),
+        input_output_aliases={4: 0} if done else {},
         compiler_params=params(),
         cost_estimate=cost(6 * length * width * width * (hi - lo) // 4, 22 << 20),
         name="input_grad",
-    )(tab, dmid, x, gains, *d, *[p for group in pieces for p in group])
+    )(tab, dmid, x, gains, *done, *d, *[p for group in pieces for p in group])
 
 
 def adam_step(weight, first, second, gradient, clip_factor, step_rate, decay_rate, shadow):
@@ -807,18 +809,23 @@
     return jnp.sum(v * v)
 
 
-def norm_kernel(parts, subs, *refs):
-    grads, rest = refs[: parts + 1 + subs], refs[parts + 1 + subs :]
-    weights, (gains, everyone, gain_grad) = rest[: parts + subs], rest[parts + subs :]
-    rows, width = grads[parts].shape
+def view(refs, views, i, lo=0, hi=None):
+    array, at, width = views[i]
+    return refs[array][:, at + lo : at + (width if hi is None else hi)].astype(f32)
+
+
+def norm_kernel(arrays, views, parts, *refs):
+    grads, rest = refs[:arrays], refs[arrays:]
+    weights, (gains, everyone, gain_grad) = rest[:-3], rest[-3:]
+    rows, width = gains.shape[1], D
     one = two = jnp.zeros((rows, 1), f32)
-    total = square(grads[parts][...])
+    total = square(view(grads, views, parts))
     for i in range(parts):
-        grad = grads[i][...]
+        grad = view(grads, views, i)
         total = total + square(grad)
         one = one + jnp.sum(weights[i][...].astype(f32) * grad, axis=1, keepdims=True)
-    for i in range(subs):
-        grad = grads[parts + 1 + i][...]
+    for i in range(len(views) - parts - 1):
+        grad = view(grads, views, parts + 1 + i)
         total = total + square(grad)
         up = weights[parts + i][...].astype(f32) * grad[:, :width]
         two = two + jnp.sum(up, axis=1, keepdims=True)
@@ -829,11 +836,11 @@
     everyone[...] = jnp.broadcast_to(total + square(both), everyone.shape)
 
 
-def square_sums(parts, out, mlp, weights, gains, ndev):
+def square_sums(arrays, views, parts, weights, gains, ndev):
     place = pl.BlockSpec(memory_space=pltpu.VMEM)
-    inputs = [*parts, out, *mlp, *weights, gains]
+    inputs = [*arrays, *weights, gains]
     return pl.pallas_call(
-        functools.partial(norm_kernel, len(parts), len(mlp)),
+        functools.partial(norm_kernel, len(arrays), views, parts),
         in_specs=[place] * len(inputs),
         out_specs=[place] * 2,
         out_shape=[
@@ -845,9 +852,9 @@
     )(*inputs)
 
 
-def adam_kernel(parts, subs, rates, decays, sums_ref, *refs):
-    count = parts + 2 + subs
-    grads, states, outs = refs[:count], refs[count : count + 20], refs[count + 20 :]
+def adam_kernel(arrays, views, parts, rates, decays, sums_ref, *refs):
+    grads, gain_grad, refs = refs[:arrays], refs[arrays], refs[arrays + 1 :]
+    states, outs = refs[:20], refs[20:]
     norm = jnp.sqrt(jnp.sum(sums_ref[...], axis=0))
     outs[20][...] = norm
     clip = jnp.minimum(1.0, CLIP_NORM / norm[:, 0:1])
@@ -858,40 +865,39 @@
         for k in range(4):
             outs[4 * i + k][rows, cols] = new[k]
 
-    wide = D // LANES // parts
     every = slice(None)
-    for c in range(3):
-        for p in range(parts):
-            for j in range(wide):
-                at = c * D + (p * wide + j) * LANES
+    col = 0
+    for p in range(parts):
+        for j in range(views[p][2] // (3 * LANES)):
+            for c in range(3):
+                at = c * D + col * LANES
                 src = (3 * j + c) * LANES
-                update(0, every, slice(at, at + LANES), grads[p][:, src : src + LANES])
-    update(1, every, every, grads[parts][...])
-    mlp = grads[parts + 1 : parts + 1 + subs]
-    own = mlp[0].shape[0]
+                update(0, every, slice(at, at + LANES), view(grads, views, p, src, src + LANES))
+            col += 1
+    update(1, every, every, view(grads, views, parts))
+    own = states[0].shape[0]
+    subs = FF // D
     size = subs * own
     for at in range(0, FF, LANES):
-        grad = jnp.concatenate(
-            [
-                mlp[q][:, dev * own : (dev + 1) * own]
-                for dev in range(at // size, (at + LANES) // size)
-                for q in range(subs)
-            ],
-            axis=1,
-        )
-        update(2, every, slice(at, at + LANES), grad)
+        pieces = [
+            view(grads, views, parts + 1 + q, dev * own, (dev + 1) * own)
+            for dev in range(at // size, (at + LANES) // size)
+            for q in range(subs)
+        ]
+        update(2, every, slice(at, at + LANES), jnp.concatenate(pieces, axis=1))
     for q in range(subs):
-        update(3, slice(q * own, (q + 1) * own), every, mlp[q][:, D:])
-    update(4, every, every, grads[-1][...])
-
-
-def adam(sums, parts, out, mlp, gain, states, rates, decays):
+        grad = view(grads, views, parts + 1 + q, D, 2 * D)
+        update(3, slice(q * own, (q + 1) * own), every, grad)
+    update(4, every, every, gain_grad[...])
+
+
+def adam(sums, arrays, views, parts, gain, states, rates, decays):
     place = pl.BlockSpec(memory_space=pltpu.VMEM)
-    inputs = [sums, *parts, out, *mlp, gain, *[v for group in states for v in group]]
+    inputs = [sums, *arrays, gain, *[v for group in states for v in group]]
     outputs = [jax.ShapeDtypeStruct(v.shape, f32) for group in states for v in group]
     outputs.append(jax.ShapeDtypeStruct((1, LANES), f32))
     done = pl.pallas_call(
-        functools.partial(adam_kernel, len(parts), len(mlp), rates, decays),
+        functools.partial(adam_kernel, len(arrays), views, parts, rates, decays),
         in_specs=[place] * len(inputs),
         out_specs=[place] * len(outputs),
         out_shape=outputs,
@@ -924,13 +930,14 @@
     local_mlp = [v for q in range(subs) for v in (up_low[q], down_low[q])]
     early = jnp.concatenate([qkv_low[:, columns:], w_out.astype(bf16)] + local_mlp[:2], axis=1)
     late = jnp.concatenate(local_mlp[2:], axis=1)
+    keep = (jnp.arange(length) < frames[0])[:, None]
+    g_low = jnp.where(keep, cotangent[0], jnp.zeros((), bf16))
 
     flow = Flow(plan)
     step = flow.step
     reach = lambda v: lax.all_gather(v, "fsdp", axis=0, tiled=True)
     early = reach(early)
-    held_q0 = reach(local_q0)
-    flow.gather("q0", held_q0)
+    flow.gather("q0", reach(local_q0))
     step(None, ["q0"])
     late = reach(late)
     flow.gather("q1", early, 0, columns)
@@ -938,7 +945,7 @@
     flow.gather("m0", early, columns + D, 2 * D)
     for k in range(1, subs):
         flow.gather(f"m{k}", late, 2 * (k - 1) * D, 2 * D)
-    step(None, ["q0"])
+    g_low = step(g_low, ["q0"])
     step(None, ["q0"])
     flow.until(None, ["q0"])
     step(None, ["q1", "o", "m0"])
@@ -955,34 +962,32 @@
     o = flow.until(o, ["o"])
     full_out = flow.done["o"]
     mid, u_two, u_two_t = middle(tab, o, x, gains, full_out, block)
-    keep = (jnp.arange(length) < frames[0])[:, None]
-    g_low = jnp.where(keep, cotangent[0], jnp.zeros((), bf16))
     u_two = step(u_two, ["m0", "m1", "m3"])
     held = [mid, None]
-    plans = [
-        ["m1", "m2", "m3", "g0"],
-        ["m2", "m3", "g0", "g1"],
-        ["m3", "g0", "g1", "g2"],
-        ["g0", "g1", "g2", "g3"],
-    ]
+    plans = [["m1", "m2", "m3", "g0"], ["m2", "m3", "g0", "g1"], ["m3", "g0", "g1", "g2"]]
     for k in range(subs):
         u_two = flow.until(u_two, [f"m{k}"])
-        out, du, sent, kept = feed_forward(
-            tab, u_two, u_two_t, g_low, flow.done[f"m{k}"], 0, held, block, k == 0, k == subs - 1
+        last = (mid, gains, o, full_out) if k == subs - 1 else None
+        out, held_du, *more, sent, kept = feed_forward(
+            tab, u_two, u_two_t, g_low, [flow.done[f"m{k}"]], held, block, k == 0, last
         )
-        held = [out, du]
         flow.scatter(f"g{k}", sent, kept)
-        held[1] = step(held[1], plans[k])
-    out, du = held
-    dmid, d_o, sent, kept = middle_back(
-        tab, frames, du, mid, cotangent[0], gains, o, full_out, block
-    )
-    flow.scatter("go", sent, kept)
-    d_o = step(d_o, ["g1", "g2", "g3", "go"])
+        if last:
+            dmid, (d_o, out_sent, out_kept) = held_du, more
+            flow.scatter("go", out_sent, out_kept)
+        else:
+            held = [out, step(held_du, plans[k])]
+    d_o = step(d_o, ["g0", "g1", "g2", "g3", "go"])
+    d_o = flow.until(d_o, ["g0"])
+    flow.own_rows("g0")
     calls = 4
     per = every // calls
     d_qkv = []
-    plans = [["g2", "g3", "go", "gq0"], ["g3", "go", "gq0", "gq1"], ["go", "gq0", "gq1", "gq2"]]
+    plans = [
+        ["g1", "g2", "g3", "go", "gq0"],
+        ["g2", "g3", "go", "gq0", "gq1"],
+        ["g3", "go", "gq0", "gq1", "gq2"],
+    ]
     for i in range(calls):
         group, at = divmod(i * per, pairs)
         d, sent, kept = attend_back(
@@ -991,30 +996,37 @@
         d_qkv.append(d)
         flow.scatter(f"gq{i}", sent, kept, True)
         if i < calls - 1:
-            d_o = step(d_o, plans[i])
-    dmid = step(dmid, ["gq1", "gq2", "gq3"])
+            d_o = step(d_o, plans[i], [f"g{i - 1}"] if i > 0 else [])
+        if i < 2:
+            d_o = flow.until(d_o, [f"g{i + 1}"])
+            flow.own_rows(f"g{i + 1}")
+        elif i == 2:
+            some = ["g3", "go", "gq0"]
+            d_o = flow.until(d_o, some)
+            flow.own_rows("joined", jnp.concatenate([flow.done[n] for n in some], axis=1))
+    dmid = step(dmid, ["gq1", "gq2", "gq3"], ["g2"])
+    dmid = flow.until(dmid, ["gq1"])
+    flow.own_rows("gq1")
     blocks = length // 256
     held_q = [flow.done["q0"], flow.done["q1"]]
     top = input_grad(tab, d_qkv, dmid, x, gains, held_q, block, 0, blocks // 2)
     top, dmid = step((top, dmid), ["gq2", "gq3"])
-    low = input_grad(tab, d_qkv, dmid, x, gains, held_q, block, blocks // 2, blocks)
-    low = step(low, ["gq3"])
+    grad_in = input_grad(tab, d_qkv, dmid, x, gains, held_q, block, blocks // 2, blocks, (top,))
+    grad_in = step(grad_in, ["gq3"], ["joined"])
     flow.until(None, list(flow.live))
-    grad_in = jnp.concatenate([top, low], axis=0)
-    own_rows = lambda n, direct=False: plan.own_rows(flow.done[n], direct)
-    mlp_shards = [own_rows(f"g{k}") for k in range(subs)]
-    out_shard = own_rows("go")
-    parts = [own_rows(f"gq{i}", i == calls - 1) for i in range(calls)]
-
     size = per * 3 * LANES
+    late_parts = [plan.own_rows(flow.done[f"gq{i}"], True) for i in range(2, calls)]
+    arrays = [flow.shards[n] for n in ("joined", "gq1", "g0", "g1", "g2")] + late_parts
+    views = [(0, 3 * D, size), (1, 0, size)] + [(5 + i, 0, size) for i in range(calls - 2)]
+    views += [(0, 2 * D, D)] + [(2 + k, 0, 2 * D) for k in range(subs - 1)] + [(0, 0, 2 * D)]
     weights = [qkv_low[:, i * size : (i + 1) * size] for i in range(calls)] + list(up_low)
-    sums, gain_shard = square_sums(parts, out_shard, mlp_shards, weights, norm_gains, ndev)
+    sums, gain_shard = square_sums(arrays, views, calls, weights, norm_gains, ndev)
     everyone = lax.all_to_all(sums, AXES, 0, 0)
     rates = (0.6 / D**0.5, 0.6 / FANO**0.5, 0.6 / D**0.5, 0.6 / FF**0.5, 1.0)
     decays = (0.1, 0.1, 0.1, 0.1, 0.0)
     states = [(masters[i], firsts[i], seconds[i], shadows[i]) for i in range(5)]
     updated, grad_norm = adam(
-        everyone, parts, out_shard, mlp_shards, gain_shard, states, rates, decays
+        everyone, arrays, views, calls, gain_shard, states, rates, decays
     )
     return (
         out[None],

time: 503 us -> 481 us (0.956)
  Pallas kernels: 309 us -> 275 us
  starting transfers between devices: 53.2 us -> 70 us
  blocking collectives: 19.2 us -> 29.3 us
  other arithmetic: 19.4 us -> 11.1 us
    pallas_call x4, Pallas kernels: 73 us -> 45.3 us  [attend_back(): pl.pallas_call(functools.partial(attend_back_kernel, 256, block), grid_sp...]
    ppermute x59, starting transfers between devices: 43.3 us -> 60.2 us  [step(): lax.ppermute(v, AXES, p)]
    all_to_all x0 -> x1, blocking collectives: none -> 10.1 us  [body(): everyone = lax.all_to_all(sums, AXES, 0, 0)]
    convert_element_type x5 -> x0, other arithmetic: 8.02 us -> none  [own_rows(): lax.psum_scatter(total, 'fsdp', scatter_dimension=0, tiled=True).astype(f32)]
    pallas_call x9 -> x8, Pallas kernels: 123 us -> 117 us  [the longest x4 87.8 us: feed_forward(): pl.pallas_call(functools.partial(mlp_kernel, [len(p) for p in pieces], bl...]
    unnamed x92 -> x84, local copies, waits for them, and re-layouts: 19.6 us -> 16.8 us
    pallas_call x22 -> x21, Pallas kernels: 55.6 us -> 54.4 us  [tie(): pl.pallas_call(functools.partial(tie_kernel, count, jobs), in_specs=[plac...]
  transfers between devices with their start and end apart: 73 -> 72, of which waited for: 11 -> 16; matrix products, arithmetic and copies ran while one was open for 4% -> 3% of each run, Pallas kernels for 60% -> 56%
where the time goes in v3:
time: 481 us; the launch traced here: 476 us
  Pallas kernels  275 us (57%)
  starting transfers between devices  70 us (15%)
  waiting for transfers between devices  51.7 us (11%)
  blocking collectives  29.3 us (6%)
  local copies, waits for them, and re-layouts  23.3 us (5%)
  between operations  16 us (3%)
  other arithmetic  11.1 us (2%)
    pallas_call x4, Pallas kernels, feed_forward(): pl.pallas_call(functools.partial(mlp_kernel, [len(p) for p in pieces], bl...  87.8 us
    ppermute x59, starting transfers between devices, step(): lax.ppermute(v, AXES, p)  60.2 us
    pallas_call x21, Pallas kernels, tie(): pl.pallas_call(functools.partial(tie_kernel, count, jobs), in_specs=[plac...  54.4 us
    ppermute x59, waiting for transfers between devices, step(): lax.ppermute(v, AXES, p)  47.3 us
    pallas_call x4, Pallas kernels, attend_back(): pl.pallas_call(functools.partial(attend_back_kernel, 256, block), grid_sp...  45.3 us
    pallas_call x2, Pallas kernels, attend(): pl.pallas_call(functools.partial(attend_kernel, 512), grid_spec=pltpu.Pre...  30.8 us
    pallas_call x2, Pallas kernels, input_grad(): pl.pallas_call(functools.partial(input_grad_kernel, groups, len(d), len(d...  20.6 us
    all_gather x1, blocking collectives, body(): reach = lambda v: lax.all_gather(v, 'fsdp', axis=0, tiled=True)  19.2 us
  transfers between devices with their start and end apart: 72, of which 16 were waited for; matrix products, arithmetic and copies ran while one was open for 3% of the time, Pallas kernels for 56%

profile of v3, /device:TPU:0, one launch (start us, length us, event | category | flops | bytes accessed | tf_op | source)
XLA Modules:
  0.0 476.1 jit_solution(13342942516845844536)
XLA Ops:
  13.8 19.2 %all_gather.9.refs_0_ = bf16[128,1664]{1,0:T(8,128)(2,1)} all-gather(bf16[32,1664]{1,0:T(8,128)(2,1)S(1)} %fusion.1), channel_id=1, replica_groups=mesh['dp'=8,'fsdp'=4] {'fsdp'}, dimensions={0}, use_global_device_ids=true | all-gather | bytes 532480 | tf_op jit(solution)/shard_map/all_gather | solution.py:938
  35.3 3.2 bitcast_select_fusion.refs_0_
  38.5 2.9 collective-permute-done.refs_2_
  46.5 10.6 %collective-permute-done.1.refs_0_ = bf16[256,1664]{1,0:T(8,128)(2,1)S(1)} collective-permute-done((bf16[256,1664]{1,0:T(8,128)(2,1)}, bf16[256,1664]{1,0:T(8,128)(2,1)S(1)}, u32[]{:S(2)}, u32[]{:S(2)}) %collective-permute-start.1) | collective-permute-done | bytes 852000 | tf_op jit(solution)/shard_map/ppermute | solution.py:253
  58.3 2.1 tie.25
  67.2 9.8 %qkv.2 = (bf16[1024,1536]{1,0:T(8,128)(2,1)}, bf16[1024,1024]{1,0:T(8,128)(2,1)}, f32[8,1024]{1,0:T(8,128)}, bf16[1024,1024]{1,0:T(8,128)(2,1)}) custom-call(s32[8]{0:T(128)} %fusion.2.tab, bf16[1024,1024]{1,0:T(8,128)(2,1)} %bitcast.31, bf16[256,1664]{1,0:T(8,128)(2,1)} %get-tuple-element.191.refs_1_.refs_5_.refs_4_, ...), custom_call_target="tpu_custom_call" | custom-call | flops 3221225472 | bytes 20971520 | tf_op jit(solution)/shard_map/qkv/pallas_call | solution.py:317
  77.6 2.2 tie.26
  82.0 15.3 %attend.2 = (bf16[1024,512]{1,0:T(8,128)(2,1)}, f32[4,2,1024]{2,1,0:T(2,128)}) custom-call(s32[1]{0:T(128)} %copy.159.n_ref, bf16[1024,1536]{1,0:T(8,128)(2,1)} %get-tuple-element.199.q_ref.k_ref.v_ref, bf16[1024,1536]{1,0:T(8,128)(2,1)} %get-tuple-element.199.q_ref.k_ref.v_ref, bf16[1024,1536]{1,0:T(8,128)(2,1)} %get-tuple-element.199.q_ref.k_ref.v_ref), custom_call_target="tpu_custom_call" | custom-call | flops 8589934592 | bytes 8388608 | tf_op jit(solution)/shard_map/attend/pallas_call | solution.py:389
  98.8 2.4 tie.27
  105.0 8.0 %qkv.3.refs_0_ = bf16[1024,1536]{1,0:T(8,128)(2,1)} custom-call(s32[8]{0:T(128)} %fusion.2.tab, bf16[1024,1024]{1,0:T(8,128)(2,1)} %get-tuple-element.208.refs_0_, bf16[256,1536]{1,0:T(8,128)(2,1)} %get-tuple-element.203.refs_1_.refs_8_.refs_9_, bf16[256,1536]{1,0:T(8,128)(2,1)} %get-tuple-element.207.refs_2_.refs_9_.refs_10_, ...), custom_call_target="tpu_custom_call" | custom-call | flops 3221225472 | bytes 20971520 | tf_op jit(solution)/shard_map/qkv/pallas_call | solution.py:317
  113.0 3.3 collective-permute-done.13.refs_4_
  116.3 2.4 tie.29
  121.4 15.5 %attend.3 = (bf16[1024,512]{1,0:T(8,128)(2,1)}, f32[4,2,1024]{2,1,0:T(2,128)}) custom-call(s32[1]{0:T(128)} %copy.159.n_ref, bf16[1024,1536]{1,0:T(8,128)(2,1)} %get-tuple-element.213.q_ref.k_ref.v_ref, bf16[1024,1536]{1,0:T(8,128)(2,1)} %get-tuple-element.213.q_ref.k_ref.v_ref, bf16[1024,1536]{1,0:T(8,128)(2,1)} %get-tuple-element.213.q_ref.k_ref.v_ref), custom_call_target="tpu_custom_call" | custom-call | flops 8589934592 | bytes 8388608 | tf_op jit(solution)/shard_map/attend/pallas_call | solution.py:389
  137.7 2.2 tie.30
  141.1 9.1 %middle.1 = (f32[1024,1024]{1,0:T(8,128)}, bf16[1024,1024]{1,0:T(8,128)(2,1)}, bf16[1024,1024]{1,0:T(8,128)(2,1)}) custom-call(s32[8]{0:T(128)} %fusion.2.tab, bf16[1024,1024]{1,0:T(8,128)(2,1)} %bitcast.32, f32[8,1024]{1,0:T(8,128)} %get-tuple-element.194.gain_ref.refs_10_, bf16[1024,512]{1,0:T(8,128)(2,1)} %get-tuple-element.217.refs_0_.refs_11_, ...), custom_call_target="tpu_custom_call" | custom-call | flops 2147483648 | bytes 16777216 | tf_op jit(solution)/shard_map/middle/pallas_call | solution.py:432
  154.4 19.9 %feed_forward.4 = (f32[1024,1024]{1,0:T(8,128)}, f32[1024,1024]{1,0:T(8,128)}, bf16[512,2048]{1,0:T(8,128)(2,1)}, bf16[512,2048]{1,0:T(8,128)(2,1)}) custom-call(s32[8]{0:T(128)} %fusion.2.tab, bf16[1024,1024]{1,0:T(8,128)(2,1)} %get-tuple-element.224.refs_0_, bf16[1024,1024]{1,0:T(8,128)(2,1)} %get-tuple-element.225.refs_1_, ...), custom_call_target="tpu_custom_call" | custom-call | flops 12884901888 | bytes 50331648 | tf_op jit(solution)/shard_map/feed_forward/pallas_call | solution.py:630
  176.0 2.2 tie.32
  180.2 20.3 %feed_forward.5 = (f32[1024,1024]{1,0:T(8,128)}, f32[1024,1024]{1,0:T(8,128)}, bf16[512,2048]{1,0:T(8,128)(2,1)}, bf16[512,2048]{1,0:T(8,128)(2,1)}) custom-call(s32[8]{0:T(128)} %fusion.2.tab, bf16[1024,1024]{1,0:T(8,128)(2,1)} %get-tuple-element.224.refs_0_, bf16[1024,1024]{1,0:T(8,128)(2,1)} %get-tuple-element.225.refs_1_, ...), custom_call_target="tpu_custom_call" | custom-call | flops 12884901888 | bytes 50331648 | tf_op jit(solution)/shard_map/feed_forward/pallas_call | solution.py:630
  201.1 3.4 tie.33
  205.2 20.1 %feed_forward.6 = (f32[1024,1024]{1,0:T(8,128)}, f32[1024,1024]{1,0:T(8,128)}, bf16[512,2048]{1,0:T(8,128)(2,1)}, bf16[512,2048]{1,0:T(8,128)(2,1)}) custom-call(s32[8]{0:T(128)} %fusion.2.tab, bf16[1024,1024]{1,0:T(8,128)(2,1)} %get-tuple-element.224.refs_0_, bf16[1024,1024]{1,0:T(8,128)(2,1)} %get-tuple-element.225.refs_1_, ...), custom_call_target="tpu_custom_call" | custom-call | flops 12884901888 | bytes 50331648 | tf_op jit(solution)/shard_map/feed_forward/pallas_call | solution.py:630
  226.4 4.5 tie.34
  233.5 27.5 %feed_forward.7 = (bf16[1024,1024]{1,0:T(8,128)(2,1)}, f32[1024,1024]{1,0:T(8,128)}, bf16[1024,1024]{1,0:T(8,128)(2,1)}, bf16[512,1024]{1,0:T(8,128)(2,1)}, bf16...) custom-call(s32[8]{0:T(128)} %fusion.2.tab, ...), custom_call_target="tpu_custom_call" | custom-call | flops 21474836480 | bytes 50331648 | tf_op jit(solution)/shard_map/feed_forward/pallas_call | solution.py:630
  262.2 5.2 %tie.35 = (bf16[1024,1024]{1,0:T(8,128)(2,1)}, f32[128,2048]{1,0:T(8,128)}, bf16[128,2048]{1,0:T(8,128)(2,1)}, bf16[128,2048]{1,0:T(8,128)(2,1)}, bf16[256,2048]{1,0:T(8,128)(2,1)}, /*index=5*/bf16[256,2048]{1,0:T(8,128)(2,1)}) custom-call(bf16[1024,1024]{1,0:T(8,128)(2,1)} %get-tuple-element.259.refs_0_, ...), custom_call_target="tpu_custom_call", output_to_operand_aliasing={{0}: (0, {})} | custom-call | tf_op jit(solution)/shard_map/tie/pallas_call | solution.py:198
  270.1 11.1 %attend_back.4 = (bf16[1024,768]{1,0:T(8,128)(2,1)}, f32[512,768]{1,0:T(8,128)}, f32[512,768]{1,0:T(8,128)}) custom-call(s32[1]{0:T(128)} %copy.159.n_ref, s32[8]{0:T(128)} %fusion.2.tab, bf16[1024,1536]{1,0:T(8,128)(2,1)} %get-tuple-element.199.q_ref.k_ref.v_ref, bf16[1024,1536]{1,0:T(8,128)(2,1)} %get-tuple-element.199.q_ref.k_ref.v_ref, ...), custom_call_target="tpu_custom_call" | custom-call | flops 10737418240 | bytes 16777216 | tf_op jit(solution)/shard_map/attend_back/pallas_call | solution.py:716
  281.2 3.5 collective-permute-done.34.refs_2_
  284.7 4.2 collective-permute-done.35.refs_4_
  288.9 5.9 %tie.36 = (bf16[1024,1024]{1,0:T(8,128)(2,1)}, f32[128,2048]{1,0:T(8,128)}, bf16[128,2048]{1,0:T(8,128)(2,1)}, bf16[128,2048]{1,0:T(8,128)(2,1)}, bf16[256,2048]...) custom-call(bf16[1024,1024]{1,0:T(8,128)(2,1)} %get-tuple-element.26, ...), custom_call_target="tpu_custom_call", output_to_operand_aliasing={{0}: (0, {})} | custom-call | tf_op jit(solution)/shard_map/tie/pallas_call | solution.py:198
  298.4 11.3 %attend_back.5 = (bf16[1024,768]{1,0:T(8,128)(2,1)}, f32[512,768]{1,0:T(8,128)}, f32[512,768]{1,0:T(8,128)}) custom-call(s32[1]{0:T(128)} %copy.159.n_ref, s32[8]{0:T(128)} %fusion.2.tab, bf16[1024,1536]{1,0:T(8,128)(2,1)} %get-tuple-element.199.q_ref.k_ref.v_ref, bf16[1024,1536]{1,0:T(8,128)(2,1)} %get-tuple-element.199.q_ref.k_ref.v_ref, ...), custom_call_target="tpu_custom_call" | custom-call | flops 10737418240 | bytes 16777216 | tf_op jit(solution)/shard_map/attend_back/pallas_call | solution.py:716
  309.7 2.4 collective-permute-done.38.refs_3_
  312.1 9.3 %collective-permute-done.40.refs_7_ = bf16[256,1024]{1,0:T(8,128)(2,1)} collective-permute-done((bf16[256,1024]{1,0:T(8,128)(2,1)}, bf16[256,1024]{1,0:T(8,128)(2,1)}, u32[]{:S(2)}, u32[]{:S(2)}) %collective-permute-start.40) | collective-permute-done | bytes 524320 | tf_op jit(solution)/shard_map/ppermute | solution.py:253
  322.5 5.1 %tie.37 = (bf16[1024,1024]{1,0:T(8,128)(2,1)}, f32[32,2048]{1,0:T(8,128)}, f32[128,2048]{1,0:T(8,128)}, bf16[128,2048]{1,0:T(8,128)(2,1)}, bf16[128,2048]{1,0:T(...) custom-call(bf16[1024,1024]{1,0:T(8,128)(2,1)} %get-tuple-element.27, ...), custom_call_target="tpu_custom_call", output_to_operand_aliasing={{0}: (0, {}), {1}: (1, {})} | custom-call | tf_op jit(solution)/shard_map/tie/pallas_call | solution.py:198
  335.2 11.5 %attend_back.6 = (bf16[1024,768]{1,0:T(8,128)(2,1)}, f32[512,768]{1,0:T(8,128)}, f32[512,768]{1,0:T(8,128)}) custom-call(s32[1]{0:T(128)} %copy.159.n_ref, s32[8]{0:T(128)} %fusion.2.tab, bf16[1024,1536]{1,0:T(8,128)(2,1)} %get-tuple-element.213.q_ref.k_ref.v_ref, bf16[1024,1536]{1,0:T(8,128)(2,1)} %get-tuple-element.213.q_ref.k_ref.v_ref, ...), custom_call_target="tpu_custom_call" | custom-call | flops 10737418240 | bytes 16777216 | tf_op jit(solution)/shard_map/attend_back/pallas_call | solution.py:716
  348.7 4.4 tie.38
  353.2 2.9 pad_maximum_fusion
  357.5 11.4 %attend_back.7 = (bf16[1024,768]{1,0:T(8,128)(2,1)}, f32[512,768]{1,0:T(8,128)}, f32[512,768]{1,0:T(8,128)}) custom-call(s32[1]{0:T(128)} %copy.159.n_ref, s32[8]{0:T(128)} %fusion.2.tab, bf16[1024,1536]{1,0:T(8,128)(2,1)} %get-tuple-element.213.q_ref.k_ref.v_ref, bf16[1024,1536]{1,0:T(8,128)(2,1)} %get-tuple-element.213.q_ref.k_ref.v_ref, ...), custom_call_target="tpu_custom_call" | custom-call | flops 10737418240 | bytes 16777216 | tf_op jit(solution)/shard_map/attend_back/pallas_call | solution.py:716
  368.8 12.8 %collective-permute-start.48 = (bf16[128,768]{1,0:T(8,128)(2,1)}, bf16[128,768]{1,0:T(8,128)(2,1)S(1)}, u32[]{:S(2)}, u32[]{:S(2)}) collective-permute-start(bf16[128,768]{1,0:T(8,128)(2,1)} %get-tuple-element.301), channel_id=1, source_target_pairs={{0,16},{1,17},{2,18},{3,19},{4,12},{5,13},{6,14},{7,15},{8,24},{9,... | collective-permute-start | bytes 589832 | tf_op jit(solution)/shard_map/ppermute | solution.py:253
  386.3 3.4 collective-permute-done.49.refs_4_
  389.7 3.1 collective-permute-done.50.refs_5_
  392.8 3.1 tie.39
  400.2 10.2 %input_grad.2.refs_0_ = f32[1024,1024]{1,0:T(8,128)} custom-call(s32[8]{0:T(128)} %fusion.2.tab, f32[1024,1024]{1,0:T(8,128)} %get-tuple-element.307.dmid_ref.refs_1_, bf16[1024,1024]{1,0:T(8,128)(2,1)} %bitcast.33, f32[8,1024]{1,0:T(8,128)} %get-tuple-element.194.gain_ref.refs_10_, bf16[1024,768]{1,0:T(8,128)(2,1)} %get-tuple-element.308.refs_0_.refs_1_, ...), custom_call_target="tpu_custom_call" | custom-call | flops 3221225472 | bytes 23068672 | tf_op jit(solution)/shard_map/input_grad/pallas_call | solution.py:775
  411.7 3.1 tie.40
  419.4 3.6 collective-permute-start.60
  423.0 10.4 %input_grad.3.refs_0_ = f32[1024,1024]{1,0:T(8,128)} custom-call(s32[8]{0:T(128)} %fusion.2.tab, f32[1024,1024]{1,0:T(8,128)} %get-tuple-element.319.dmid_ref, bf16[1024,1024]{1,0:T(8,128)(2,1)} %bitcast.34, f32[8,1024]{1,0:T(8,128)} %get-tuple-element.194.gain_ref.refs_10_, ...), custom_call_target="tpu_custom_call", output_to_operand_aliasing={{}: (4, {})} | custom-call | flops 3221225472 | bytes 23068672 | tf_op jit(solution)/shard_map/input_grad/pallas_call | solution.py:775
  438.2 3.6 collective-permute-start.63
  444.1 2.2 collective-permute-done.63
  449.8 2.5 square_sums.1
  452.4 10.1 %all_to_all.5.sums_ref = f32[32,1,128]{2,1,0:T(1,128)} all-to-all(f32[32,1,128]{2,1,0:T(1,128)} %get-tuple-element.336), channel_id=1, replica_groups=mesh['dp'=8,'fsdp'=4] {'dp','fsdp'}, dimensions={0} | all-to-all | bytes 32768 | tf_op jit(solution)/shard_map/all_to_all | solution.py:1024
  462.5 6.6 %adam.1 = (f32[32,3072]{1,0:T(8,128)}, f32[32,3072]{1,0:T(8,128)}, f32[32,3072]{1,0:T(8,128)}, f32[32,3072]{1,0:T(8,128)}, f32[32,1024]{1,0:T(8,128)}, /*index=5...) custom-call(f32[32,1,128]{2,1,0:T(1,128)} %all_to_all.5.sums_ref, ...), custom_call_target="tpu_custom_call" | custom-call | tf_op jit(solution)/shard_map/adam/pallas_call | solution.py:899
  (255 shorter events, 91.1 us)
Async XLA Ops:
  7.2 51.1 %all-gather.3.cloned.1.call-start = ((), (), s32[]{:S(2)}) async-start(), calls=%async_computation.6 | async-start | bytes 1474560 | tf_op jit(solution)/shard_map/all_gather | solution.py:938
  13.6 83.7 %all-gather.5.cloned.1.call-start = ((), (), s32[]{:S(2)}) async-start(), calls=%async_computation.7 | async-start | bytes 1966080 | tf_op jit(solution)/shard_map/all_gather | solution.py:938
  45.8 275.6 %reduce-scatter.6.cloned.1.call-start = ((), (), s32[]{:S(2)}) async-start(), calls=%async_computation.8 | async-start | bytes 1310720 | tf_op jit(solution)/shard_map/reduce_scatter | solution.py:114
  46.5 18.8 %collective-permute-start.2 = (bf16[256,1664]{1,0:T(8,128)(2,1)}, bf16[256,1664]{1,0:T(8,128)(2,1)S(1)}, u32[]{:S(2)}, u32[]{:S(2)}) collective-permute-start(bf16[256,1664]{1,0:T(8,128)(2,1)} %get-tuple-element.191.refs_1_.refs_5_.refs_4_), channel_id=1, source_target_pairs={{0,4},{1,5},{2,6},{3,7},{4,0},{5,1},{6,2},{7,3},{8,12},{9,13},{10,... | collective-permute-start | bytes 2555912 | tf_op jit(solution)/shard_map/ppermute | solution.py:253
  60.4 16.6 %collective-permute-start.4 = (bf16[128,1536]{1,0:T(8,128)(2,1)}, bf16[128,1536]{1,0:T(8,128)(2,1)}, u32[]{:S(2)}, u32[]{:S(2)}) collective-permute-start(bf16[128,1536]{1,0:T(8,128)(2,1)} %get-tuple-element.197.refs_2_), channel_id=1, source_target_pairs={{0,16},{1,17},{2,18},{3,19},{4,12},{5,13},{6,14},{7,15},{8,24},{9,... | collective-permute-start | bytes 1179656 | tf_op jit(solution)/shard_map/ppermute | solution.py:253
  63.7 33.6 %collective-permute-start.8 = (bf16[128,2048]{1,0:T(8,128)(2,1)}, bf16[128,2048]{1,0:T(8,128)(2,1)}, u32[]{:S(2)}, u32[]{:S(2)}) collective-permute-start(bf16[128,2048]{1,0:T(8,128)(2,1)} %get-tuple-element.204.refs_4_), channel_id=1, source_target_pairs={{0,16},{1,17},{2,18},{3,19},{4,12},{5,13},{6,14},{7,15},{8,24},{9,... | collective-permute-start | bytes 1572872 | tf_op jit(solution)/shard_map/ppermute | solution.py:253
  79.9 18.0 %collective-permute-start.7 = (bf16[256,1536]{1,0:T(8,128)(2,1)}, bf16[256,1536]{1,0:T(8,128)(2,1)S(1)}, u32[]{:S(2)}, u32[]{:S(2)}) collective-permute-start(bf16[256,1536]{1,0:T(8,128)(2,1)} %get-tuple-element.203.refs_1_.refs_8_.refs_9_), channel_id=1, source_target_pairs={{0,8},{1,9},{2,10},{3,11},{4,20},{5,21},{6,22},{7,23},{8,0},{9,1},... | collective-permute-start | bytes 2359304 | tf_op jit(solution)/shard_map/ppermute | solution.py:253
  81.5 21.3 %collective-permute-start.9 = (bf16[256,1536]{1,0:T(8,128)(2,1)}, bf16[256,1536]{1,0:T(8,128)(2,1)S(1)}, u32[]{:S(2)}, u32[]{:S(2)}) collective-permute-start(bf16[256,1536]{1,0:T(8,128)(2,1)} %get-tuple-element.203.refs_1_.refs_8_.refs_9_), channel_id=1, source_target_pairs={{0,4},{1,5},{2,6},{3,7},{4,0},{5,1},{6,2},{7,3},{8,12},{9,13},{10,... | collective-permute-start | bytes 2359304 | tf_op jit(solution)/shard_map/ppermute | solution.py:253
  81.5 16.4 %collective-permute-start.6 = (bf16[256,1024]{1,0:T(8,128)(2,1)}, bf16[256,1024]{1,0:T(8,128)(2,1)}, u32[]{:S(2)}, u32[]{:S(2)}) collective-permute-start(bf16[256,1024]{1,0:T(8,128)(2,1)} %get-tuple-element.202.refs_2_.refs_13_), channel_id=1, source_target_pairs={{0,8},{1,9},{2,10},{3,11},{4,20},{5,21},{6,22},{7,23},{8,0},{9,1},... | collective-permute-start | bytes 1572872 | tf_op jit(solution)/shard_map/ppermute | solution.py:253
  102.8 34.1 %collective-permute-start.14 = (bf16[256,2048]{1,0:T(8,128)(2,1)}, bf16[256,2048]{1,0:T(8,128)(2,1)}, u32[]{:S(2)}, u32[]{:S(2)}) collective-permute-start(bf16[256,2048]{1,0:T(8,128)(2,1)} %get-tuple-element.215.refs_3_), channel_id=1, source_target_pairs={{0,8},{1,9},{2,10},{3,11},{4,20},{5,21},{6,22},{7,23},{8,0},{9,1},... | collective-permute-start | bytes 3145736 | tf_op jit(solution)/shard_map/ppermute | solution.py:253
  104.1 46.1 %collective-permute-start.16 = (bf16[256,2048]{1,0:T(8,128)(2,1)}, bf16[256,2048]{1,0:T(8,128)(2,1)}, u32[]{:S(2)}, u32[]{:S(2)}) collective-permute-start(bf16[256,2048]{1,0:T(8,128)(2,1)} %get-tuple-element.215.refs_3_), channel_id=1, source_target_pairs={{0,4},{1,5},{2,6},{3,7},{4,0},{5,1},{6,2},{7,3},{8,12},{9,13},{10,... | collective-permute-start | bytes 3145736 | tf_op jit(solution)/shard_map/ppermute | solution.py:253
  118.7 18.2 %collective-permute-start.15 = (bf16[128,2048]{1,0:T(8,128)(2,1)}, bf16[128,2048]{1,0:T(8,128)(2,1)S(1)}, u32[]{:S(2)}, u32[]{:S(2)}) collective-permute-start(bf16[128,2048]{1,0:T(8,128)(2,1)} %get-tuple-element.216.refs_3_), channel_id=1, source_target_pairs={{0,16},{1,17},{2,18},{3,19},{4,12},{5,13},{6,14},{7,15},{8,24},{9,... | collective-permute-start | bytes 1572872 | tf_op jit(solution)/shard_map/ppermute | solution.py:253
  120.1 30.0 %collective-permute-start.18 = (bf16[256,2048]{1,0:T(8,128)(2,1)}, bf16[256,2048]{1,0:T(8,128)(2,1)S(1)}, u32[]{:S(2)}, u32[]{:S(2)}) collective-permute-start(bf16[256,2048]{1,0:T(8,128)(2,1)} %get-tuple-element.223.refs_3_), channel_id=1, source_target_pairs={{0,8},{1,9},{2,10},{3,11},{4,20},{5,21},{6,22},{7,23},{8,0},{9,1},... | collective-permute-start | bytes 3145736 | tf_op jit(solution)/shard_map/ppermute | solution.py:253
  140.0 34.8 %collective-permute-start.19 = (bf16[256,2048]{1,0:T(8,128)(2,1)}, bf16[256,2048]{1,0:T(8,128)(2,1)}, u32[]{:S(2)}, u32[]{:S(2)}) collective-permute-start(bf16[256,2048]{1,0:T(8,128)(2,1)} %get-tuple-element.223.refs_3_), channel_id=1, source_target_pairs={{0,4},{1,5},{2,6},{3,7},{4,0},{5,1},{6,2},{7,3},{8,12},{9,13},{10,... | collective-permute-start | bytes 3145736 | tf_op jit(solution)/shard_map/ppermute | solution.py:253
  140.5 34.4 %collective-permute-start.21 = (bf16[256,2048]{1,0:T(8,128)(2,1)}, bf16[256,2048]{1,0:T(8,128)(2,1)}, u32[]{:S(2)}, u32[]{:S(2)}) collective-permute-start(bf16[256,2048]{1,0:T(8,128)(2,1)} %get-tuple-element.232.refs_3_), channel_id=1, source_target_pairs={{0,8},{1,9},{2,10},{3,11},{4,20},{5,21},{6,22},{7,23},{8,0},{9,1},... | collective-permute-start | bytes 3145736 | tf_op jit(solution)/shard_map/ppermute | solution.py:253
  153.0 21.8 %collective-permute-start.20 = (bf16[256,2048]{1,0:T(8,128)(2,1)}, bf16[256,2048]{1,0:T(8,128)(2,1)S(1)}, u32[]{:S(2)}, u32[]{:S(2)}) collective-permute-start(bf16[256,2048]{1,0:T(8,128)(2,1)} %get-tuple-element.231.refs_4_), channel_id=1, source_target_pairs={{0,4},{1,5},{2,6},{3,7},{4,0},{5,1},{6,2},{7,3},{8,12},{9,13},{10,... | collective-permute-start | bytes 3145736 | tf_op jit(solution)/shard_map/ppermute | solution.py:253
  153.9 21.0 %collective-permute-start.22 = (bf16[128,2048]{1,0:T(8,128)(2,1)}, bf16[128,2048]{1,0:T(8,128)(2,1)S(1)}, u32[]{:S(2)}, u32[]{:S(2)}) collective-permute-start(bf16[128,2048]{1,0:T(8,128)(2,1)} %get-tuple-element.233.refs_4_), channel_id=1, source_target_pairs={{0,16},{1,17},{2,18},{3,19},{4,12},{5,13},{6,14},{7,15},{8,24},{9,... | collective-permute-start | bytes 1572872 | tf_op jit(solution)/shard_map/ppermute | solution.py:253
  174.3 26.8 %collective-permute-start.26 = (bf16[512,2048]{1,0:T(8,128)(2,1)}, bf16[512,2048]{1,0:T(8,128)(2,1)}, u32[]{:S(2)}, u32[]{:S(2)}) collective-permute-start(bf16[512,2048]{1,0:T(8,128)(2,1)} %get-tuple-element.242), channel_id=1, source_target_pairs={{0,4},{1,5},{2,6},{3,7},{4,0},{5,1},{6,2},{7,3},{8,12},{9,13},{10,... | collective-permute-start | bytes 6291464 | tf_op jit(solution)/shard_map/ppermute | solution.py:253
  174.7 25.8 %collective-permute-start.23 = (bf16[256,2048]{1,0:T(8,128)(2,1)}, bf16[256,2048]{1,0:T(8,128)(2,1)}, u32[]{:S(2)}, u32[]{:S(2)}) collective-permute-start(bf16[256,2048]{1,0:T(8,128)(2,1)} %get-tuple-element.232.refs_3_), channel_id=1, source_target_pairs={{0,4},{1,5},{2,6},{3,7},{4,0},{5,1},{6,2},{7,3},{8,12},{9,13},{10,... | collective-permute-start | bytes 3145736 | tf_op jit(solution)/shard_map/ppermute | solution.py:253
  178.2 22.9 %collective-permute-start.24 = (bf16[256,2048]{1,0:T(8,128)(2,1)}, bf16[256,2048]{1,0:T(8,128)(2,1)}, u32[]{:S(2)}, u32[]{:S(2)}) collective-permute-start(bf16[256,2048]{1,0:T(8,128)(2,1)} %get-tuple-element.240.refs_4_), channel_id=1, source_target_pairs={{0,4},{1,5},{2,6},{3,7},{4,0},{5,1},{6,2},{7,3},{8,12},{9,13},{10,... | collective-permute-start | bytes 3145736 | tf_op jit(solution)/shard_map/ppermute | solution.py:253
  178.7 22.4 %collective-permute-start.25 = (bf16[256,2048]{1,0:T(8,128)(2,1)}, bf16[256,2048]{1,0:T(8,128)(2,1)}, u32[]{:S(2)}, u32[]{:S(2)}) collective-permute-start(bf16[256,2048]{1,0:T(8,128)(2,1)} %get-tuple-element.234.refs_3_), channel_id=1, source_target_pairs={{0,8},{1,9},{2,10},{3,11},{4,20},{5,21},{6,22},{7,23},{8,0},{9,1},... | collective-permute-start | bytes 3145736 | tf_op jit(solution)/shard_map/ppermute | solution.py:253
  200.5 25.0 %collective-permute-start.30 = (bf16[512,2048]{1,0:T(8,128)(2,1)}, bf16[512,2048]{1,0:T(8,128)(2,1)}, u32[]{:S(2)}, u32[]{:S(2)}) collective-permute-start(bf16[512,2048]{1,0:T(8,128)(2,1)} %get-tuple-element.252), channel_id=1, source_target_pairs={{0,4},{1,5},{2,6},{3,7},{4,0},{5,1},{6,2},{7,3},{8,12},{9,13},{10,... | collective-permute-start | bytes 6291464 | tf_op jit(solution)/shard_map/ppermute | solution.py:253
  200.6 24.9 %collective-permute-start.27 = (bf16[256,2048]{1,0:T(8,128)(2,1)}, bf16[256,2048]{1,0:T(8,128)(2,1)S(1)}, u32[]{:S(2)}, u32[]{:S(2)}) collective-permute-start(bf16[256,2048]{1,0:T(8,128)(2,1)} %get-tuple-element.234.refs_3_), channel_id=1, source_target_pairs={{0,4},{1,5},{2,6},{3,7},{4,0},{5,1},{6,2},{7,3},{8,12},{9,13},{10,... | collective-permute-start | bytes 3145736 | tf_op jit(solution)/shard_map/ppermute | solution.py:253
  204.5 20.9 %collective-permute-start.28 = (bf16[256,2048]{1,0:T(8,128)(2,1)}, bf16[256,2048]{1,0:T(8,128)(2,1)}, u32[]{:S(2)}, u32[]{:S(2)}) collective-permute-start(bf16[256,2048]{1,0:T(8,128)(2,1)} %get-tuple-element.243.refs_4_), channel_id=1, source_target_pairs={{0,4},{1,5},{2,6},{3,7},{4,0},{5,1},{6,2},{7,3},{8,12},{9,13},{10,... | collective-permute-start | bytes 3145736 | tf_op jit(solution)/shard_map/ppermute | solution.py:253
  204.7 20.8 %collective-permute-start.29 = (bf16[256,2048]{1,0:T(8,128)(2,1)}, bf16[256,2048]{1,0:T(8,128)(2,1)}, u32[]{:S(2)}, u32[]{:S(2)}) collective-permute-start(bf16[256,2048]{1,0:T(8,128)(2,1)} %get-tuple-element.250), channel_id=1, source_target_pairs={{0,8},{1,9},{2,10},{3,11},{4,20},{5,21},{6,22},{7,23},{8,0},{9,1},... | collective-permute-start | bytes 3145736 | tf_op jit(solution)/shard_map/ppermute | solution.py:253
  225.3 35.8 %collective-permute-start.33 = (bf16[512,2048]{1,0:T(8,128)(2,1)}, bf16[512,2048]{1,0:T(8,128)(2,1)}, u32[]{:S(2)}, u32[]{:S(2)}) collective-permute-start(bf16[512,2048]{1,0:T(8,128)(2,1)} %get-tuple-element.265), channel_id=1, source_target_pairs={{0,4},{1,5},{2,6},{3,7},{4,0},{5,1},{6,2},{7,3},{8,12},{9,13},{10,... | collective-permute-start | bytes 6291464 | tf_op jit(solution)/shard_map/ppermute | solution.py:253
  231.0 30.1 %collective-permute-start.32 = (bf16[256,2048]{1,0:T(8,128)(2,1)}, bf16[256,2048]{1,0:T(8,128)(2,1)S(1)}, u32[]{:S(2)}, u32[]{:S(2)}) collective-permute-start(bf16[256,2048]{1,0:T(8,128)(2,1)} %get-tuple-element.263), channel_id=1, source_target_pairs={{0,8},{1,9},{2,10},{3,11},{4,20},{5,21},{6,22},{7,23},{8,0},{9,1},... | collective-permute-start | bytes 3145736 | tf_op jit(solution)/shard_map/ppermute | solution.py:253
  233.1 28.0 %collective-permute-start.31 = (bf16[128,2048]{1,0:T(8,128)(2,1)}, bf16[128,2048]{1,0:T(8,128)(2,1)S(1)}, u32[]{:S(2)}, u32[]{:S(2)}) collective-permute-start(bf16[128,2048]{1,0:T(8,128)(2,1)} %get-tuple-element.261), channel_id=1, source_target_pairs={{0,16},{1,17},{2,18},{3,19},{4,12},{5,13},{6,14},{7,15},{8,24},{9,... | collective-permute-start | bytes 1572872 | tf_op jit(solution)/shard_map/ppermute | solution.py:253
  261.0 27.8 %collective-permute-start.36 = (bf16[512,2048]{1,0:T(8,128)(2,1)}, bf16[512,2048]{1,0:T(8,128)(2,1)}, u32[]{:S(2)}, u32[]{:S(2)}) collective-permute-start(bf16[512,2048]{1,0:T(8,128)(2,1)} %get-tuple-element.272), channel_id=1, source_target_pairs={{0,4},{1,5},{2,6},{3,7},{4,0},{5,1},{6,2},{7,3},{8,12},{9,13},{10,... | collective-permute-start | bytes 6291464 | tf_op jit(solution)/shard_map/ppermute | solution.py:253
  267.5 80.0 %reduce-scatter.10.cloned.1.call-start = ((), (), s32[]{:S(2)}) async-start(), calls=%async_computation.10 | async-start | bytes 1310720 | tf_op jit(solution)/shard_map/reduce_scatter | solution.py:114
  268.1 20.7 %collective-permute-start.35 = (bf16[256,2048]{1,0:T(8,128)(2,1)}, bf16[256,2048]{1,0:T(8,128)(2,1)}, u32[]{:S(2)}, u32[]{:S(2)}) collective-permute-start(bf16[256,2048]{1,0:T(8,128)(2,1)} %get-tuple-element.270), channel_id=1, source_target_pairs={{0,8},{1,9},{2,10},{3,11},{4,20},{5,21},{6,22},{7,23},{8,0},{9,1},... | collective-permute-start | bytes 3145736 | tf_op jit(solution)/shard_map/ppermute | solution.py:253
  294.8 98.0 %reduce-scatter.8.cloned.1.call-start = ((), (), s32[]{:S(2)}) async-start(), calls=%async_computation.9 | async-start | bytes 1310720 | tf_op jit(solution)/shard_map/reduce_scatter | solution.py:114
  294.9 26.5 %collective-permute-start.41 = (f32[512,768]{1,0:T(8,128)}, f32[512,768]{1,0:T(8,128)S(1)}, u32[]{:S(2)}, u32[]{:S(2)}) collective-permute-start(f32[512,768]{1,0:T(8,128)} %get-tuple-element.286), channel_id=1, source_target_pairs={{0,4},{1,5},{2,6},{3,7},{4,0},{5,1},{6,2},{7,3},{8,12},{9,13},{10,... | collective-permute-start | bytes 4718600 | tf_op jit(solution)/shard_map/ppermute | solution.py:253
  295.0 26.4 %collective-permute-start.39 = (bf16[256,2048]{1,0:T(8,128)(2,1)}, bf16[256,2048]{1,0:T(8,128)(2,1)}, u32[]{:S(2)}, u32[]{:S(2)}) collective-permute-start(bf16[256,2048]{1,0:T(8,128)(2,1)} %get-tuple-element.280), channel_id=1, source_target_pairs={{0,8},{1,9},{2,10},{3,11},{4,20},{5,21},{6,22},{7,23},{8,0},{9,1},... | collective-permute-start | bytes 3145736 | tf_op jit(solution)/shard_map/ppermute | solution.py:253
  297.0 24.4 %collective-permute-start.40 = (bf16[256,1024]{1,0:T(8,128)(2,1)}, bf16[256,1024]{1,0:T(8,128)(2,1)}, u32[]{:S(2)}, u32[]{:S(2)}) collective-permute-start(bf16[256,1024]{1,0:T(8,128)(2,1)} %get-tuple-element.282), channel_id=1, source_target_pairs={{0,8},{1,9},{2,10},{3,11},{4,20},{5,21},{6,22},{7,23},{8,0},{9,1},... | collective-permute-start | bytes 1572872 | tf_op jit(solution)/shard_map/ppermute | solution.py:253
  327.7 106.6 %reduce-scatter.12.cloned.1.call-start = ((), (), s32[]{:S(2)}) async-start(), calls=%async_computation.11 | async-start | bytes 2457600 | tf_op jit(solution)/shard_map/reduce_scatter | solution.py:114
  327.7 19.8 %collective-permute-start.47 = (f32[512,768]{1,0:T(8,128)}, f32[512,768]{1,0:T(8,128)S(1)}, u32[]{:S(2)}, u32[]{:S(2)}) collective-permute-start(f32[512,768]{1,0:T(8,128)} %get-tuple-element.299), channel_id=1, source_target_pairs={{0,4},{1,5},{2,6},{3,7},{4,0},{5,1},{6,2},{7,3},{8,12},{9,13},{10,... | collective-permute-start | bytes 4718600 | tf_op jit(solution)/shard_map/ppermute | solution.py:253
  329.2 18.3 %collective-permute-start.42 = (bf16[128,2048]{1,0:T(8,128)(2,1)}, bf16[128,2048]{1,0:T(8,128)(2,1)}, u32[]{:S(2)}, u32[]{:S(2)}) collective-permute-start(bf16[128,2048]{1,0:T(8,128)(2,1)} %get-tuple-element.291), channel_id=1, source_target_pairs={{0,16},{1,17},{2,18},{3,19},{4,12},{5,13},{6,14},{7,15},{8,24},{9,... | collective-permute-start | bytes 1572872 | tf_op jit(solution)/shard_map/ppermute | solution.py:253
  329.9 17.6 %collective-permute-start.43 = (bf16[128,1024]{1,0:T(8,128)(2,1)}, bf16[128,1024]{1,0:T(8,128)(2,1)S(1)}, u32[]{:S(2)}, u32[]{:S(2)}) collective-permute-start(bf16[128,1024]{1,0:T(8,128)(2,1)} %get-tuple-element.293), channel_id=1, source_target_pairs={{0,16},{1,17},{2,18},{3,19},{4,12},{5,13},{6,14},{7,15},{8,24},{9,... | collective-permute-start | bytes 786440 | tf_op jit(solution)/shard_map/ppermute | solution.py:253
  356.2 93.7 %reduce-scatter.14.cloned.1.call-start = ((), (), s32[]{:S(2)}) async-start(), calls=%async_computation.12 | async-start | bytes 491520 | tf_op jit(solution)/shard_map/reduce_scatter | solution.py:114
  356.2 36.6 %collective-permute-start.51 = (f32[512,768]{1,0:T(8,128)}, f32[512,768]{1,0:T(8,128)}, u32[]{:S(2)}, u32[]{:S(2)}) collective-permute-start(f32[512,768]{1,0:T(8,128)} %get-tuple-element.306), channel_id=1, source_target_pairs={{0,4},{1,5},{2,6},{3,7},{4,0},{5,1},{6,2},{7,3},{8,12},{9,13},{10,... | collective-permute-start | bytes 4718600 | tf_op jit(solution)/shard_map/ppermute | solution.py:253
  368.8 41.7 %collective-permute-start.55 = (f32[512,768]{1,0:T(8,128)}, f32[512,768]{1,0:T(8,128)S(1)}, u32[]{:S(2)}, u32[]{:S(2)}) collective-permute-start(f32[512,768]{1,0:T(8,128)} %get-tuple-element.318), channel_id=1, source_target_pairs={{0,4},{1,5},{2,6},{3,7},{4,0},{5,1},{6,2},{7,3},{8,12},{9,13},{10,... | collective-permute-start | bytes 4718600 | tf_op jit(solution)/shard_map/ppermute | solution.py:253
  368.8 17.5 %collective-permute-start.48 = (bf16[128,768]{1,0:T(8,128)(2,1)}, bf16[128,768]{1,0:T(8,128)(2,1)S(1)}, u32[]{:S(2)}, u32[]{:S(2)}) collective-permute-start(bf16[128,768]{1,0:T(8,128)(2,1)} %get-tuple-element.301), channel_id=1, source_target_pairs={{0,16},{1,17},{2,18},{3,19},{4,12},{5,13},{6,14},{7,15},{8,24},{9,... | collective-permute-start | bytes 589832 | tf_op jit(solution)/shard_map/ppermute | solution.py:253
  414.8 18.6 %collective-permute-start.56 = (bf16[128,768]{1,0:T(8,128)(2,1)}, bf16[128,768]{1,0:T(8,128)(2,1)S(1)}, u32[]{:S(2)}, u32[]{:S(2)}) collective-permute-start(bf16[128,768]{1,0:T(8,128)(2,1)} %get-tuple-element.325), channel_id=1, source_target_pairs={{0,16},{1,17},{2,18},{3,19},{4,12},{5,13},{6,14},{7,15},{8,24},{9,... | collective-permute-start | bytes 589832 | tf_op jit(solution)/shard_map/ppermute | solution.py:253
  416.0 18.3 %collective-permute-start.57 = (bf16[128,768]{1,0:T(8,128)(2,1)}, bf16[128,768]{1,0:T(8,128)(2,1)S(1)}, u32[]{:S(2)}, u32[]{:S(2)}) collective-permute-start(bf16[128,768]{1,0:T(8,128)(2,1)} %get-tuple-element.326), channel_id=1, source_target_pairs={{0,8},{1,9},{2,10},{3,11},{4,20},{5,21},{6,22},{7,23},{8,0},{9,1},... | collective-permute-start | bytes 589832 | tf_op jit(solution)/shard_map/ppermute | solution.py:253
  417.8 16.5 %collective-permute-start.58 = (bf16[128,768]{1,0:T(8,128)(2,1)}, bf16[128,768]{1,0:T(8,128)(2,1)S(1)}, u32[]{:S(2)}, u32[]{:S(2)}) collective-permute-start(bf16[128,768]{1,0:T(8,128)(2,1)} %get-tuple-element.327), channel_id=1, source_target_pairs={{0,24},{1,25},{2,26},{3,27},{4,28},{5,29},{6,30},{7,31},{8,16},{9,... | collective-permute-start | bytes 589832 | tf_op jit(solution)/shard_map/ppermute | solution.py:253
  419.4 22.4 %collective-permute-start.59 = (f32[32,768]{1,0:T(8,128)S(1)}, f32[32,768]{1,0:T(8,128)S(1)}, u32[]{:S(2)}, u32[]{:S(2)}) collective-permute-start(f32[32,768]{1,0:T(8,128)S(1)} %get-tuple-element.366), channel_id=1, source_target_pairs={{0,1},{1,0},{2,3},{3,2},{4,5},{5,4},{6,7},{7,6},{8,9},{9,8},{10,11... | collective-permute-start | bytes 294920 | tf_op jit(solution)/shard_map/ppermute | solution.py:120
  419.4 23.1 %collective-permute-start.60 = (f32[32,768]{1,0:T(8,128)S(1)}, f32[32,768]{1,0:T(8,128)S(1)}, u32[]{:S(2)}, u32[]{:S(2)}) collective-permute-start(f32[32,768]{1,0:T(8,128)S(1)} %get-tuple-element.368), channel_id=1, source_target_pairs={{0,2},{1,3},{2,0},{3,1},{4,6},{5,7},{6,4},{7,5},{8,10},{9,11},{10,... | collective-permute-start | bytes 294920 | tf_op jit(solution)/shard_map/ppermute | solution.py:120
  (63 other events, 399.1 us)
Sparse Core Ops, SparseCore 0:
  13.7 35.2 all-gather.2
  51.1 35.9 all-gather.4
  267.6 27.2 reduce-scatter.5
  297.2 25.7 reduce-scatter.9
  327.8 27.0 reduce-scatter.7
  357.1 45.7 reduce-scatter.11
  405.9 20.4 reduce-scatter.13

commit v4 on v3

--- a/solution.py
+++ b/solution.py
@@ -24,7 +24,7 @@
 AXES = ("dp", "fsdp")
 GROUPS = 2
 LANES = 128
-VMEM = 62 << 20
+VMEM = (64 << 20) - (256 << 10)
 f32 = jnp.float32
 bf16 = jnp.bfloat16
 NT = (((1,), (1,)), ((), ()))
@@ -477,7 +477,7 @@
         o_hbm, w_hbm = take(outs[0]), take(outs[1])
     (out_hbm,) = take(1)
     if last:
-        dmid_hbm, do_hbm, out_sent, out_kept = take(4)
+        dmid_hbm, do_hbm = take(2)
     else:
         (du_hbm,) = take(1)
     sent, kept = take(2)
@@ -602,7 +602,7 @@
         wait(waiting)
         turned = lax.dot_general(a_s[...], u[...], TN, preferred_element_type=f32)
         grad[:, 0:width] = turned.astype(bf16)
-        waiting = back(width, out_sent, out_kept, 0)
+        waiting = back(width, sent, kept, 2 * subs * width)
         start(waiting)
     wait(waiting + saved)
 
@@ -620,11 +620,11 @@
     if last:
         mid, gains, o, w_out = last
         inputs += [mid, gains, *o, *w_out]
-        outputs = [low, acc, low, shard(width), shard(width)]
+        outputs = [low, acc, low]
         outs = (len(o), len(w_out))
     else:
         outputs = [acc, acc]
-    outputs += [shard(2 * width * len(pieces))] * 2
+    outputs += [shard(2 * width * len(pieces) + (width if last else 0))] * 2
     blocks = width // block
     subs = len(pieces)
     return pl.pallas_call(
@@ -973,20 +973,19 @@
         )
         flow.scatter(f"g{k}", sent, kept)
         if last:
-            dmid, (d_o, out_sent, out_kept) = held_du, more
-            flow.scatter("go", out_sent, out_kept)
+            dmid, (d_o,) = held_du, more
         else:
             held = [out, step(held_du, plans[k])]
-    d_o = step(d_o, ["g0", "g1", "g2", "g3", "go"])
+    d_o = step(d_o, ["g0", "g1", "g2", "g3"])
     d_o = flow.until(d_o, ["g0"])
     flow.own_rows("g0")
     calls = 4
     per = every // calls
     d_qkv = []
     plans = [
-        ["g1", "g2", "g3", "go", "gq0"],
-        ["g2", "g3", "go", "gq0", "gq1"],
-        ["g3", "go", "gq0", "gq1", "gq2"],
+        ["g1", "g2", "g3", "gq0"],
+        ["g2", "g3", "gq0", "gq1"],
+        ["g3", "gq0", "gq1", "gq2"],
     ]
     for i in range(calls):
         group, at = divmod(i * per, pairs)
@@ -1001,7 +1000,7 @@
             d_o = flow.until(d_o, [f"g{i + 1}"])
             flow.own_rows(f"g{i + 1}")
         elif i == 2:
-            some = ["g3", "go", "gq0"]
+            some = ["g3", "gq0"]
             d_o = flow.until(d_o, some)
             flow.own_rows("joined", jnp.concatenate([flow.done[n] for n in some], axis=1))
     dmid = step(dmid, ["gq1", "gq2", "gq3"], ["g2"])

time: 481 us -> 473 us (0.983)
  local copies, waits for them, and re-layouts: 23.3 us -> 10.7 us
  Pallas kernels: 275 us -> 287 us
  starting transfers between devices: 70 us -> 60.9 us
    unnamed x84 -> x34, local copies, waits for them, and re-layouts: 16.8 us -> 3.53 us
    pallas_call x4, Pallas kernels: 45.3 us -> 57.7 us  [attend_back(): pl.pallas_call(functools.partial(attend_back_kernel, 256, block), grid_sp...]
    ppermute x59 -> x56, starting transfers between devices: 60.2 us -> 51.1 us  [step(): lax.ppermute(v, AXES, p)]
    ppermute x59 -> x56, waiting for transfers between devices: 47.3 us -> 49.2 us  [step(): lax.ppermute(v, AXES, p)]
  transfers between devices with their start and end apart: 72 -> 69, of which waited for: 16 -> 15; matrix products, arithmetic and copies ran while one was open for 3% -> 3% of each run, Pallas kernels for 56% -> 59%
where the time goes in v4:
time: 473 us; the launch traced here: 469 us
  Pallas kernels  287 us (61%)
  starting transfers between devices  60.9 us (13%)
  waiting for transfers between devices  53.7 us (11%)
  blocking collectives  29.5 us (6%)
  between operations  16.2 us (3%)
  other arithmetic  11.3 us (2%)
  local copies, waits for them, and re-layouts  10.7 us (2%)
    pallas_call x4, Pallas kernels, feed_forward(): pl.pallas_call(functools.partial(mlp_kernel, [len(p) for p in pieces], bl...  87.9 us
    pallas_call x4, Pallas kernels, attend_back(): pl.pallas_call(functools.partial(attend_back_kernel, 256, block), grid_sp...  57.7 us
    pallas_call x21, Pallas kernels, tie(): pl.pallas_call(functools.partial(tie_kernel, count, jobs), in_specs=[plac...  54.6 us
    ppermute x56, starting transfers between devices, step(): lax.ppermute(v, AXES, p)  51.1 us
    ppermute x56, waiting for transfers between devices, step(): lax.ppermute(v, AXES, p)  49.2 us
    pallas_call x2, Pallas kernels, attend(): pl.pallas_call(functools.partial(attend_kernel, 512), grid_spec=pltpu.Pre...  30.5 us
    pallas_call x2, Pallas kernels, input_grad(): pl.pallas_call(functools.partial(input_grad_kernel, groups, len(d), len(d...  20.6 us
    all_gather x1, blocking collectives, body(): reach = lambda v: lax.all_gather(v, 'fsdp', axis=0, tiled=True)  19.2 us
  transfers between devices with their start and end apart: 69, of which 15 were waited for; matrix products, arithmetic and copies ran while one was open for 3% of the time, Pallas kernels for 59%

profile of v4, /device:TPU:0, one launch (start us, length us, event | category | flops | bytes accessed | tf_op | source)
XLA Modules:
  0.0 469.3 jit_solution(16044147171572197621)
XLA Ops:
  13.8 19.2 %all_gather.9.refs_0_ = bf16[128,1664]{1,0:T(8,128)(2,1)} all-gather(bf16[32,1664]{1,0:T(8,128)(2,1)S(1)} %fusion.1), channel_id=1, replica_groups=mesh['dp'=8,'fsdp'=4] {'fsdp'}, dimensions={0}, use_global_device_ids=true | all-gather | bytes 532480 | tf_op jit(solution)/shard_map/all_gather | solution.py:938
  35.3 3.1 bitcast_select_fusion.refs_0_
  38.4 3.1 collective-permute-done.refs_2_
  41.5 2.1 tie.22
  45.9 10.8 %collective-permute-done.1.refs_0_ = bf16[256,1664]{1,0:T(8,128)(2,1)} collective-permute-done((bf16[256,1664]{1,0:T(8,128)(2,1)}, bf16[256,1664]{1,0:T(8,128)(2,1)}, u32[]{:S(2)}, u32[]{:S(2)}) %collective-permute-start.1) | collective-permute-done | bytes 852000 | tf_op jit(solution)/shard_map/ppermute | solution.py:253
  56.8 2.2 tie.25
  63.9 9.7 %qkv.2 = (bf16[1024,1536]{1,0:T(8,128)(2,1)}, bf16[1024,1024]{1,0:T(8,128)(2,1)}, f32[8,1024]{1,0:T(8,128)}, bf16[1024,1024]{1,0:T(8,128)(2,1)}) custom-call(s32[8]{0:T(128)} %fusion.2.tab, bf16[1024,1024]{1,0:T(8,128)(2,1)} %bitcast.31, bf16[256,1664]{1,0:T(8,128)(2,1)} %get-tuple-element.184.refs_1_.refs_5_.refs_4_, ...), custom_call_target="tpu_custom_call" | custom-call | flops 3221225472 | bytes 20971520 | tf_op jit(solution)/shard_map/qkv/pallas_call | solution.py:317
  73.6 2.2 tie.26
  78.0 15.2 %attend.2 = (bf16[1024,512]{1,0:T(8,128)(2,1)}, f32[4,2,1024]{2,1,0:T(2,128)}) custom-call(s32[1]{0:T(128)} %copy.159.n_ref, bf16[1024,1536]{1,0:T(8,128)(2,1)} %get-tuple-element.192.q_ref.k_ref.v_ref, bf16[1024,1536]{1,0:T(8,128)(2,1)} %get-tuple-element.192.q_ref.k_ref.v_ref, bf16[1024,1536]{1,0:T(8,128)(2,1)} %get-tuple-element.192.q_ref.k_ref.v_ref), custom_call_target="tpu_custom_call" | custom-call | flops 8589934592 | bytes 8388608 | tf_op jit(solution)/shard_map/attend/pallas_call | solution.py:389
  93.9 2.4 tie.27
  99.1 8.0 %qkv.3.refs_0_ = bf16[1024,1536]{1,0:T(8,128)(2,1)} custom-call(s32[8]{0:T(128)} %fusion.2.tab, bf16[1024,1024]{1,0:T(8,128)(2,1)} %get-tuple-element.201.refs_0_, bf16[256,1536]{1,0:T(8,128)(2,1)} %get-tuple-element.196.refs_1_.refs_8_.refs_9_, bf16[256,1536]{1,0:T(8,128)(2,1)} %get-tuple-element.200.refs_2_.refs_9_.refs_10_, ...), custom_call_target="tpu_custom_call" | custom-call | flops 3221225472 | bytes 20971520 | tf_op jit(solution)/shard_map/qkv/pallas_call | solution.py:317
  107.1 4.3 collective-permute-done.13.refs_4_
  111.4 2.4 tie.29
  116.4 15.3 %attend.3 = (bf16[1024,512]{1,0:T(8,128)(2,1)}, f32[4,2,1024]{2,1,0:T(2,128)}) custom-call(s32[1]{0:T(128)} %copy.159.n_ref, bf16[1024,1536]{1,0:T(8,128)(2,1)} %get-tuple-element.206.q_ref.k_ref.v_ref, bf16[1024,1536]{1,0:T(8,128)(2,1)} %get-tuple-element.206.q_ref.k_ref.v_ref, bf16[1024,1536]{1,0:T(8,128)(2,1)} %get-tuple-element.206.q_ref.k_ref.v_ref), custom_call_target="tpu_custom_call" | custom-call | flops 8589934592 | bytes 8388608 | tf_op jit(solution)/shard_map/attend/pallas_call | solution.py:389
  131.8 2.2 tie.30
  134.7 9.1 %middle.1 = (f32[1024,1024]{1,0:T(8,128)}, bf16[1024,1024]{1,0:T(8,128)(2,1)}, bf16[1024,1024]{1,0:T(8,128)(2,1)}) custom-call(s32[8]{0:T(128)} %fusion.2.tab, bf16[1024,1024]{1,0:T(8,128)(2,1)} %bitcast.32, f32[8,1024]{1,0:T(8,128)} %get-tuple-element.187.gain_ref.refs_10_, bf16[1024,512]{1,0:T(8,128)(2,1)} %get-tuple-element.210.refs_0_.refs_11_, ...), custom_call_target="tpu_custom_call" | custom-call | flops 2147483648 | bytes 16777216 | tf_op jit(solution)/shard_map/middle/pallas_call | solution.py:432
  147.5 19.9 %feed_forward.4 = (f32[1024,1024]{1,0:T(8,128)}, f32[1024,1024]{1,0:T(8,128)}, bf16[512,2048]{1,0:T(8,128)(2,1)}, bf16[512,2048]{1,0:T(8,128)(2,1)}) custom-call(s32[8]{0:T(128)} %fusion.2.tab, bf16[1024,1024]{1,0:T(8,128)(2,1)} %get-tuple-element.217.refs_0_, bf16[1024,1024]{1,0:T(8,128)(2,1)} %get-tuple-element.218.refs_1_, ...), custom_call_target="tpu_custom_call" | custom-call | flops 12884901888 | bytes 50331648 | tf_op jit(solution)/shard_map/feed_forward/pallas_call | solution.py:630
  168.0 2.2 tie.32
  172.2 20.3 %feed_forward.5 = (f32[1024,1024]{1,0:T(8,128)}, f32[1024,1024]{1,0:T(8,128)}, bf16[512,2048]{1,0:T(8,128)(2,1)}, bf16[512,2048]{1,0:T(8,128)(2,1)}) custom-call(s32[8]{0:T(128)} %fusion.2.tab, bf16[1024,1024]{1,0:T(8,128)(2,1)} %get-tuple-element.217.refs_0_, bf16[1024,1024]{1,0:T(8,128)(2,1)} %get-tuple-element.218.refs_1_, ...), custom_call_target="tpu_custom_call" | custom-call | flops 12884901888 | bytes 50331648 | tf_op jit(solution)/shard_map/feed_forward/pallas_call | solution.py:630
  193.1 3.4 tie.33
  197.2 20.1 %feed_forward.6 = (f32[1024,1024]{1,0:T(8,128)}, f32[1024,1024]{1,0:T(8,128)}, bf16[512,2048]{1,0:T(8,128)(2,1)}, bf16[512,2048]{1,0:T(8,128)(2,1)}) custom-call(s32[8]{0:T(128)} %fusion.2.tab, bf16[1024,1024]{1,0:T(8,128)(2,1)} %get-tuple-element.217.refs_0_, bf16[1024,1024]{1,0:T(8,128)(2,1)} %get-tuple-element.218.refs_1_, ...), custom_call_target="tpu_custom_call" | custom-call | flops 12884901888 | bytes 50331648 | tf_op jit(solution)/shard_map/feed_forward/pallas_call | solution.py:630
  217.5 4.5 tie.34
  224.1 27.6 %feed_forward.7 = (bf16[1024,1024]{1,0:T(8,128)(2,1)}, f32[1024,1024]{1,0:T(8,128)}, bf16[1024,1024]{1,0:T(8,128)(2,1)}, bf16[512,3072]{1,0:T(8,128)(2,1)}, bf16[512,3072]{1,0:T(8,128)(2,1)}) custom-call(s32[8]{0:T(128)} %fusion.2.tab, bf16[1024,1024]{1,0:T(8,128)(2,1)} %get-tuple-element.217.refs_0_, bf16[1024,1024]{1,0:T(8,128)(2,1)} %get-tuple-element.218.refs_1_, ...), custom_call_target="tpu_custom_call" | custom-call | flops 21474836480 | bytes 50331648 | tf_op jit(solution)/shard_map/feed_forward/pallas_call | solution.py:630
  252.3 9.1 %collective-permute-done.31.refs_2_ = bf16[128,2048]{1,0:T(8,128)(2,1)} collective-permute-done((bf16[128,2048]{1,0:T(8,128)(2,1)}, bf16[128,2048]{1,0:T(8,128)(2,1)}, u32[]{:S(2)}, u32[]{:S(2)}) %collective-permute-start.31) | collective-permute-done | bytes 524320 | tf_op jit(solution)/shard_map/ppermute | solution.py:253
  261.4 5.3 %tie.35 = (bf16[1024,1024]{1,0:T(8,128)(2,1)}, f32[128,2048]{1,0:T(8,128)}, bf16[128,2048]{1,0:T(8,128)(2,1)}, bf16[128,2048]{1,0:T(8,128)(2,1)}, bf16[256,2048]{1,0:T(8,128)(2,1)}, /*index=5*/bf16[256,2048]{1,0:T(8,128)(2,1)}) custom-call(bf16[1024,1024]{1,0:T(8,128)(2,1)} %get-tuple-element.252.refs_0_, ...), custom_call_target="tpu_custom_call", output_to_operand_aliasing={{0}: (0, {})} | custom-call | tf_op jit(solution)/shard_map/tie/pallas_call | solution.py:198
  268.8 14.2 %attend_back.4 = (bf16[1024,768]{1,0:T(8,128)(2,1)}, f32[512,768]{1,0:T(8,128)}, f32[512,768]{1,0:T(8,128)}) custom-call(s32[1]{0:T(128)} %copy.159.n_ref, s32[8]{0:T(128)} %fusion.2.tab, bf16[1024,1536]{1,0:T(8,128)(2,1)} %get-tuple-element.192.q_ref.k_ref.v_ref, bf16[1024,1536]{1,0:T(8,128)(2,1)} %get-tuple-element.192.q_ref.k_ref.v_ref, ...), custom_call_target="tpu_custom_call" | custom-call | flops 10737418240 | bytes 16777216 | tf_op jit(solution)/shard_map/attend_back/pallas_call | solution.py:716
  283.0 3.3 collective-permute-done.35.refs_4_
  286.3 6.2 %tie.36 = (bf16[1024,1024]{1,0:T(8,128)(2,1)}, f32[128,2048]{1,0:T(8,128)}, bf16[128,2048]{1,0:T(8,128)(2,1)}, bf16[128,2048]{1,0:T(8,128)(2,1)}, bf16[256,3072]{1,0:T(8,128)(2,1)}, /*index=5*/bf16[256,3072]{1,0:T(8,128)(2,1)}) custom-call(bf16[1024,1024]{1,0:T(8,128)(2,1)} %get-tuple-element.259.refs_0_.g_ref, ...), custom_call_target="tpu_custom_call", output_to_operand_aliasing={{0}: (0, {})} | custom-call | tf_op jit(solution)/shard_map/tie/pallas_call | solution.py:198
  295.5 14.4 %attend_back.5 = (bf16[1024,768]{1,0:T(8,128)(2,1)}, f32[512,768]{1,0:T(8,128)}, f32[512,768]{1,0:T(8,128)}) custom-call(s32[1]{0:T(128)} %copy.159.n_ref, s32[8]{0:T(128)} %fusion.2.tab, bf16[1024,1536]{1,0:T(8,128)(2,1)} %get-tuple-element.192.q_ref.k_ref.v_ref, bf16[1024,1536]{1,0:T(8,128)(2,1)} %get-tuple-element.192.q_ref.k_ref.v_ref, ...), custom_call_target="tpu_custom_call" | custom-call | flops 10737418240 | bytes 16777216 | tf_op jit(solution)/shard_map/attend_back/pallas_call | solution.py:716
  309.9 9.2 %collective-permute-done.38.refs_5_ = bf16[256,3072]{1,0:T(8,128)(2,1)} collective-permute-done((bf16[256,3072]{1,0:T(8,128)(2,1)}, bf16[256,3072]{1,0:T(8,128)(2,1)}, u32[]{:S(2)}, u32[]{:S(2)}) %collective-permute-start.38) | collective-permute-done | bytes 1572896 | tf_op jit(solution)/shard_map/ppermute | solution.py:253
  319.1 5.1 %tie.37 = (bf16[1024,1024]{1,0:T(8,128)(2,1)}, f32[32,2048]{1,0:T(8,128)}, f32[128,2048]{1,0:T(8,128)}, bf16[128,3072]{1,0:T(8,128)(2,1)}, bf16[128,3072]{1,0:T(...) custom-call(bf16[1024,1024]{1,0:T(8,128)(2,1)} %get-tuple-element.26, ...), custom_call_target="tpu_custom_call", output_to_operand_aliasing={{0}: (0, {}), {1}: (1, {})} | custom-call | tf_op jit(solution)/shard_map/tie/pallas_call | solution.py:198
  329.1 14.7 %attend_back.6 = (bf16[1024,768]{1,0:T(8,128)(2,1)}, f32[512,768]{1,0:T(8,128)}, f32[512,768]{1,0:T(8,128)}) custom-call(s32[1]{0:T(128)} %copy.159.n_ref, s32[8]{0:T(128)} %fusion.2.tab, bf16[1024,1536]{1,0:T(8,128)(2,1)} %get-tuple-element.206.q_ref.k_ref.v_ref, bf16[1024,1536]{1,0:T(8,128)(2,1)} %get-tuple-element.206.q_ref.k_ref.v_ref, ...), custom_call_target="tpu_custom_call" | custom-call | flops 10737418240 | bytes 16777216 | tf_op jit(solution)/shard_map/attend_back/pallas_call | solution.py:716
  344.6 4.0 tie.38
  348.6 3.0 pad_maximum_fusion
  352.7 14.5 %attend_back.7 = (bf16[1024,768]{1,0:T(8,128)(2,1)}, f32[512,768]{1,0:T(8,128)}, f32[512,768]{1,0:T(8,128)}) custom-call(s32[1]{0:T(128)} %copy.159.n_ref, s32[8]{0:T(128)} %fusion.2.tab, bf16[1024,1536]{1,0:T(8,128)(2,1)} %get-tuple-element.206.q_ref.k_ref.v_ref, bf16[1024,1536]{1,0:T(8,128)(2,1)} %get-tuple-element.206.q_ref.k_ref.v_ref, ...), custom_call_target="tpu_custom_call" | custom-call | flops 10737418240 | bytes 16777216 | tf_op jit(solution)/shard_map/attend_back/pallas_call | solution.py:716
  367.1 8.4 %collective-permute-start.45 = (bf16[128,768]{1,0:T(8,128)(2,1)}, bf16[128,768]{1,0:T(8,128)(2,1)}, u32[]{:S(2)}, u32[]{:S(2)}) collective-permute-start(bf16[128,768]{1,0:T(8,128)(2,1)} %get-tuple-element.288), channel_id=1, source_target_pairs={{0,16},{1,17},{2,18},{3,19},{4,12},{5,13},{6,14},{7,15},{8,24},{9,... | collective-permute-start | bytes 589832 | tf_op jit(solution)/shard_map/ppermute | solution.py:253
  377.9 4.2 collective-permute-done.45.refs_3_
  383.2 3.2 collective-permute-done.47.refs_5_
  386.4 3.1 tie.39
  393.1 10.2 %input_grad.2.refs_0_ = f32[1024,1024]{1,0:T(8,128)} custom-call(s32[8]{0:T(128)} %fusion.2.tab, f32[1024,1024]{1,0:T(8,128)} %get-tuple-element.294.dmid_ref.refs_1_, bf16[1024,1024]{1,0:T(8,128)(2,1)} %bitcast.33, f32[8,1024]{1,0:T(8,128)} %get-tuple-element.187.gain_ref.refs_10_, bf16[1024,768]{1,0:T(8,128)(2,1)} %get-tuple-element.295.refs_0_.refs_1_, ...), custom_call_target="tpu_custom_call" | custom-call | flops 3221225472 | bytes 23068672 | tf_op jit(solution)/shard_map/input_grad/pallas_call | solution.py:775
  404.0 3.3 tie.40
  412.5 4.2 collective-permute-start.57
  416.8 10.4 %input_grad.3.refs_0_ = f32[1024,1024]{1,0:T(8,128)} custom-call(s32[8]{0:T(128)} %fusion.2.tab, f32[1024,1024]{1,0:T(8,128)} %get-tuple-element.306.dmid_ref, bf16[1024,1024]{1,0:T(8,128)(2,1)} %bitcast.34, f32[8,1024]{1,0:T(8,128)} %get-tuple-element.187.gain_ref.refs_10_, ...), custom_call_target="tpu_custom_call", output_to_operand_aliasing={{}: (4, {})} | custom-call | flops 3221225472 | bytes 23068672 | tf_op jit(solution)/shard_map/input_grad/pallas_call | solution.py:775
  431.0 3.8 collective-permute-start.60
  439.2 2.1 collective-permute-done.61
  442.9 2.5 square_sums.1
  445.4 10.3 %all_to_all.5.sums_ref = f32[32,1,128]{2,1,0:T(1,128)} all-to-all(f32[32,1,128]{2,1,0:T(1,128)} %get-tuple-element.322), channel_id=1, replica_groups=mesh['dp'=8,'fsdp'=4] {'dp','fsdp'}, dimensions={0} | all-to-all | bytes 32768 | tf_op jit(solution)/shard_map/all_to_all | solution.py:1023
  455.7 6.6 %adam.1 = (f32[32,3072]{1,0:T(8,128)}, f32[32,3072]{1,0:T(8,128)}, f32[32,3072]{1,0:T(8,128)}, f32[32,3072]{1,0:T(8,128)}, f32[32,1024]{1,0:T(8,128)}, /*index=5...) custom-call(f32[32,1,128]{2,1,0:T(1,128)} %all_to_all.5.sums_ref, ...), custom_call_target="tpu_custom_call" | custom-call | tf_op jit(solution)/shard_map/adam/pallas_call | solution.py:899
  (199 shorter events, 68.7 us)
Async XLA Ops:
  7.2 49.6 %all-gather.3.cloned.1.call-start = ((), (), s32[]{:S(2)}) async-start(), calls=%async_computation.6 | async-start | bytes 1474560 | tf_op jit(solution)/shard_map/all_gather | solution.py:938
  13.6 79.5 %all-gather.5.cloned.1.call-start = ((), (), s32[]{:S(2)}) async-start(), calls=%async_computation.7 | async-start | bytes 1966080 | tf_op jit(solution)/shard_map/all_gather | solution.py:938
  45.2 264.7 %reduce-scatter.6.cloned.1.call-start = ((), (), s32[]{:S(2)}) async-start(), calls=%async_computation.8 | async-start | bytes 1310720 | tf_op jit(solution)/shard_map/reduce_scatter | solution.py:114
  45.8 18.0 %collective-permute-start.2 = (bf16[256,1664]{1,0:T(8,128)(2,1)}, bf16[256,1664]{1,0:T(8,128)(2,1)}, u32[]{:S(2)}, u32[]{:S(2)}) collective-permute-start(bf16[256,1664]{1,0:T(8,128)(2,1)} %get-tuple-element.184.refs_1_.refs_5_.refs_4_), channel_id=1, source_target_pairs={{0,4},{1,5},{2,6},{3,7},{4,0},{5,1},{6,2},{7,3},{8,12},{9,13},{10,... | collective-permute-start | bytes 2555912 | tf_op jit(solution)/shard_map/ppermute | solution.py:253
  62.3 30.8 %collective-permute-start.8 = (bf16[128,2048]{1,0:T(8,128)(2,1)}, bf16[128,2048]{1,0:T(8,128)(2,1)}, u32[]{:S(2)}, u32[]{:S(2)}) collective-permute-start(bf16[128,2048]{1,0:T(8,128)(2,1)} %get-tuple-element.197.refs_4_), channel_id=1, source_target_pairs={{0,16},{1,17},{2,18},{3,19},{4,12},{5,13},{6,14},{7,15},{8,24},{9,... | collective-permute-start | bytes 1572872 | tf_op jit(solution)/shard_map/ppermute | solution.py:253
  75.9 18.0 %collective-permute-start.7 = (bf16[256,1536]{1,0:T(8,128)(2,1)}, bf16[256,1536]{1,0:T(8,128)(2,1)}, u32[]{:S(2)}, u32[]{:S(2)}) collective-permute-start(bf16[256,1536]{1,0:T(8,128)(2,1)} %get-tuple-element.196.refs_1_.refs_8_.refs_9_), channel_id=1, source_target_pairs={{0,8},{1,9},{2,10},{3,11},{4,20},{5,21},{6,22},{7,23},{8,0},{9,1},... | collective-permute-start | bytes 2359304 | tf_op jit(solution)/shard_map/ppermute | solution.py:253
  77.4 20.0 %collective-permute-start.9 = (bf16[256,1536]{1,0:T(8,128)(2,1)}, bf16[256,1536]{1,0:T(8,128)(2,1)}, u32[]{:S(2)}, u32[]{:S(2)}) collective-permute-start(bf16[256,1536]{1,0:T(8,128)(2,1)} %get-tuple-element.196.refs_1_.refs_8_.refs_9_), channel_id=1, source_target_pairs={{0,4},{1,5},{2,6},{3,7},{4,0},{5,1},{6,2},{7,3},{8,12},{9,13},{10,... | collective-permute-start | bytes 2359304 | tf_op jit(solution)/shard_map/ppermute | solution.py:253
  77.4 16.4 %collective-permute-start.6 = (bf16[256,1024]{1,0:T(8,128)(2,1)}, bf16[256,1024]{1,0:T(8,128)(2,1)}, u32[]{:S(2)}, u32[]{:S(2)}) collective-permute-start(bf16[256,1024]{1,0:T(8,128)(2,1)} %get-tuple-element.195.refs_2_.refs_13_), channel_id=1, source_target_pairs={{0,8},{1,9},{2,10},{3,11},{4,20},{5,21},{6,22},{7,23},{8,0},{9,1},... | collective-permute-start | bytes 1572872 | tf_op jit(solution)/shard_map/ppermute | solution.py:253
  97.5 34.3 %collective-permute-start.14 = (bf16[256,2048]{1,0:T(8,128)(2,1)}, bf16[256,2048]{1,0:T(8,128)(2,1)}, u32[]{:S(2)}, u32[]{:S(2)}) collective-permute-start(bf16[256,2048]{1,0:T(8,128)(2,1)} %get-tuple-element.208.refs_3_), channel_id=1, source_target_pairs={{0,8},{1,9},{2,10},{3,11},{4,20},{5,21},{6,22},{7,23},{8,0},{9,1},... | collective-permute-start | bytes 3145736 | tf_op jit(solution)/shard_map/ppermute | solution.py:253
  98.9 44.8 %collective-permute-start.16 = (bf16[256,2048]{1,0:T(8,128)(2,1)}, bf16[256,2048]{1,0:T(8,128)(2,1)}, u32[]{:S(2)}, u32[]{:S(2)}) collective-permute-start(bf16[256,2048]{1,0:T(8,128)(2,1)} %get-tuple-element.208.refs_3_), channel_id=1, source_target_pairs={{0,4},{1,5},{2,6},{3,7},{4,0},{5,1},{6,2},{7,3},{8,12},{9,13},{10,... | collective-permute-start | bytes 3145736 | tf_op jit(solution)/shard_map/ppermute | solution.py:253
  113.8 18.0 %collective-permute-start.15 = (bf16[128,2048]{1,0:T(8,128)(2,1)}, bf16[128,2048]{1,0:T(8,128)(2,1)}, u32[]{:S(2)}, u32[]{:S(2)}) collective-permute-start(bf16[128,2048]{1,0:T(8,128)(2,1)} %get-tuple-element.209.refs_3_), channel_id=1, source_target_pairs={{0,16},{1,17},{2,18},{3,19},{4,12},{5,13},{6,14},{7,15},{8,24},{9,... | collective-permute-start | bytes 1572872 | tf_op jit(solution)/shard_map/ppermute | solution.py:253
  114.5 29.3 %collective-permute-start.18 = (bf16[256,2048]{1,0:T(8,128)(2,1)}, bf16[256,2048]{1,0:T(8,128)(2,1)}, u32[]{:S(2)}, u32[]{:S(2)}) collective-permute-start(bf16[256,2048]{1,0:T(8,128)(2,1)} %get-tuple-element.216.refs_3_), channel_id=1, source_target_pairs={{0,8},{1,9},{2,10},{3,11},{4,20},{5,21},{6,22},{7,23},{8,0},{9,1},... | collective-permute-start | bytes 3145736 | tf_op jit(solution)/shard_map/ppermute | solution.py:253
  134.1 33.8 %collective-permute-start.19 = (bf16[256,2048]{1,0:T(8,128)(2,1)}, bf16[256,2048]{1,0:T(8,128)(2,1)}, u32[]{:S(2)}, u32[]{:S(2)}) collective-permute-start(bf16[256,2048]{1,0:T(8,128)(2,1)} %get-tuple-element.216.refs_3_), channel_id=1, source_target_pairs={{0,4},{1,5},{2,6},{3,7},{4,0},{5,1},{6,2},{7,3},{8,12},{9,13},{10,... | collective-permute-start | bytes 3145736 | tf_op jit(solution)/shard_map/ppermute | solution.py:253
  134.6 33.4 %collective-permute-start.21 = (bf16[256,2048]{1,0:T(8,128)(2,1)}, bf16[256,2048]{1,0:T(8,128)(2,1)}, u32[]{:S(2)}, u32[]{:S(2)}) collective-permute-start(bf16[256,2048]{1,0:T(8,128)(2,1)} %get-tuple-element.225.refs_3_), channel_id=1, source_target_pairs={{0,8},{1,9},{2,10},{3,11},{4,20},{5,21},{6,22},{7,23},{8,0},{9,1},... | collective-permute-start | bytes 3145736 | tf_op jit(solution)/shard_map/ppermute | solution.py:253
  145.7 22.3 %collective-permute-start.20 = (bf16[256,2048]{1,0:T(8,128)(2,1)}, bf16[256,2048]{1,0:T(8,128)(2,1)}, u32[]{:S(2)}, u32[]{:S(2)}) collective-permute-start(bf16[256,2048]{1,0:T(8,128)(2,1)} %get-tuple-element.224.refs_4_), channel_id=1, source_target_pairs={{0,4},{1,5},{2,6},{3,7},{4,0},{5,1},{6,2},{7,3},{8,12},{9,13},{10,... | collective-permute-start | bytes 3145736 | tf_op jit(solution)/shard_map/ppermute | solution.py:253
  147.0 21.0 %collective-permute-start.22 = (bf16[128,2048]{1,0:T(8,128)(2,1)}, bf16[128,2048]{1,0:T(8,128)(2,1)}, u32[]{:S(2)}, u32[]{:S(2)}) collective-permute-start(bf16[128,2048]{1,0:T(8,128)(2,1)} %get-tuple-element.226.refs_4_), channel_id=1, source_target_pairs={{0,16},{1,17},{2,18},{3,19},{4,12},{5,13},{6,14},{7,15},{8,24},{9,... | collective-permute-start | bytes 1572872 | tf_op jit(solution)/shard_map/ppermute | solution.py:253
  167.4 25.7 %collective-permute-start.26 = (bf16[512,2048]{1,0:T(8,128)(2,1)}, bf16[512,2048]{1,0:T(8,128)(2,1)}, u32[]{:S(2)}, u32[]{:S(2)}) collective-permute-start(bf16[512,2048]{1,0:T(8,128)(2,1)} %get-tuple-element.235), channel_id=1, source_target_pairs={{0,4},{1,5},{2,6},{3,7},{4,0},{5,1},{6,2},{7,3},{8,12},{9,13},{10,... | collective-permute-start | bytes 6291464 | tf_op jit(solution)/shard_map/ppermute | solution.py:253
  167.9 24.7 %collective-permute-start.23 = (bf16[256,2048]{1,0:T(8,128)(2,1)}, bf16[256,2048]{1,0:T(8,128)(2,1)}, u32[]{:S(2)}, u32[]{:S(2)}) collective-permute-start(bf16[256,2048]{1,0:T(8,128)(2,1)} %get-tuple-element.225.refs_3_), channel_id=1, source_target_pairs={{0,4},{1,5},{2,6},{3,7},{4,0},{5,1},{6,2},{7,3},{8,12},{9,13},{10,... | collective-permute-start | bytes 3145736 | tf_op jit(solution)/shard_map/ppermute | solution.py:253
  170.2 22.9 %collective-permute-start.24 = (bf16[256,2048]{1,0:T(8,128)(2,1)}, bf16[256,2048]{1,0:T(8,128)(2,1)}, u32[]{:S(2)}, u32[]{:S(2)}) collective-permute-start(bf16[256,2048]{1,0:T(8,128)(2,1)} %get-tuple-element.233.refs_4_), channel_id=1, source_target_pairs={{0,4},{1,5},{2,6},{3,7},{4,0},{5,1},{6,2},{7,3},{8,12},{9,13},{10,... | collective-permute-start | bytes 3145736 | tf_op jit(solution)/shard_map/ppermute | solution.py:253
  170.7 22.4 %collective-permute-start.25 = (bf16[256,2048]{1,0:T(8,128)(2,1)}, bf16[256,2048]{1,0:T(8,128)(2,1)}, u32[]{:S(2)}, u32[]{:S(2)}) collective-permute-start(bf16[256,2048]{1,0:T(8,128)(2,1)} %get-tuple-element.227.refs_3_), channel_id=1, source_target_pairs={{0,8},{1,9},{2,10},{3,11},{4,20},{5,21},{6,22},{7,23},{8,0},{9,1},... | collective-permute-start | bytes 3145736 | tf_op jit(solution)/shard_map/ppermute | solution.py:253
  192.5 25.0 %collective-permute-start.30 = (bf16[512,2048]{1,0:T(8,128)(2,1)}, bf16[512,2048]{1,0:T(8,128)(2,1)}, u32[]{:S(2)}, u32[]{:S(2)}) collective-permute-start(bf16[512,2048]{1,0:T(8,128)(2,1)} %get-tuple-element.245), channel_id=1, source_target_pairs={{0,4},{1,5},{2,6},{3,7},{4,0},{5,1},{6,2},{7,3},{8,12},{9,13},{10,... | collective-permute-start | bytes 6291464 | tf_op jit(solution)/shard_map/ppermute | solution.py:253
  192.6 24.9 %collective-permute-start.27 = (bf16[256,2048]{1,0:T(8,128)(2,1)}, bf16[256,2048]{1,0:T(8,128)(2,1)}, u32[]{:S(2)}, u32[]{:S(2)}) collective-permute-start(bf16[256,2048]{1,0:T(8,128)(2,1)} %get-tuple-element.227.refs_3_), channel_id=1, source_target_pairs={{0,4},{1,5},{2,6},{3,7},{4,0},{5,1},{6,2},{7,3},{8,12},{9,13},{10,... | collective-permute-start | bytes 3145736 | tf_op jit(solution)/shard_map/ppermute | solution.py:253
  196.6 20.9 %collective-permute-start.28 = (bf16[256,2048]{1,0:T(8,128)(2,1)}, bf16[256,2048]{1,0:T(8,128)(2,1)}, u32[]{:S(2)}, u32[]{:S(2)}) collective-permute-start(bf16[256,2048]{1,0:T(8,128)(2,1)} %get-tuple-element.236.refs_4_), channel_id=1, source_target_pairs={{0,4},{1,5},{2,6},{3,7},{4,0},{5,1},{6,2},{7,3},{8,12},{9,13},{10,... | collective-permute-start | bytes 3145736 | tf_op jit(solution)/shard_map/ppermute | solution.py:253
  196.7 20.8 %collective-permute-start.29 = (bf16[256,2048]{1,0:T(8,128)(2,1)}, bf16[256,2048]{1,0:T(8,128)(2,1)}, u32[]{:S(2)}, u32[]{:S(2)}) collective-permute-start(bf16[256,2048]{1,0:T(8,128)(2,1)} %get-tuple-element.243), channel_id=1, source_target_pairs={{0,8},{1,9},{2,10},{3,11},{4,20},{5,21},{6,22},{7,23},{8,0},{9,1},... | collective-permute-start | bytes 3145736 | tf_op jit(solution)/shard_map/ppermute | solution.py:253
  217.3 44.1 %collective-permute-start.33 = (bf16[512,2048]{1,0:T(8,128)(2,1)}, bf16[512,2048]{1,0:T(8,128)(2,1)}, u32[]{:S(2)}, u32[]{:S(2)}) collective-permute-start(bf16[512,2048]{1,0:T(8,128)(2,1)} %get-tuple-element.258), channel_id=1, source_target_pairs={{0,4},{1,5},{2,6},{3,7},{4,0},{5,1},{6,2},{7,3},{8,12},{9,13},{10,... | collective-permute-start | bytes 6291464 | tf_op jit(solution)/shard_map/ppermute | solution.py:253
  222.0 39.4 %collective-permute-start.32 = (bf16[256,2048]{1,0:T(8,128)(2,1)}, bf16[256,2048]{1,0:T(8,128)(2,1)}, u32[]{:S(2)}, u32[]{:S(2)}) collective-permute-start(bf16[256,2048]{1,0:T(8,128)(2,1)} %get-tuple-element.256), channel_id=1, source_target_pairs={{0,8},{1,9},{2,10},{3,11},{4,20},{5,21},{6,22},{7,23},{8,0},{9,1},... | collective-permute-start | bytes 3145736 | tf_op jit(solution)/shard_map/ppermute | solution.py:253
  251.7 34.6 %collective-permute-start.36 = (bf16[512,3072]{1,0:T(8,128)(2,1)}, bf16[512,3072]{1,0:T(8,128)(2,1)}, u32[]{:S(2)}, u32[]{:S(2)}) collective-permute-start(bf16[512,3072]{1,0:T(8,128)(2,1)} %get-tuple-element.265), channel_id=1, source_target_pairs={{0,4},{1,5},{2,6},{3,7},{4,0},{5,1},{6,2},{7,3},{8,12},{9,13},{10,... | collective-permute-start | bytes 9437192 | tf_op jit(solution)/shard_map/ppermute | solution.py:253
  266.7 77.2 %reduce-scatter.10.cloned.1.call-start = ((), (), s32[]{:S(2)}) async-start(), calls=%async_computation.10 | async-start | bytes 1310720 | tf_op jit(solution)/shard_map/reduce_scatter | solution.py:114
  266.8 19.5 %collective-permute-start.35 = (bf16[256,2048]{1,0:T(8,128)(2,1)}, bf16[256,2048]{1,0:T(8,128)(2,1)}, u32[]{:S(2)}, u32[]{:S(2)}) collective-permute-start(bf16[256,2048]{1,0:T(8,128)(2,1)} %get-tuple-element.263), channel_id=1, source_target_pairs={{0,8},{1,9},{2,10},{3,11},{4,20},{5,21},{6,22},{7,23},{8,0},{9,1},... | collective-permute-start | bytes 3145736 | tf_op jit(solution)/shard_map/ppermute | solution.py:253
  267.2 15.7 %collective-permute-start.34 = (bf16[128,2048]{1,0:T(8,128)(2,1)}, bf16[128,2048]{1,0:T(8,128)(2,1)}, u32[]{:S(2)}, u32[]{:S(2)}) collective-permute-start(bf16[128,2048]{1,0:T(8,128)(2,1)} %get-tuple-element.261), channel_id=1, source_target_pairs={{0,16},{1,17},{2,18},{3,19},{4,12},{5,13},{6,14},{7,15},{8,24},{9,... | collective-permute-start | bytes 1572872 | tf_op jit(solution)/shard_map/ppermute | solution.py:253
  292.5 93.8 %reduce-scatter.8.cloned.1.call-start = ((), (), s32[]{:S(2)}) async-start(), calls=%async_computation.9 | async-start | bytes 1310720 | tf_op jit(solution)/shard_map/reduce_scatter | solution.py:114
  292.6 17.3 %collective-permute-start.39 = (f32[512,768]{1,0:T(8,128)}, f32[512,768]{1,0:T(8,128)}, u32[]{:S(2)}, u32[]{:S(2)}) collective-permute-start(f32[512,768]{1,0:T(8,128)} %get-tuple-element.275), channel_id=1, source_target_pairs={{0,4},{1,5},{2,6},{3,7},{4,0},{5,1},{6,2},{7,3},{8,12},{9,13},{10,... | collective-permute-start | bytes 4718600 | tf_op jit(solution)/shard_map/ppermute | solution.py:253
  292.7 26.4 %collective-permute-start.38 = (bf16[256,3072]{1,0:T(8,128)(2,1)}, bf16[256,3072]{1,0:T(8,128)(2,1)}, u32[]{:S(2)}, u32[]{:S(2)}) collective-permute-start(bf16[256,3072]{1,0:T(8,128)(2,1)} %get-tuple-element.271), channel_id=1, source_target_pairs={{0,8},{1,9},{2,10},{3,11},{4,20},{5,21},{6,22},{7,23},{8,0},{9,1},... | collective-permute-start | bytes 4718600 | tf_op jit(solution)/shard_map/ppermute | solution.py:253
  294.3 15.6 %collective-permute-start.37 = (bf16[128,2048]{1,0:T(8,128)(2,1)}, bf16[128,2048]{1,0:T(8,128)(2,1)}, u32[]{:S(2)}, u32[]{:S(2)}) collective-permute-start(bf16[128,2048]{1,0:T(8,128)(2,1)} %get-tuple-element.269), channel_id=1, source_target_pairs={{0,16},{1,17},{2,18},{3,19},{4,12},{5,13},{6,14},{7,15},{8,24},{9,... | collective-permute-start | bytes 1572872 | tf_op jit(solution)/shard_map/ppermute | solution.py:253
  324.2 103.1 %reduce-scatter.12.cloned.1.call-start = ((), (), s32[]{:S(2)}) async-start(), calls=%async_computation.11 | async-start | bytes 2457600 | tf_op jit(solution)/shard_map/reduce_scatter | solution.py:114
  324.3 19.5 %collective-permute-start.44 = (f32[512,768]{1,0:T(8,128)}, f32[512,768]{1,0:T(8,128)}, u32[]{:S(2)}, u32[]{:S(2)}) collective-permute-start(f32[512,768]{1,0:T(8,128)} %get-tuple-element.286), channel_id=1, source_target_pairs={{0,4},{1,5},{2,6},{3,7},{4,0},{5,1},{6,2},{7,3},{8,12},{9,13},{10,... | collective-permute-start | bytes 4718600 | tf_op jit(solution)/shard_map/ppermute | solution.py:253
  324.4 19.6 %collective-permute-start.40 = (bf16[128,3072]{1,0:T(8,128)(2,1)}, bf16[128,3072]{1,0:T(8,128)(2,1)}, u32[]{:S(2)}, u32[]{:S(2)}) collective-permute-start(bf16[128,3072]{1,0:T(8,128)(2,1)} %get-tuple-element.280), channel_id=1, source_target_pairs={{0,16},{1,17},{2,18},{3,19},{4,12},{5,13},{6,14},{7,15},{8,24},{9,... | collective-permute-start | bytes 2359304 | tf_op jit(solution)/shard_map/ppermute | solution.py:253
  325.6 18.3 %collective-permute-start.41 = (bf16[128,768]{1,0:T(8,128)(2,1)}, bf16[128,768]{1,0:T(8,128)(2,1)S(1)}, u32[]{:S(2)}, u32[]{:S(2)}) collective-permute-start(bf16[128,768]{1,0:T(8,128)(2,1)} %get-tuple-element.282), channel_id=1, source_target_pairs={{0,16},{1,17},{2,18},{3,19},{4,12},{5,13},{6,14},{7,15},{8,24},{9,... | collective-permute-start | bytes 589832 | tf_op jit(solution)/shard_map/ppermute | solution.py:253
  326.4 17.5 %collective-permute-start.42 = (bf16[128,768]{1,0:T(8,128)(2,1)}, bf16[128,768]{1,0:T(8,128)(2,1)}, u32[]{:S(2)}, u32[]{:S(2)}) collective-permute-start(bf16[128,768]{1,0:T(8,128)(2,1)} %get-tuple-element.283), channel_id=1, source_target_pairs={{0,8},{1,9},{2,10},{3,11},{4,20},{5,21},{6,22},{7,23},{8,0},{9,1},... | collective-permute-start | bytes 589832 | tf_op jit(solution)/shard_map/ppermute | solution.py:253
  328.0 16.0 %collective-permute-start.43 = (bf16[128,768]{1,0:T(8,128)(2,1)}, bf16[128,768]{1,0:T(8,128)(2,1)}, u32[]{:S(2)}, u32[]{:S(2)}) collective-permute-start(bf16[128,768]{1,0:T(8,128)(2,1)} %get-tuple-element.284), channel_id=1, source_target_pairs={{0,24},{1,25},{2,26},{3,27},{4,28},{5,29},{6,30},{7,31},{8,16},{9,... | collective-permute-start | bytes 589832 | tf_op jit(solution)/shard_map/ppermute | solution.py:253
  351.7 91.2 %reduce-scatter.14.cloned.1.call-start = ((), (), s32[]{:S(2)}) async-start(), calls=%async_computation.12 | async-start | bytes 491520 | tf_op jit(solution)/shard_map/reduce_scatter | solution.py:114
  351.7 34.7 %collective-permute-start.48 = (f32[512,768]{1,0:T(8,128)}, f32[512,768]{1,0:T(8,128)}, u32[]{:S(2)}, u32[]{:S(2)}) collective-permute-start(f32[512,768]{1,0:T(8,128)} %get-tuple-element.293), channel_id=1, source_target_pairs={{0,4},{1,5},{2,6},{3,7},{4,0},{5,1},{6,2},{7,3},{8,12},{9,13},{10,... | collective-permute-start | bytes 4718600 | tf_op jit(solution)/shard_map/ppermute | solution.py:253
  367.1 36.2 %collective-permute-start.52 = (f32[512,768]{1,0:T(8,128)}, f32[512,768]{1,0:T(8,128)}, u32[]{:S(2)}, u32[]{:S(2)}) collective-permute-start(f32[512,768]{1,0:T(8,128)} %get-tuple-element.305), channel_id=1, source_target_pairs={{0,4},{1,5},{2,6},{3,7},{4,0},{5,1},{6,2},{7,3},{8,12},{9,13},{10,... | collective-permute-start | bytes 4718600 | tf_op jit(solution)/shard_map/ppermute | solution.py:253
  407.3 19.9 %collective-permute-start.53 = (bf16[128,768]{1,0:T(8,128)(2,1)}, bf16[128,768]{1,0:T(8,128)(2,1)S(1)}, u32[]{:S(2)}, u32[]{:S(2)}) collective-permute-start(bf16[128,768]{1,0:T(8,128)(2,1)} %get-tuple-element.311), channel_id=1, source_target_pairs={{0,16},{1,17},{2,18},{3,19},{4,12},{5,13},{6,14},{7,15},{8,24},{9,... | collective-permute-start | bytes 589832 | tf_op jit(solution)/shard_map/ppermute | solution.py:253
  408.4 18.9 %collective-permute-start.54 = (bf16[128,768]{1,0:T(8,128)(2,1)}, bf16[128,768]{1,0:T(8,128)(2,1)}, u32[]{:S(2)}, u32[]{:S(2)}) collective-permute-start(bf16[128,768]{1,0:T(8,128)(2,1)} %get-tuple-element.312), channel_id=1, source_target_pairs={{0,8},{1,9},{2,10},{3,11},{4,20},{5,21},{6,22},{7,23},{8,0},{9,1},... | collective-permute-start | bytes 589832 | tf_op jit(solution)/shard_map/ppermute | solution.py:253
  409.9 17.4 %collective-permute-start.55 = (bf16[128,768]{1,0:T(8,128)(2,1)}, bf16[128,768]{1,0:T(8,128)(2,1)}, u32[]{:S(2)}, u32[]{:S(2)}) collective-permute-start(bf16[128,768]{1,0:T(8,128)(2,1)} %get-tuple-element.313), channel_id=1, source_target_pairs={{0,24},{1,25},{2,26},{3,27},{4,28},{5,29},{6,30},{7,31},{8,16},{9,... | collective-permute-start | bytes 589832 | tf_op jit(solution)/shard_map/ppermute | solution.py:253
  412.5 22.3 %collective-permute-start.56 = (f32[32,768]{1,0:T(8,128)}, f32[32,768]{1,0:T(8,128)}, u32[]{:S(2)}, u32[]{:S(2)}) collective-permute-start(f32[32,768]{1,0:T(8,128)} %get-tuple-element.352), channel_id=1, source_target_pairs={{0,1},{1,0},{2,3},{3,2},{4,5},{5,4},{6,7},{7,6},{8,9},{9,8},{10,11... | collective-permute-start | bytes 294920 | tf_op jit(solution)/shard_map/ppermute | solution.py:120
  412.5 22.9 %collective-permute-start.57 = (f32[32,768]{1,0:T(8,128)}, f32[32,768]{1,0:T(8,128)}, u32[]{:S(2)}, u32[]{:S(2)}) collective-permute-start(f32[32,768]{1,0:T(8,128)} %get-tuple-element.354), channel_id=1, source_target_pairs={{0,2},{1,3},{2,0},{3,1},{4,6},{5,7},{6,4},{7,5},{8,10},{9,11},{10,... | collective-permute-start | bytes 294920 | tf_op jit(solution)/shard_map/ppermute | solution.py:120
  (35 other events, 256.5 us)
Sparse Core Ops, SparseCore 0:
  13.7 35.2 all-gather.2
  51.2 36.0 all-gather.4
  266.8 27.1 reduce-scatter.5
  296.3 25.8 reduce-scatter.9
  324.3 27.4 reduce-scatter.7
  354.1 42.8 reduce-scatter.11
  399.9 20.4 reduce-scatter.13

commit v5 on v4

--- a/solution.py
+++ b/solution.py
@@ -88,12 +88,12 @@
         held = [mine, got]
         return held + (yield held, self.core_pairs(), None)
 
-    def scatter(self, sent, kept):
+    def scatter(self, sent, kept, kind=f32):
         pairs = self.core_pairs()
         for s in range(self.bits - 1):
             kept, sent = yield [sent], pairs, ("sum", [kept], [bf16, bf16])
             pairs = self.mix_pairs(s)
-        (total,) = yield [sent], pairs, ("sum", [kept], [f32])
+        (total,) = yield [sent], pairs, ("sum", [kept], [kind])
         return total
 
     def scatter_direct(self, sent, kept):
@@ -219,12 +219,12 @@
     def gather(self, name, array, at=None, wide=None):
         self.waiting[name] = (array, at, wide)
 
-    def scatter(self, name, sent, kept, direct=False):
-        way = self.plan.scatter_direct if direct else self.plan.scatter
-        self.live[name] = way(sent, kept)
-
-    def own_rows(self, name, total=None):
-        self.shards[name] = self.plan.own_rows(self.done[name] if total is None else total)
+    def scatter(self, name, sent, kept, direct=False, kind=f32):
+        way = self.plan.scatter_direct
+        self.live[name] = way(sent, kept) if direct else self.plan.scatter(sent, kept, kind)
+
+    def own_rows(self, name):
+        self.shards[name] = self.plan.own_rows(self.done[name])
 
     def step(self, x, names, pinned=()):
         names = [n for n in names if n not in self.done]
@@ -753,9 +753,12 @@
             natural(nat, slice(None), weights[i * count : (i + 1) * count], slice(None), tab, block)
 
     du = None
-    for i, nat in enumerate(nats):
-        mine = d_refs[i * parts // groups : (i + 1) * parts // groups]
-        d = jnp.concatenate([ref[...] for ref in mine], axis=1)
+    d_refs = list(d_refs)
+    for nat in nats:
+        mine = []
+        while sum(v.shape[1] for v in mine) < nat.shape[1]:
+            mine.append(d_refs.pop(0)[...])
+        d = mine[0] if len(mine) == 1 else jnp.concatenate(mine, axis=1)
         part = lax.dot_general(d, nat[...], NT, preferred_element_type=f32)
         du = part if du is None else du + part
     out_ref[...] = dmid_ref[...] + norm_back(x_ref[...].astype(f32), gain_ref[0:1, :], du)
@@ -971,7 +974,7 @@
         out, held_du, *more, sent, kept = feed_forward(
             tab, u_two, u_two_t, g_low, [flow.done[f"m{k}"]], held, block, k == 0, last
         )
-        flow.scatter(f"g{k}", sent, kept)
+        flow.scatter(f"g{k}", sent, kept, kind=bf16 if last else f32)
         if last:
             dmid, (d_o,) = held_du, more
         else:
@@ -979,46 +982,41 @@
     d_o = step(d_o, ["g0", "g1", "g2", "g3"])
     d_o = flow.until(d_o, ["g0"])
     flow.own_rows("g0")
-    calls = 4
-    per = every // calls
+    sizes = [pairs] + [pairs // 2] * (2 * (GROUPS - 1))
+    calls = len(sizes)
+    starts = [sum(sizes[:i]) for i in range(calls)]
+    plans = [["g1", "g2", "g3", "gq0"], ["g2", "g3", "gq0", "gq1"]]
     d_qkv = []
-    plans = [
-        ["g1", "g2", "g3", "gq0"],
-        ["g2", "g3", "gq0", "gq1"],
-        ["g3", "gq0", "gq1", "gq2"],
-    ]
     for i in range(calls):
-        group, at = divmod(i * per, pairs)
+        group, at = divmod(starts[i], pairs)
         d, sent, kept = attend_back(
-            frames, tab, qkv[group], d_o, lse[group], u_one_t, i * per, at, per, block
+            frames, tab, qkv[group], d_o, lse[group], u_one_t, starts[i], at, sizes[i], block
         )
         d_qkv.append(d)
         flow.scatter(f"gq{i}", sent, kept, True)
         if i < calls - 1:
             d_o = step(d_o, plans[i], [f"g{i - 1}"] if i > 0 else [])
-        if i < 2:
             d_o = flow.until(d_o, [f"g{i + 1}"])
             flow.own_rows(f"g{i + 1}")
-        elif i == 2:
-            some = ["g3", "gq0"]
-            d_o = flow.until(d_o, some)
-            flow.own_rows("joined", jnp.concatenate([flow.done[n] for n in some], axis=1))
-    dmid = step(dmid, ["gq1", "gq2", "gq3"], ["g2"])
-    dmid = flow.until(dmid, ["gq1"])
-    flow.own_rows("gq1")
+    some = ["g3", "gq0"]
+    dmid, d_qkv = step((dmid, d_qkv), some + ["gq1", "gq2"], ["g1"])
+    dmid = flow.until(dmid, some)
+    flow.own_rows("g3")
+    flow.own_rows("gq0")
     blocks = length // 256
     held_q = [flow.done["q0"], flow.done["q1"]]
     top = input_grad(tab, d_qkv, dmid, x, gains, held_q, block, 0, blocks // 2)
-    top, dmid = step((top, dmid), ["gq2", "gq3"])
+    top, dmid = step((top, dmid), ["gq1", "gq2"], ["g2"])
     grad_in = input_grad(tab, d_qkv, dmid, x, gains, held_q, block, blocks // 2, blocks, (top,))
-    grad_in = step(grad_in, ["gq3"], ["joined"])
+    grad_in = step(grad_in, ["gq2"], ["g3"])
     flow.until(None, list(flow.live))
-    size = per * 3 * LANES
-    late_parts = [plan.own_rows(flow.done[f"gq{i}"], True) for i in range(2, calls)]
-    arrays = [flow.shards[n] for n in ("joined", "gq1", "g0", "g1", "g2")] + late_parts
-    views = [(0, 3 * D, size), (1, 0, size)] + [(5 + i, 0, size) for i in range(calls - 2)]
-    views += [(0, 2 * D, D)] + [(2 + k, 0, 2 * D) for k in range(subs - 1)] + [(0, 0, 2 * D)]
-    weights = [qkv_low[:, i * size : (i + 1) * size] for i in range(calls)] + list(up_low)
+    width = [3 * n * LANES for n in sizes]
+    at = [3 * n * LANES for n in starts]
+    late_parts = [plan.own_rows(flow.done[f"gq{i}"], True) for i in range(1, calls)]
+    arrays = [flow.shards[n] for n in ("g3", "g0", "g1", "g2", "gq0")] + late_parts
+    views = [(4 + i, 0, width[i]) for i in range(calls)]
+    views += [(0, 2 * D, D)] + [(1 + k, 0, 2 * D) for k in range(subs - 1)] + [(0, 0, 2 * D)]
+    weights = [qkv_low[:, a : a + w] for a, w in zip(at, width)] + list(up_low)
     sums, gain_shard = square_sums(arrays, views, calls, weights, norm_gains, ndev)
     everyone = lax.all_to_all(sums, AXES, 0, 0)
     rates = (0.6 / D**0.5, 0.6 / FANO**0.5, 0.6 / D**0.5, 0.6 / FF**0.5, 1.0)

time: 473 us -> 463 us (0.979)
  starting transfers between devices: 60.9 us -> 55.5 us
  Pallas kernels: 287 us -> 282 us
  waiting for transfers between devices: 53.7 us -> 58.5 us
    ppermute x6, waiting for transfers between devices: 4.26 us -> 12.5 us  [own_rows(): sum_ = sum_ + lax.ppermute(block(me ^ flip), AXES, pairs)]
    pallas_call x4 -> x3, Pallas kernels: 57.7 us -> 53.5 us  [attend_back(): pl.pallas_call(functools.partial(attend_back_kernel, 256, block), grid_sp...]
    ppermute x56 -> x52, waiting for transfers between devices: 49.2 us -> 45.2 us  [step(): lax.ppermute(v, AXES, p)]
    ppermute x56 -> x52, starting transfers between devices: 51.1 us -> 47.9 us  [step(): lax.ppermute(v, AXES, p)]
    pallas_call x21 -> x20, Pallas kernels: 54.6 us -> 53.1 us  [tie(): pl.pallas_call(functools.partial(tie_kernel, count, jobs), in_specs=[plac...]
  transfers between devices with their start and end apart: 69 -> 65, of which waited for: 15 -> 12; matrix products, arithmetic and copies ran while one was open for 3% -> 2% of each run, Pallas kernels for 59% -> 59%
where the time goes in v5:
time: 463 us; the launch traced here: 459 us
  Pallas kernels  282 us (61%)
  waiting for transfers between devices  58.5 us (13%)
  starting transfers between devices  55.5 us (12%)
  blocking collectives  29.7 us (6%)
  between operations  16 us (3%)
  other arithmetic  9.3 us (2%)
  local copies, waits for them, and re-layouts  7.87 us (2%)
    pallas_call x4, Pallas kernels, feed_forward(): pl.pallas_call(functools.partial(mlp_kernel, [len(p) for p in pieces], bl...  88 us
    pallas_call x3, Pallas kernels, attend_back(): pl.pallas_call(functools.partial(attend_back_kernel, 256, block), grid_sp...  53.5 us
    pallas_call x20, Pallas kernels, tie(): pl.pallas_call(functools.partial(tie_kernel, count, jobs), in_specs=[plac...  53.1 us
    ppermute x52, starting transfers between devices, step(): lax.ppermute(v, AXES, p)  47.9 us
    ppermute x52, waiting for transfers between devices, step(): lax.ppermute(v, AXES, p)  45.2 us
    pallas_call x2, Pallas kernels, attend(): pl.pallas_call(functools.partial(attend_kernel, 512), grid_spec=pltpu.Pre...  30.9 us
    pallas_call x2, Pallas kernels, input_grad(): pl.pallas_call(functools.partial(input_grad_kernel, groups, len(d), len(d...  20.6 us
    all_gather x1, blocking collectives, body(): reach = lambda v: lax.all_gather(v, 'fsdp', axis=0, tiled=True)  19.2 us
  transfers between devices with their start and end apart: 65, of which 12 were waited for; matrix products, arithmetic and copies ran while one was open for 2% of the time, Pallas kernels for 59%

profile of v5, /device:TPU:0, one launch (start us, length us, event | category | flops | bytes accessed | tf_op | source)
XLA Modules:
  0.0 458.8 jit_solution(11880630971191943201)
XLA Ops:
  13.1 19.2 %all_gather.9.refs_0_ = bf16[128,1664]{1,0:T(8,128)(2,1)} all-gather(bf16[32,1664]{1,0:T(8,128)(2,1)S(1)} %fusion.1), channel_id=1, replica_groups=mesh['dp'=8,'fsdp'=4] {'fsdp'}, dimensions={0}, use_global_device_ids=true | all-gather | bytes 532480 | tf_op jit(solution)/shard_map/all_gather | solution.py:941
  34.7 3.2 bitcast_select_fusion.refs_0_
  37.9 3.0 collective-permute-done.refs_2_
  40.9 2.1 tie.21
  45.0 11.0 %collective-permute-done.1.refs_0_ = bf16[256,1664]{1,0:T(8,128)(2,1)} collective-permute-done((bf16[256,1664]{1,0:T(8,128)(2,1)}, bf16[256,1664]{1,0:T(8,128)(2,1)}, u32[]{:S(2)}, u32[]{:S(2)}) %collective-permute-start.1) | collective-permute-done | bytes 852000 | tf_op jit(solution)/shard_map/ppermute | solution.py:253
  56.2 2.2 tie.24
  63.3 9.7 %qkv.2 = (bf16[1024,1536]{1,0:T(8,128)(2,1)}, bf16[1024,1024]{1,0:T(8,128)(2,1)}, f32[8,1024]{1,0:T(8,128)}, bf16[1024,1024]{1,0:T(8,128)(2,1)}) custom-call(s32[8]{0:T(128)} %fusion.2.tab, bf16[1024,1024]{1,0:T(8,128)(2,1)} %bitcast.31, bf16[256,1664]{1,0:T(8,128)(2,1)} %get-tuple-element.178.refs_1_.refs_5_.refs_3_.refs_4_, ...), custom_call_target="tpu_custom_call" | custom-call | flops 3221225472 | bytes 20971520 | tf_op jit(solution)/shard_map/qkv/pallas_call | solution.py:317
  73.0 2.2 tie.25
  77.4 15.2 %attend.2 = (bf16[1024,512]{1,0:T(8,128)(2,1)}, f32[4,2,1024]{2,1,0:T(2,128)}) custom-call(s32[1]{0:T(128)} %copy.163.n_ref, bf16[1024,1536]{1,0:T(8,128)(2,1)} %get-tuple-element.186.q_ref.k_ref.v_ref, bf16[1024,1536]{1,0:T(8,128)(2,1)} %get-tuple-element.186.q_ref.k_ref.v_ref, bf16[1024,1536]{1,0:T(8,128)(2,1)} %get-tuple-element.186.q_ref.k_ref.v_ref), custom_call_target="tpu_custom_call" | custom-call | flops 8589934592 | bytes 8388608 | tf_op jit(solution)/shard_map/attend/pallas_call | solution.py:389
  93.3 2.4 tie.26
  99.9 8.0 %qkv.3.refs_0_ = bf16[1024,1536]{1,0:T(8,128)(2,1)} custom-call(s32[8]{0:T(128)} %fusion.2.tab, bf16[1024,1024]{1,0:T(8,128)(2,1)} %get-tuple-element.195.refs_0_, bf16[256,1536]{1,0:T(8,128)(2,1)} %get-tuple-element.190.refs_1_.refs_7_.refs_8_, bf16[256,1536]{1,0:T(8,128)(2,1)} %get-tuple-element.194.refs_2_.refs_8_.refs_9_, ...), custom_call_target="tpu_custom_call" | custom-call | flops 3221225472 | bytes 20971520 | tf_op jit(solution)/shard_map/qkv/pallas_call | solution.py:317
  107.9 2.2 collective-permute-done.13.refs_4_
  110.1 2.4 tie.28
  114.5 15.7 %attend.3 = (bf16[1024,512]{1,0:T(8,128)(2,1)}, f32[4,2,1024]{2,1,0:T(2,128)}) custom-call(s32[1]{0:T(128)} %copy.163.n_ref, bf16[1024,1536]{1,0:T(8,128)(2,1)} %get-tuple-element.200.q_ref.k_ref.v_ref, bf16[1024,1536]{1,0:T(8,128)(2,1)} %get-tuple-element.200.q_ref.k_ref.v_ref, bf16[1024,1536]{1,0:T(8,128)(2,1)} %get-tuple-element.200.q_ref.k_ref.v_ref), custom_call_target="tpu_custom_call" | custom-call | flops 8589934592 | bytes 8388608 | tf_op jit(solution)/shard_map/attend/pallas_call | solution.py:389
  130.2 2.2 tie.29
  133.1 9.1 %middle.1 = (f32[1024,1024]{1,0:T(8,128)}, bf16[1024,1024]{1,0:T(8,128)(2,1)}, bf16[1024,1024]{1,0:T(8,128)(2,1)}) custom-call(s32[8]{0:T(128)} %fusion.2.tab, bf16[1024,1024]{1,0:T(8,128)(2,1)} %bitcast.32, f32[8,1024]{1,0:T(8,128)} %get-tuple-element.181.gain_ref.refs_10_, bf16[1024,512]{1,0:T(8,128)(2,1)} %get-tuple-element.204.refs_0_.refs_11_, ...), custom_call_target="tpu_custom_call" | custom-call | flops 2147483648 | bytes 16777216 | tf_op jit(solution)/shard_map/middle/pallas_call | solution.py:432
  143.5 1.9 tie.30
  146.3 20.0 %feed_forward.4 = (f32[1024,1024]{1,0:T(8,128)}, f32[1024,1024]{1,0:T(8,128)}, bf16[512,2048]{1,0:T(8,128)(2,1)}, bf16[512,2048]{1,0:T(8,128)(2,1)}) custom-call(s32[8]{0:T(128)} %fusion.2.tab, bf16[1024,1024]{1,0:T(8,128)(2,1)} %get-tuple-element.211.refs_0_, bf16[1024,1024]{1,0:T(8,128)(2,1)} %get-tuple-element.212.refs_1_, ...), custom_call_target="tpu_custom_call" | custom-call | flops 12884901888 | bytes 50331648 | tf_op jit(solution)/shard_map/feed_forward/pallas_call | solution.py:630
  166.8 2.3 tie.31
  170.7 20.1 %feed_forward.5 = (f32[1024,1024]{1,0:T(8,128)}, f32[1024,1024]{1,0:T(8,128)}, bf16[512,2048]{1,0:T(8,128)(2,1)}, bf16[512,2048]{1,0:T(8,128)(2,1)}) custom-call(s32[8]{0:T(128)} %fusion.2.tab, bf16[1024,1024]{1,0:T(8,128)(2,1)} %get-tuple-element.211.refs_0_, bf16[1024,1024]{1,0:T(8,128)(2,1)} %get-tuple-element.212.refs_1_, ...), custom_call_target="tpu_custom_call" | custom-call | flops 12884901888 | bytes 50331648 | tf_op jit(solution)/shard_map/feed_forward/pallas_call | solution.py:630
  191.5 3.4 tie.32
  195.5 20.3 %feed_forward.6 = (f32[1024,1024]{1,0:T(8,128)}, f32[1024,1024]{1,0:T(8,128)}, bf16[512,2048]{1,0:T(8,128)(2,1)}, bf16[512,2048]{1,0:T(8,128)(2,1)}) custom-call(s32[8]{0:T(128)} %fusion.2.tab, bf16[1024,1024]{1,0:T(8,128)(2,1)} %get-tuple-element.211.refs_0_, bf16[1024,1024]{1,0:T(8,128)(2,1)} %get-tuple-element.212.refs_1_, ...), custom_call_target="tpu_custom_call" | custom-call | flops 12884901888 | bytes 50331648 | tf_op jit(solution)/shard_map/feed_forward/pallas_call | solution.py:630
  216.4 4.5 tie.33
  223.2 27.6 %feed_forward.7 = (bf16[1024,1024]{1,0:T(8,128)(2,1)}, f32[1024,1024]{1,0:T(8,128)}, bf16[1024,1024]{1,0:T(8,128)(2,1)}, bf16[512,3072]{1,0:T(8,128)(2,1)}, bf16[512,3072]{1,0:T(8,128)(2,1)}) custom-call(s32[8]{0:T(128)} %fusion.2.tab, bf16[1024,1024]{1,0:T(8,128)(2,1)} %get-tuple-element.211.refs_0_, bf16[1024,1024]{1,0:T(8,128)(2,1)} %get-tuple-element.212.refs_1_, ...), custom_call_target="tpu_custom_call" | custom-call | flops 21474836480 | bytes 50331648 | tf_op jit(solution)/shard_map/feed_forward/pallas_call | solution.py:630
  250.9 5.2 %tie.34 = (bf16[1024,1024]{1,0:T(8,128)(2,1)}, f32[128,2048]{1,0:T(8,128)}, bf16[128,2048]{1,0:T(8,128)(2,1)}, bf16[128,2048]{1,0:T(8,128)(2,1)}, bf16[256,2048]{1,0:T(8,128)(2,1)}, /*index=5*/bf16[256,2048]{1,0:T(8,128)(2,1)}) custom-call(bf16[1024,1024]{1,0:T(8,128)(2,1)} %get-tuple-element.246.refs_0_, ...), custom_call_target="tpu_custom_call", output_to_operand_aliasing={{0}: (0, {})} | custom-call | tf_op jit(solution)/shard_map/tie/pallas_call | solution.py:198
  257.6 24.5 %attend_back.3 = (bf16[1024,1536]{1,0:T(8,128)(2,1)}, f32[512,1536]{1,0:T(8,128)}, f32[512,1536]{1,0:T(8,128)}) custom-call(s32[1]{0:T(128)} %copy.163.n_ref, s32[8]{0:T(128)} %fusion.2.tab, bf16[1024,1536]{1,0:T(8,128)(2,1)} %get-tuple-element.186.q_ref.k_ref.v_ref, bf16[1024,1536]{1,0:T(8,128)(2,1)} %get-tuple-element.186.q_ref.k_ref.v_ref, ...), custom_call_target="tpu_custom_call" | custom-call | flops 21474836480 | bytes 16777216 | tf_op jit(solution)/shard_map/attend_back/pallas_call | solution.py:716
  282.0 8.3 %collective-permute-start.39 = (f32[512,1536]{1,0:T(8,128)}, f32[512,1536]{1,0:T(8,128)}, u32[]{:S(2)}, u32[]{:S(2)}) collective-permute-start(f32[512,1536]{1,0:T(8,128)} %get-tuple-element.272), channel_id=1, source_target_pairs={{0,4},{1,5},{2,6},{3,7},{4,0},{5,1},{6,2},{7,3},{8,12},{9,13},{10,... | collective-permute-start | bytes 9437192 | tf_op jit(solution)/shard_map/ppermute | solution.py:253
  290.8 9.0 %collective-permute-done.34.refs_2_ = bf16[128,2048]{1,0:T(8,128)(2,1)} collective-permute-done((bf16[128,2048]{1,0:T(8,128)(2,1)}, bf16[128,2048]{1,0:T(8,128)(2,1)}, u32[]{:S(2)}, u32[]{:S(2)}) %collective-permute-start.34) | collective-permute-done | bytes 524320 | tf_op jit(solution)/shard_map/ppermute | solution.py:253
  299.9 6.2 %tie.35 = (bf16[1024,1024]{1,0:T(8,128)(2,1)}, f32[128,2048]{1,0:T(8,128)}, bf16[128,2048]{1,0:T(8,128)(2,1)}, bf16[128,2048]{1,0:T(8,128)(2,1)}, bf16[256,3072]{1,0:T(8,128)(2,1)}, /*index=5*/bf16[256,3072]{1,0:T(8,128)(2,1)}) custom-call(bf16[1024,1024]{1,0:T(8,128)(2,1)} %get-tuple-element.253.g_ref.refs_0_, ...), custom_call_target="tpu_custom_call", output_to_operand_aliasing={{0}: (0, {})} | custom-call | tf_op jit(solution)/shard_map/tie/pallas_call | solution.py:198
  306.2 1.9 collective-permute-start.37
  308.1 14.6 %attend_back.4 = (bf16[1024,768]{1,0:T(8,128)(2,1)}, f32[512,768]{1,0:T(8,128)}, f32[512,768]{1,0:T(8,128)}) custom-call(s32[1]{0:T(128)} %copy.163.n_ref, s32[8]{0:T(128)} %fusion.2.tab, bf16[1024,1536]{1,0:T(8,128)(2,1)} %get-tuple-element.200.q_ref.k_ref.v_ref, bf16[1024,1536]{1,0:T(8,128)(2,1)} %get-tuple-element.200.q_ref.k_ref.v_ref, ...), custom_call_target="tpu_custom_call" | custom-call | flops 10737418240 | bytes 16777216 | tf_op jit(solution)/shard_map/attend_back/pallas_call | solution.py:716
  322.8 8.5 %collective-permute-done.38.refs_5_ = bf16[256,3072]{1,0:T(8,128)(2,1)} collective-permute-done((bf16[256,3072]{1,0:T(8,128)(2,1)}, bf16[256,3072]{1,0:T(8,128)(2,1)}, u32[]{:S(2)}, u32[]{:S(2)}) %collective-permute-start.38) | collective-permute-done | bytes 1572896 | tf_op jit(solution)/shard_map/ppermute | solution.py:253
  331.3 6.4 %tie.36 = (bf16[1024,1024]{1,0:T(8,128)(2,1)}, f32[32,2048]{1,0:T(8,128)}, f32[128,2048]{1,0:T(8,128)}, bf16[128,3072]{1,0:T(8,128)(2,1)}, bf16[128,3072]{1,0:T(...) custom-call(bf16[1024,1024]{1,0:T(8,128)(2,1)} %get-tuple-element.26, ...), custom_call_target="tpu_custom_call", output_to_operand_aliasing={{0}: (0, {}), {1}: (1, {})} | custom-call | tf_op jit(solution)/shard_map/tie/pallas_call | solution.py:198
  342.6 14.4 %attend_back.5 = (bf16[1024,768]{1,0:T(8,128)(2,1)}, f32[512,768]{1,0:T(8,128)}, f32[512,768]{1,0:T(8,128)}) custom-call(s32[1]{0:T(128)} %copy.163.n_ref, s32[8]{0:T(128)} %fusion.2.tab, bf16[1024,1536]{1,0:T(8,128)(2,1)} %get-tuple-element.200.q_ref.k_ref.v_ref, bf16[1024,1536]{1,0:T(8,128)(2,1)} %get-tuple-element.200.q_ref.k_ref.v_ref, ...), custom_call_target="tpu_custom_call" | custom-call | flops 10737418240 | bytes 16777216 | tf_op jit(solution)/shard_map/attend_back/pallas_call | solution.py:716
  357.0 3.2 collective-permute-done.43.refs_10_
  360.2 6.9 %collective-permute-done.40.refs_6_ = bf16[128,3072]{1,0:T(8,128)(2,1)} collective-permute-done((bf16[128,3072]{1,0:T(8,128)(2,1)}, bf16[128,3072]{1,0:T(8,128)(2,1)}, u32[]{:S(2)}, u32[]{:S(2)}) %collective-permute-start.40) | collective-permute-done | bytes 786464 | tf_op jit(solution)/shard_map/ppermute | solution.py:253
  367.1 4.6 tie.37
  376.6 10.3 %input_grad.2.refs_0_ = f32[1024,1024]{1,0:T(8,128)} custom-call(s32[8]{0:T(128)} %fusion.2.tab, f32[1024,1024]{1,0:T(8,128)} %get-tuple-element.284.dmid_ref.refs_1_, bf16[1024,1024]{1,0:T(8,128)(2,1)} %bitcast.33, f32[8,1024]{1,0:T(8,128)} %get-tuple-element.181.gain_ref.refs_10_, bf16[1024,1536]{1,0:T(8,128)(2,1)} %get-tuple-element.285.refs_0_.refs_1_, ...), custom_call_target="tpu_custom_call" | custom-call | flops 3221225472 | bytes 23068672 | tf_op jit(solution)/shard_map/input_grad/pallas_call | solution.py:778
  387.6 3.1 tie.38
  398.2 10.3 %input_grad.3.refs_0_ = f32[1024,1024]{1,0:T(8,128)} custom-call(s32[8]{0:T(128)} %fusion.2.tab, f32[1024,1024]{1,0:T(8,128)} %get-tuple-element.295.dmid_ref, bf16[1024,1024]{1,0:T(8,128)(2,1)} %bitcast.34, f32[8,1024]{1,0:T(8,128)} %get-tuple-element.181.gain_ref.refs_10_, ...), custom_call_target="tpu_custom_call", output_to_operand_aliasing={{}: (4, {})} | custom-call | flops 3221225472 | bytes 23068672 | tf_op jit(solution)/shard_map/input_grad/pallas_call | solution.py:778
  409.8 2.1 tie.39
  412.9 2.0 collective-permute-start.55
  416.5 5.5 %collective-permute-done.53 = f32[32,768]{1,0:T(8,128)} collective-permute-done((f32[32,768]{1,0:T(8,128)}, f32[32,768]{1,0:T(8,128)}, u32[]{:S(2)}, u32[]{:S(2)}) %collective-permute-start.53) | collective-permute-done | bytes 98336 | tf_op jit(solution)/shard_map/ppermute | solution.py:120
  423.7 2.3 collective-permute-done.57
  426.0 4.7 %collective-permute-done.56 = f32[32,768]{1,0:T(8,128)S(1)} collective-permute-done((f32[32,768]{1,0:T(8,128)S(1)}, f32[32,768]{1,0:T(8,128)S(1)}, u32[]{:S(2)}, u32[]{:S(2)}) %collective-permute-start.56) | collective-permute-done | bytes 98336 | tf_op jit(solution)/shard_map/ppermute | solution.py:120
  432.2 2.4 square_sums.1
  434.6 10.5 %all_to_all.5.sums_ref = f32[32,1,128]{2,1,0:T(1,128)} all-to-all(f32[32,1,128]{2,1,0:T(1,128)} %get-tuple-element.310), channel_id=1, replica_groups=mesh['dp'=8,'fsdp'=4] {'dp','fsdp'}, dimensions={0} | all-to-all | bytes 32768 | tf_op jit(solution)/shard_map/all_to_all | solution.py:1021
  445.1 6.6 %adam.1 = (f32[32,3072]{1,0:T(8,128)}, f32[32,3072]{1,0:T(8,128)}, f32[32,3072]{1,0:T(8,128)}, f32[32,3072]{1,0:T(8,128)}, f32[32,1024]{1,0:T(8,128)}, /*index=5...) custom-call(f32[32,1,128]{2,1,0:T(1,128)} %all_to_all.5.sums_ref, ...), custom_call_target="tpu_custom_call" | custom-call | tf_op jit(solution)/shard_map/adam/pallas_call | solution.py:902
  (186 shorter events, 59.4 us)
Async XLA Ops:
  7.2 49.0 %all-gather.3.cloned.1.call-start = ((), (), s32[]{:S(2)}) async-start(), calls=%async_computation.6 | async-start | bytes 1474560 | tf_op jit(solution)/shard_map/all_gather | solution.py:941
  12.9 79.7 %all-gather.5.cloned.1.call-start = ((), (), s32[]{:S(2)}) async-start(), calls=%async_computation.7 | async-start | bytes 1966080 | tf_op jit(solution)/shard_map/all_gather | solution.py:941
  44.6 278.2 %reduce-scatter.6.cloned.1.call-start = ((), (), s32[]{:S(2)}) async-start(), calls=%async_computation.8 | async-start | bytes 1310720 | tf_op jit(solution)/shard_map/reduce_scatter | solution.py:114
  45.0 18.3 %collective-permute-start.2 = (bf16[256,1664]{1,0:T(8,128)(2,1)}, bf16[256,1664]{1,0:T(8,128)(2,1)}, u32[]{:S(2)}, u32[]{:S(2)}) collective-permute-start(bf16[256,1664]{1,0:T(8,128)(2,1)} %get-tuple-element.178.refs_1_.refs_5_.refs_3_.refs_4_), channel_id=1, source_target_pairs={{0,4},{1,5},{2,6},{3,7},{4,0},{5,1},{6,2},{7,3},{8,12},{9,13},{10,... | collective-permute-start | bytes 2555912 | tf_op jit(solution)/shard_map/ppermute | solution.py:253
  58.4 14.6 %collective-permute-start.4 = (bf16[128,1536]{1,0:T(8,128)(2,1)}, bf16[128,1536]{1,0:T(8,128)(2,1)}, u32[]{:S(2)}, u32[]{:S(2)}) collective-permute-start(bf16[128,1536]{1,0:T(8,128)(2,1)} %get-tuple-element.184.refs_2_), channel_id=1, source_target_pairs={{0,16},{1,17},{2,18},{3,19},{4,12},{5,13},{6,14},{7,15},{8,24},{9,... | collective-permute-start | bytes 1179656 | tf_op jit(solution)/shard_map/ppermute | solution.py:253
  61.7 30.9 %collective-permute-start.8 = (bf16[128,2048]{1,0:T(8,128)(2,1)}, bf16[128,2048]{1,0:T(8,128)(2,1)}, u32[]{:S(2)}, u32[]{:S(2)}) collective-permute-start(bf16[128,2048]{1,0:T(8,128)(2,1)} %get-tuple-element.191.refs_4_), channel_id=1, source_target_pairs={{0,16},{1,17},{2,18},{3,19},{4,12},{5,13},{6,14},{7,15},{8,24},{9,... | collective-permute-start | bytes 1572872 | tf_op jit(solution)/shard_map/ppermute | solution.py:253
  75.2 22.4 %collective-permute-start.9 = (bf16[256,1536]{1,0:T(8,128)(2,1)}, bf16[256,1536]{1,0:T(8,128)(2,1)}, u32[]{:S(2)}, u32[]{:S(2)}) collective-permute-start(bf16[256,1536]{1,0:T(8,128)(2,1)} %get-tuple-element.190.refs_1_.refs_7_.refs_8_), channel_id=1, source_target_pairs={{0,4},{1,5},{2,6},{3,7},{4,0},{5,1},{6,2},{7,3},{8,12},{9,13},{10,... | collective-permute-start | bytes 2359304 | tf_op jit(solution)/shard_map/ppermute | solution.py:253
  75.3 18.0 %collective-permute-start.7 = (bf16[256,1536]{1,0:T(8,128)(2,1)}, bf16[256,1536]{1,0:T(8,128)(2,1)}, u32[]{:S(2)}, u32[]{:S(2)}) collective-permute-start(bf16[256,1536]{1,0:T(8,128)(2,1)} %get-tuple-element.190.refs_1_.refs_7_.refs_8_), channel_id=1, source_target_pairs={{0,8},{1,9},{2,10},{3,11},{4,20},{5,21},{6,22},{7,23},{8,0},{9,1},... | collective-permute-start | bytes 2359304 | tf_op jit(solution)/shard_map/ppermute | solution.py:253
  76.9 16.4 %collective-permute-start.6 = (bf16[256,1024]{1,0:T(8,128)(2,1)}, bf16[256,1024]{1,0:T(8,128)(2,1)}, u32[]{:S(2)}, u32[]{:S(2)}) collective-permute-start(bf16[256,1024]{1,0:T(8,128)(2,1)} %get-tuple-element.189.refs_2_.refs_13_), channel_id=1, source_target_pairs={{0,8},{1,9},{2,10},{3,11},{4,20},{5,21},{6,22},{7,23},{8,0},{9,1},... | collective-permute-start | bytes 1572872 | tf_op jit(solution)/shard_map/ppermute | solution.py:253
  97.6 44.6 %collective-permute-start.16 = (bf16[256,2048]{1,0:T(8,128)(2,1)}, bf16[256,2048]{1,0:T(8,128)(2,1)}, u32[]{:S(2)}, u32[]{:S(2)}) collective-permute-start(bf16[256,2048]{1,0:T(8,128)(2,1)} %get-tuple-element.202.refs_3_), channel_id=1, source_target_pairs={{0,4},{1,5},{2,6},{3,7},{4,0},{5,1},{6,2},{7,3},{8,12},{9,13},{10,... | collective-permute-start | bytes 3145736 | tf_op jit(solution)/shard_map/ppermute | solution.py:253
  98.4 31.8 %collective-permute-start.14 = (bf16[256,2048]{1,0:T(8,128)(2,1)}, bf16[256,2048]{1,0:T(8,128)(2,1)}, u32[]{:S(2)}, u32[]{:S(2)}) collective-permute-start(bf16[256,2048]{1,0:T(8,128)(2,1)} %get-tuple-element.202.refs_3_), channel_id=1, source_target_pairs={{0,8},{1,9},{2,10},{3,11},{4,20},{5,21},{6,22},{7,23},{8,0},{9,1},... | collective-permute-start | bytes 3145736 | tf_op jit(solution)/shard_map/ppermute | solution.py:253
  112.5 17.7 %collective-permute-start.15 = (bf16[128,2048]{1,0:T(8,128)(2,1)}, bf16[128,2048]{1,0:T(8,128)(2,1)}, u32[]{:S(2)}, u32[]{:S(2)}) collective-permute-start(bf16[128,2048]{1,0:T(8,128)(2,1)} %get-tuple-element.203.refs_3_), channel_id=1, source_target_pairs={{0,16},{1,17},{2,18},{3,19},{4,12},{5,13},{6,14},{7,15},{8,24},{9,... | collective-permute-start | bytes 1572872 | tf_op jit(solution)/shard_map/ppermute | solution.py:253
  113.5 30.0 %collective-permute-start.18 = (bf16[256,2048]{1,0:T(8,128)(2,1)}, bf16[256,2048]{1,0:T(8,128)(2,1)}, u32[]{:S(2)}, u32[]{:S(2)}) collective-permute-start(bf16[256,2048]{1,0:T(8,128)(2,1)} %get-tuple-element.210.refs_3_), channel_id=1, source_target_pairs={{0,8},{1,9},{2,10},{3,11},{4,20},{5,21},{6,22},{7,23},{8,0},{9,1},... | collective-permute-start | bytes 3145736 | tf_op jit(solution)/shard_map/ppermute | solution.py:253
  132.5 33.7 %collective-permute-start.19 = (bf16[256,2048]{1,0:T(8,128)(2,1)}, bf16[256,2048]{1,0:T(8,128)(2,1)}, u32[]{:S(2)}, u32[]{:S(2)}) collective-permute-start(bf16[256,2048]{1,0:T(8,128)(2,1)} %get-tuple-element.210.refs_3_), channel_id=1, source_target_pairs={{0,4},{1,5},{2,6},{3,7},{4,0},{5,1},{6,2},{7,3},{8,12},{9,13},{10,... | collective-permute-start | bytes 3145736 | tf_op jit(solution)/shard_map/ppermute | solution.py:253
  133.0 57.9 %collective-permute-start.23 = (bf16[256,2048]{1,0:T(8,128)(2,1)}, bf16[256,2048]{1,0:T(8,128)(2,1)}, u32[]{:S(2)}, u32[]{:S(2)}) collective-permute-start(bf16[256,2048]{1,0:T(8,128)(2,1)} %get-tuple-element.219.refs_3_), channel_id=1, source_target_pairs={{0,4},{1,5},{2,6},{3,7},{4,0},{5,1},{6,2},{7,3},{8,12},{9,13},{10,... | collective-permute-start | bytes 3145736 | tf_op jit(solution)/shard_map/ppermute | solution.py:253
  142.2 24.6 %collective-permute-start.21 = (bf16[256,2048]{1,0:T(8,128)(2,1)}, bf16[256,2048]{1,0:T(8,128)(2,1)}, u32[]{:S(2)}, u32[]{:S(2)}) collective-permute-start(bf16[256,2048]{1,0:T(8,128)(2,1)} %get-tuple-element.219.refs_3_), channel_id=1, source_target_pairs={{0,8},{1,9},{2,10},{3,11},{4,20},{5,21},{6,22},{7,23},{8,0},{9,1},... | collective-permute-start | bytes 3145736 | tf_op jit(solution)/shard_map/ppermute | solution.py:253
  145.4 21.4 %collective-permute-start.22 = (bf16[128,2048]{1,0:T(8,128)(2,1)}, bf16[128,2048]{1,0:T(8,128)(2,1)}, u32[]{:S(2)}, u32[]{:S(2)}) collective-permute-start(bf16[128,2048]{1,0:T(8,128)(2,1)} %get-tuple-element.220.refs_4_), channel_id=1, source_target_pairs={{0,16},{1,17},{2,18},{3,19},{4,12},{5,13},{6,14},{7,15},{8,24},{9,... | collective-permute-start | bytes 1572872 | tf_op jit(solution)/shard_map/ppermute | solution.py:253
  146.3 20.5 %collective-permute-start.20 = (bf16[256,2048]{1,0:T(8,128)(2,1)}, bf16[256,2048]{1,0:T(8,128)(2,1)}, u32[]{:S(2)}, u32[]{:S(2)}) collective-permute-start(bf16[256,2048]{1,0:T(8,128)(2,1)} %get-tuple-element.218.refs_4_), channel_id=1, source_target_pairs={{0,4},{1,5},{2,6},{3,7},{4,0},{5,1},{6,2},{7,3},{8,12},{9,13},{10,... | collective-permute-start | bytes 3145736 | tf_op jit(solution)/shard_map/ppermute | solution.py:253
  166.2 25.2 %collective-permute-start.26 = (bf16[512,2048]{1,0:T(8,128)(2,1)}, bf16[512,2048]{1,0:T(8,128)(2,1)}, u32[]{:S(2)}, u32[]{:S(2)}) collective-permute-start(bf16[512,2048]{1,0:T(8,128)(2,1)} %get-tuple-element.229), channel_id=1, source_target_pairs={{0,4},{1,5},{2,6},{3,7},{4,0},{5,1},{6,2},{7,3},{8,12},{9,13},{10,... | collective-permute-start | bytes 6291464 | tf_op jit(solution)/shard_map/ppermute | solution.py:253
  169.1 22.4 %collective-permute-start.24 = (bf16[256,2048]{1,0:T(8,128)(2,1)}, bf16[256,2048]{1,0:T(8,128)(2,1)}, u32[]{:S(2)}, u32[]{:S(2)}) collective-permute-start(bf16[256,2048]{1,0:T(8,128)(2,1)} %get-tuple-element.227.refs_4_), channel_id=1, source_target_pairs={{0,4},{1,5},{2,6},{3,7},{4,0},{5,1},{6,2},{7,3},{8,12},{9,13},{10,... | collective-permute-start | bytes 3145736 | tf_op jit(solution)/shard_map/ppermute | solution.py:253
  169.2 22.3 %collective-permute-start.25 = (bf16[256,2048]{1,0:T(8,128)(2,1)}, bf16[256,2048]{1,0:T(8,128)(2,1)}, u32[]{:S(2)}, u32[]{:S(2)}) collective-permute-start(bf16[256,2048]{1,0:T(8,128)(2,1)} %get-tuple-element.221.refs_3_), channel_id=1, source_target_pairs={{0,8},{1,9},{2,10},{3,11},{4,20},{5,21},{6,22},{7,23},{8,0},{9,1},... | collective-permute-start | bytes 3145736 | tf_op jit(solution)/shard_map/ppermute | solution.py:253
  190.9 25.6 %collective-permute-start.30 = (bf16[512,2048]{1,0:T(8,128)(2,1)}, bf16[512,2048]{1,0:T(8,128)(2,1)}, u32[]{:S(2)}, u32[]{:S(2)}) collective-permute-start(bf16[512,2048]{1,0:T(8,128)(2,1)} %get-tuple-element.239), channel_id=1, source_target_pairs={{0,4},{1,5},{2,6},{3,7},{4,0},{5,1},{6,2},{7,3},{8,12},{9,13},{10,... | collective-permute-start | bytes 6291464 | tf_op jit(solution)/shard_map/ppermute | solution.py:253
  190.9 25.5 %collective-permute-start.27 = (bf16[256,2048]{1,0:T(8,128)(2,1)}, bf16[256,2048]{1,0:T(8,128)(2,1)}, u32[]{:S(2)}, u32[]{:S(2)}) collective-permute-start(bf16[256,2048]{1,0:T(8,128)(2,1)} %get-tuple-element.221.refs_3_), channel_id=1, source_target_pairs={{0,4},{1,5},{2,6},{3,7},{4,0},{5,1},{6,2},{7,3},{8,12},{9,13},{10,... | collective-permute-start | bytes 3145736 | tf_op jit(solution)/shard_map/ppermute | solution.py:253
  194.9 21.5 %collective-permute-start.29 = (bf16[256,2048]{1,0:T(8,128)(2,1)}, bf16[256,2048]{1,0:T(8,128)(2,1)}, u32[]{:S(2)}, u32[]{:S(2)}) collective-permute-start(bf16[256,2048]{1,0:T(8,128)(2,1)} %get-tuple-element.237), channel_id=1, source_target_pairs={{0,8},{1,9},{2,10},{3,11},{4,20},{5,21},{6,22},{7,23},{8,0},{9,1},... | collective-permute-start | bytes 3145736 | tf_op jit(solution)/shard_map/ppermute | solution.py:253
  195.5 20.9 %collective-permute-start.28 = (bf16[256,2048]{1,0:T(8,128)(2,1)}, bf16[256,2048]{1,0:T(8,128)(2,1)}, u32[]{:S(2)}, u32[]{:S(2)}) collective-permute-start(bf16[256,2048]{1,0:T(8,128)(2,1)} %get-tuple-element.230.refs_4_), channel_id=1, source_target_pairs={{0,4},{1,5},{2,6},{3,7},{4,0},{5,1},{6,2},{7,3},{8,12},{9,13},{10,... | collective-permute-start | bytes 3145736 | tf_op jit(solution)/shard_map/ppermute | solution.py:253
  215.9 35.1 %collective-permute-start.33 = (bf16[512,2048]{1,0:T(8,128)(2,1)}, bf16[512,2048]{1,0:T(8,128)(2,1)}, u32[]{:S(2)}, u32[]{:S(2)}) collective-permute-start(bf16[512,2048]{1,0:T(8,128)(2,1)} %get-tuple-element.252), channel_id=1, source_target_pairs={{0,4},{1,5},{2,6},{3,7},{4,0},{5,1},{6,2},{7,3},{8,12},{9,13},{10,... | collective-permute-start | bytes 6291464 | tf_op jit(solution)/shard_map/ppermute | solution.py:253
  221.0 29.9 %collective-permute-start.31 = (bf16[128,2048]{1,0:T(8,128)(2,1)}, bf16[128,2048]{1,0:T(8,128)(2,1)}, u32[]{:S(2)}, u32[]{:S(2)}) collective-permute-start(bf16[128,2048]{1,0:T(8,128)(2,1)} %get-tuple-element.248), channel_id=1, source_target_pairs={{0,16},{1,17},{2,18},{3,19},{4,12},{5,13},{6,14},{7,15},{8,24},{9,... | collective-permute-start | bytes 1572872 | tf_op jit(solution)/shard_map/ppermute | solution.py:253
  222.4 28.5 %collective-permute-start.32 = (bf16[256,2048]{1,0:T(8,128)(2,1)}, bf16[256,2048]{1,0:T(8,128)(2,1)}, u32[]{:S(2)}, u32[]{:S(2)}) collective-permute-start(bf16[256,2048]{1,0:T(8,128)(2,1)} %get-tuple-element.250), channel_id=1, source_target_pairs={{0,8},{1,9},{2,10},{3,11},{4,20},{5,21},{6,22},{7,23},{8,0},{9,1},... | collective-permute-start | bytes 3145736 | tf_op jit(solution)/shard_map/ppermute | solution.py:253
  250.8 49.1 %collective-permute-start.36 = (bf16[512,3072]{1,0:T(8,128)(2,1)}, bf16[512,3072]{1,0:T(8,128)(2,1)}, u32[]{:S(2)}, u32[]{:S(2)}) collective-permute-start(bf16[512,3072]{1,0:T(8,128)(2,1)} %get-tuple-element.262), channel_id=1, source_target_pairs={{0,4},{1,5},{2,6},{3,7},{4,0},{5,1},{6,2},{7,3},{8,12},{9,13},{10,... | collective-permute-start | bytes 9437192 | tf_op jit(solution)/shard_map/ppermute | solution.py:253
  256.2 104.0 %reduce-scatter.8.cloned.1.call-start = ((), (), s32[]{:S(2)}) async-start(), calls=%async_computation.9 | async-start | bytes 1310720 | tf_op jit(solution)/shard_map/reduce_scatter | solution.py:114
  256.2 43.7 %collective-permute-start.35 = (bf16[256,2048]{1,0:T(8,128)(2,1)}, bf16[256,2048]{1,0:T(8,128)(2,1)}, u32[]{:S(2)}, u32[]{:S(2)}) collective-permute-start(bf16[256,2048]{1,0:T(8,128)(2,1)} %get-tuple-element.260), channel_id=1, source_target_pairs={{0,8},{1,9},{2,10},{3,11},{4,20},{5,21},{6,22},{7,23},{8,0},{9,1},... | collective-permute-start | bytes 3145736 | tf_op jit(solution)/shard_map/ppermute | solution.py:253
  282.0 40.8 %collective-permute-start.39 = (f32[512,1536]{1,0:T(8,128)}, f32[512,1536]{1,0:T(8,128)}, u32[]{:S(2)}, u32[]{:S(2)}) collective-permute-start(f32[512,1536]{1,0:T(8,128)} %get-tuple-element.272), channel_id=1, source_target_pairs={{0,4},{1,5},{2,6},{3,7},{4,0},{5,1},{6,2},{7,3},{8,12},{9,13},{10,... | collective-permute-start | bytes 9437192 | tf_op jit(solution)/shard_map/ppermute | solution.py:253
  306.1 80.9 %reduce-scatter.10.cloned.1.call-start = ((), (), s32[]{:S(2)}) async-start(), calls=%async_computation.10 | async-start | bytes 1310720 | tf_op jit(solution)/shard_map/reduce_scatter | solution.py:114
  306.2 25.2 %collective-permute-start.38 = (bf16[256,3072]{1,0:T(8,128)(2,1)}, bf16[256,3072]{1,0:T(8,128)(2,1)}, u32[]{:S(2)}, u32[]{:S(2)}) collective-permute-start(bf16[256,3072]{1,0:T(8,128)(2,1)} %get-tuple-element.270), channel_id=1, source_target_pairs={{0,8},{1,9},{2,10},{3,11},{4,20},{5,21},{6,22},{7,23},{8,0},{9,1},... | collective-permute-start | bytes 4718600 | tf_op jit(solution)/shard_map/ppermute | solution.py:253
  306.2 16.6 %collective-permute-start.37 = (bf16[128,2048]{1,0:T(8,128)(2,1)}, bf16[128,2048]{1,0:T(8,128)(2,1)}, u32[]{:S(2)}, u32[]{:S(2)}) collective-permute-start(bf16[128,2048]{1,0:T(8,128)(2,1)} %get-tuple-element.268), channel_id=1, source_target_pairs={{0,16},{1,17},{2,18},{3,19},{4,12},{5,13},{6,14},{7,15},{8,24},{9,... | collective-permute-start | bytes 1572872 | tf_op jit(solution)/shard_map/ppermute | solution.py:253
  337.7 72.0 %reduce-scatter.12.cloned.1.call-start = ((), (), s32[]{:S(2)}) async-start(), calls=%async_computation.11 | async-start | bytes 983040 | tf_op jit(solution)/shard_map/reduce_scatter | solution.py:114
  337.8 19.2 %collective-permute-start.44 = (f32[512,768]{1,0:T(8,128)}, f32[512,768]{1,0:T(8,128)}, u32[]{:S(2)}, u32[]{:S(2)}) collective-permute-start(f32[512,768]{1,0:T(8,128)} %get-tuple-element.283), channel_id=1, source_target_pairs={{0,4},{1,5},{2,6},{3,7},{4,0},{5,1},{6,2},{7,3},{8,12},{9,13},{10,... | collective-permute-start | bytes 4718600 | tf_op jit(solution)/shard_map/ppermute | solution.py:253
  337.9 19.2 %collective-permute-start.41 = (bf16[128,1536]{1,0:T(8,128)(2,1)}, bf16[128,1536]{1,0:T(8,128)(2,1)}, u32[]{:S(2)}, u32[]{:S(2)}) collective-permute-start(bf16[128,1536]{1,0:T(8,128)(2,1)} %get-tuple-element.279), channel_id=1, source_target_pairs={{0,16},{1,17},{2,18},{3,19},{4,12},{5,13},{6,14},{7,15},{8,24},{9,... | collective-permute-start | bytes 1179656 | tf_op jit(solution)/shard_map/ppermute | solution.py:253
  339.1 17.9 %collective-permute-start.42 = (bf16[128,1536]{1,0:T(8,128)(2,1)}, bf16[128,1536]{1,0:T(8,128)(2,1)}, u32[]{:S(2)}, u32[]{:S(2)}) collective-permute-start(bf16[128,1536]{1,0:T(8,128)(2,1)} %get-tuple-element.280), channel_id=1, source_target_pairs={{0,8},{1,9},{2,10},{3,11},{4,20},{5,21},{6,22},{7,23},{8,0},{9,1},... | collective-permute-start | bytes 1179656 | tf_op jit(solution)/shard_map/ppermute | solution.py:253
  339.8 20.4 %collective-permute-start.43 = (bf16[128,1536]{1,0:T(8,128)(2,1)}, bf16[128,1536]{1,0:T(8,128)(2,1)}, u32[]{:S(2)}, u32[]{:S(2)}) collective-permute-start(bf16[128,1536]{1,0:T(8,128)(2,1)} %get-tuple-element.281), channel_id=1, source_target_pairs={{0,24},{1,25},{2,26},{3,27},{4,28},{5,29},{6,30},{7,31},{8,16},{9,... | collective-permute-start | bytes 1179656 | tf_op jit(solution)/shard_map/ppermute | solution.py:253
  341.4 25.7 %collective-permute-start.40 = (bf16[128,3072]{1,0:T(8,128)(2,1)}, bf16[128,3072]{1,0:T(8,128)(2,1)}, u32[]{:S(2)}, u32[]{:S(2)}) collective-permute-start(bf16[128,3072]{1,0:T(8,128)(2,1)} %get-tuple-element.277), channel_id=1, source_target_pairs={{0,16},{1,17},{2,18},{3,19},{4,12},{5,13},{6,14},{7,15},{8,24},{9,... | collective-permute-start | bytes 2359304 | tf_op jit(solution)/shard_map/ppermute | solution.py:253
  371.7 60.5 %reduce-scatter.14.cloned.1.call-start = ((), (), s32[]{:S(2)}) async-start(), calls=%async_computation.12 | async-start | bytes 983040 | tf_op jit(solution)/shard_map/reduce_scatter | solution.py:114
  371.7 15.3 %collective-permute-start.48 = (f32[512,768]{1,0:T(8,128)}, f32[512,768]{1,0:T(8,128)}, u32[]{:S(2)}, u32[]{:S(2)}) collective-permute-start(f32[512,768]{1,0:T(8,128)} %get-tuple-element.294), channel_id=1, source_target_pairs={{0,4},{1,5},{2,6},{3,7},{4,0},{5,1},{6,2},{7,3},{8,12},{9,13},{10,... | collective-permute-start | bytes 4718600 | tf_op jit(solution)/shard_map/ppermute | solution.py:253
  390.8 17.7 %collective-permute-start.49 = (bf16[128,768]{1,0:T(8,128)(2,1)}, bf16[128,768]{1,0:T(8,128)(2,1)S(1)}, u32[]{:S(2)}, u32[]{:S(2)}) collective-permute-start(bf16[128,768]{1,0:T(8,128)(2,1)} %get-tuple-element.299), channel_id=1, source_target_pairs={{0,16},{1,17},{2,18},{3,19},{4,12},{5,13},{6,14},{7,15},{8,24},{9,... | collective-permute-start | bytes 589832 | tf_op jit(solution)/shard_map/ppermute | solution.py:253
  391.9 17.8 %collective-permute-start.50 = (bf16[128,768]{1,0:T(8,128)(2,1)}, bf16[128,768]{1,0:T(8,128)(2,1)}, u32[]{:S(2)}, u32[]{:S(2)}) collective-permute-start(bf16[128,768]{1,0:T(8,128)(2,1)} %get-tuple-element.300), channel_id=1, source_target_pairs={{0,8},{1,9},{2,10},{3,11},{4,20},{5,21},{6,22},{7,23},{8,0},{9,1},... | collective-permute-start | bytes 589832 | tf_op jit(solution)/shard_map/ppermute | solution.py:253
  392.8 16.9 %collective-permute-start.51 = (bf16[128,768]{1,0:T(8,128)(2,1)}, bf16[128,768]{1,0:T(8,128)(2,1)}, u32[]{:S(2)}, u32[]{:S(2)}) collective-permute-start(bf16[128,768]{1,0:T(8,128)(2,1)} %get-tuple-element.301), channel_id=1, source_target_pairs={{0,24},{1,25},{2,26},{3,27},{4,28},{5,29},{6,30},{7,31},{8,16},{9,... | collective-permute-start | bytes 589832 | tf_op jit(solution)/shard_map/ppermute | solution.py:253
  396.0 20.1 %collective-permute-start.52 = (f32[32,768]{1,0:T(8,128)}, f32[32,768]{1,0:T(8,128)}, u32[]{:S(2)}, u32[]{:S(2)}) collective-permute-start(f32[32,768]{1,0:T(8,128)} %get-tuple-element.340), channel_id=1, source_target_pairs={{0,1},{1,0},{2,3},{3,2},{4,5},{5,4},{6,7},{7,6},{8,9},{9,8},{10,11... | collective-permute-start | bytes 294920 | tf_op jit(solution)/shard_map/ppermute | solution.py:120
  397.1 19.3 %collective-permute-start.54 = (f32[32,768]{1,0:T(8,128)}, f32[32,768]{1,0:T(8,128)}, u32[]{:S(2)}, u32[]{:S(2)}) collective-permute-start(f32[32,768]{1,0:T(8,128)} %get-tuple-element.341), channel_id=1, source_target_pairs={{0,3},{1,2},{2,1},{3,0},{4,7},{5,6},{6,5},{7,4},{8,11},{9,10},{10,... | collective-permute-start | bytes 294920 | tf_op jit(solution)/shard_map/ppermute | solution.py:120
  (30 other events, 217.3 us)
Sparse Core Ops, SparseCore 0:
  13.0 35.2 all-gather.2
  50.5 35.9 all-gather.4
  256.3 27.5 reduce-scatter.5
  306.2 26.4 reduce-scatter.7
  337.9 27.0 reduce-scatter.9
  371.8 22.6 reduce-scatter.11
  397.0 29.0 reduce-scatter.13
